TPU v7x, 32 devices: a whole 2x2x4 slice. The times are simulated.
32 devices in a mesh: wide: 16 (over z, x, core), narrow: 2 (over y).
Axes of the slice: x: 2, y: 2, z: 4, core: 2. Of those that a mesh axis runs over, the one named last changes fastest.
Arguments:
- tokens: bfloat16 [8192, 1536], P(('wide', 'narrow')), may hold values from -6 to 6
- cotangent: bfloat16 [8192, 1536], P(('wide', 'narrow')), may hold values from -6 to 6
- segments: int32 [16, 512], replicated, may hold values from 0 to 3, never falling along the last dimension, each value on 1 to 256 neighbouring positions
- owner_list: int32 [1440], replicated, may hold values from 0 to 1428, as said below
- masters: float32 [2880, 128, 128], P(('wide', 'narrow'))
- first_moment: float32 [2880, 128, 128], P(('wide', 'narrow'))
- second_moment: float32 [2880, 128, 128], P(('wide', 'narrow')), as said below
- left_basis: float32 [2880, 128, 128], P(('wide', 'narrow')), may hold values from -1 to 1, as said below
- right_basis: float32 [2880, 128, 128], P(('wide', 'narrow')), may hold values from -1 to 1, as said below
- gains: float32 [3072], P(('wide', 'narrow')), may hold values from 0.5 to 1.5
- gain_first: float32 [3072], P(('wide', 'narrow'))
- gain_second: float32 [3072], P(('wide', 'narrow')), as said below
- biases: float32 [2, 1024], P('narrow', 'wide'), may hold values from -1.5 to 1.5
- bias_first: float32 [2, 1024], P('narrow', 'wide')
- bias_second: float32 [2, 1024], P('narrow', 'wide'), as said below
Outputs:
- output: bfloat16 [8192, 1536], P(('wide', 'narrow'))
- input_grad: float32 [8192, 1536], P(('wide', 'narrow'))
- block_grad: float32 [2880, 128, 128], P(('wide', 'narrow'))
- new_masters: float32 [2880, 128, 128], P(('wide', 'narrow'))
- new_first: float32 [2880, 128, 128], P(('wide', 'narrow'))
- new_second: float32 [2880, 128, 128], P(('wide', 'narrow'))
- gain_grad: float32 [3072], P(('wide', 'narrow'))
- new_gains: float32 [3072], P(('wide', 'narrow'))
- new_gain_first: float32 [3072], P(('wide', 'narrow'))
- new_gain_second: float32 [3072], P(('wide', 'narrow'))
- bias_grad: float32 [2, 1024], P('narrow', 'wide')
- new_biases: float32 [2, 1024], P('narrow', 'wide')
- new_bias_first: float32 [2, 1024], P('narrow', 'wide')
- new_bias_second: float32 [2, 1024], P('narrow', 'wide')
Inputs may be any that keep to these rules, and one draw needn't show every extreme that they name: `owner_list`: each block number 0 to 1427 stands exactly once; the other entries equal 1428 and mark empty slots. `left_basis`: every 128 x 128 block is orthogonal. `right_basis`: every 128 x 128 block is orthogonal. `second_moment`: every entry is positive. `gain_second`: every entry is positive. `bias_second`: every entry is positive.
All inputs are finite; a program needn't handle non-finite values.
Results may differ from a plain program's by a relative error of at most 0.012.
Values may be sent and summed in bfloat16 or wider, within the bound.
A program may use at most 384 MiB of HBM per device.

v0:
```python
import jax
import jax.numpy as jnp
from jax import lax
from jax.sharding import PartitionSpec as P

D = 1536
FF = 8960
HEADS = 12
KV_HEADS = 2
HEAD_DIM = 128
BLK = 128
STEP_COUNT = 5


beta_first = 0.95
beta_second = 0.95
adam_eps = 1e-08
rate_blocks = 0.03
rate_small = 0.4
rate_gains = 0.6
norm_eps = 1e-06
rope_base = 10000.0
masked_score = -1e30


def piece_layout(narrow_count):
    row_blocks = D // BLK
    query_cols = HEADS * HEAD_DIM // narrow_count // BLK
    pair_cols = KV_HEADS * HEAD_DIM // narrow_count // BLK
    hidden_cols = FF // narrow_count // BLK
    shapes = [
        (row_blocks, query_cols),
        (row_blocks, pair_cols),
        (row_blocks, pair_cols),
        (query_cols, row_blocks),
        (row_blocks, hidden_cols),
        (row_blocks, hidden_cols),
        (hidden_cols, row_blocks),
    ]
    left_starts = [
        0,
        0,
        0,
        row_blocks,
        row_blocks + query_cols,
        row_blocks + query_cols,
        2 * row_blocks + query_cols,
    ]
    right_base = query_cols + 2 * pair_cols
    right_starts = [
        0,
        query_cols,
        query_cols + pair_cols,
        right_base,
        right_base + row_blocks,
        right_base + row_blocks + hidden_cols,
        right_base + row_blocks + 2 * hidden_cols,
    ]
    bases = []
    running = 0
    for shape_here in shapes:
        bases.append(running)
        running += shape_here[0] * shape_here[1]
    return (shapes, bases, left_starts, right_starts, running)


def apply_blocks(inputs_low, weight_blocks):
    rows_here = inputs_low.shape[0]
    grouped = inputs_low.reshape(rows_here, weight_blocks.shape[0], BLK)
    result = jnp.einsum("tra,rcab->tcb", grouped, weight_blocks, preferred_element_type=jnp.float32)
    return result.reshape(rows_here, weight_blocks.shape[1] * BLK)


def apply_back(grads_low, weight_blocks):
    rows_here = grads_low.shape[0]
    grouped = grads_low.reshape(rows_here, weight_blocks.shape[1], BLK)
    result = jnp.einsum("tcb,rcab->tra", grouped, weight_blocks, preferred_element_type=jnp.float32)
    return result.reshape(rows_here, weight_blocks.shape[0] * BLK)


def block_terms(inputs_low, grads_low, row_blocks, col_blocks):
    rows_here = inputs_low.shape[0]
    result = jnp.einsum(
        "tra,tcb->rcab",
        inputs_low.reshape(rows_here, row_blocks, BLK),
        grads_low.reshape(rows_here, col_blocks, BLK),
        preferred_element_type=jnp.float32,
    )
    return result.reshape(row_blocks * col_blocks, BLK, BLK)


def rotate_half(vector):
    middle = vector.shape[-1] // 2
    return jnp.concatenate([-vector[..., middle:], vector[..., :middle]], axis=-1)


def rope_tables(segment_row):
    token_index = jnp.arange(segment_row.shape[0], dtype=jnp.int32)
    changed = jnp.concatenate([jnp.ones((1,), dtype=bool), segment_row[1:] != segment_row[:-1]])
    begins = lax.cummax(jnp.where(changed, token_index, jnp.zeros_like(token_index)), axis=0)
    places = (token_index - begins).astype(jnp.float32)
    frequency = rope_base ** (-(jnp.arange(HEAD_DIM // 2, dtype=jnp.float32) * 2.0) / HEAD_DIM)
    angles = places[:, None] * frequency[None, :]
    cosine = jnp.concatenate([jnp.cos(angles), jnp.cos(angles)], axis=-1)[:, None, :]
    sine_table = jnp.concatenate([jnp.sin(angles), jnp.sin(angles)], axis=-1)[:, None, :]
    return (cosine, sine_table)


def rms_parts(values):
    inverse = lax.rsqrt(jnp.mean(values * values, axis=-1, keepdims=True) + norm_eps)
    return (inverse, values * inverse)


def norm_back(grad_scaled, normed, inverse):
    return inverse * (grad_scaled - normed * jnp.mean(grad_scaled * normed, axis=-1, keepdims=True))


def masked_scores(grouped, keys_all, allowed):
    scores = jnp.einsum(
        "ikgd,jkd->kgij", grouped, keys_all, preferred_element_type=jnp.float32
    ) * HEAD_DIM ** (-0.5)
    return jnp.where(allowed, scores, masked_score)


def adam_small(param_now, gradient, first_now, second_now, rate_here):
    first_new = beta_first * first_now + (1.0 - beta_first) * gradient
    second_new = beta_second * second_now + (1.0 - beta_second) * gradient * gradient
    first_fix = 1.0 - beta_first**STEP_COUNT
    second_fix = 1.0 - beta_second**STEP_COUNT
    param_new = param_now - rate_here * (first_new / first_fix) / (
        jnp.sqrt(second_new / second_fix) + adam_eps
    )
    return (param_new, first_new, second_new)


def body(
    tokens,
    cotangent,
    segments,
    owner_list,
    masters,
    first_moment,
    second_moment,
    left_basis,
    right_basis,
    gains,
    gain_first,
    gain_second,
    biases,
    bias_first,
    bias_second,
):
    narrow_count = lax.axis_size("narrow")
    shapes, bases, left_starts, right_starts, block_total = piece_layout(narrow_count)
    query_width = HEADS * HEAD_DIM // narrow_count
    pair_width = KV_HEADS * HEAD_DIM // narrow_count
    query_heads = HEADS // narrow_count
    pair_heads = KV_HEADS // narrow_count
    group_size = HEADS // KV_HEADS
    slots_half = owner_list.shape[0]
    scaling = HEAD_DIM ** (-0.5)
    row_length = tokens.shape[0] * narrow_count
    gathered, bias_full = (
        lax.all_gather(masters.astype(jnp.bfloat16), "wide", axis=0, tiled=True),
        lax.all_gather(biases.reshape(-1).astype(jnp.bfloat16), "wide", axis=0, tiled=True),
    )
    gain_full = lax.all_gather(gains, ("wide", "narrow"), axis=0, tiled=True)
    slot_of = (
        jnp.zeros((block_total + 1,), jnp.int32)
        .at[owner_list]
        .set(jnp.arange(slots_half, dtype=jnp.int32))[:block_total]
    )
    stacked = jnp.take(gathered, slot_of, axis=0)
    weights_list = []
    for kind_index in range(7):
        rows_here, cols_here = shapes[kind_index]
        weights_list.append(
            stacked[bases[kind_index] : bases[kind_index] + rows_here * cols_here].reshape(
                rows_here, cols_here, BLK, BLK
            )
        )
    w_query, w_key, w_value, w_out, w_gate, w_up, w_down = weights_list
    bias_query = bias_full[:query_width].astype(jnp.float32)
    bias_key = bias_full[query_width : query_width + pair_width].astype(jnp.float32)
    bias_value = bias_full[query_width + pair_width :].astype(jnp.float32)
    gain_one = gain_full[:D]
    gain_two = gain_full[D:]
    wide_index = lax.axis_index("wide")
    segment_row = lax.dynamic_index_in_dim(segments, wide_index, 0, keepdims=False)
    cosine, sine_table = rope_tables(segment_row)
    token_index = jnp.arange(row_length, dtype=jnp.int32)
    allowed = (segment_row[:, None] == segment_row[None, :]) & (
        token_index[:, None] >= token_index[None, :]
    )
    hidden_in = tokens.astype(jnp.float32)
    inverse_one, normed_one = rms_parts(hidden_in)
    norm_one_row = lax.all_gather(
        (normed_one * gain_one).astype(jnp.bfloat16), "narrow", axis=0, tiled=True
    )
    queries_pre = (apply_blocks(norm_one_row, w_query) + bias_query).reshape(
        row_length, query_heads, HEAD_DIM
    )
    keys_pre = (apply_blocks(norm_one_row, w_key) + bias_key).reshape(
        row_length, pair_heads, HEAD_DIM
    )
    values = (
        (apply_blocks(norm_one_row, w_value) + bias_value)
        .astype(jnp.bfloat16)
        .reshape(row_length, pair_heads, HEAD_DIM)
    )
    queries_rot = (queries_pre * cosine + rotate_half(queries_pre) * sine_table).astype(
        jnp.bfloat16
    )
    keys_rot = (keys_pre * cosine + rotate_half(keys_pre) * sine_table).astype(jnp.bfloat16)
    grouped = queries_rot.reshape(row_length, pair_heads, group_size, HEAD_DIM)
    scores = masked_scores(grouped, keys_rot, allowed)
    peak = jnp.max(scores, axis=-1, keepdims=True)
    expo_scores = jnp.exp(scores - peak)
    total_sum = jnp.sum(expo_scores, axis=-1, keepdims=True)
    log_total = peak + jnp.log(total_sum)
    probs_low = (expo_scores / total_sum).astype(jnp.bfloat16)
    mixed_heads = jnp.einsum(
        "kgij,jkd->ikgd", probs_low, values, preferred_element_type=jnp.float32
    )
    mixed_heads = mixed_heads.reshape(row_length, query_width).astype(jnp.bfloat16)
    attention_part = apply_blocks(mixed_heads, w_out)
    attention_local = lax.psum_scatter(attention_part, "narrow", scatter_dimension=0, tiled=True)
    residual = hidden_in + attention_local
    inverse_two, normed_two = rms_parts(residual)
    norm_two_row = lax.all_gather(
        (normed_two * gain_two).astype(jnp.bfloat16), "narrow", axis=0, tiled=True
    )
    gate_pre = apply_blocks(norm_two_row, w_gate)
    upper_pre = apply_blocks(norm_two_row, w_up)
    sigmoid_gate = jax.nn.sigmoid(gate_pre)
    silu_gate = gate_pre * sigmoid_gate
    active = (silu_gate * upper_pre).astype(jnp.bfloat16)
    branch_part = apply_blocks(active, w_down)
    branch_local = lax.psum_scatter(
        branch_part.astype(jnp.bfloat16), "narrow", scatter_dimension=0, tiled=True
    ).astype(jnp.float32)
    output = (residual + branch_local).astype(jnp.bfloat16)
    cotangent_row = lax.all_gather(cotangent, "narrow", axis=0, tiled=True)
    grad_active = apply_back(cotangent_row, w_down)
    grad_gate = (
        grad_active * upper_pre * sigmoid_gate * (1.0 + gate_pre * (1.0 - sigmoid_gate))
    ).astype(jnp.bfloat16)
    grad_upper = (grad_active * silu_gate).astype(jnp.bfloat16)
    grad_norm_two_part = apply_back(grad_gate, w_gate) + apply_back(grad_upper, w_up)
    grad_norm_two = lax.psum_scatter(grad_norm_two_part, "narrow", scatter_dimension=0, tiled=True)
    gain_two_part = jnp.sum(grad_norm_two * normed_two, axis=0)
    grad_residual = cotangent.astype(jnp.float32) + norm_back(
        grad_norm_two * gain_two, normed_two, inverse_two
    )
    grad_attention_row = lax.all_gather(
        grad_residual.astype(jnp.bfloat16), "narrow", axis=0, tiled=True
    )
    grad_mixed = (
        apply_back(grad_attention_row, w_out)
        .astype(jnp.bfloat16)
        .reshape(row_length, pair_heads, group_size, HEAD_DIM)
    )
    scores_again = masked_scores(grouped, keys_rot, allowed)
    weights_soft = jnp.exp(scores_again - log_total)
    probs_again = weights_soft.astype(jnp.bfloat16)
    grad_probs = jnp.einsum(
        "ikgd,jkd->kgij", grad_mixed, values, preferred_element_type=jnp.float32
    )
    row_dot = jnp.sum(weights_soft * grad_probs, axis=-1, keepdims=True)
    grad_scores = (weights_soft * (grad_probs - row_dot)).astype(jnp.bfloat16)
    grad_queries_rot = (
        jnp.einsum("kgij,jkd->ikgd", grad_scores, keys_rot, preferred_element_type=jnp.float32)
        * scaling
    )
    grad_keys_rot = (
        jnp.einsum("kgij,ikgd->jkd", grad_scores, grouped, preferred_element_type=jnp.float32)
        * scaling
    )
    grad_values_all = jnp.einsum(
        "kgij,ikgd->jkd", probs_again, grad_mixed, preferred_element_type=jnp.float32
    )
    grad_values = grad_values_all.reshape(row_length, pair_width).astype(jnp.bfloat16)
    grad_queries_rot = grad_queries_rot.reshape(row_length, query_heads, HEAD_DIM)
    grad_queries = (
        (grad_queries_rot * cosine - rotate_half(grad_queries_rot) * sine_table)
        .reshape(row_length, query_width)
        .astype(jnp.bfloat16)
    )
    grad_keys = (
        (grad_keys_rot * cosine - rotate_half(grad_keys_rot) * sine_table)
        .reshape(row_length, pair_width)
        .astype(jnp.bfloat16)
    )
    grad_norm_one_part = (
        apply_back(grad_queries, w_query)
        + apply_back(grad_keys, w_key)
        + apply_back(grad_values, w_value)
    )
    grad_norm_one = lax.psum_scatter(grad_norm_one_part, "narrow", scatter_dimension=0, tiled=True)
    gain_one_part = jnp.sum(grad_norm_one * normed_one, axis=0)
    input_grad = grad_residual + norm_back(grad_norm_one * gain_one, normed_one, inverse_one)
    bias_part = jnp.concatenate(
        [
            jnp.sum(grad_queries.astype(jnp.float32), axis=0),
            jnp.sum(grad_keys.astype(jnp.float32), axis=0),
            jnp.sum(grad_values.astype(jnp.float32), axis=0),
        ]
    )
    inputs_by_kind = [
        norm_one_row,
        norm_one_row,
        norm_one_row,
        mixed_heads,
        norm_two_row,
        norm_two_row,
        active,
    ]
    grads_by_kind = [
        grad_queries,
        grad_keys,
        grad_values,
        grad_attention_row,
        grad_gate,
        grad_upper,
        cotangent_row,
    ]
    term_all = jnp.zeros((slots_half, BLK, BLK), jnp.float32)
    for kind_index in range(7):
        rows_here, cols_here = shapes[kind_index]
        blocks_here = block_terms(
            inputs_by_kind[kind_index], grads_by_kind[kind_index], rows_here, cols_here
        )
        term_all = term_all.at[
            slot_of[bases[kind_index] : bases[kind_index] + rows_here * cols_here]
        ].set(blocks_here)
    reduced, bias_reduced = (
        lax.psum_scatter(term_all, "wide", scatter_dimension=0, tiled=True),
        lax.psum_scatter(bias_part, "wide", scatter_dimension=0, tiled=True),
    )
    gain_reduced = lax.psum_scatter(
        jnp.concatenate([gain_one_part, gain_two_part]),
        ("wide", "narrow"),
        scatter_dimension=0,
        tiled=True,
    )
    highest = lax.Precision.HIGHEST
    rotated = jnp.matmul(
        jnp.swapaxes(left_basis, 1, 2),
        jnp.matmul(reduced, right_basis, precision=highest),
        precision=highest,
    )
    new_first = beta_first * first_moment + (1.0 - beta_first) * rotated
    new_second = beta_second * second_moment + (1.0 - beta_second) * rotated * rotated
    first_fix = 1.0 - beta_first**STEP_COUNT
    second_fix = 1.0 - beta_second**STEP_COUNT
    normalized = new_first / first_fix / (jnp.sqrt(new_second / second_fix) + adam_eps)
    update = jnp.matmul(
        left_basis,
        jnp.matmul(normalized, jnp.swapaxes(right_basis, 1, 2), precision=highest),
        precision=highest,
    )
    new_masters = masters - rate_blocks * update
    new_gains, new_gain_first, new_gain_second = adam_small(
        gains, gain_reduced, gain_first, gain_second, rate_gains
    )
    bias_grad = bias_reduced.reshape(biases.shape)
    new_biases, new_bias_first, new_bias_second = adam_small(
        biases, bias_grad, bias_first, bias_second, rate_small
    )
    return (
        output,
        input_grad,
        reduced,
        new_masters,
        new_first,
        new_second,
        gain_reduced,
        new_gains,
        new_gain_first,
        new_gain_second,
        bias_grad,
        new_biases,
        new_bias_first,
        new_bias_second,
    )


def solution(mesh):
    in_specs = (
        P(("wide", "narrow"), None),
        P(("wide", "narrow"), None),
        P(),
        P(),
        P(("wide", "narrow"), None, None),
        P(("wide", "narrow"), None, None),
        P(("wide", "narrow"), None, None),
        P(("wide", "narrow"), None, None),
        P(("wide", "narrow"), None, None),
        P(("wide", "narrow")),
        P(("wide", "narrow")),
        P(("wide", "narrow")),
        P("narrow", "wide"),
        P("narrow", "wide"),
        P("narrow", "wide"),
    )
    out_specs = (
        P(("wide", "narrow"), None),
        P(("wide", "narrow"), None),
        P(("wide", "narrow"), None, None),
        P(("wide", "narrow"), None, None),
        P(("wide", "narrow"), None, None),
        P(("wide", "narrow"), None, None),
        P(("wide", "narrow")),
        P(("wide", "narrow")),
        P(("wide", "narrow")),
        P(("wide", "narrow")),
        P("narrow", "wide"),
        P("narrow", "wide"),
        P("narrow", "wide"),
        P("narrow", "wide"),
    )
    return jax.shard_map(body, mesh=mesh, in_specs=in_specs, out_specs=out_specs, check_vma=False)
```

profile of v0, /device:TPU:0, one launch (start us, length us, event | category | flops | bytes accessed | tf_op | source)
XLA Modules:
  0.0 2157.0 jit_solution(17512884004349208721)
XLA Ops:
  8.1 42.1 %all-reduce = f32[3072]{0:T(1024)S(1)} all-reduce(f32[3072]{0:T(1024)S(1)} %dynamic-update-slice), channel_id=1, replica_groups=mesh['wide'=16,'narrow'=2] {'wide','narrow'}, use_global_device_ids=true, to_apply=%add | all-reduce | flops 3072 | bytes 24576
  54.6 4.9 convert_element_type.149
  62.5 31.2 %all-reduce.1 = bf16[1024]{0:T(1024)(128)(2,1)S(1)} all-reduce(bf16[1024]{0:T(1024)(128)(2,1)S(1)} %dynamic-update-slice.1), channel_id=2, replica_groups=mesh['wide'=16,'narrow'=2] {'wide'}, use_global_device_ids=true, to_apply=%add.1 | all-reduce | flops 1024 | bytes 4096
  93.8 7.8 scatter_custom_fusion
  105.8 210.4 %all-gather.9.cloned.1.call-done = bf16[1440,128,128]{2,1,0:T(8,128)(2,1)} async-done(((bf16[90,128,128]{2,1,0:T(8,128)(2,1)}), bf16[1440,128,128]{2,1,0:T(8,128)(2,1)}) %all-gather.9.cloned.1.call-update) | async-done | bytes 47185936 | tf_op jit(solution)/shard_map/all_gather | solution.py:164
  316.2 38.1 %gather_fusion = bf16[1428,128,128]{2,1,0:T(8,128)(2,1)} fusion(bf16[1440,128,128]{2,1,0:T(8,128)(2,1)} %all-gather.9.cloned.1.call-done, s32[2048]{0:T(1024)S(1)} %pad_clamp_fusion), kind=kCustom, calls=%fused_computation | custom fusion | bytes 93591120 | tf_op jit(solution)/shard_map/jit(_take)/gather | solution.py:173
  354.3 31.1 %broadcast_select_fusion = bf16[1428,128,128]{2,1,0:T(8,128)(2,1)} fusion(bf16[1428,128,128]{2,1,0:T(8,128)(2,1)} %gather_fusion, pred[1428]{0:T(1024)(128)(4,1)S(1)} %compare_and_fusion), kind=kLoop, calls=%fused_computation.9 | loop fusion | flops 23396352 | bytes 93586832 | tf_op jit(solution)/shard_map/jit(_take)/select_n | solution.py:173
  385.5 6.3 fusion.107
  394.0 4.3 copy.137
  398.3 4.2 bitcast_add_fusion
  408.0 4.6 copy.144
  421.5 3.1 convolution_bitcast_fusion.6
  425.9 28.8 %fusion.106 = (bf16[420,128,128]{2,1,0:T(8,128)(2,1)}, bf16[420,128,128]{2,1,0:T(8,128)(2,1)}, bf16[420,128,128]{2,1,0:T(8,128)(2,1)}) fusion(bf16[1428,128,128]{2,1,0:T(8,128)(2,1)} %broadcast_select_fusion), kind=kLoop, calls=%fused_computation.203 | loop fusion | bytes 82575360 | tf_op jit(solution)/shard_map/slice | solution.py:178
  454.7 13.4 reduce-scatter.6.cloned.1.call-done
  471.2 26.2 %all-gather.13.cloned.1.call-done = bf16[512,1536]{0,1:T(8,128)(2,1)} async-done(((bf16[256,1536]{0,1:T(8,128)(2,1)}), bf16[512,1536]{0,1:T(8,128)(2,1)}) %all-gather.13.cloned.1.call-update) | async-done | bytes 1572880 | tf_op jit(solution)/shard_map/all_gather | solution.py:243
  497.4 13.2 fusion.112
  510.6 9.5 copy.156
  520.0 18.4 copy.147
  538.4 18.4 copy.149
  556.8 12.9 copy.162
  569.7 12.9 copy.158
  584.3 13.5 fusion.111
  597.8 20.8 fusion.3
  618.6 6.5 copy.161
  625.2 6.5 copy.157
  631.7 12.4 convolution_bitcast_fusion.3
  644.1 12.0 fusion.20
  656.2 43.4 %reduce-scatter.10.cloned.1.call-done = f32[256,1536]{1,0:T(8,128)} async-done(((f32[512,1536]{1,0:T(8,128)}), f32[256,1536]{1,0:T(8,128)}) %reduce-scatter.10.cloned.1.call-update) | async-done | bytes 1572880 | tf_op jit(solution)/shard_map/reduce_scatter | solution.py:250
  704.9 3.5 copy.170
  712.2 20.0 all-gather.15.cloned.1.call-done
  735.0 4.6 bitcast_convert_fusion
  741.0 4.2 fusion.8
  759.5 17.9 copy.152
  777.4 6.5 copy.151
  783.9 13.2 fusion.28
  797.2 14.2 convolution_bitcast_fusion.1
  811.3 13.9 convolution_bitcast_fusion
  825.2 27.4 %copy.183 = f32[12,35,128,128]{3,2,1,0:T(8,128)} copy(f32[12,35,128,128]{2,3,0,1:T(8,128)} %convolution_bitcast_fusion.1) | data formatting | bytes 55050240 | tf_op jit(solution)/shard_map/tra,tcb->rcab/transpose | solution.py:83
  852.6 27.5 %copy.185 = f32[12,35,128,128]{3,2,1,0:T(8,128)} copy(f32[12,35,128,128]{2,3,0,1:T(8,128)} %convolution_bitcast_fusion) | data formatting | bytes 55050240 | tf_op jit(solution)/shard_map/tra,tcb->rcab/transpose | solution.py:83
  880.1 13.8 fusion.114
  895.3 3.0 convolution_bitcast_fusion.8
  898.3 6.1 copy.175
  911.2 4.2 convolution_bitcast_fusion.7
  915.3 6.0 copy.181
  921.4 29.5 %broadcast_in_dim.88 = f32[1440,128,128]{2,1,0:T(8,128)} broadcast(f32[]{:T(128)} %constant.28.clone.1), dimensions={} | broadcast | bytes 94371840 | tf_op jit(solution)/shard_map/broadcast_in_dim | solution.py:327
  950.9 14.4 scatter_fusion
  971.1 14.4 scatter_fusion.3
  985.5 76.8 %scatter_fusion.4 = f32[1440,128,128]{2,1,0:T(8,128)} fusion(f32[1440,128,128]{2,1,0:T(8,128)} %scatter_fusion.3, s32[420]{0:T(512)S(1)} %get-tuple-element.105, f32[420,128,128]{2,1,0:T(8,128)} %bitcast.381), kind=kCustom, calls=%fused_computation.6 | custom fusion | bytes 82577040 | tf_op jit(solution)/shard_map/scatter | solution.py:335
  1062.3 77.0 %scatter_fusion.5 = f32[1440,128,128]{2,1,0:T(8,128)} fusion(f32[1440,128,128]{2,1,0:T(8,128)} %scatter_fusion.4, s32[420]{0:T(512)S(1)} %copy-done.61, f32[420,128,128]{2,1,0:T(8,128)} %bitcast.380), kind=kCustom, calls=%fused_computation.7 | custom fusion | bytes 82577040 | tf_op jit(solution)/shard_map/scatter | solution.py:335
  1139.3 77.5 %scatter_fusion.6 = f32[1440,128,128]{2,1,0:T(8,128)} fusion(f32[1440,128,128]{2,1,0:T(8,128)} %scatter_fusion.5, s32[420]{0:T(512)S(1)} %copy-done.60, f32[420,128,128]{2,1,0:T(8,128)} %bitcast.384), kind=kCustom, calls=%fused_computation.8 | custom fusion | bytes 82577040 | tf_op jit(solution)/shard_map/scatter | solution.py:335
  1216.8 6.6 copy.192
  1223.3 6.9 copy.187
  1230.4 8.5 copy.189
  1239.7 33.8 %all-reduce.3 = f32[1024]{0:T(1024)S(1)} all-reduce(f32[1024]{0:T(1024)S(1)} %pad_maximum_fusion.3), channel_id=9, replica_groups=mesh['wide'=16,'narrow'=2] {'wide'}, use_global_device_ids=true, to_apply=%region_28.29.clone | all-reduce | flops 1024 | bytes 8192
  1277.1 37.1 %all-reduce.2 = f32[3072]{0:T(1024)S(1)} all-reduce(f32[3072]{0:T(1024)S(1)} %pad_maximum_fusion.2), channel_id=8, replica_groups=mesh['wide'=16,'narrow'=2] {'wide','narrow'}, use_global_device_ids=true, to_apply=%region_24.25.clone | all-reduce | flops 3072 | bytes 24576
  1314.8 5.4 fusion.39
  1320.2 752.9 %reduce-scatter.14.cloned.1.call-done = f32[90,128,128]{2,1,0:T(8,128)} async-done(((f32[1440,128,128]{2,1,0:T(8,128)}), f32[90,128,128]{2,1,0:T(8,128)}) %reduce-scatter.14.cloned.1.call-update) | async-done | bytes 5898256 | tf_op jit(solution)/shard_map/reduce_scatter | solution.py:337
  2073.1 12.4 fusion.115
  2085.6 13.5 multiply_add_fusion
  2099.1 6.4 copy.194
  2105.4 14.2 fusion.12
  2119.7 6.4 copy.195
  2126.0 17.6 bitcast_subtract_fusion.1
  2143.6 6.4 copy.193
  (260 shorter events, 79.8 us)
Async XLA Ops:
  7.2 96.8 %all-gather.7.cloned.1.call-start = ((), (), s32[]{:S(2)}) async-start(), calls=%async_computation.5 | async-start | bytes 2359296 | tf_op jit(solution)/shard_map/all_gather | solution.py:197
  50.2 651.8 %copy-start.40 = (f32[1536]{0:T(1024)}, f32[1536]{0:T(1024)S(1)}, u32[]{:S(2)}) copy-start(f32[1536]{0:T(1024)S(1)} %get-tuple-element.101) | copy-start | bytes 18436
  54.5 6.5 copy-start.66
  54.5 7.7 copy-start.70
  54.5 39.2 %copy-start.62 = (s32[1440]{0:T(1024)S(1)}, s32[1440]{0:T(1024)}, u32[]{:S(2)}) copy-start(s32[1440]{0:T(1024)} %param.18) | copy-start | bytes 17284
  54.6 261.6 %all-gather.9.cloned.1.call-start = ((), (), s32[]{:S(2)}) async-start(), calls=%async_computation.6 | async-start | bytes 50135040 | tf_op jit(solution)/shard_map/all_gather | solution.py:164
  59.5 408.6 %reduce-scatter.6.cloned.1.call-start = ((), (), s32[]{:S(2)}) async-start(), calls=%async_computation.7 | async-start | bytes 4718592 | tf_op jit(solution)/shard_map/reduce_scatter | solution.py:227
  103.8 308.8 %copy-start.30 = (f32[512,64]{0,1:T(8,128)}, f32[512,64]{0,1:T(8,128)S(1)}, u32[]{:S(2)}) copy-start(f32[512,64]{0,1:T(8,128)S(1)} %get-tuple-element.114) | copy-start | bytes 393220
  105.8 300.0 %copy-start.3 = (bf16[512,1536]{0,1:T(8,128)(2,1)}, bf16[512,1536]{0,1:T(8,128)(2,1)S(1)}, u32[]{:S(2)}) copy-start(bf16[512,1536]{0,1:T(8,128)(2,1)S(1)} %copy.133) | copy-start | bytes 4718596
  393.2 5.1 copy-start.37
  408.0 6.6 copy-start.18
  408.0 6.6 copy-start.19
  417.3 2.7 copy-start.42
  418.4 3.1 copy-start.23
  421.5 3.2 copy-start.12
  424.6 72.7 %all-gather.13.cloned.1.call-start = ((), (), s32[]{:S(2)}) async-start(), calls=%async_computation.10 | async-start | bytes 2359296 | tf_op jit(solution)/shard_map/all_gather | solution.py:243
  425.9 42.2 %copy-start.6 = (bf16[256,1536]{1,0:T(8,128)(2,1)S(1)}, bf16[256,1536]{1,0:T(8,128)(2,1)}, u32[]{:S(2)}) copy-start(bf16[256,1536]{1,0:T(8,128)(2,1)} %param.15) | copy-start | bytes 2359300
  425.9 156.7 %all-gather.11.cloned.1.call-start = ((), (), s32[]{:S(2)}) async-start(), calls=%async_computation.8 | async-start | bytes 2359296 | tf_op jit(solution)/shard_map/all_gather | solution.py:230
  469.8 232.3 %copy-start.1 = (f32[256,1536]{1,0:T(8,128)}, f32[256,1536]{1,0:T(8,128)S(1)}, u32[]{:S(2)}) copy-start(f32[256,1536]{1,0:T(8,128)S(1)} %get-tuple-element.72) | copy-start | bytes 4718596
  469.8 232.3 %copy-start.53 = (f32[256]{0:T(256)}, f32[256]{0:T(256)S(1)}, u32[]{:S(2)}) copy-start(f32[256]{0:T(256)S(1)} %add_rsqrt_fusion) | copy-start | bytes 3076
  471.1 228.5 %reduce-scatter.10.cloned.1.call-start = ((), (), s32[]{:S(2)}) async-start(), calls=%async_computation.11 | async-start | bytes 4718592 | tf_op jit(solution)/shard_map/reduce_scatter | solution.py:250
  584.3 13.5 copy-start.24
  631.7 12.4 copy-start.16
  656.1 46.0 %copy-start.13 = (bf16[256,1536]{1,0:T(8,128)(2,1)S(1)}, bf16[256,1536]{1,0:T(8,128)(2,1)}, u32[]{:S(2)}) copy-start(bf16[256,1536]{1,0:T(8,128)(2,1)} %param.16) | copy-start | bytes 2359300
  656.1 76.1 %all-gather.15.cloned.1.call-start = ((), (), s32[]{:S(2)}) async-start(), calls=%async_computation.12 | async-start | bytes 2359296 | tf_op jit(solution)/shard_map/all_gather | solution.py:255
  702.1 6.3 copy-start.58
  704.8 3.6 copy-start.5
  704.9 569.9 %reduce-scatter.12.cloned.1.call-start = ((), (), s32[]{:S(2)}) async-start(), calls=%async_computation.13 | async-start | bytes 4718592 | tf_op jit(solution)/shard_map/reduce_scatter | solution.py:299
  704.9 5.1 copy-start.43
  704.9 5.1 copy-start.51
  735.0 6.0 copy-start.45
  735.0 10.3 slice-start
  741.0 4.3 slice-start.1
  748.2 3.4 copy-start.8
  758.2 556.6 %reduce-scatter.8.cloned.1.call-start = ((), (), s32[]{:S(2)}) async-start(), calls=%async_computation.9 | async-start | bytes 2359296 | tf_op jit(solution)/shard_map/reduce_scatter | solution.py:239
  783.9 13.2 copy-start.25
  797.1 1276.0 %reduce-scatter.14.cloned.1.call-start = ((), (), s32[]{:S(2)}) async-start(), calls=%async_computation.14 | async-start | bytes 100270080 | tf_op jit(solution)/shard_map/reduce_scatter | solution.py:337
  852.6 27.5 %copy-start.74 = (bf16[512,1536]{0,1:T(8,128)(2,1)S(1)}, bf16[512,1536]{0,1:T(8,128)(2,1)}, u32[]{:S(2)}) copy-start(bf16[512,1536]{0,1:T(8,128)(2,1)} %all-gather.13.cloned.1.call-done) | copy-start | bytes 4718596
  880.1 13.8 copy-start.9
  880.1 13.8 copy-start.34
  898.3 6.1 copy-start.33
  904.4 6.7 copy-start.15
  921.4 29.5 %copy-start.65 = (s32[72]{0:T(128)S(1)}, s32[72]{0:T(128)}, u32[]{:S(2)}) copy-start(s32[72]{0:T(128)} %get-tuple-element.107) | copy-start | bytes 868
  950.9 14.4 copy-start.17
  985.5 76.8 %copy-start.61 = (s32[420]{0:T(512)S(1)}, s32[420]{0:T(512)}, u32[]{:S(2)}) copy-start(s32[420]{0:T(512)} %get-tuple-element.104) | copy-start | bytes 5044
  1062.3 77.0 %copy-start.60 = (s32[420]{0:T(512)S(1)}, s32[420]{0:T(512)}, u32[]{:S(2)}) copy-start(s32[420]{0:T(512)} %get-tuple-element.103) | copy-start | bytes 5044
  1230.3 9.4 copy-start.55
  1230.3 9.4 copy-start.63
  1230.3 9.4 copy-start.64
  1230.3 43.8 %copy-start.71 = (f32[1,64]{1,0:T(1,128)S(1)}, f32[1,64]{1,0:T(1,128)}, u32[]{:S(2)}) copy-start(f32[1,64]{1,0:T(1,128)} %param.27) | copy-start | bytes 772
  1230.3 43.8 %copy-start.72 = (f32[1,64]{1,0:T(1,128)S(1)}, f32[1,64]{1,0:T(1,128)}, u32[]{:S(2)}) copy-start(f32[1,64]{1,0:T(1,128)} %param.28) | copy-start | bytes 772
  1230.3 43.8 %copy-start.73 = (f32[1,64]{1,0:T(1,128)S(1)}, f32[1,64]{1,0:T(1,128)}, u32[]{:S(2)}) copy-start(f32[1,64]{1,0:T(1,128)} %param.29) | copy-start | bytes 772
  1230.3 44.4 %copy-start.7 = (bf16[256,1536]{1,0:T(8,128)(2,1)S(1)}, bf16[256,1536]{1,0:T(8,128)(2,1)}, u32[]{:S(2)}) copy-start(bf16[256,1536]{1,0:T(8,128)(2,1)} %param.15) | copy-start | bytes 2359300
  1230.3 44.4 %copy-start.49 = (f32[1536]{0:T(1024)S(1)}, f32[1536]{0:T(1024)}, u32[]{:S(2)}) copy-start(f32[1536]{0:T(1024)} %copy-done.48) | copy-start | bytes 18436
  1230.3 44.4 %copy-start.57 = (f32[256]{0:T(256)S(1)}, f32[256]{0:T(256)}, u32[]{:S(2)}) copy-start(f32[256]{0:T(256)} %copy-done.56) | copy-start | bytes 3076
  1230.3 46.7 %copy-start.52 = (f32[1536]{0:T(1024)S(1)}, f32[1536]{0:T(1024)}, u32[]{:S(2)}) copy-start(f32[1536]{0:T(1024)} %get-tuple-element.56) | copy-start | bytes 18436
  1230.4 83.8 %copy-start.67 = (f32[96]{0:T(128)S(1)}, f32[96]{0:T(128)}, u32[]{:S(2)}) copy-start(f32[96]{0:T(128)} %param.24) | copy-start | bytes 1156
  1230.4 83.8 %copy-start.68 = (f32[96]{0:T(128)S(1)}, f32[96]{0:T(128)}, u32[]{:S(2)}) copy-start(f32[96]{0:T(128)} %param.25) | copy-start | bytes 1156
  1230.4 83.8 %copy-start.69 = (f32[96]{0:T(128)S(1)}, f32[96]{0:T(128)}, u32[]{:S(2)}) copy-start(f32[96]{0:T(128)} %param.26) | copy-start | bytes 1156
  1230.4 84.4 %copy-start.2 = (f32[256,1536]{1,0:T(8,128)S(1)}, f32[256,1536]{1,0:T(8,128)}, u32[]{:S(2)}) copy-start(f32[256,1536]{1,0:T(8,128)} %copy-done.1) | copy-start | bytes 4718596
  1230.4 84.4 %copy-start.14 = (bf16[256,1536]{1,0:T(8,128)(2,1)S(1)}, bf16[256,1536]{1,0:T(8,128)(2,1)}, u32[]{:S(2)}) copy-start(bf16[256,1536]{1,0:T(8,128)(2,1)} %param.16) | copy-start | bytes 2359300
  1230.4 84.4 %copy-start.41 = (f32[1536]{0:T(1024)S(1)}, f32[1536]{0:T(1024)}, u32[]{:S(2)}) copy-start(f32[1536]{0:T(1024)} %copy-done.40) | copy-start | bytes 18436
  1230.4 84.4 %copy-start.54 = (f32[256]{0:T(256)S(1)}, f32[256]{0:T(256)}, u32[]{:S(2)}) copy-start(f32[256]{0:T(256)} %copy-done.53) | copy-start | bytes 3076
  1230.4 84.4 %copy-start.59 = (f32[256]{0:T(256)S(1)}, f32[256]{0:T(256)}, u32[]{:S(2)}) copy-start(f32[256]{0:T(256)} %copy-done.58) | copy-start | bytes 3076
  (23 other events, 38.4 us)
Sparse Core Ops, SparseCore 0:
  54.6 27.0 all-gather.6
  83.9 232.2 all-gather.8
  424.8 43.3 reduce-scatter.5
  470.2 27.1 all-gather.12
  499.4 27.2 all-gather.10
  656.3 43.3 reduce-scatter.9
  705.0 27.1 all-gather.14
  758.3 43.3 reduce-scatter.11
  804.0 26.0 reduce-scatter.7
  1216.9 856.1 reduce-scatter.13
where the time goes:
time: 2170 us; the launch traced here: 2160 us
  waiting for transfers between devices  1070 us (49%)
  local copies, waits for them, and re-layouts  634 us (29%)
  matrix products  225 us (10%)
  blocking collectives  144 us (7%)
  other arithmetic  70.3 us (3%)
    reduce_scatter x1, waiting for transfers between devices, body(): lax.psum_scatter(term_all, 'wide', scatter_dimension=0, tiled=True)  753 us
    scatter x7, local copies, waits for them, and re-layouts, body(): term_all = term_all.at[slot_of[bases[kind_index]:bases[kind_index] + rows...  266 us
    all_gather x1, waiting for transfers between devices, body(): lax.all_gather(masters.astype(jnp.bfloat16), 'wide', axis=0, tiled=True)  210 us
    unnamed x4, blocking collectives  144 us
    transpose x4, local copies, waits for them, and re-layouts, block_terms(): jnp.einsum('tra,tcb->rcab', inputs_low.reshape(rows_here, row_blocks, BLK...  67 us
    dot_general x5, local copies, waits for them, and re-layouts, apply_blocks(): jnp.einsum('tra,rcab->tcb', grouped, weight_blocks, preferred_element_typ...  63.5 us
    dot_general x7, matrix products, apply_blocks(): jnp.einsum('tra,rcab->tcb', grouped, weight_blocks, preferred_element_typ...  58.5 us
    dot_general x7, matrix products, block_terms(): jnp.einsum('tra,tcb->rcab', inputs_low.reshape(rows_here, row_blocks, BLK...  52.1 us
  transfers between devices with their start and end apart: 10, of which 6 were waited for; matrix products, arithmetic and copies ran while one was open for 29% of the time, Pallas kernels for 0%

commit v1 on v0

v1 whole, which is shorter than its diff:
```python
import functools

import jax
import jax.numpy as jnp
from jax import lax
from jax.experimental import pallas as pl
from jax.experimental.pallas import tpu as pltpu
from jax.sharding import PartitionSpec as P

D = 1536
FF = 8960
HEADS = 12
KV_HEADS = 2
HEAD_DIM = 128
BLK = 128
STEP_COUNT = 5


beta_first = 0.95
beta_second = 0.95
adam_eps = 1e-08
rate_blocks = 0.03
rate_small = 0.4
rate_gains = 0.6
norm_eps = 1e-06
rope_base = 10000.0
masked_score = -1e30
first_fix = 1.0 - beta_first**STEP_COUNT
second_fix = 1.0 - beta_second**STEP_COUNT
scaling = HEAD_DIM ** (-0.5)

bf16 = jnp.bfloat16
f32 = jnp.float32

NARROW = 2
ROW_BLOCKS = D // BLK
QUERY_COLS = HEADS * HEAD_DIM // NARROW // BLK
PAIR_COLS = KV_HEADS * HEAD_DIM // NARROW // BLK
HIDDEN_COLS = FF // NARROW // BLK
QKV_COLS = QUERY_COLS + 2 * PAIR_COLS
QUERY_WIDTH = QUERY_COLS * BLK
QKV_WIDTH = QKV_COLS * BLK
KEY_BASE = ROW_BLOCKS * QUERY_COLS
VALUE_BASE = KEY_BASE + ROW_BLOCKS * PAIR_COLS
OUT_BASE = VALUE_BASE + ROW_BLOCKS * PAIR_COLS
GATE_BASE = OUT_BASE + QUERY_COLS * ROW_BLOCKS
UP_BASE = GATE_BASE + ROW_BLOCKS * HIDDEN_COLS
DOWN_BASE = UP_BASE + ROW_BLOCKS * HIDDEN_COLS
BLOCK_TOTAL = DOWN_BASE + HIDDEN_COLS * ROW_BLOCKS

TILE_BLOCKS = 5
TILES = HIDDEN_COLS // TILE_BLOCKS
TILE = TILE_BLOCKS * BLK
COLS = 256
ROWS = 64
SMALL_ROWS = 16
VMEM_LIMIT = 60 * 2**20

EARLY = 4
DEPTH = 3
CROSS_LAG = 2
HOP_LAG = 1

VMEM_SPEC = pl.BlockSpec(memory_space=pltpu.VMEM)
SMEM_SPEC = pl.BlockSpec(memory_space=pltpu.SMEM)
ANY_SPEC = pl.BlockSpec(memory_space=pl.ANY)


def spans(total, step):
    return [(begin, min(step, total - begin)) for begin in range(0, total, step)]


def dot_nn(left, right):
    return jnp.dot(left, right, preferred_element_type=f32)


def dot_nt(left, right):
    return lax.dot_general(left, right, (((1,), (1,)), ((), ())), preferred_element_type=f32)


def block_ref(ref, row_block, col_block):
    return ref.at[pl.ds(row_block * BLK, BLK), pl.ds(col_block * BLK, BLK)]


def fetch_piece(rows_ref, weights, target, base, pitch, row_blocks, col_blocks, first_col, sem):
    @pl.loop(0, row_blocks)
    def _(i):
        for j in range(col_blocks):
            pltpu.make_async_copy(
                weights.at[rows_ref[base + i * pitch + j]],
                block_ref(target, i, first_col + j),
                sem,
            ).start()


def store_piece(rows_ref, source, grads, base, pitch, row_blocks, col_blocks, first_col, sem):
    @pl.loop(0, row_blocks)
    def _(i):
        for j in range(col_blocks):
            pltpu.make_async_copy(
                block_ref(source, i, first_col + j),
                grads.at[rows_ref[base + i * pitch + j]],
                sem,
            ).start()


def wait_bytes(ref, sem):
    pltpu.make_async_copy(ref, ref, sem).wait()


def fetch_attention(rows_ref, weights, w_qkv, w_out, sems):
    fetch_piece(rows_ref, weights, w_qkv, 0, QUERY_COLS, ROW_BLOCKS, QUERY_COLS, 0, sems.at[0])
    fetch_piece(rows_ref, weights, w_qkv, KEY_BASE, PAIR_COLS, ROW_BLOCKS, PAIR_COLS, QUERY_COLS, sems.at[0])
    fetch_piece(
        rows_ref, weights, w_qkv, VALUE_BASE, PAIR_COLS, ROW_BLOCKS, PAIR_COLS, QUERY_COLS + PAIR_COLS, sems.at[0]
    )
    fetch_piece(rows_ref, weights, w_out, OUT_BASE, ROW_BLOCKS, QUERY_COLS, ROW_BLOCKS, 0, sems.at[1])


def rms_inverse(values):
    return lax.rsqrt(jnp.mean(values * values, axis=-1, keepdims=True) + norm_eps)


def row_chunks(total, step, run):
    @pl.loop(0, total // step)
    def _(chunk):
        run(pl.ds(pl.multiple_of(chunk * step, step), step))


def small_places(owner, wide_count):
    gain_first = owner * (2 * D // wide_count)
    bias_first = owner * (QKV_WIDTH // wide_count)
    gain_row = min(gain_first // BLK, 2 * D // BLK - 2)
    return (gain_row, gain_first - gain_row * BLK, bias_first // BLK, bias_first % BLK)


def scores_turned(keys, queries, allowed):
    return jnp.where(allowed, dot_nt(keys, queries) * scaling, masked_score)


def attention_forward(
    rows_ref,
    x_ref,
    gain_ref,
    bias_ref,
    cos_ref,
    sin_ref,
    allowed_ref,
    weights,
    part_ref,
    normed_turned_ref,
    qkv_ref,
    mixed_turned_ref,
    log_ref,
    w_qkv,
    w_out,
    normed,
    mixed,
    sems,
):
    fetch_attention(rows_ref, weights, w_qkv, w_out, sems)
    length = x_ref.shape[0]

    def norm_rows(rows):
        values = x_ref[rows, :].astype(f32)
        normed[rows, :] = (values * rms_inverse(values) * gain_ref[...]).astype(bf16)

    row_chunks(length, ROWS, norm_rows)
    for begin, size in spans(D, COLS):
        normed_turned_ref[pl.ds(begin, size), :] = normed[:, pl.ds(begin, size)].T
    wait_bytes(w_qkv, sems.at[0])
    for begin, size in spans(QKV_WIDTH, COLS):
        products = dot_nn(normed[...], w_qkv[:, pl.ds(begin, size)]) + bias_ref[:, pl.ds(begin, size)]
        for offset, width in spans(size, HEAD_DIM):
            head = products[:, offset : offset + width]
            if begin + offset < QUERY_WIDTH + PAIR_COLS * BLK:
                head = head * cos_ref[...] + pltpu.roll(head, HEAD_DIM // 2, 1) * sin_ref[...]
            qkv_ref[:, pl.ds(begin + offset, width)] = head.astype(bf16)
    keys = qkv_ref[:, pl.ds(QUERY_WIDTH, HEAD_DIM)]
    values_turned = qkv_ref[:, pl.ds(QUERY_WIDTH + HEAD_DIM, HEAD_DIM)].T
    for head in range(QUERY_COLS):
        columns = pl.ds(head * HEAD_DIM, HEAD_DIM)
        scores = scores_turned(keys, qkv_ref[:, columns], allowed_ref[...] > 0)
        peak = jnp.max(scores, axis=0, keepdims=True)
        expo = jnp.exp(scores - peak)
        total = jnp.sum(expo, axis=0, keepdims=True)
        log_ref[pl.ds(head, 1), :] = peak + jnp.log(total)
        probs = (expo / total).astype(bf16)
        mixed_head = dot_nn(values_turned, probs).astype(bf16)
        mixed_turned_ref[columns, :] = mixed_head
        mixed[:, columns] = mixed_head.T
    wait_bytes(w_out, sems.at[1])
    for begin, size in spans(D, COLS):
        part_ref[:, pl.ds(begin, size)] = dot_nn(mixed[...], w_out[:, pl.ds(begin, size)]).astype(bf16)


def hidden_grads(
    rows_ref,
    x_ref,
    own_ref,
    other_ref,
    gain_ref,
    cot_ref,
    weights,
    branch_ref,
    grad_ref,
    resid_ref,
    normed_turned_ref,
    gain_part_ref,
    pair_grads,
    active_turned,
    w_pair,
    w_down,
    pair,
    grad_active,
    active,
    turned,
    grads,
    normed,
    branch_sum,
    grad_sum,
    load_sems,
    store_sems,
):
    length = x_ref.shape[0]

    def fetch(tile, slot):
        first = tile * TILE_BLOCKS
        fetch_piece(
            rows_ref, weights, w_down.at[slot], DOWN_BASE + first * ROW_BLOCKS, ROW_BLOCKS, TILE_BLOCKS, ROW_BLOCKS, 0,
            load_sems.at[slot, 1],
        )
        fetch_piece(
            rows_ref, weights, w_pair.at[slot], GATE_BASE + first, HIDDEN_COLS, ROW_BLOCKS, TILE_BLOCKS, 0,
            load_sems.at[slot, 0],
        )
        fetch_piece(
            rows_ref, weights, w_pair.at[slot], UP_BASE + first, HIDDEN_COLS, ROW_BLOCKS, TILE_BLOCKS, TILE_BLOCKS,
            load_sems.at[slot, 0],
        )

    fetch(0, 0)

    def norm_rows(rows):
        values = x_ref[rows, :].astype(f32) + own_ref[rows, :].astype(f32) + other_ref[rows, :].astype(f32)
        resid_ref[rows, :] = values
        normed[rows, :] = (values * rms_inverse(values) * gain_ref[...]).astype(bf16)

    row_chunks(length, ROWS, norm_rows)
    for begin, size in spans(D, COLS):
        normed_turned_ref[pl.ds(begin, size), :] = normed[:, pl.ds(begin, size)].T
    branch_sum[...] = jnp.zeros_like(branch_sum)
    grad_sum[...] = jnp.zeros_like(grad_sum)

    @pl.loop(0, TILES)
    def _(tile):
        slot = lax.rem(tile, 2)

        @pl.when(tile + 1 < TILES)
        def _():
            fetch(tile + 1, 1 - slot)

        wait_bytes(w_down.at[slot], load_sems.at[slot, 1])
        for begin, size in spans(TILE, COLS):
            grad_active[:, pl.ds(begin, size)] = dot_nt(cot_ref[...], w_down[slot, pl.ds(begin, size), :])
        wait_bytes(w_pair.at[slot], load_sems.at[slot, 0])
        for begin, size in spans(2 * TILE, COLS):
            pair[:, pl.ds(begin, size)] = dot_nn(normed[...], w_pair[slot, :, pl.ds(begin, size)])

        @pl.when(tile >= 2)
        def _():
            wait_bytes(turned.at[slot], store_sems.at[slot, 0])
            wait_bytes(grads.at[slot], store_sems.at[slot, 1])

        for begin, size in spans(TILE, BLK):
            gate = pair[:, pl.ds(begin, size)]
            upper = pair[:, pl.ds(TILE + begin, size)]
            grad = grad_active[:, pl.ds(begin, size)]
            sigmoid = jax.nn.sigmoid(gate)
            silu = gate * sigmoid
            active_here = (silu * upper).astype(bf16)
            active[:, pl.ds(begin, size)] = active_here
            turned[slot, pl.ds(begin, size), :] = active_here.T
            grads[slot, :, pl.ds(begin, size)] = (
                grad * upper * sigmoid * (1.0 + gate * (1.0 - sigmoid))
            ).astype(bf16)
            grads[slot, :, pl.ds(TILE + begin, size)] = (grad * silu).astype(bf16)
        pltpu.make_async_copy(turned.at[slot], active_turned.at[tile], store_sems.at[slot, 0]).start()
        pltpu.make_async_copy(grads.at[slot], pair_grads.at[tile], store_sems.at[slot, 1]).start()
        for begin, size in spans(D, COLS):
            columns = pl.ds(begin, size)
            branch_sum[:, columns] += dot_nn(active[...], w_down[slot, :, columns])
            grad_sum[:, columns] += dot_nt(grads[slot], w_pair[slot, columns, :])

    branch_ref[...] = branch_sum[...].astype(bf16)
    grad_ref[...] = grad_sum[...].astype(bf16)
    gain_part_ref[...] = jnp.zeros_like(gain_part_ref)

    def gain_rows(rows):
        values = resid_ref[rows, :]
        gain_part_ref[...] += jnp.sum(grad_sum[rows, :] * values * rms_inverse(values), axis=0, keepdims=True)

    row_chunks(length, ROWS, gain_rows)
    for tile in range(max(TILES - 2, 0), TILES):
        slot = tile % 2
        wait_bytes(turned.at[slot], store_sems.at[slot, 0])
        wait_bytes(grads.at[slot], store_sems.at[slot, 1])


def hidden_weight_grads(
    rows_ref, normed_turned_ref, cot_ref, pair_ref, turned_ref, grads, pair_stage, down_stage, sems
):
    tile = pl.program_id(0)
    slot = lax.rem(tile, 2)

    def drain(which):
        wait_bytes(pair_stage.at[which], sems.at[which, 0])
        wait_bytes(down_stage.at[which], sems.at[which, 1])

    @pl.when(tile >= 2)
    def _():
        drain(slot)

    first = tile * TILE_BLOCKS
    for row_begin, row_size in spans(D, 512):
        for begin, size in spans(2 * TILE, COLS):
            pair_stage[slot, pl.ds(row_begin, row_size), pl.ds(begin, size)] = dot_nn(
                normed_turned_ref[pl.ds(row_begin, row_size), :], pair_ref[0, :, pl.ds(begin, size)]
            ).astype(bf16)
    store_piece(
        rows_ref, pair_stage.at[slot], grads, GATE_BASE + first, HIDDEN_COLS, ROW_BLOCKS, TILE_BLOCKS, 0, sems.at[slot, 0]
    )
    store_piece(
        rows_ref, pair_stage.at[slot], grads, UP_BASE + first, HIDDEN_COLS, ROW_BLOCKS, TILE_BLOCKS, TILE_BLOCKS,
        sems.at[slot, 0],
    )
    for begin, size in spans(D, COLS):
        down_stage[slot, :, pl.ds(begin, size)] = dot_nn(turned_ref[0], cot_ref[:, pl.ds(begin, size)]).astype(bf16)
    store_piece(
        rows_ref, down_stage.at[slot], grads, DOWN_BASE + first * ROW_BLOCKS, ROW_BLOCKS, TILE_BLOCKS, ROW_BLOCKS, 0,
        sems.at[slot, 1],
    )

    @pl.when(tile == TILES - 1)
    def _():
        for which in range(2 if TILES > 1 else 1):
            drain(which)


def attention_backward(
    rows_ref,
    x_ref,
    resid_ref,
    own_ref,
    other_ref,
    cot_ref,
    gain_ref,
    cos_ref,
    sin_ref,
    allowed_ref,
    normed_turned_ref,
    qkv_ref,
    mixed_turned_ref,
    log_ref,
    gain_two_ref,
    weights,
    grads_in,
    grad_resid_ref,
    grad_ref,
    grads,
    w_qkv,
    w_out,
    grad_attention,
    grad_mixed,
    grad_qkv,
    grad_sum,
    gain_part,
    bias_part,
    qkv_stage,
    out_stage,
    small_stage,
    blank,
    load_sems,
    store_sems,
):
    del grads_in
    wide_count = small_stage.shape[0]
    owner_rows = grads.shape[0] // wide_count
    small_stage[...] = jnp.zeros_like(small_stage)
    fetch_attention(rows_ref, weights, w_qkv, w_out, load_sems)
    length = x_ref.shape[0]
    empty_count = rows_ref.shape[0] - BLOCK_TOTAL
    blank[...] = jnp.zeros_like(blank)
    for index in range(empty_count):
        pltpu.make_async_copy(blank.at[index], grads.at[rows_ref[BLOCK_TOTAL + index]], store_sems.at[2]).start()

    def resid_rows(rows):
        values = resid_ref[rows, :]
        inverse = rms_inverse(values)
        normed = values * inverse
        scaled = (own_ref[rows, :].astype(f32) + other_ref[rows, :].astype(f32)) * gain_ref[1:2, :]
        total = cot_ref[rows, :].astype(f32) + inverse * (
            scaled - normed * jnp.mean(scaled * normed, axis=-1, keepdims=True)
        )
        grad_resid_ref[rows, :] = total
        grad_attention[rows, :] = total.astype(bf16)

    row_chunks(length, ROWS, resid_rows)
    wait_bytes(w_out, load_sems.at[1])
    for begin, size in spans(QUERY_WIDTH, COLS):
        grad_mixed[:, pl.ds(begin, size)] = dot_nt(grad_attention[...], w_out[pl.ds(begin, size), :]).astype(bf16)
    keys = qkv_ref[:, pl.ds(QUERY_WIDTH, HEAD_DIM)]
    keys_turned = keys.T
    values = qkv_ref[:, pl.ds(QUERY_WIDTH + HEAD_DIM, HEAD_DIM)]

    def rope_back(vector):
        return vector * cos_ref[...] - pltpu.roll(vector, HEAD_DIM // 2, 1) * sin_ref[...]

    grad_keys = jnp.zeros((length, HEAD_DIM), f32)
    grad_values = jnp.zeros((length, HEAD_DIM), f32)
    for head in range(QUERY_COLS):
        columns = pl.ds(head * HEAD_DIM, HEAD_DIM)
        queries = qkv_ref[:, columns]
        scores = scores_turned(keys, queries, allowed_ref[...] > 0)
        probs = jnp.exp(scores - log_ref[pl.ds(head, 1), :])
        grad_values += dot_nn(probs.astype(bf16), grad_mixed[:, columns])
        grad_probs = dot_nt(values, grad_mixed[:, columns])
        row_dot = jnp.sum(probs * grad_probs, axis=0, keepdims=True)
        grad_scores = (probs * (grad_probs - row_dot)).astype(bf16)
        grad_keys += dot_nn(grad_scores, queries)
        grad_queries = dot_nn(keys_turned, grad_scores).T * scaling
        grad_qkv[:, columns] = rope_back(grad_queries).astype(bf16)
    grad_qkv[:, pl.ds(QUERY_WIDTH, HEAD_DIM)] = rope_back(grad_keys * scaling).astype(bf16)
    grad_qkv[:, pl.ds(QUERY_WIDTH + HEAD_DIM, HEAD_DIM)] = grad_values.astype(bf16)

    for begin, size in spans(D, COLS):
        out_stage[:, pl.ds(begin, size)] = dot_nn(
            mixed_turned_ref[...], grad_attention[:, pl.ds(begin, size)]
        ).astype(bf16)
    store_piece(rows_ref, out_stage, grads, OUT_BASE, ROW_BLOCKS, QUERY_COLS, ROW_BLOCKS, 0, store_sems.at[1])
    for begin, size in spans(QKV_WIDTH, COLS):
        qkv_stage[:, pl.ds(begin, size)] = dot_nn(
            normed_turned_ref[...], grad_qkv[:, pl.ds(begin, size)]
        ).astype(bf16)
    store_piece(rows_ref, qkv_stage, grads, 0, QUERY_COLS, ROW_BLOCKS, QUERY_COLS, 0, store_sems.at[0])
    store_piece(rows_ref, qkv_stage, grads, KEY_BASE, PAIR_COLS, ROW_BLOCKS, PAIR_COLS, QUERY_COLS, store_sems.at[0])
    store_piece(
        rows_ref, qkv_stage, grads, VALUE_BASE, PAIR_COLS, ROW_BLOCKS, PAIR_COLS, QUERY_COLS + PAIR_COLS, store_sems.at[0]
    )
    wait_bytes(w_qkv, load_sems.at[0])
    for begin, size in spans(D, COLS):
        products = dot_nt(grad_qkv[...], w_qkv[pl.ds(begin, size), :])
        grad_sum[:, pl.ds(begin, size)] = products
        grad_ref[:, pl.ds(begin, size)] = products.astype(bf16)
    gain_part[...] = jnp.zeros_like(gain_part)
    bias_part[...] = jnp.zeros_like(bias_part)

    def gain_rows(rows):
        tokens = x_ref[rows, :].astype(f32)
        gain_part[...] += jnp.sum(grad_sum[rows, :] * tokens * rms_inverse(tokens), axis=0, keepdims=True)
        bias_part[...] += jnp.sum(grad_qkv[rows, :].astype(f32), axis=0, keepdims=True)

    row_chunks(length, ROWS, gain_rows)
    for owner in range(wide_count):
        gain_row, bias_row = small_places(owner, wide_count)[::2]
        small_rows = []
        for row in (gain_row, gain_row + 1):
            source = gain_part if row < D // BLK else gain_two_ref
            small_rows.append(source[:, pl.ds(row % (D // BLK) * BLK, BLK)])
        small_rows.append(bias_part[:, pl.ds(bias_row * BLK, BLK)])
        small_rows.append(jnp.zeros((SMALL_ROWS - len(small_rows), BLK), f32))
        small_stage[owner, pl.ds(0, SMALL_ROWS), :] = jnp.concatenate(small_rows, axis=0).astype(bf16)
        pltpu.make_async_copy(
            small_stage.at[owner], grads.at[owner * owner_rows + owner_rows - 1], store_sems.at[3]
        ).start()
    wait_bytes(small_stage, store_sems.at[3])
    wait_bytes(qkv_stage, store_sems.at[0])
    wait_bytes(out_stage, store_sems.at[1])
    if empty_count > 0:
        wait_bytes(blank.at[pl.ds(0, empty_count)], store_sems.at[2])


def soap_update(
    grad_in,
    masters_ref,
    first_ref,
    second_ref,
    left_ref,
    right_ref,
    grad_ref,
    new_masters_ref,
    new_first_ref,
    new_second_ref,
):
    for index in range(masters_ref.shape[0]):
        left = left_ref[index].astype(bf16)
        left_turned = left_ref[index].T.astype(bf16)
        right = right_ref[index].astype(bf16)
        grad_ref[index] = grad_in[index].astype(f32)
        rotated = dot_nn(left_turned, dot_nn(grad_in[index].astype(bf16), right).astype(bf16))
        new_first = beta_first * first_ref[index] + (1.0 - beta_first) * rotated
        new_second = beta_second * second_ref[index] + (1.0 - beta_second) * rotated * rotated
        new_first_ref[index] = new_first
        new_second_ref[index] = new_second
        normalized = new_first / first_fix / (jnp.sqrt(new_second / second_fix) + adam_eps)
        update = dot_nn(left, dot_nt(normalized.astype(bf16), right).astype(bf16))
        new_masters_ref[index] = masters_ref[index] - rate_blocks * update


def params(**options):
    return pltpu.CompilerParams(vmem_limit_bytes=VMEM_LIMIT, **options)


def run_attention_forward(rows, x, gain, bias, cosine, sine, allowed, weights):
    length = x.shape[0]
    shape = jax.ShapeDtypeStruct
    return pl.pallas_call(
        attention_forward,
        out_shape=[
            shape((length, D), bf16),
            shape((D, length), bf16),
            shape((length, QKV_WIDTH), bf16),
            shape((QUERY_WIDTH, length), bf16),
            shape((8, length), f32),
        ],
        in_specs=[SMEM_SPEC] + [VMEM_SPEC] * 6 + [ANY_SPEC],
        out_specs=[VMEM_SPEC] * 5,
        scratch_shapes=[
            pltpu.VMEM((D, QKV_WIDTH), bf16),
            pltpu.VMEM((QUERY_WIDTH, D), bf16),
            pltpu.VMEM((length, D), bf16),
            pltpu.VMEM((length, QUERY_WIDTH), bf16),
            pltpu.SemaphoreType.DMA((2,)),
        ],
        compiler_params=params(),
        name="attention_forward",
    )(rows, x, gain, bias, cosine, sine, allowed, weights)


def run_hidden_grads(rows, x, own, other, gain, cotangent, weights):
    length = x.shape[0]
    shape = jax.ShapeDtypeStruct
    return pl.pallas_call(
        hidden_grads,
        out_shape=[
            shape((length, D), bf16),
            shape((length, D), bf16),
            shape((length, D), f32),
            shape((D, length), bf16),
            shape((1, D), f32),
            shape((TILES, length, 2 * TILE), bf16),
            shape((TILES, TILE, length), bf16),
        ],
        in_specs=[SMEM_SPEC] + [VMEM_SPEC] * 5 + [ANY_SPEC],
        out_specs=[VMEM_SPEC] * 5 + [ANY_SPEC] * 2,
        scratch_shapes=[
            pltpu.VMEM((2, D, 2 * TILE), bf16),
            pltpu.VMEM((2, TILE, D), bf16),
            pltpu.VMEM((length, 2 * TILE), f32),
            pltpu.VMEM((length, TILE), f32),
            pltpu.VMEM((length, TILE), bf16),
            pltpu.VMEM((2, TILE, length), bf16),
            pltpu.VMEM((2, length, 2 * TILE), bf16),
            pltpu.VMEM((length, D), bf16),
            pltpu.VMEM((length, D), f32),
            pltpu.VMEM((length, D), f32),
            pltpu.SemaphoreType.DMA((2, 2)),
            pltpu.SemaphoreType.DMA((2, 2)),
        ],
        compiler_params=params(),
        name="hidden_grads",
    )(rows, x, own, other, gain, cotangent, weights)


def run_hidden_weight_grads(rows, normed_turned, cotangent, pair_grads, active_turned, slots):
    length = cotangent.shape[0]
    flops = 2 * length * 3 * D * TILE * TILES
    bytes_moved = 2 * (3 * D * TILE * TILES + 3 * TILE * TILES * length)
    return pl.pallas_call(
        hidden_weight_grads,
        grid=(TILES,),
        out_shape=jax.ShapeDtypeStruct((slots, BLK, BLK), bf16),
        in_specs=[
            SMEM_SPEC,
            VMEM_SPEC,
            VMEM_SPEC,
            pl.BlockSpec((1, length, 2 * TILE), lambda tile: (tile, 0, 0)),
            pl.BlockSpec((1, TILE, length), lambda tile: (tile, 0, 0)),
        ],
        out_specs=ANY_SPEC,
        scratch_shapes=[
            pltpu.VMEM((2, D, 2 * TILE), bf16),
            pltpu.VMEM((2, TILE, D), bf16),
            pltpu.SemaphoreType.DMA((2, 2)),
        ],
        compiler_params=params(),
        cost_estimate=pl.CostEstimate(flops=flops, bytes_accessed=bytes_moved, transcendentals=0),
        name="hidden_weight_grads",
    )(rows, normed_turned, cotangent, pair_grads, active_turned)


def run_attention_backward(
    rows, x, resid, own, other, cotangent, gains, cosine, sine, allowed, normed_turned, qkv, mixed_turned, log_total,
    gain_two_part, weights, grads, wide_count,
):
    length = x.shape[0]
    shape = jax.ShapeDtypeStruct
    empty_count = max(rows.shape[0] - BLOCK_TOTAL, 1)
    return pl.pallas_call(
        attention_backward,
        out_shape=[
            shape((length, D), f32),
            shape((length, D), bf16),
            shape(grads.shape, bf16),
        ],
        in_specs=[SMEM_SPEC] + [VMEM_SPEC] * 14 + [ANY_SPEC] * 2,
        out_specs=[VMEM_SPEC] * 2 + [ANY_SPEC],
        input_output_aliases={16: 2},
        scratch_shapes=[
            pltpu.VMEM((D, QKV_WIDTH), bf16),
            pltpu.VMEM((QUERY_WIDTH, D), bf16),
            pltpu.VMEM((length, D), bf16),
            pltpu.VMEM((length, QUERY_WIDTH), bf16),
            pltpu.VMEM((length, QKV_WIDTH), bf16),
            pltpu.VMEM((length, D), f32),
            pltpu.VMEM((1, D), f32),
            pltpu.VMEM((1, QKV_WIDTH), f32),
            pltpu.VMEM((D, QKV_WIDTH), bf16),
            pltpu.VMEM((QUERY_WIDTH, D), bf16),
            pltpu.VMEM((wide_count, BLK, BLK), bf16),
            pltpu.VMEM((empty_count, BLK, BLK), bf16),
            pltpu.SemaphoreType.DMA((2,)),
            pltpu.SemaphoreType.DMA((4,)),
        ],
        compiler_params=params(),
        name="attention_backward",
    )(
        rows, x, resid, own, other, cotangent, gains, cosine, sine, allowed, normed_turned, qkv, mixed_turned, log_total,
        gain_two_part, weights, grads,
    )


def run_soap(reduced, masters, first_moment, second_moment, left_basis, right_basis):
    slots = masters.shape[0]
    group = max(size for size in range(1, 11) if slots % size == 0)
    spec = pl.BlockSpec((group, BLK, BLK), lambda step: (step, 0, 0))
    shape = jax.ShapeDtypeStruct(masters.shape, f32)
    return pl.pallas_call(
        soap_update,
        grid=(slots // group,),
        out_shape=[shape] * 4,
        in_specs=[spec] * 6,
        out_specs=[spec] * 4,
        compiler_params=params(),
        name="soap_update",
    )(reduced, masters, first_moment, second_moment, left_basis, right_basis)


def sum_for_owners(
    line, steps, late_steps, grads, out,
    a_in, a_own, a_sum, a_send, a_cross, a_up, a_down,
    b_in, b_own, b_sum, b_keep, b_send, b_cross, b_up, b_down,
    result,
    core_send, core_recv, own_sems, cross_send, cross_recv, up_send, up_recv, down_send, down_recv,
    b_core_send, b_core_recv, b_own_sems, b_cross_send, b_cross_recv, b_up_send, b_up_recv, b_down_send, b_down_recv,
    out_sem, credits,
):
    wide = lax.axis_index("wide")
    narrow = lax.axis_index("narrow")
    z = wide // 4
    x = lax.rem(wide // 2, 2)
    core = lax.rem(wide, 2)
    mesh_id = pl.DeviceIdType.MESH
    core_peer = (wide + 1 - 2 * core, narrow)
    cross_peer = (wide + 2 - 4 * x, narrow)
    upper = (lax.rem(wide + 4, 4 * line), narrow)
    lower = (lax.rem(wide + 4 * line - 4, 4 * line), narrow)
    has_upper = z < line - 1
    has_lower = z > 0
    sum_depth = a_sum.shape[0]
    hop_depth = a_up.shape[0]
    b_sum_depth = b_sum.shape[0]

    barrier = pltpu.get_barrier_semaphore()
    pl.semaphore_signal(barrier, inc=1, device_id=core_peer, device_id_type=mesh_id)
    pl.semaphore_signal(barrier, inc=1, device_id=cross_peer, device_id_type=mesh_id)

    @pl.when(has_upper)
    def _():
        pl.semaphore_signal(barrier, inc=1, device_id=upper, device_id_type=mesh_id)

    @pl.when(has_lower)
    def _():
        pl.semaphore_signal(barrier, inc=1, device_id=lower, device_id_type=mesh_id)

    pl.semaphore_wait(barrier, 2 + has_upper.astype(jnp.int32) + has_lower.astype(jnp.int32))

    def remote(source, target, send_sem, recv_sem, peer):
        return pltpu.make_async_remote_copy(
            src_ref=source, dst_ref=target, send_sem=send_sem, recv_sem=recv_sem, device_id=peer, device_id_type=mesh_id
        )

    def core_copy(step):
        slot = lax.rem(step, DEPTH)
        source = grads.at[:, :, 1 - core, pl.ds(step * EARLY, EARLY)]
        return remote(source, a_in.at[slot], core_send.at[slot], core_recv.at[slot], core_peer)

    def own_copy(step):
        slot = lax.rem(step, DEPTH)
        return pltpu.make_async_copy(
            grads.at[:, :, core, pl.ds(step * EARLY, EARLY)], a_own.at[slot], own_sems.at[slot]
        )

    def b_core_copy(step):
        slot = lax.rem(step, DEPTH)
        source = grads.at[:, :, 1 - core, steps * EARLY + step]
        return remote(source, b_in.at[slot], b_core_send.at[slot], b_core_recv.at[slot], core_peer)

    def b_own_copy(step):
        slot = lax.rem(step, DEPTH)
        return pltpu.make_async_copy(
            grads.at[:, :, core, steps * EARLY + step], b_own.at[slot], b_own_sems.at[slot]
        )

    def cross_copy(step):
        slot = lax.rem(step, DEPTH)
        return remote(a_send.at[slot], a_cross.at[slot], cross_send.at[slot], cross_recv.at[slot], cross_peer)

    def b_cross_copy(step):
        slot = lax.rem(step, DEPTH)
        return remote(b_send.at[slot], b_cross.at[slot], b_cross_send.at[slot], b_cross_recv.at[slot], cross_peer)

    def up_copy(step, target):
        slot = lax.rem(step, hop_depth)
        return remote(
            a_sum.at[lax.rem(step, sum_depth), target], a_up.at[slot, target],
            up_send.at[slot, target], up_recv.at[slot, target], upper,
        )

    def down_copy(step, target):
        slot = lax.rem(step, hop_depth)
        return remote(
            a_sum.at[lax.rem(step, sum_depth), target], a_down.at[slot, target],
            down_send.at[slot, target], down_recv.at[slot, target], lower,
        )

    def b_up_copy(step, target):
        slot = lax.rem(step, hop_depth)
        return remote(
            b_sum.at[lax.rem(step, b_sum_depth), target], b_up.at[slot, target],
            b_up_send.at[slot, target], b_up_recv.at[slot, target], upper,
        )

    def b_down_copy(step, target):
        slot = lax.rem(step, hop_depth)
        return remote(
            b_sum.at[lax.rem(step, b_sum_depth), target], b_down.at[slot, target],
            b_down_send.at[slot, target], b_down_recv.at[slot, target], lower,
        )

    def give(channel, peer):
        pl.semaphore_signal(credits.at[channel], inc=1, device_id=peer, device_id_type=mesh_id)

    def take(channel, step, depth):
        @pl.when(step >= depth)
        def _():
            pl.semaphore_wait(credits.at[channel], 1)

    def feed(step, count, channel, remote_copy, local_copy):
        @pl.when(step < count)
        def _():
            take(channel, step, DEPTH)
            remote_copy(step).start()
            local_copy(step).start()

    for early in range(DEPTH - 1):
        feed(early, steps, 0, core_copy, own_copy)
        feed(early, late_steps, 1, b_core_copy, b_own_copy)

    def active(step, count):
        return (step >= 0) & (step < count)

    far = jnp.maximum(z, line - 1 - z)

    def hops(step_up, step_down, count, sums, depth, ups, downs, up, down, channel):
        @pl.when(active(step_up, count) & has_upper)
        def _():
            take(channel, step_up, hop_depth)
            slot = lax.rem(step_up, hop_depth)
            place = lax.rem(step_up, depth)

            def one(target, _):
                @pl.when(has_lower)
                def _():
                    up(step_up, target).wait_recv()
                    sums[place, target] += ups[slot, target]

                up(step_up, target).start()
                return 0

            lax.fori_loop(z + 1, line, one, 0)

        @pl.when(active(step_down, count) & has_lower)
        def _():
            take(channel + 1, step_down, hop_depth)
            slot = lax.rem(step_down, hop_depth)
            place = lax.rem(step_down, depth)

            def one(target, _):
                @pl.when(has_upper)
                def _():
                    down(step_down, target).wait_recv()
                    sums[place, target] += downs[slot, target]

                down(step_down, target).start()
                return 0

            lax.fori_loop(0, z, one, 0)

    def gather_hops(step, count, sums, depth, ups, downs, up, down, channel, total):
        slot = lax.rem(step, hop_depth)
        total[...] = sums[lax.rem(step, depth), z].astype(f32)

        @pl.when(has_lower)
        def _():
            up(step, z).wait_recv()
            total[...] += ups[slot, z].astype(f32)

            @pl.when(step < count - hop_depth)
            def _():
                give(channel, lower)

        @pl.when(has_upper)
        def _():
            down(step, z).wait_recv()
            total[...] += downs[slot, z].astype(f32)

            @pl.when(step < count - hop_depth)
            def _():
                give(channel + 1, upper)

    def retire(step, count, up, down):
        @pl.when(active(step, count))
        def _():
            def sent_up(target, _):
                up(step, target).wait_send()
                return 0

            def sent_down(target, _):
                down(step, target).wait_send()
                return 0

            lax.fori_loop(z + 1, line, sent_up, 0)
            lax.fori_loop(0, z, sent_down, 0)

    def iteration(step, _):
        feed(step + DEPTH - 1, steps, 0, core_copy, own_copy)
        feed(step + DEPTH - 1, late_steps, 1, b_core_copy, b_own_copy)

        retire(step - CROSS_LAG - HOP_LAG * far - 1, steps, up_copy, down_copy)
        retire(step - HOP_LAG * far - 1, late_steps, b_up_copy, b_down_copy)

        @pl.when(step < steps)
        def _():
            slot = lax.rem(step, DEPTH)
            place = lax.rem(step, sum_depth)
            core_copy(step).wait()
            own_copy(step).wait()

            @pl.when(step >= DEPTH)
            def _():
                cross_copy(step - DEPTH).wait_send()

            for target in range(line):
                a_send[slot, target] = a_own[slot, target, 1 - x] + a_in[slot, target, 1 - x]
            take(2, step, DEPTH)
            cross_copy(step).start()
            for target in range(line):
                a_sum[place, target] = a_own[slot, target, x] + a_in[slot, target, x]

            @pl.when(step < steps - DEPTH)
            def _():
                give(0, core_peer)

        @pl.when(step < late_steps)
        def _():
            slot = lax.rem(step, DEPTH)
            b_core_copy(step).wait()
            b_own_copy(step).wait()
            b_sum[lax.rem(step, b_sum_depth)] = b_own[slot] + b_in[slot]

            @pl.when(step < late_steps - DEPTH)
            def _():
                give(1, core_peer)

        crossed = step - CROSS_LAG

        @pl.when(active(crossed, steps))
        def _():
            slot = lax.rem(crossed, DEPTH)
            place = lax.rem(crossed, sum_depth)
            cross_copy(crossed).wait_recv()
            for target in range(line):
                a_sum[place, target] += a_cross[slot, target]

            @pl.when(crossed < steps - DEPTH)
            def _():
                give(2, cross_peer)

        hops(
            step - HOP_LAG * z, step - HOP_LAG * (line - 1 - z), late_steps, b_sum, b_sum_depth, b_up, b_down,
            b_up_copy, b_down_copy, 6,
        )
        hops(
            crossed - HOP_LAG * z, crossed - HOP_LAG * (line - 1 - z), steps, a_sum, sum_depth, a_up, a_down,
            up_copy, down_copy, 4,
        )

        last = crossed - HOP_LAG * far

        @pl.when(active(last, steps))
        def _():
            total = result.at[pl.ds(last * EARLY, EARLY)]
            gather_hops(last, steps, a_sum, sum_depth, a_up, a_down, up_copy, down_copy, 4, total)
            pltpu.make_async_copy(total, out.at[pl.ds(last * EARLY, EARLY)], out_sem).start()

        arrived = step - HOP_LAG * far

        @pl.when(active(arrived, late_steps))
        def _():
            slot = lax.rem(arrived, DEPTH)

            @pl.when(arrived >= DEPTH)
            def _():
                b_cross_copy(arrived - DEPTH).wait_send()

            gather_hops(
                arrived, late_steps, b_sum, b_sum_depth, b_up, b_down, b_up_copy, b_down_copy, 6, b_keep.at[slot]
            )
            b_send[slot] = b_keep[slot, 1 - x].astype(bf16)
            take(3, arrived, DEPTH)
            b_cross_copy(arrived).start()

        paired = arrived - CROSS_LAG

        @pl.when(active(paired, late_steps))
        def _():
            slot = lax.rem(paired, DEPTH)
            b_cross_copy(paired).wait_recv()
            place = steps * EARLY + paired
            result[place] = b_keep[slot, x] + b_cross[slot].astype(f32)

            @pl.when(paired < late_steps - DEPTH)
            def _():
                give(3, cross_peer)

            pltpu.make_async_copy(result.at[place], out.at[place], out_sem).start()

        return 0

    lag = HOP_LAG * (line - 1) + CROSS_LAG
    lax.fori_loop(0, max(steps, late_steps) + lag + 2, iteration, 0)
    for step in range(max(steps - DEPTH, 0), steps):
        cross_copy(step).wait_send()
    for step in range(max(late_steps - DEPTH, 0), late_steps):
        b_cross_copy(step).wait_send()
    pltpu.make_async_copy(result, out, out_sem).wait()


def run_sum_for_owners(grads, wide_count):
    line = wide_count // 4
    slots, block = grads.shape[0] // wide_count, grads.shape[1:]
    steps = (slots - 1) // (EARLY + 1)
    late_steps = slots - EARLY * steps
    sum_depth = CROSS_LAG + HOP_LAG * (line - 1) + 2
    b_sum_depth = HOP_LAG * (line - 1) + 2
    hop_depth = 2 * HOP_LAG + 2
    dma = pltpu.SemaphoreType.DMA

    def vmem(*shape):
        return pltpu.VMEM(shape + block, bf16)

    def wide_vmem(*shape):
        return pltpu.VMEM(shape + block, f32)

    return pl.pallas_call(
        functools.partial(sum_for_owners, line, steps, late_steps),
        out_shape=jax.ShapeDtypeStruct((slots,) + block, f32),
        in_specs=[ANY_SPEC],
        out_specs=ANY_SPEC,
        scratch_shapes=[
            vmem(DEPTH, line, 2, EARLY),
            vmem(DEPTH, line, 2, EARLY),
            vmem(sum_depth, line, EARLY),
            vmem(DEPTH, line, EARLY),
            vmem(DEPTH, line, EARLY),
            vmem(hop_depth, line, EARLY),
            vmem(hop_depth, line, EARLY),
            vmem(DEPTH, line, 2),
            vmem(DEPTH, line, 2),
            vmem(b_sum_depth, line, 2),
            wide_vmem(DEPTH, 2),
            vmem(DEPTH),
            vmem(DEPTH),
            vmem(hop_depth, line, 2),
            vmem(hop_depth, line, 2),
            wide_vmem(slots),
        ]
        + ([dma((DEPTH,))] * 5 + [dma((hop_depth, line))] * 4) * 2
        + [dma, pltpu.SemaphoreType.REGULAR((8,))],
        compiler_params=params(collective_id=0, has_side_effects=True),
        cost_estimate=pl.CostEstimate(flops=0, bytes_accessed=2 * grads.size * 8, transcendentals=0),
        name="sum_for_owners",
    )(grads.reshape((line, 2, 2, slots) + block))


def rope_tables(segment_row):
    token_index = jnp.arange(segment_row.shape[0], dtype=jnp.int32)
    changed = jnp.concatenate([jnp.ones((1,), dtype=bool), segment_row[1:] != segment_row[:-1]])
    begins = lax.cummax(jnp.where(changed, token_index, jnp.zeros_like(token_index)), axis=0)
    places = (token_index - begins).astype(f32)
    frequency = rope_base ** (-(jnp.arange(HEAD_DIM // 2, dtype=f32) * 2.0) / HEAD_DIM)
    angles = places[:, None] * frequency[None, :]
    cosine = jnp.concatenate([jnp.cos(angles), jnp.cos(angles)], axis=-1)
    sine_signed = jnp.concatenate([-jnp.sin(angles), jnp.sin(angles)], axis=-1)
    return (cosine, sine_signed)


def rms_parts(values):
    inverse = rms_inverse(values)
    return (inverse, values * inverse)


def norm_back(grad_scaled, normed, inverse):
    return inverse * (grad_scaled - normed * jnp.mean(grad_scaled * normed, axis=-1, keepdims=True))


def adam_small(param_now, gradient, first_now, second_now, rate_here):
    first_new = beta_first * first_now + (1.0 - beta_first) * gradient
    second_new = beta_second * second_now + (1.0 - beta_second) * gradient * gradient
    param_new = param_now - rate_here * (first_new / first_fix) / (
        jnp.sqrt(second_new / second_fix) + adam_eps
    )
    return (param_new, first_new, second_new)


def swap_halves(values):
    return lax.ppermute(values, "narrow", [(0, 1), (1, 0)])


def body(
    tokens,
    cotangent,
    segments,
    owner_list,
    masters,
    first_moment,
    second_moment,
    left_basis,
    right_basis,
    gains,
    gain_first,
    gain_second,
    biases,
    bias_first,
    bias_second,
):
    half = lax.axis_index("narrow")
    wide_index = lax.axis_index("wide")
    wide_count = lax.axis_size("wide")
    tokens_here = tokens.shape[0]
    slots_here = masters.shape[0]
    slots_half = owner_list.shape[0]
    own_start = half * tokens_here
    gains_here = gains.shape[0]
    biases_here = biases.shape[1]

    def join_halves(own, other, axis=0):
        return jnp.where(
            half == 0, jnp.concatenate([own, other], axis=axis), jnp.concatenate([other, own], axis=axis)
        )

    gain_pair = join_halves(gains, swap_halves(gains))
    gain_high = lax.reduce_precision(gain_pair, 8, 7)
    small_values = jnp.concatenate([gain_high, gain_pair - gain_high, biases.reshape(-1)]).astype(bf16)
    pair_gains = 2 * gains_here
    small_block = jnp.pad(small_values, (0, BLK * BLK - small_values.shape[0])).reshape(1, BLK, BLK)
    weights = lax.all_gather(
        jnp.concatenate([masters.astype(bf16), small_block], axis=0), "wide", axis=0, tiled=True
    )
    position = jnp.arange(slots_half, dtype=jnp.int32)
    empty = owner_list == BLOCK_TOTAL
    number = jnp.where(empty, BLOCK_TOTAL - 1 + jnp.cumsum(empty.astype(jnp.int32)), owner_list)
    slot_rows = position + position // slots_here
    rows = jnp.zeros((slots_half,), jnp.int32).at[number].set(slot_rows, unique_indices=True)

    segment_row = lax.dynamic_index_in_dim(segments, wide_index, 0, keepdims=False)
    cosine, sine = rope_tables(segment_row)
    token_index = jnp.arange(segment_row.shape[0], dtype=jnp.int32)
    allowed_turned = (
        (segment_row[None, :] == segment_row[:, None]) & (token_index[None, :] >= token_index[:, None])
    ).astype(f32)
    tokens_row = join_halves(tokens, swap_halves(tokens))
    cotangent_row = join_halves(cotangent, swap_halves(cotangent))
    weights, tokens_row, cotangent_row = lax.optimization_barrier((weights, tokens_row, cotangent_row))
    small_all = weights[slots_here :: slots_here + 1].reshape(wide_count, BLK * BLK)[:, : small_values.shape[0]]
    small_all = small_all.astype(f32)
    gain_full = (small_all[:, :pair_gains] + small_all[:, pair_gains : 2 * pair_gains]).reshape(2, D)
    bias_full = small_all[:, 2 * pair_gains :].reshape(1, QKV_WIDTH)

    attention_part, normed_one_turned, qkv, mixed_turned, log_total = run_attention_forward(
        rows, tokens_row, gain_full[0:1], bias_full, cosine, sine, allowed_turned, weights
    )
    attention_other = swap_halves(attention_part)
    branch_part, grad_two_part, resid, normed_two_turned, gain_two_part, pair_grads, active_turned = run_hidden_grads(
        rows, tokens_row, attention_part, attention_other, gain_full[1:2], cotangent_row, weights
    )
    grad_two_other = swap_halves(grad_two_part)
    grads = run_hidden_weight_grads(
        rows, normed_two_turned, cotangent_row, pair_grads, active_turned, wide_count * (slots_here + 1)
    )
    grad_resid, grad_one_part, grads = run_attention_backward(
        rows, tokens_row, resid, grad_two_part, grad_two_other, cotangent_row, gain_full, cosine, sine, allowed_turned,
        normed_one_turned, qkv, mixed_turned, log_total, gain_two_part, weights, grads, wide_count,
    )

    def own_rows(values):
        return lax.dynamic_slice_in_dim(values, own_start, tokens_here, 0)

    def other_rows(values):
        return lax.dynamic_slice_in_dim(values, tokens_here - own_start, tokens_here, 0)

    branch_send, grad_resid = lax.optimization_barrier((other_rows(branch_part), grad_resid))
    branch_other = swap_halves(branch_send)
    output = (
        own_rows(resid) + own_rows(branch_part).astype(f32) + branch_other.astype(f32)
    ).astype(bf16)
    grad_one_other = swap_halves(other_rows(grad_one_part))

    if wide_count == 16:
        reduced = run_sum_for_owners(grads, wide_count)
    else:
        reduced = lax.psum_scatter(grads, "wide", scatter_dimension=0, tiled=True)

    block_grad, new_masters, new_first, new_second = run_soap(
        reduced, masters, first_moment, second_moment, left_basis, right_basis
    )
    places = [small_places(owner, wide_count) for owner in range(wide_count)]
    gain_offset = jnp.asarray([place[1] for place in places], jnp.int32)[wide_index]
    bias_offset = jnp.asarray([place[3] for place in places], jnp.int32)[wide_index]
    small_sums = reduced[slots_here, :8].astype(f32)
    gain_sums = lax.dynamic_slice_in_dim(small_sums[:2].reshape(-1), gain_offset, pair_gains, 0)
    gain_sums = gain_sums.reshape(2, gains_here)
    gain_sums = gain_sums + swap_halves(gain_sums)
    gain_grad = lax.dynamic_index_in_dim(gain_sums, half, 0, keepdims=False)
    bias_grad = lax.dynamic_slice_in_dim(small_sums[2], bias_offset, biases_here, 0).reshape(biases.shape)
    new_gains, new_gain_first, new_gain_second = adam_small(gains, gain_grad, gain_first, gain_second, rate_gains)
    new_biases, new_bias_first, new_bias_second = adam_small(biases, bias_grad, bias_first, bias_second, rate_small)

    inverse_one, normed_one = rms_parts(tokens.astype(f32))
    grad_one = own_rows(grad_one_part).astype(f32) + grad_one_other.astype(f32)
    input_grad = own_rows(grad_resid) + norm_back(grad_one * gain_full[0:1], normed_one, inverse_one)
    return (
        output,
        input_grad,
        block_grad,
        new_masters,
        new_first,
        new_second,
        gain_grad,
        new_gains,
        new_gain_first,
        new_gain_second,
        bias_grad,
        new_biases,
        new_bias_first,
        new_bias_second,
    )


def solution(mesh):
    tokens_spec = P(("wide", "narrow"), None)
    blocks_spec = P(("wide", "narrow"), None, None)
    gains_spec = P(("wide", "narrow"))
    bias_spec = P("narrow", "wide")
    in_specs = (
        (tokens_spec, tokens_spec, P(), P()) + (blocks_spec,) * 5 + (gains_spec,) * 3 + (bias_spec,) * 3
    )
    out_specs = (tokens_spec, tokens_spec) + (blocks_spec,) * 4 + (gains_spec,) * 4 + (bias_spec,) * 4
    return jax.shard_map(body, mesh=mesh, in_specs=in_specs, out_specs=out_specs, check_vma=False)
```

time: 2170 us -> 765 us (0.35)
  waiting for transfers between devices: 1070 us -> 245 us
  local copies, waits for them, and re-layouts: 634 us -> 23.1 us
  Pallas kernels: 0 us -> 440 us
  matrix products: 225 us -> 0 us
  blocking collectives: 144 us -> 0 us
  other arithmetic: 70.3 us -> 22.4 us
    reduce_scatter x5 -> x0, waiting for transfers between devices: 810 us -> none  [the longest x1 753 us: body(): lax.psum_scatter(term_all, 'wide', scatter_dimension=0, tiled=True)]
    pallas_call x0 -> x6, Pallas kernels: none -> 440 us  [the longest x1 253 us: run_sum_for_owners(): pl.pallas_call(functools.partial(sum_for_owners, line, steps, late_steps)...]
    scatter x8 -> x1, local copies, waits for them, and re-layouts: 274 us -> 8.66 us  [body(): jnp.zeros((slots_half,), jnp.int32).at[number]]
    dot_general x31 -> x0, matrix products: 225 us -> none  [the longest x7 58.5 us: apply_blocks(): jnp.einsum('tra,rcab->tcb', grouped, weight_blocks, preferred_element_typ...]
    unnamed x4 -> x0, blocking collectives: 144 us -> none
    dot_general x9 -> x0, local copies, waits for them, and re-layouts: 94.3 us -> none  [the longest x5 63.5 us: apply_blocks(): jnp.einsum('tra,rcab->tcb', grouped, weight_blocks, preferred_element_typ...]
    transpose x4 -> x0, local copies, waits for them, and re-layouts: 67 us -> none  [block_terms(): jnp.einsum('tra,tcb->rcab', inputs_low.reshape(rows_here, row_blocks, BLK...]
    all_gather x5 -> x1, waiting for transfers between devices: 257 us -> 196 us  [body(): lax.all_gather(jnp.concatenate([masters.astype(bf16), small_block], axis=...]
  transfers between devices with their start and end apart: 10 -> 9, of which waited for: 6 -> 5; matrix products, arithmetic and copies ran while one was open for 29% -> 4% of each run, Pallas kernels for 0% -> 43%
where the time goes in v1:
time: 765 us; the launch traced here: 761 us
  Pallas kernels  440 us (58%)
  waiting for transfers between devices  245 us (32%)
  local copies, waits for them, and re-layouts  23.1 us (3%)
  other arithmetic  22.4 us (3%)
  between operations  17.8 us (2%)
  starting transfers between devices  11.4 us (1%)
    pallas_call x1, Pallas kernels, run_sum_for_owners(): pl.pallas_call(functools.partial(sum_for_owners, line, steps, late_steps)...  253 us
    all_gather x1, waiting for transfers between devices, body(): lax.all_gather(jnp.concatenate([masters.astype(bf16), small_block], axis=...  196 us
    pallas_call x1, Pallas kernels, run_hidden_grads(): pl.pallas_call(hidden_grads, out_shape=[shape((length, D), bf16), shape((...  75.1 us
    ppermute x8, waiting for transfers between devices, swap_halves(): return lax.ppermute(values, 'narrow', [(0, 1), (1, 0)])  49 us
    pallas_call x1, Pallas kernels, run_soap(): pl.pallas_call(soap_update, grid=(slots // group,), out_shape=[shape] * 4...  44.7 us
    pallas_call x1, Pallas kernels, run_hidden_weight_grads(): pl.pallas_call(hidden_weight_grads, grid=(TILES,), out_shape=jax.ShapeDty...  31.4 us
    pallas_call x1, Pallas kernels, run_attention_backward(): pl.pallas_call(attention_backward, out_shape=[shape((length, D), f32), sh...  23.9 us
  transfers between devices with their start and end apart: 9, of which 5 were waited for; matrix products, arithmetic and copies ran while one was open for 4% of the time, Pallas kernels for 43%

profile of v1, /device:TPU:0, one launch (start us, length us, event | category | flops | bytes accessed | tf_op | source)
XLA Modules:
  0.0 760.6 jit_solution(13524933215361910845)
XLA Ops:
  7.2 3.0 collective-permute-start
  10.3 0.7 convert_bitcast_fusion.1
  10.9 3.3 convert_element_type.38
  14.3 0.1 reduce-precision_convert_fusion
  14.3 0.1 fusion.15
  14.4 1.9 pad_maximum_fusion
  16.3 1.1 copy-done
  17.4 0.2 copy-done.7
  17.7 1.8 collective-permute-start.2
  19.5 0.9 compare_reduce_fusion
  20.3 0.1 add_select_fusion.1
  20.4 0.3 reduce-window.24
  20.7 0.1 slice.76
  20.9 0.3 reduce-window.16
  21.1 0.1 slice.82
  21.3 0.1 slice_reduce_fusion.1
  21.4 0.1 slice_reduce_fusion
  21.5 0.1 fusion.22
  21.6 1.0 fusion.9
  22.7 8.7 %scatter_custom_fusion.rows_ref = s32[1440]{0:T(1024)} fusion(s32[1440]{0:T(1024)S(1)} %get-tuple-element.77, s32[1440]{0:T(1024)S(1)} %get-tuple-element.78, s32[]{:T(128)} %constant.32.clone.1), kind=kCustom, calls=%fused_computation.49 | custom fusion | bytes 5764 | tf_op jit(solution)/shard_map/scatter | solution.py:1095
  31.3 0.7 constant_dynamic-slice_fusion.5
  32.1 1.0 pad_maximum_fusion.1
  33.1 1.2 fusion.8.allowed_ref
  34.3 3.7 collective-permute-done.1
  38.0 2.9 maximum_select_fusion.x_ref
  40.9 12.4 %collective-permute-done.2 = bf16[256,1536]{1,0:T(8,128)(2,1)S(1)} collective-permute-done((bf16[256,1536]{1,0:T(8,128)(2,1)S(1)}, bf16[256,1536]{1,0:T(8,128)(2,1)S(1)}, u32[]{:S(2)}, u32[]{:S(2)}) %collective-permute-start.2) | collective-permute-done | bytes 786464 | tf_op jit(solution)/shard_map/ppermute | solution.py:1048
  53.3 1.8 maximum_select_fusion.1.cot_ref
  55.1 196.4 %all-gather.2.cloned.1.call-done.weights = bf16[1456,128,128]{2,1,0:T(8,128)(2,1)} async-done(((bf16[91,128,128]{2,1,0:T(8,128)(2,1)}), bf16[1456,128,128]{2,1,0:T(8,128)(2,1)}) %all-gather.2.cloned.1.call-update) | async-done | bytes 47710224 | tf_op jit(solution)/shard_map/all_gather | solution.py:1088
  251.5 1.1 slice.67
  252.6 0.3 copy.34
  253.0 0.1 slice_add_fusion
  253.0 0.7 slice.72.gain_ref
  253.7 0.7 reshape.166.bias_ref
  254.4 12.4 %attention_forward.1 = (bf16[512,1536]{1,0:T(8,128)(2,1)}, bf16[1536,512]{1,0:T(8,128)(2,1)}, bf16[512,1024]{1,0:T(8,128)(2,1)}, bf16[768,512]{1,0:T(8,128)(2,1)}, f32[8,512]{1,0:T(8,128)}) custom-call(s32[1440]{0:T(1024)} %scatter_custom_fusion.rows_ref, bf16[512,1536]{1,0:T(8,128)(2,1)} %maximum_select_fusion.x_ref, f32[1,1536]{1,0:T(1,128)} %slice.72.gain_ref, ...), custom_call_target="tpu_custom_call" | custom-call | tf_op jit(solution)/shard_map/attention_forward/pallas_call | solution.py:517
  266.8 1.5 collective-permute-start.3
  268.4 0.6 dynamic_slice.45
  272.2 0.2 fusion.6
  272.4 0.7 reshape.168.gain_ref
  273.2 0.7 slice.79.gain_ref
  273.8 29.8 %collective-permute-done.3.other_ref = bf16[512,1536]{1,0:T(8,128)(2,1)S(1)} collective-permute-done((bf16[512,1536]{1,0:T(8,128)(2,1)}, bf16[512,1536]{1,0:T(8,128)(2,1)S(1)}, u32[]{:S(2)}, u32[]{:S(2)}) %collective-permute-start.3) | collective-permute-done | bytes 1572896 | tf_op jit(solution)/shard_map/ppermute | solution.py:1048
  303.6 1.1 copy-done.2
  304.8 75.1 %hidden_grads.1 = (bf16[512,1536]{1,0:T(8,128)(2,1)}, bf16[512,1536]{1,0:T(8,128)(2,1)}, f32[512,1536]{1,0:T(8,128)}, bf16[1536,512]{1,0:T(8,128)(2,1)}, f32[1,1...) custom-call(s32[1440]{0:T(1024)} %scatter_custom_fusion.rows_ref, ...), custom_call_target="tpu_custom_call" | custom-call | tf_op jit(solution)/shard_map/hidden_grads/pallas_call | solution.py:543
  379.9 1.5 collective-permute-start.4
  381.4 31.4 %hidden_weight_grads.1.grads_in = bf16[1456,128,128]{2,1,0:T(8,128)(2,1)} custom-call(s32[1440]{0:T(1024)} %scatter_custom_fusion.rows_ref, bf16[1536,512]{1,0:T(8,128)(2,1)} %get-tuple-element.50.normed_turned_ref, bf16[512,1536]{1,0:T(8,128)(2,1)} %maximum_select_fusion.1.cot_ref, bf16[7,512,1280]{2,1,0:T(8,128)(2,1)} %get-tuple-element.51.pair_ref, ...), custom_call_target="tpu_custom_call" | custom-call | flops 21139292160 | bytes 55050240 | tf_op jit(solution)/shard_map/hidden_weight_grads/pallas_call | solution.py:579
  412.8 3.1 collective-permute-done.4.other_ref
  415.9 1.1 copy-done.5
  417.0 23.9 %attention_backward.1 = (f32[512,1536]{1,0:T(8,128)}, bf16[512,1536]{1,0:T(8,128)(2,1)}, bf16[1456,128,128]{2,1,0:T(8,128)(2,1)}) custom-call(s32[1440]{0:T(1024)} %scatter_custom_fusion.rows_ref, bf16[512,1536]{1,0:T(8,128)(2,1)} %maximum_select_fusion.x_ref, f32[512,1536]{1,0:T(8,128)} %get-tuple-element.42.resid_ref, ...), custom_call_target="tpu_custom_call", output_to_operand_aliasing={{2}: (16, {})} | custom-call | tf_op jit(solution)/shard_map/attention_backward/pallas_call | solution.py:609
  440.9 2.2 constant_dynamic-slice_fusion.2
  443.1 1.4 collective-permute-start.6
  444.5 0.9 constant_dynamic-slice_fusion.3
  445.5 253.1 %sum_for_owners.1.grad_in = f32[91,128,128]{2,1,0:T(8,128)} custom-call(bf16[4,2,2,91,128,128]{5,4,3,2,1,0:T(8,128)(2,1)} %bitcast.31), custom_call_target="tpu_custom_call" | custom-call | bytes 381681664 | tf_op jit(solution)/shard_map/sum_for_owners/pallas_call | solution.py:986
  698.6 0.7 slice.81
  699.3 0.7 slice_bitcast_fusion
  699.9 0.1 dynamic_slice.46
  700.0 0.1 reshape.171
  700.1 0.5 collective-permute-start.7
  700.6 1.5 collective-permute-start.5
  702.1 0.6 divide_subtract_fusion
  702.7 44.7 %soap_update.1 = (f32[90,128,128]{2,1,0:T(8,128)}, f32[90,128,128]{2,1,0:T(8,128)}, f32[90,128,128]{2,1,0:T(8,128)}, f32[90,128,128]{2,1,0:T(8,128)}) custom-call(f32[91,128,128]{2,1,0:T(8,128)} %sum_for_owners.1.grad_in, f32[90,128,128]{2,1,0:T(8,128)} %masters_ref.1, f32[90,128,128]{2,1,0:T(8,128)} %first_ref.1, f32[90,128,128]{2,1,0:T(8,128)} %second_ref.1, ...), custom_call_target="tpu_custom_call" | custom-call | tf_op jit(solution)/shard_map/soap_update/pallas_call | solution.py:648
  747.5 0.5 divide_subtract_fusion.1
  748.0 0.5 fusion.2
  748.5 0.3 copy-done.4
  748.8 3.0 add_convert_fusion
  751.8 1.7 fusion.5
  (49 shorter events, 0.4 us)
Async XLA Ops:
  7.2 244.3 %all-gather.2.cloned.1.call-start = ((), (), s32[]{:S(2)}) async-start(), calls=%async_computation | async-start | bytes 50692096 | tf_op jit(solution)/shard_map/all_gather | solution.py:1088
  7.2 7.0 collective-permute-start
  10.9 3.3 copy-start.9
  16.3 1.1 copy-start
  16.3 1.4 copy-start.7
  16.3 4.5 copy-start.8
  17.4 20.6 %collective-permute-start.1 = (bf16[256,1536]{1,0:T(8,128)(2,1)S(1)}, bf16[256,1536]{1,0:T(8,128)(2,1)}, u32[]{:S(2)}, u32[]{:S(2)}) collective-permute-start(bf16[256,1536]{1,0:T(8,128)(2,1)S(1)} %copy-done), channel_id=1, source_target_pairs={{0,1},{1,0},{2,3},{3,2},{4,5},{5,4},{6,7},{7,6},{8,9},{9,8},{10,11... | collective-permute-start | bytes 2359304 | tf_op jit(solution)/shard_map/ppermute | solution.py:1048
  17.7 35.6 %collective-permute-start.2 = (bf16[256,1536]{1,0:T(8,128)(2,1)S(1)}, bf16[256,1536]{1,0:T(8,128)(2,1)S(1)}, u32[]{:S(2)}, u32[]{:S(2)}) collective-permute-start(bf16[256,1536]{1,0:T(8,128)(2,1)S(1)} %copy-done.7), channel_id=1, source_target_pairs={{0,1},{1,0},{2,3},{3,2},{4,5},{5,4},{6,7},{7,6},{8,9},{9,8},{10,11... | collective-permute-start | bytes 2359304 | tf_op jit(solution)/shard_map/ppermute | solution.py:1048
  254.4 14.0 %copy-start.15 = (s32[16]{0:T(128)S(1)}, s32[16]{0:T(128)}, u32[]{:S(2)}) copy-start(s32[16]{0:T(128)} %constant.100.clone) | copy-start | bytes 196
  266.8 36.8 %collective-permute-start.3 = (bf16[512,1536]{1,0:T(8,128)(2,1)}, bf16[512,1536]{1,0:T(8,128)(2,1)S(1)}, u32[]{:S(2)}, u32[]{:S(2)}) collective-permute-start(bf16[512,1536]{1,0:T(8,128)(2,1)} %get-tuple-element.40.own_ref), channel_id=1, source_target_pairs={{0,1},{1,0},{2,3},{3,2},{4,5},{5,4},{6,7},{7,6},{8,9},{9,8},{10,11... | collective-permute-start | bytes 4718600 | tf_op jit(solution)/shard_map/ppermute | solution.py:1048
  303.6 1.1 copy-start.2
  379.9 36.0 %collective-permute-start.4 = (bf16[512,1536]{1,0:T(8,128)(2,1)}, bf16[512,1536]{1,0:T(8,128)(2,1)S(1)}, u32[]{:S(2)}, u32[]{:S(2)}) collective-permute-start(bf16[512,1536]{1,0:T(8,128)(2,1)} %get-tuple-element.44.own_ref), channel_id=1, source_target_pairs={{0,1},{1,0},{2,3},{3,2},{4,5},{5,4},{6,7},{7,6},{8,9},{9,8},{10,11... | collective-permute-start | bytes 4718600 | tf_op jit(solution)/shard_map/ppermute | solution.py:1048
  415.9 1.1 copy-start.5
  440.9 3.6 copy-start.3
  443.1 304.9 %collective-permute-start.6 = (bf16[256,1536]{1,0:T(8,128)(2,1)}, bf16[256,1536]{1,0:T(8,128)(2,1)S(1)}, u32[]{:S(2)}, u32[]{:S(2)}) collective-permute-start(bf16[256,1536]{1,0:T(8,128)(2,1)} %constant_dynamic-slice_fusion.2), channel_id=1, source_target_pairs={{0,1},{1,0},{2,3},{3,2},{4,5},{5,4},{6,7},{7,6},{8,9},{9,8},{10,11... | collective-permute-start | bytes 2359304 | tf_op jit(solution)/shard_map/ppermute | solution.py:1048
  445.5 256.7 %copy-start.10 = (f32[1,64]{1,0:T(1,128)S(1)}, f32[1,64]{1,0:T(1,128)}, u32[]{:S(2)}) copy-start(f32[1,64]{1,0:T(1,128)} %param.29) | copy-start | bytes 772
  445.5 256.7 %copy-start.11 = (f32[1,64]{1,0:T(1,128)S(1)}, f32[1,64]{1,0:T(1,128)}, u32[]{:S(2)}) copy-start(f32[1,64]{1,0:T(1,128)} %param.30) | copy-start | bytes 772
  445.5 256.7 %copy-start.12 = (f32[1,64]{1,0:T(1,128)S(1)}, f32[1,64]{1,0:T(1,128)}, u32[]{:S(2)}) copy-start(f32[1,64]{1,0:T(1,128)} %param.31) | copy-start | bytes 772
  700.1 47.3 %collective-permute-start.7 = (f32[2,96]{1,0:T(2,128)S(1)}, f32[2,96]{1,0:T(2,128)S(1)}, u32[]{:S(2)}, u32[]{:S(2)}) collective-permute-start(f32[2,96]{1,0:T(2,128)S(1)} %reshape.171), channel_id=1, source_target_pairs={{0,1},{1,0},{2,3},{3,2},{4,5},{5,4},{6,7},{7,6},{8,9},{9,8},{10,11... | collective-permute-start | bytes 2312 | tf_op jit(solution)/shard_map/ppermute | solution.py:1048
  700.6 47.9 %collective-permute-start.5 = (bf16[256,1536]{1,0:T(8,128)(2,1)}, bf16[256,1536]{1,0:T(8,128)(2,1)}, u32[]{:S(2)}, u32[]{:S(2)}) collective-permute-start(bf16[256,1536]{1,0:T(8,128)(2,1)} %constant_dynamic-slice_fusion.3), channel_id=1, source_target_pairs={{0,1},{1,0},{2,3},{3,2},{4,5},{5,4},{6,7},{7,6},{8,9},{9,8},{10,11... | collective-permute-start | bytes 2359304 | tf_op jit(solution)/shard_map/ppermute | solution.py:1048
  702.7 44.7 %copy-start.13 = (f32[96]{0:T(128)S(1)}, f32[96]{0:T(128)}, u32[]{:S(2)}) copy-start(f32[96]{0:T(128)} %param.27) | copy-start | bytes 1156
  702.7 44.7 %copy-start.14 = (f32[96]{0:T(128)S(1)}, f32[96]{0:T(128)}, u32[]{:S(2)}) copy-start(f32[96]{0:T(128)} %param.28) | copy-start | bytes 1156
  702.7 45.3 %copy-start.1 = (bf16[512,1536]{1,0:T(8,128)(2,1)S(1)}, bf16[512,1536]{1,0:T(8,128)(2,1)}, u32[]{:S(2)}) copy-start(bf16[512,1536]{1,0:T(8,128)(2,1)} %get-tuple-element.56) | copy-start | bytes 4718596
  747.4 1.4 copy-start.4
  748.5 3.3 copy-start.6
Sparse Core Ops, SparseCore 0:
  16.4 235.0 all-gather.1

commit v2 on v1

--- a/solution.py
+++ b/solution.py
@@ -48,8 +48,9 @@
 DOWN_BASE = UP_BASE + ROW_BLOCKS * HIDDEN_COLS
 BLOCK_TOTAL = DOWN_BASE + HIDDEN_COLS * ROW_BLOCKS
 
-TILE_BLOCKS = 5
-TILES = HIDDEN_COLS // TILE_BLOCKS
+TILE_BLOCKS = 6
+TILES = -(-HIDDEN_COLS // TILE_BLOCKS)
+LAST_BLOCKS = HIDDEN_COLS - (TILES - 1) * TILE_BLOCKS
 TILE = TILE_BLOCKS * BLK
 COLS = 256
 ROWS = 64
@@ -194,52 +195,115 @@
         part_ref[:, pl.ds(begin, size)] = dot_nn(mixed[...], w_out[:, pl.ds(begin, size)]).astype(bf16)
 
 
+def pair_copies(rows_ref, blocks_hbm, pair, sem, column, place, outward=False):
+    return [
+        block_copy(blocks_hbm.at[rows_ref[base + i * HIDDEN_COLS + column]], block_ref(pair, i, which), sem, outward)
+        for i in range(ROW_BLOCKS)
+        for base, which in ((GATE_BASE, 2 * place), (UP_BASE, 2 * place + 1))
+    ]
+
+
+def down_copies(rows_ref, blocks_hbm, down, sem, column, place, outward=False):
+    return [
+        block_copy(blocks_hbm.at[rows_ref[DOWN_BASE + column * ROW_BLOCKS + i]], block_ref(down, place, i), sem, outward)
+        for i in range(ROW_BLOCKS)
+    ]
+
+
+def block_copy(in_hbm, in_vmem, sem, outward):
+    return pltpu.make_async_copy(*((in_vmem, in_hbm) if outward else (in_hbm, in_vmem)), sem)
+
+
+def start_all(copies):
+    for copy in copies:
+        copy.start()
+
+
+def hidden_column(tile, place):
+    return jnp.minimum(tile * TILE_BLOCKS + place, HIDDEN_COLS - 1)
+
+
+def hidden_tiles(run):
+    @pl.loop(0, TILES - 1)
+    def _(tile):
+        run(tile, lax.rem(tile, 2), TILE_BLOCKS, True)
+
+    run(TILES - 1, (TILES - 1) % 2, LAST_BLOCKS, False)
+
+
+def active_grads(rows_ref, cot_ref, weights, out, w_down, stage, load_sems, store_sems):
+    def fetch(tile, slot, place):
+        start_all(
+            down_copies(rows_ref, weights, w_down.at[slot], load_sems.at[slot], hidden_column(tile, place), place)
+        )
+
+    for place in range(TILE_BLOCKS):
+        fetch(0, 0, place)
+
+    def run(tile, slot, blocks, more):
+        wait_bytes(w_down.at[slot], load_sems.at[slot])
+
+        @pl.when(tile >= 2)
+        def _():
+            wait_bytes(stage.at[slot], store_sems.at[slot])
+
+        if more:
+            for place in range(TILE_BLOCKS):
+                fetch(tile + 1, 1 - slot, place)
+        for begin, size in spans(blocks * BLK, COLS):
+            stage[slot, :, pl.ds(begin, size)] = dot_nt(cot_ref[...], w_down[slot, pl.ds(begin, size), :])
+        pltpu.make_async_copy(stage.at[slot], out.at[tile], store_sems.at[slot]).start()
+
+    hidden_tiles(run)
+    for tile in range(max(TILES - 2, 0), TILES):
+        wait_bytes(stage.at[tile % 2], store_sems.at[tile % 2])
+
+
 def hidden_grads(
     rows_ref,
     x_ref,
     own_ref,
     other_ref,
     gain_ref,
-    cot_ref,
+    active_grad,
     weights,
-    branch_ref,
     grad_ref,
     resid_ref,
     normed_turned_ref,
     gain_part_ref,
     pair_grads,
+    active,
     active_turned,
     w_pair,
-    w_down,
-    pair,
     grad_active,
-    active,
+    straight,
     turned,
     grads,
     normed,
-    branch_sum,
     grad_sum,
     load_sems,
     store_sems,
 ):
     length = x_ref.shape[0]
 
-    def fetch(tile, slot):
-        first = tile * TILE_BLOCKS
-        fetch_piece(
-            rows_ref, weights, w_down.at[slot], DOWN_BASE + first * ROW_BLOCKS, ROW_BLOCKS, TILE_BLOCKS, ROW_BLOCKS, 0,
-            load_sems.at[slot, 1],
-        )
-        fetch_piece(
-            rows_ref, weights, w_pair.at[slot], GATE_BASE + first, HIDDEN_COLS, ROW_BLOCKS, TILE_BLOCKS, 0,
-            load_sems.at[slot, 0],
-        )
-        fetch_piece(
-            rows_ref, weights, w_pair.at[slot], UP_BASE + first, HIDDEN_COLS, ROW_BLOCKS, TILE_BLOCKS, TILE_BLOCKS,
-            load_sems.at[slot, 0],
-        )
-
-    fetch(0, 0)
+    def fetch(tile, slot, place):
+        start_all(
+            pair_copies(rows_ref, weights, w_pair.at[slot], load_sems.at[slot, 0], hidden_column(tile, place), place)
+        )
+
+    def load_grad(tile, slot):
+        return pltpu.make_async_copy(active_grad.at[tile], grad_active.at[slot], load_sems.at[slot, 1])
+
+    def stores(tile, slot):
+        return (
+            pltpu.make_async_copy(turned.at[slot], active_turned.at[tile], store_sems.at[slot, 0]),
+            pltpu.make_async_copy(grads.at[slot], pair_grads.at[tile], store_sems.at[slot, 1]),
+            pltpu.make_async_copy(straight.at[slot], active.at[tile], store_sems.at[slot, 2]),
+        )
+
+    for place in range(TILE_BLOCKS):
+        fetch(0, 0, place)
+    load_grad(0, 0).start()
 
     def norm_rows(rows):
         values = x_ref[rows, :].astype(f32) + own_ref[rows, :].astype(f32) + other_ref[rows, :].astype(f32)
@@ -247,52 +311,48 @@
         normed[rows, :] = (values * rms_inverse(values) * gain_ref[...]).astype(bf16)
 
     row_chunks(length, ROWS, norm_rows)
-    for begin, size in spans(D, COLS):
-        normed_turned_ref[pl.ds(begin, size), :] = normed[:, pl.ds(begin, size)].T
-    branch_sum[...] = jnp.zeros_like(branch_sum)
     grad_sum[...] = jnp.zeros_like(grad_sum)
 
-    @pl.loop(0, TILES)
-    def _(tile):
-        slot = lax.rem(tile, 2)
-
-        @pl.when(tile + 1 < TILES)
-        def _():
-            fetch(tile + 1, 1 - slot)
-
-        wait_bytes(w_down.at[slot], load_sems.at[slot, 1])
-        for begin, size in spans(TILE, COLS):
-            grad_active[:, pl.ds(begin, size)] = dot_nt(cot_ref[...], w_down[slot, pl.ds(begin, size), :])
+    def run(tile, slot, blocks, more):
         wait_bytes(w_pair.at[slot], load_sems.at[slot, 0])
-        for begin, size in spans(2 * TILE, COLS):
-            pair[:, pl.ds(begin, size)] = dot_nn(normed[...], w_pair[slot, :, pl.ds(begin, size)])
+        load_grad(tile, slot).wait()
+        if more:
+            load_grad(tile + 1, 1 - slot).start()
 
         @pl.when(tile >= 2)
         def _():
-            wait_bytes(turned.at[slot], store_sems.at[slot, 0])
-            wait_bytes(grads.at[slot], store_sems.at[slot, 1])
-
-        for begin, size in spans(TILE, BLK):
-            gate = pair[:, pl.ds(begin, size)]
-            upper = pair[:, pl.ds(TILE + begin, size)]
-            grad = grad_active[:, pl.ds(begin, size)]
+            for copy in stores(tile - 2, slot):
+                copy.wait()
+
+        for place in range(blocks):
+            columns = pl.ds(place * BLK, BLK)
+            pair = dot_nn(normed[...], w_pair[slot, :, pl.ds(2 * place * BLK, 2 * BLK)])
+            gate = pair[:, :BLK]
+            upper = pair[:, BLK:]
+            grad = grad_active[slot, :, columns]
             sigmoid = jax.nn.sigmoid(gate)
             silu = gate * sigmoid
             active_here = (silu * upper).astype(bf16)
-            active[:, pl.ds(begin, size)] = active_here
-            turned[slot, pl.ds(begin, size), :] = active_here.T
-            grads[slot, :, pl.ds(begin, size)] = (
+            straight[slot, :, columns] = active_here
+            turned[slot, columns, :] = active_here.T
+            grads[slot, :, pl.ds(2 * place * BLK, BLK)] = (
                 grad * upper * sigmoid * (1.0 + gate * (1.0 - sigmoid))
             ).astype(bf16)
-            grads[slot, :, pl.ds(TILE + begin, size)] = (grad * silu).astype(bf16)
-        pltpu.make_async_copy(turned.at[slot], active_turned.at[tile], store_sems.at[slot, 0]).start()
-        pltpu.make_async_copy(grads.at[slot], pair_grads.at[tile], store_sems.at[slot, 1]).start()
+            grads[slot, :, pl.ds((2 * place + 1) * BLK, BLK)] = (grad * silu).astype(bf16)
+            if more:
+                fetch(tile + 1, 1 - slot, place)
+        if more:
+            for place in range(blocks, TILE_BLOCKS):
+                fetch(tile + 1, 1 - slot, place)
+        turn = pl.ds(pl.multiple_of(tile * COLS, COLS), COLS)
+        normed_turned_ref[turn, :] = normed[:, turn].T
+        width = 2 * blocks * BLK
         for begin, size in spans(D, COLS):
             columns = pl.ds(begin, size)
-            branch_sum[:, columns] += dot_nn(active[...], w_down[slot, :, columns])
-            grad_sum[:, columns] += dot_nt(grads[slot], w_pair[slot, columns, :])
-
-    branch_ref[...] = branch_sum[...].astype(bf16)
+            grad_sum[:, columns] += dot_nt(grads[slot, :, :width], w_pair[slot, columns, :width])
+        start_all(stores(tile, slot))
+
+    hidden_tiles(run)
     grad_ref[...] = grad_sum[...].astype(bf16)
     gain_part_ref[...] = jnp.zeros_like(gain_part_ref)
 
@@ -302,49 +362,78 @@
 
     row_chunks(length, ROWS, gain_rows)
     for tile in range(max(TILES - 2, 0), TILES):
-        slot = tile % 2
-        wait_bytes(turned.at[slot], store_sems.at[slot, 0])
-        wait_bytes(grads.at[slot], store_sems.at[slot, 1])
+        for copy in stores(tile, tile % 2):
+            copy.wait()
 
 
 def hidden_weight_grads(
-    rows_ref, normed_turned_ref, cot_ref, pair_ref, turned_ref, grads, pair_stage, down_stage, sems
+    rows_ref, normed_turned_ref, cot_ref, pair_grads, active, active_turned, weights, branch_ref, grads,
+    pair, straight, turned, w_down, branch_sum, pair_stage, down_stage, load_sems, store_sems,
 ):
-    tile = pl.program_id(0)
-    slot = lax.rem(tile, 2)
-
-    def drain(which):
-        wait_bytes(pair_stage.at[which], sems.at[which, 0])
-        wait_bytes(down_stage.at[which], sems.at[which, 1])
-
-    @pl.when(tile >= 2)
-    def _():
-        drain(slot)
-
-    first = tile * TILE_BLOCKS
-    for row_begin, row_size in spans(D, 512):
-        for begin, size in spans(2 * TILE, COLS):
-            pair_stage[slot, pl.ds(row_begin, row_size), pl.ds(begin, size)] = dot_nn(
-                normed_turned_ref[pl.ds(row_begin, row_size), :], pair_ref[0, :, pl.ds(begin, size)]
-            ).astype(bf16)
-    store_piece(
-        rows_ref, pair_stage.at[slot], grads, GATE_BASE + first, HIDDEN_COLS, ROW_BLOCKS, TILE_BLOCKS, 0, sems.at[slot, 0]
-    )
-    store_piece(
-        rows_ref, pair_stage.at[slot], grads, UP_BASE + first, HIDDEN_COLS, ROW_BLOCKS, TILE_BLOCKS, TILE_BLOCKS,
-        sems.at[slot, 0],
-    )
-    for begin, size in spans(D, COLS):
-        down_stage[slot, :, pl.ds(begin, size)] = dot_nn(turned_ref[0], cot_ref[:, pl.ds(begin, size)]).astype(bf16)
-    store_piece(
-        rows_ref, down_stage.at[slot], grads, DOWN_BASE + first * ROW_BLOCKS, ROW_BLOCKS, TILE_BLOCKS, ROW_BLOCKS, 0,
-        sems.at[slot, 1],
-    )
-
-    @pl.when(tile == TILES - 1)
-    def _():
-        for which in range(2 if TILES > 1 else 1):
-            drain(which)
+    def loads(tile, slot):
+        return (
+            pltpu.make_async_copy(pair_grads.at[tile], pair.at[slot], load_sems.at[slot, 0]),
+            pltpu.make_async_copy(active_turned.at[tile], turned.at[slot], load_sems.at[slot, 1]),
+            pltpu.make_async_copy(active.at[tile], straight.at[slot], load_sems.at[slot, 2]),
+        )
+
+    def fetch(tile, slot, place):
+        start_all(
+            down_copies(rows_ref, weights, w_down.at[slot], load_sems.at[slot, 3], hidden_column(tile, place), place)
+        )
+
+    def drain(slot, blocks):
+        wait_bytes(pair_stage.at[slot, :, pl.ds(0, 2 * blocks * BLK)], store_sems.at[slot, 0])
+        wait_bytes(down_stage.at[slot, pl.ds(0, blocks * BLK)], store_sems.at[slot, 1])
+
+    start_all(loads(0, 0))
+    for place in range(TILE_BLOCKS):
+        fetch(0, 0, place)
+    branch_sum[...] = jnp.zeros_like(branch_sum)
+
+    def run(tile, slot, blocks, more):
+        for copy in loads(tile, slot):
+            copy.wait()
+        wait_bytes(w_down.at[slot], load_sems.at[slot, 3])
+        if more:
+            start_all(loads(tile + 1, 1 - slot))
+
+        @pl.when(tile >= 2)
+        def _():
+            drain(slot, TILE_BLOCKS)
+
+        width = blocks * BLK
+        down = turned[slot, pl.ds(0, width), :]
+        for begin, size in spans(D, COLS):
+            columns = pl.ds(begin, size)
+            down_stage[slot, pl.ds(0, width), columns] = dot_nn(down, cot_ref[:, columns]).astype(bf16)
+        for place in range(blocks):
+            column = tile * TILE_BLOCKS + place
+            start_all(
+                down_copies(rows_ref, grads, down_stage.at[slot], store_sems.at[slot, 1], column, place, outward=True)
+            )
+            columns = pl.ds(2 * place * BLK, 2 * BLK)
+            for begin, size in spans(D, 512):
+                pair_stage[slot, pl.ds(begin, size), columns] = dot_nn(
+                    normed_turned_ref[pl.ds(begin, size), :], pair[slot, :, columns]
+                ).astype(bf16)
+            start_all(
+                pair_copies(rows_ref, grads, pair_stage.at[slot], store_sems.at[slot, 0], column, place, outward=True)
+            )
+            if more:
+                fetch(tile + 1, 1 - slot, place)
+        if more:
+            for place in range(blocks, TILE_BLOCKS):
+                fetch(tile + 1, 1 - slot, place)
+        for begin, size in spans(D, COLS):
+            columns = pl.ds(begin, size)
+            branch_sum[:, columns] += dot_nn(straight[slot, :, :width], w_down[slot, :width, columns])
+
+    hidden_tiles(run)
+    branch_ref[...] = branch_sum[...].astype(bf16)
+    if TILES > 1:
+        drain((TILES - 2) % 2, TILE_BLOCKS)
+    drain((TILES - 1) % 2, LAST_BLOCKS)
 
 
 def attention_backward(
@@ -492,19 +581,25 @@
     new_first_ref,
     new_second_ref,
 ):
-    for index in range(masters_ref.shape[0]):
-        left = left_ref[index].astype(bf16)
-        left_turned = left_ref[index].T.astype(bf16)
-        right = right_ref[index].astype(bf16)
-        grad_ref[index] = grad_in[index].astype(f32)
-        rotated = dot_nn(left_turned, dot_nn(grad_in[index].astype(bf16), right).astype(bf16))
+    blocks = range(masters_ref.shape[0])
+    rights = [right_ref[index].astype(bf16) for index in blocks]
+    products = [dot_nn(grad_in[index].astype(bf16), rights[index]).astype(bf16) for index in blocks]
+    lefts = [left_ref[index].astype(bf16) for index in blocks]
+    rotated_blocks = [dot_nn(lefts[index].T, products[index]) for index in blocks]
+    normalized = []
+    for index in blocks:
+        rotated = rotated_blocks[index]
+        grad_ref[index] = grad_in[index]
         new_first = beta_first * first_ref[index] + (1.0 - beta_first) * rotated
         new_second = beta_second * second_ref[index] + (1.0 - beta_second) * rotated * rotated
         new_first_ref[index] = new_first
         new_second_ref[index] = new_second
-        normalized = new_first / first_fix / (jnp.sqrt(new_second / second_fix) + adam_eps)
-        update = dot_nn(left, dot_nt(normalized.astype(bf16), right).astype(bf16))
-        new_masters_ref[index] = masters_ref[index] - rate_blocks * update
+        normalized.append(
+            (new_first / first_fix / (jnp.sqrt(new_second / second_fix) + adam_eps)).astype(bf16)
+        )
+    products = [dot_nt(normalized[index], rights[index]).astype(bf16) for index in blocks]
+    for index in blocks:
+        new_masters_ref[index] = masters_ref[index] - rate_blocks * dot_nn(lefts[index], products[index])
 
 
 def params(**options):
@@ -537,66 +632,89 @@
     )(rows, x, gain, bias, cosine, sine, allowed, weights)
 
 
-def run_hidden_grads(rows, x, own, other, gain, cotangent, weights):
+def hidden_cost(length, products, bytes_moved):
+    return pl.CostEstimate(
+        flops=2 * products * length * D * TILE * TILES, bytes_accessed=bytes_moved, transcendentals=0
+    )
+
+
+def run_active_grads(rows, cotangent, weights):
+    length = cotangent.shape[0]
+    return pl.pallas_call(
+        active_grads,
+        out_shape=jax.ShapeDtypeStruct((TILES, length, TILE), f32),
+        in_specs=[SMEM_SPEC, VMEM_SPEC, ANY_SPEC],
+        out_specs=ANY_SPEC,
+        scratch_shapes=[
+            pltpu.VMEM((2, TILE, D), bf16),
+            pltpu.VMEM((2, length, TILE), f32),
+            pltpu.SemaphoreType.DMA((2,)),
+            pltpu.SemaphoreType.DMA((2,)),
+        ],
+        compiler_params=params(),
+        cost_estimate=hidden_cost(length, 1, TILES * TILE * (2 * D + 4 * length)),
+        name="active_grads",
+    )(rows, cotangent, weights)
+
+
+def run_hidden_grads(rows, x, own, other, gain, active_grad, weights):
     length = x.shape[0]
     shape = jax.ShapeDtypeStruct
     return pl.pallas_call(
         hidden_grads,
         out_shape=[
             shape((length, D), bf16),
-            shape((length, D), bf16),
             shape((length, D), f32),
             shape((D, length), bf16),
             shape((1, D), f32),
             shape((TILES, length, 2 * TILE), bf16),
+            shape((TILES, length, TILE), bf16),
             shape((TILES, TILE, length), bf16),
         ],
-        in_specs=[SMEM_SPEC] + [VMEM_SPEC] * 5 + [ANY_SPEC],
-        out_specs=[VMEM_SPEC] * 5 + [ANY_SPEC] * 2,
+        in_specs=[SMEM_SPEC] + [VMEM_SPEC] * 4 + [ANY_SPEC] * 2,
+        out_specs=[VMEM_SPEC] * 4 + [ANY_SPEC] * 3,
         scratch_shapes=[
             pltpu.VMEM((2, D, 2 * TILE), bf16),
-            pltpu.VMEM((2, TILE, D), bf16),
-            pltpu.VMEM((length, 2 * TILE), f32),
-            pltpu.VMEM((length, TILE), f32),
-            pltpu.VMEM((length, TILE), bf16),
+            pltpu.VMEM((2, length, TILE), f32),
+            pltpu.VMEM((2, length, TILE), bf16),
             pltpu.VMEM((2, TILE, length), bf16),
             pltpu.VMEM((2, length, 2 * TILE), bf16),
             pltpu.VMEM((length, D), bf16),
             pltpu.VMEM((length, D), f32),
+            pltpu.SemaphoreType.DMA((2, 2)),
+            pltpu.SemaphoreType.DMA((2, 3)),
+        ],
+        compiler_params=params(),
+        cost_estimate=hidden_cost(length, 4, 2 * TILES * TILE * (2 * D + 6 * length)),
+        name="hidden_grads",
+    )(rows, x, own, other, gain, active_grad, weights)
+
+
+def run_hidden_weight_grads(
+    rows, normed_turned, cotangent, pair_grads, active, active_turned, weights, slots
+):
+    length = cotangent.shape[0]
+    shape = jax.ShapeDtypeStruct
+    return pl.pallas_call(
+        hidden_weight_grads,
+        out_shape=[shape((length, D), bf16), shape((slots, BLK, BLK), bf16)],
+        in_specs=[SMEM_SPEC] + [VMEM_SPEC] * 2 + [ANY_SPEC] * 4,
+        out_specs=[VMEM_SPEC, ANY_SPEC],
+        scratch_shapes=[
+            pltpu.VMEM((2, length, 2 * TILE), bf16),
+            pltpu.VMEM((2, length, TILE), bf16),
+            pltpu.VMEM((2, TILE, length), bf16),
+            pltpu.VMEM((2, TILE, D), bf16),
             pltpu.VMEM((length, D), f32),
-            pltpu.SemaphoreType.DMA((2, 2)),
+            pltpu.VMEM((2, D, 2 * TILE), bf16),
+            pltpu.VMEM((2, TILE, D), bf16),
+            pltpu.SemaphoreType.DMA((2, 4)),
             pltpu.SemaphoreType.DMA((2, 2)),
         ],
         compiler_params=params(),
-        name="hidden_grads",
-    )(rows, x, own, other, gain, cotangent, weights)
-
-
-def run_hidden_weight_grads(rows, normed_turned, cotangent, pair_grads, active_turned, slots):
-    length = cotangent.shape[0]
-    flops = 2 * length * 3 * D * TILE * TILES
-    bytes_moved = 2 * (3 * D * TILE * TILES + 3 * TILE * TILES * length)
-    return pl.pallas_call(
-        hidden_weight_grads,
-        grid=(TILES,),
-        out_shape=jax.ShapeDtypeStruct((slots, BLK, BLK), bf16),
-        in_specs=[
-            SMEM_SPEC,
-            VMEM_SPEC,
-            VMEM_SPEC,
-            pl.BlockSpec((1, length, 2 * TILE), lambda tile: (tile, 0, 0)),
-            pl.BlockSpec((1, TILE, length), lambda tile: (tile, 0, 0)),
-        ],
-        out_specs=ANY_SPEC,
-        scratch_shapes=[
-            pltpu.VMEM((2, D, 2 * TILE), bf16),
-            pltpu.VMEM((2, TILE, D), bf16),
-            pltpu.SemaphoreType.DMA((2, 2)),
-        ],
-        compiler_params=params(),
-        cost_estimate=pl.CostEstimate(flops=flops, bytes_accessed=bytes_moved, transcendentals=0),
+        cost_estimate=hidden_cost(length, 4, 2 * TILES * TILE * (4 * D + 4 * length)),
         name="hidden_weight_grads",
-    )(rows, normed_turned, cotangent, pair_grads, active_turned)
+    )(rows, normed_turned, cotangent, pair_grads, active, active_turned, weights)
 
 
 def run_attention_backward(
@@ -1112,12 +1230,14 @@
         rows, tokens_row, gain_full[0:1], bias_full, cosine, sine, allowed_turned, weights
     )
     attention_other = swap_halves(attention_part)
-    branch_part, grad_two_part, resid, normed_two_turned, gain_two_part, pair_grads, active_turned = run_hidden_grads(
-        rows, tokens_row, attention_part, attention_other, gain_full[1:2], cotangent_row, weights
+    active_grad = run_active_grads(rows, cotangent_row, weights)
+    grad_two_part, resid, normed_two_turned, gain_two_part, pair_grads, active, active_turned = run_hidden_grads(
+        rows, tokens_row, attention_part, attention_other, gain_full[1:2], active_grad, weights
     )
     grad_two_other = swap_halves(grad_two_part)
-    grads = run_hidden_weight_grads(
-        rows, normed_two_turned, cotangent_row, pair_grads, active_turned, wide_count * (slots_here + 1)
+    branch_part, grads = run_hidden_weight_grads(
+        rows, normed_two_turned, cotangent_row, pair_grads, active, active_turned, weights,
+        wide_count * (slots_here + 1),
     )
     grad_resid, grad_one_part, grads = run_attention_backward(
         rows, tokens_row, resid, grad_two_part, grad_two_other, cotangent_row, gain_full, cosine, sine, allowed_turned,
@@ -1130,8 +1250,7 @@
     def other_rows(values):
         return lax.dynamic_slice_in_dim(values, tokens_here - own_start, tokens_here, 0)
 
-    branch_send, grad_resid = lax.optimization_barrier((other_rows(branch_part), grad_resid))
-    branch_other = swap_halves(branch_send)
+    branch_other = swap_halves(other_rows(branch_part))
     output = (
         own_rows(resid) + own_rows(branch_part).astype(f32) + branch_other.astype(f32)
     ).astype(bf16)
@@ -1143,7 +1262,7 @@
         reduced = lax.psum_scatter(grads, "wide", scatter_dimension=0, tiled=True)
 
     block_grad, new_masters, new_first, new_second = run_soap(
-        reduced, masters, first_moment, second_moment, left_basis, right_basis
+        reduced.astype(f32), masters, first_moment, second_moment, left_basis, right_basis
     )
     places = [small_places(owner, wide_count) for owner in range(wide_count)]
     gain_offset = jnp.asarray([place[1] for place in places], jnp.int32)[wide_index]

time: 765 us -> 720 us (0.941)
  Pallas kernels: 440 us -> 407 us
  waiting for transfers between devices: 245 us -> 233 us
    pallas_call x1, Pallas kernels: 75.1 us -> 41.5 us  [run_hidden_grads(): pl.pallas_call(hidden_grads, out_shape=[shape((length, D), bf16), shape((...]
    pallas_call x1 -> x2, Pallas kernels: 31.4 us -> 52.6 us  [the longest x1 37.6 us: run_hidden_weight_grads(): pl.pallas_call(hidden_weight_grads, out_shape=[shape((length, D), bf16),...]
    pallas_call x1, Pallas kernels: 44.7 us -> 23.9 us  [run_soap(): pl.pallas_call(soap_update, grid=(slots // group,), out_shape=[shape] * 4...]
    ppermute x8, waiting for transfers between devices: 49 us -> 36.1 us  [swap_halves(): return lax.ppermute(values, 'narrow', [(0, 1), (1, 0)])]
  transfers between devices with their start and end apart: 9 -> 9, of which waited for: 5 -> 4; matrix products, arithmetic and copies ran while one was open for 4% -> 5% of each run, Pallas kernels for 43% -> 49%
where the time goes in v2:
time: 720 us; the launch traced here: 714 us
  Pallas kernels  407 us (57%)
  waiting for transfers between devices  233 us (32%)
  other arithmetic  23.6 us (3%)
  local copies, waits for them, and re-layouts  22.5 us (3%)
  between operations  17.7 us (2%)
  starting transfers between devices  10.5 us (1%)
    pallas_call x1, Pallas kernels, run_sum_for_owners(): pl.pallas_call(functools.partial(sum_for_owners, line, steps, late_steps)...  253 us
    all_gather x1, waiting for transfers between devices, body(): lax.all_gather(jnp.concatenate([masters.astype(bf16), small_block], axis=...  196 us
    pallas_call x1, Pallas kernels, run_hidden_grads(): pl.pallas_call(hidden_grads, out_shape=[shape((length, D), bf16), shape((...  41.5 us
    pallas_call x1, Pallas kernels, run_hidden_weight_grads(): pl.pallas_call(hidden_weight_grads, out_shape=[shape((length, D), bf16),...  37.6 us
    ppermute x8, waiting for transfers between devices, swap_halves(): return lax.ppermute(values, 'narrow', [(0, 1), (1, 0)])  36.1 us
    pallas_call x1, Pallas kernels, run_soap(): pl.pallas_call(soap_update, grid=(slots // group,), out_shape=[shape] * 4...  23.9 us
    pallas_call x1, Pallas kernels, run_attention_backward(): pl.pallas_call(attention_backward, out_shape=[shape((length, D), f32), sh...  23.9 us
    pallas_call x1, Pallas kernels, run_active_grads(): pl.pallas_call(active_grads, out_shape=jax.ShapeDtypeStruct((TILES, lengt...  15 us
  transfers between devices with their start and end apart: 9, of which 4 were waited for; matrix products, arithmetic and copies ran while one was open for 5% of the time, Pallas kernels for 49%

profile of v2, /device:TPU:0, one launch (start us, length us, event | category | flops | bytes accessed | tf_op | source)
XLA Modules:
  0.0 714.3 jit_solution(5343625567544064178)
XLA Ops:
  7.2 3.0 collective-permute-start
  10.3 0.7 convert_bitcast_fusion.1
  10.9 3.3 convert_element_type.38
  14.3 0.1 reduce-precision_convert_fusion
  14.3 0.1 fusion.15
  14.4 1.9 pad_maximum_fusion
  16.3 1.1 copy-done
  17.4 0.2 copy-done.4
  17.7 1.8 collective-permute-start.2
  19.5 0.3 reduce-window.16
  19.8 0.1 slice.82
  19.9 0.9 compare_reduce_fusion
  20.8 0.1 add_select_fusion.1
  20.8 0.3 reduce-window.24
  21.1 0.1 slice.76
  21.3 0.1 slice_reduce_fusion.1
  21.4 0.1 slice_reduce_fusion
  21.5 0.1 fusion.22
  21.6 1.0 fusion.9
  22.6 0.1 add_bitcast_fusion
  22.7 8.3 %scatter_custom_fusion.rows_ref = s32[1440]{0:T(1024)} fusion(s32[1440]{0:T(1024)S(1)} %get-tuple-element.77, s32[1440]{0:T(1024)S(1)} %get-tuple-element.78, s32[]{:T(128)} %constant.32.clone.1), kind=kCustom, calls=%fused_computation.49 | custom fusion | bytes 5764 | tf_op jit(solution)/shard_map/scatter | solution.py:1213
  31.0 0.7 constant_dynamic-slice_fusion.5
  31.7 1.0 pad_maximum_fusion.1
  32.7 1.2 fusion.8.allowed_ref
  33.9 4.1 collective-permute-done.1
  38.0 2.9 maximum_select_fusion.x_ref
  40.9 12.4 %collective-permute-done.2 = bf16[256,1536]{1,0:T(8,128)(2,1)S(1)} collective-permute-done((bf16[256,1536]{1,0:T(8,128)(2,1)S(1)}, bf16[256,1536]{1,0:T(8,128)(2,1)S(1)}, u32[]{:S(2)}, u32[]{:S(2)}) %collective-permute-start.2) | collective-permute-done | bytes 786464 | tf_op jit(solution)/shard_map/ppermute | solution.py:1166
  53.3 1.8 maximum_select_fusion.1.cot_ref
  55.0 196.5 %all-gather.2.cloned.1.call-done.weights = bf16[1456,128,128]{2,1,0:T(8,128)(2,1)} async-done(((bf16[91,128,128]{2,1,0:T(8,128)(2,1)}), bf16[1456,128,128]{2,1,0:T(8,128)(2,1)}) %all-gather.2.cloned.1.call-update) | async-done | bytes 47710224 | tf_op jit(solution)/shard_map/all_gather | solution.py:1206
  251.5 1.1 slice.67
  252.6 0.3 copy.34
  253.0 0.1 slice_add_fusion
  253.0 0.7 slice.72.gain_ref
  253.7 0.7 reshape.166.bias_ref
  254.4 12.4 %attention_forward.1 = (bf16[512,1536]{1,0:T(8,128)(2,1)}, bf16[1536,512]{1,0:T(8,128)(2,1)}, bf16[512,1024]{1,0:T(8,128)(2,1)}, bf16[768,512]{1,0:T(8,128)(2,1)}, f32[8,512]{1,0:T(8,128)}) custom-call(s32[1440]{0:T(1024)} %scatter_custom_fusion.rows_ref, bf16[512,1536]{1,0:T(8,128)(2,1)} %maximum_select_fusion.x_ref, f32[1,1536]{1,0:T(1,128)} %slice.72.gain_ref, ...), custom_call_target="tpu_custom_call" | custom-call | tf_op jit(solution)/shard_map/attention_forward/pallas_call | solution.py:612
  266.8 1.5 collective-permute-start.3
  268.3 0.7 slice.79.gain_ref
  269.0 15.0 %active_grads.1.active_grad = f32[6,512,768]{2,1,0:T(8,128)} custom-call(s32[1440]{0:T(1024)} %scatter_custom_fusion.rows_ref, bf16[512,1536]{1,0:T(8,128)(2,1)} %maximum_select_fusion.1.cot_ref, bf16[1456,128,128]{2,1,0:T(8,128)(2,1)} %all-gather.2.cloned.1.call-done.weights), custom_call_target="tpu_custom_call" | custom-call | flops 7247757312 | bytes 23592960 | tf_op jit(solution)/shard_map/active_grads/pallas_call | solution.py:643
  284.1 19.7 %collective-permute-done.3.other_ref = bf16[512,1536]{1,0:T(8,128)(2,1)} collective-permute-done((bf16[512,1536]{1,0:T(8,128)(2,1)}, bf16[512,1536]{1,0:T(8,128)(2,1)}, u32[]{:S(2)}, u32[]{:S(2)}) %collective-permute-start.3) | collective-permute-done | bytes 1572896 | tf_op jit(solution)/shard_map/ppermute | solution.py:1166
  303.7 41.5 %hidden_grads.1 = (bf16[512,1536]{1,0:T(8,128)(2,1)}, f32[512,1536]{1,0:T(8,128)}, bf16[1536,512]{1,0:T(8,128)(2,1)}, f32[1,1536]{1,0:T(1,128)}, bf16[6,512,1536...) custom-call(s32[1440]{0:T(1024)} %scatter_custom_fusion.rows_ref, ...), custom_call_target="tpu_custom_call" | custom-call | flops 28991029248 | bytes 56623104 | tf_op jit(solution)/shard_map/hidden_grads/pallas_call | solution.py:663
  345.2 1.5 collective-permute-start.5
  346.7 37.6 %hidden_weight_grads.1 = (bf16[512,1536]{1,0:T(8,128)(2,1)}, bf16[1456,128,128]{2,1,0:T(8,128)(2,1)}) custom-call(s32[1440]{0:T(1024)} %scatter_custom_fusion.rows_ref, bf16[1536,512]{1,0:T(8,128)(2,1)} %get-tuple-element.43.normed_turned_ref, bf16[512,1536]{1,0:T(8,128)(2,1)} %maximum_select_fusion.1.cot_ref, ...), custom_call_target="tpu_custom_call" | custom-call | flops 28991029248 | bytes 75497472 | tf_op jit(solution)/shard_map/hidden_weight_grads/pallas_call | solution.py:698
  384.4 2.1 constant_dynamic-slice_fusion.3
  386.4 0.5 collective-permute-start.4
  387.0 0.6 dynamic_slice.45
  390.8 0.2 fusion.6
  391.1 0.7 reshape.168.gain_ref
  391.7 0.1 mul.130
  391.8 1.1 copy-done.3
  393.0 23.9 %attention_backward.1 = (f32[512,1536]{1,0:T(8,128)}, bf16[512,1536]{1,0:T(8,128)(2,1)}, bf16[1456,128,128]{2,1,0:T(8,128)(2,1)}) custom-call(s32[1440]{0:T(1024)} %scatter_custom_fusion.rows_ref, bf16[512,1536]{1,0:T(8,128)(2,1)} %maximum_select_fusion.x_ref, f32[512,1536]{1,0:T(8,128)} %get-tuple-element.42.resid_ref, ...), custom_call_target="tpu_custom_call", output_to_operand_aliasing={{2}: (16, {})} | custom-call | tf_op jit(solution)/shard_map/attention_backward/pallas_call | solution.py:727
  416.8 2.2 constant_dynamic-slice_fusion.2
  419.0 1.5 collective-permute-start.6
  420.5 2.8 add_convert_fusion
  423.3 253.1 %sum_for_owners.1.grad_in = f32[91,128,128]{2,1,0:T(8,128)} custom-call(bf16[4,2,2,91,128,128]{5,4,3,2,1,0:T(8,128)(2,1)} %bitcast.31), custom_call_target="tpu_custom_call" | custom-call | bytes 381681664 | tf_op jit(solution)/shard_map/sum_for_owners/pallas_call | solution.py:1104
  676.4 0.7 slice.81
  677.1 0.7 slice_bitcast_fusion
  677.8 0.1 dynamic_slice.46
  677.9 0.1 reshape.171
  678.0 0.5 collective-permute-start.7
  678.5 0.6 divide_subtract_fusion
  679.1 23.9 %soap_update.1 = (f32[90,128,128]{2,1,0:T(8,128)}, f32[90,128,128]{2,1,0:T(8,128)}, f32[90,128,128]{2,1,0:T(8,128)}, f32[90,128,128]{2,1,0:T(8,128)}) custom-call(f32[91,128,128]{2,1,0:T(8,128)} %sum_for_owners.1.grad_in, f32[90,128,128]{2,1,0:T(8,128)} %masters_ref.1, f32[90,128,128]{2,1,0:T(8,128)} %first_ref.1, f32[90,128,128]{2,1,0:T(8,128)} %second_ref.1, ...), custom_call_target="tpu_custom_call" | custom-call | tf_op jit(solution)/shard_map/soap_update/pallas_call | solution.py:766
  703.1 0.5 divide_subtract_fusion.1
  703.7 0.5 fusion.2
  704.2 3.1 fusion.5
  (46 shorter events, 0.3 us)
Async XLA Ops:
  7.2 244.3 %all-gather.2.cloned.1.call-start = ((), (), s32[]{:S(2)}) async-start(), calls=%async_computation | async-start | bytes 50692096 | tf_op jit(solution)/shard_map/all_gather | solution.py:1206
  7.2 7.0 collective-permute-start
  10.9 3.3 copy-start.6
  16.3 1.1 copy-start
  16.3 1.4 copy-start.4
  16.3 3.2 copy-start.5
  17.4 20.6 %collective-permute-start.1 = (bf16[256,1536]{1,0:T(8,128)(2,1)S(1)}, bf16[256,1536]{1,0:T(8,128)(2,1)}, u32[]{:S(2)}, u32[]{:S(2)}) collective-permute-start(bf16[256,1536]{1,0:T(8,128)(2,1)S(1)} %copy-done), channel_id=1, source_target_pairs={{0,1},{1,0},{2,3},{3,2},{4,5},{5,4},{6,7},{7,6},{8,9},{9,8},{10,11... | collective-permute-start | bytes 2359304 | tf_op jit(solution)/shard_map/ppermute | solution.py:1166
  17.7 35.6 %collective-permute-start.2 = (bf16[256,1536]{1,0:T(8,128)(2,1)S(1)}, bf16[256,1536]{1,0:T(8,128)(2,1)S(1)}, u32[]{:S(2)}, u32[]{:S(2)}) collective-permute-start(bf16[256,1536]{1,0:T(8,128)(2,1)S(1)} %copy-done.4), channel_id=1, source_target_pairs={{0,1},{1,0},{2,3},{3,2},{4,5},{5,4},{6,7},{7,6},{8,9},{9,8},{10,11... | collective-permute-start | bytes 2359304 | tf_op jit(solution)/shard_map/ppermute | solution.py:1166
  266.8 36.9 %collective-permute-start.3 = (bf16[512,1536]{1,0:T(8,128)(2,1)}, bf16[512,1536]{1,0:T(8,128)(2,1)}, u32[]{:S(2)}, u32[]{:S(2)}) collective-permute-start(bf16[512,1536]{1,0:T(8,128)(2,1)} %get-tuple-element.40.own_ref), channel_id=1, source_target_pairs={{0,1},{1,0},{2,3},{3,2},{4,5},{5,4},{6,7},{7,6},{8,9},{9,8},{10,11... | collective-permute-start | bytes 4718600 | tf_op jit(solution)/shard_map/ppermute | solution.py:1166
  345.2 46.6 %collective-permute-start.5 = (bf16[512,1536]{1,0:T(8,128)(2,1)}, bf16[512,1536]{1,0:T(8,128)(2,1)S(1)}, u32[]{:S(2)}, u32[]{:S(2)}) collective-permute-start(bf16[512,1536]{1,0:T(8,128)(2,1)} %get-tuple-element.48.own_ref), channel_id=1, source_target_pairs={{0,1},{1,0},{2,3},{3,2},{4,5},{5,4},{6,7},{7,6},{8,9},{9,8},{10,11... | collective-permute-start | bytes 4718600 | tf_op jit(solution)/shard_map/ppermute | solution.py:1166
  384.4 2.6 copy-start.13
  386.4 34.1 %collective-permute-start.4 = (bf16[256,1536]{1,0:T(8,128)(2,1)}, bf16[256,1536]{1,0:T(8,128)(2,1)}, u32[]{:S(2)}, u32[]{:S(2)}) collective-permute-start(bf16[256,1536]{1,0:T(8,128)(2,1)} %constant_dynamic-slice_fusion.3), channel_id=1, source_target_pairs={{0,1},{1,0},{2,3},{3,2},{4,5},{5,4},{6,7},{7,6},{8,9},{9,8},{10,11... | collective-permute-start | bytes 2359304 | tf_op jit(solution)/shard_map/ppermute | solution.py:1166
  391.8 1.1 copy-start.3
  416.8 3.7 copy-start.2
  419.0 284.6 %collective-permute-start.6 = (bf16[256,1536]{1,0:T(8,128)(2,1)}, bf16[256,1536]{1,0:T(8,128)(2,1)S(1)}, u32[]{:S(2)}, u32[]{:S(2)}) collective-permute-start(bf16[256,1536]{1,0:T(8,128)(2,1)} %constant_dynamic-slice_fusion.2), channel_id=1, source_target_pairs={{0,1},{1,0},{2,3},{3,2},{4,5},{5,4},{6,7},{7,6},{8,9},{9,8},{10,11... | collective-permute-start | bytes 2359304 | tf_op jit(solution)/shard_map/ppermute | solution.py:1166
  423.3 255.2 %copy-start.8 = (f32[1,64]{1,0:T(1,128)S(1)}, f32[1,64]{1,0:T(1,128)}, u32[]{:S(2)}) copy-start(f32[1,64]{1,0:T(1,128)} %param.29) | copy-start | bytes 772
  423.3 255.2 %copy-start.9 = (f32[1,64]{1,0:T(1,128)S(1)}, f32[1,64]{1,0:T(1,128)}, u32[]{:S(2)}) copy-start(f32[1,64]{1,0:T(1,128)} %param.30) | copy-start | bytes 772
  423.3 255.2 %copy-start.10 = (f32[1,64]{1,0:T(1,128)S(1)}, f32[1,64]{1,0:T(1,128)}, u32[]{:S(2)}) copy-start(f32[1,64]{1,0:T(1,128)} %param.31) | copy-start | bytes 772
  678.0 25.1 %collective-permute-start.7 = (f32[2,96]{1,0:T(2,128)S(1)}, f32[2,96]{1,0:T(2,128)S(1)}, u32[]{:S(2)}, u32[]{:S(2)}) collective-permute-start(f32[2,96]{1,0:T(2,128)S(1)} %reshape.171), channel_id=1, source_target_pairs={{0,1},{1,0},{2,3},{3,2},{4,5},{5,4},{6,7},{7,6},{8,9},{9,8},{10,11... | collective-permute-start | bytes 2312 | tf_op jit(solution)/shard_map/ppermute | solution.py:1166
  679.1 24.0 %copy-start.7 = (f32[96]{0:T(128)S(1)}, f32[96]{0:T(128)}, u32[]{:S(2)}) copy-start(f32[96]{0:T(128)} %param.26) | copy-start | bytes 1156
  679.1 24.0 %copy-start.11 = (f32[96]{0:T(128)S(1)}, f32[96]{0:T(128)}, u32[]{:S(2)}) copy-start(f32[96]{0:T(128)} %param.27) | copy-start | bytes 1156
  679.1 24.0 %copy-start.12 = (f32[96]{0:T(128)S(1)}, f32[96]{0:T(128)}, u32[]{:S(2)}) copy-start(f32[96]{0:T(128)} %param.28) | copy-start | bytes 1156
  679.1 24.5 %copy-start.1 = (bf16[512,1536]{1,0:T(8,128)(2,1)S(1)}, bf16[512,1536]{1,0:T(8,128)(2,1)}, u32[]{:S(2)}) copy-start(bf16[512,1536]{1,0:T(8,128)(2,1)} %get-tuple-element.56) | copy-start | bytes 4718596
Sparse Core Ops, SparseCore 0:
  16.4 235.0 all-gather.1

commit v3 on v2

--- a/solution.py
+++ b/solution.py
@@ -148,7 +148,8 @@
     sin_ref,
     allowed_ref,
     weights,
-    part_ref,
+    part_low_ref,
+    part_high_ref,
     normed_turned_ref,
     qkv_ref,
     mixed_turned_ref,
@@ -191,8 +192,11 @@
         mixed_turned_ref[columns, :] = mixed_head
         mixed[:, columns] = mixed_head.T
     wait_bytes(w_out, sems.at[1])
-    for begin, size in spans(D, COLS):
-        part_ref[:, pl.ds(begin, size)] = dot_nn(mixed[...], w_out[:, pl.ds(begin, size)]).astype(bf16)
+    for part_ref, first in ((part_low_ref, 0), (part_high_ref, length // NARROW)):
+        for begin, size in spans(D, COLS):
+            part_ref[:, pl.ds(begin, size)] = dot_nn(
+                mixed[pl.ds(first, length // NARROW), :], w_out[:, pl.ds(begin, size)]
+            ).astype(bf16)
 
 
 def pair_copies(rows_ref, blocks_hbm, pair, sem, column, place, outward=False):
@@ -219,6 +223,11 @@
         copy.start()
 
 
+def half_rows(half_ref, length):
+    begin = pl.multiple_of(half_ref[0] * length, length)
+    return (pl.ds(begin, length), pl.ds(pl.multiple_of(length - begin, length), length))
+
+
 def hidden_column(tile, place):
     return jnp.minimum(tile * TILE_BLOCKS + place, HIDDEN_COLS - 1)
 
@@ -260,6 +269,7 @@
 
 
 def hidden_grads(
+    first_row,
     rows_ref,
     x_ref,
     own_ref,
@@ -284,7 +294,7 @@
     load_sems,
     store_sems,
 ):
-    length = x_ref.shape[0]
+    length = own_ref.shape[0]
 
     def fetch(tile, slot, place):
         start_all(
@@ -292,7 +302,7 @@
         )
 
     def load_grad(tile, slot):
-        return pltpu.make_async_copy(active_grad.at[tile], grad_active.at[slot], load_sems.at[slot, 1])
+        return pltpu.make_async_copy(active_grad.at[tile, pl.ds(first_row, length)], grad_active.at[slot], load_sems.at[slot, 1])
 
     def stores(tile, slot):
         return (
@@ -306,7 +316,8 @@
     load_grad(0, 0).start()
 
     def norm_rows(rows):
-        values = x_ref[rows, :].astype(f32) + own_ref[rows, :].astype(f32) + other_ref[rows, :].astype(f32)
+        tokens = x_ref[pl.ds(rows.start + first_row, rows.size), :]
+        values = tokens.astype(f32) + own_ref[rows, :].astype(f32) + other_ref[rows, :].astype(f32)
         resid_ref[rows, :] = values
         normed[rows, :] = (values * rms_inverse(values) * gain_ref[...]).astype(bf16)
 
@@ -367,34 +378,52 @@
 
 
 def hidden_weight_grads(
-    rows_ref, normed_turned_ref, cot_ref, pair_grads, active, active_turned, weights, branch_ref, grads,
-    pair, straight, turned, w_down, branch_sum, pair_stage, down_stage, load_sems, store_sems,
+    weight_rows_ref, rows_ref, half_ref, cot_ref, *refs
 ):
+    parts, (weights, branch_own_ref, branch_other_ref, grads), scratch = refs[: 4 * NARROW], refs[8:12], refs[12:]
+    normed_turned, pair, straight, turned, w_down, branch_sum, pair_stage, down_stage, load_sems, store_sems, sems = scratch
+    length = cot_ref.shape[0] // NARROW
+
     def loads(tile, slot):
-        return (
-            pltpu.make_async_copy(pair_grads.at[tile], pair.at[slot], load_sems.at[slot, 0]),
-            pltpu.make_async_copy(active_turned.at[tile], turned.at[slot], load_sems.at[slot, 1]),
-            pltpu.make_async_copy(active.at[tile], straight.at[slot], load_sems.at[slot, 2]),
-        )
+        copies = []
+        for part in range(NARROW):
+            pair_grads, active, active_turned = parts[part * 4 + 1 : part * 4 + 4]
+            tokens = pl.ds(part * length, length)
+            copies += [
+                pltpu.make_async_copy(pair_grads.at[tile], pair.at[slot, tokens], load_sems.at[slot, part * 3]),
+                pltpu.make_async_copy(active.at[tile], straight.at[slot, tokens], load_sems.at[slot, part * 3 + 1]),
+                pltpu.make_async_copy(
+                    active_turned.at[tile], turned.at[slot, :, tokens], load_sems.at[slot, part * 3 + 2]
+                ),
+            ]
+        return copies
 
     def fetch(tile, slot, place):
         start_all(
-            down_copies(rows_ref, weights, w_down.at[slot], load_sems.at[slot, 3], hidden_column(tile, place), place)
+            down_copies(
+                weight_rows_ref, weights, w_down.at[slot], load_sems.at[slot, 3 * NARROW], hidden_column(tile, place), place
+            )
         )
 
     def drain(slot, blocks):
         wait_bytes(pair_stage.at[slot, :, pl.ds(0, 2 * blocks * BLK)], store_sems.at[slot, 0])
         wait_bytes(down_stage.at[slot, pl.ds(0, blocks * BLK)], store_sems.at[slot, 1])
 
-    start_all(loads(0, 0))
+    turned_loads = [
+        pltpu.make_async_copy(parts[part * 4], normed_turned.at[:, pl.ds(part * length, length)], sems.at[part])
+        for part in range(NARROW)
+    ]
+    start_all(loads(0, 0) + turned_loads)
     for place in range(TILE_BLOCKS):
         fetch(0, 0, place)
     branch_sum[...] = jnp.zeros_like(branch_sum)
+    for copy in turned_loads:
+        copy.wait()
 
     def run(tile, slot, blocks, more):
         for copy in loads(tile, slot):
             copy.wait()
-        wait_bytes(w_down.at[slot], load_sems.at[slot, 3])
+        wait_bytes(w_down.at[slot], load_sems.at[slot, 3 * NARROW])
         if more:
             start_all(loads(tile + 1, 1 - slot))
 
@@ -415,7 +444,7 @@
             columns = pl.ds(2 * place * BLK, 2 * BLK)
             for begin, size in spans(D, 512):
                 pair_stage[slot, pl.ds(begin, size), columns] = dot_nn(
-                    normed_turned_ref[pl.ds(begin, size), :], pair[slot, :, columns]
+                    normed_turned[pl.ds(begin, size), :], pair[slot, :, columns]
                 ).astype(bf16)
             start_all(
                 pair_copies(rows_ref, grads, pair_stage.at[slot], store_sems.at[slot, 0], column, place, outward=True)
@@ -430,18 +459,25 @@
             branch_sum[:, columns] += dot_nn(straight[slot, :, :width], w_down[slot, :width, columns])
 
     hidden_tiles(run)
-    branch_ref[...] = branch_sum[...].astype(bf16)
+    own, other = half_rows(half_ref, length)
+    branch_own_ref[...] = branch_sum[own, :].astype(bf16)
+    branch_other_ref[...] = branch_sum[other, :].astype(bf16)
     if TILES > 1:
         drain((TILES - 2) % 2, TILE_BLOCKS)
     drain((TILES - 1) % 2, LAST_BLOCKS)
 
 
 def attention_backward(
+    weight_rows_ref,
     rows_ref,
+    half_ref,
     x_ref,
-    resid_ref,
-    own_ref,
-    other_ref,
+    resid_low_ref,
+    own_low_ref,
+    other_low_ref,
+    resid_high_ref,
+    own_high_ref,
+    other_high_ref,
     cot_ref,
     gain_ref,
     cos_ref,
@@ -451,14 +487,17 @@
     qkv_ref,
     mixed_turned_ref,
     log_ref,
-    gain_two_ref,
+    gain_two_low_ref,
+    gain_two_high_ref,
     weights,
     grads_in,
     grad_resid_ref,
-    grad_ref,
+    grad_own_ref,
+    grad_other_ref,
     grads,
     w_qkv,
     w_out,
+    grad_resid,
     grad_attention,
     grad_mixed,
     grad_qkv,
@@ -476,25 +515,34 @@
     wide_count = small_stage.shape[0]
     owner_rows = grads.shape[0] // wide_count
     small_stage[...] = jnp.zeros_like(small_stage)
-    fetch_attention(rows_ref, weights, w_qkv, w_out, load_sems)
+    fetch_attention(weight_rows_ref, weights, w_qkv, w_out, load_sems)
     length = x_ref.shape[0]
     empty_count = rows_ref.shape[0] - BLOCK_TOTAL
     blank[...] = jnp.zeros_like(blank)
     for index in range(empty_count):
         pltpu.make_async_copy(blank.at[index], grads.at[rows_ref[BLOCK_TOTAL + index]], store_sems.at[2]).start()
 
-    def resid_rows(rows):
-        values = resid_ref[rows, :]
-        inverse = rms_inverse(values)
-        normed = values * inverse
-        scaled = (own_ref[rows, :].astype(f32) + other_ref[rows, :].astype(f32)) * gain_ref[1:2, :]
-        total = cot_ref[rows, :].astype(f32) + inverse * (
-            scaled - normed * jnp.mean(scaled * normed, axis=-1, keepdims=True)
-        )
-        grad_resid_ref[rows, :] = total
-        grad_attention[rows, :] = total.astype(bf16)
-
-    row_chunks(length, ROWS, resid_rows)
+    part = length // NARROW
+    own_rows, other_rows = half_rows(half_ref, part)
+    for first, resid_ref, own_ref, other_ref in (
+        (0, resid_low_ref, own_low_ref, other_low_ref),
+        (part, resid_high_ref, own_high_ref, other_high_ref),
+    ):
+
+        def resid_rows(rows, first=first, resid_ref=resid_ref, own_ref=own_ref, other_ref=other_ref):
+            values = resid_ref[rows, :]
+            inverse = rms_inverse(values)
+            normed = values * inverse
+            scaled = (own_ref[rows, :].astype(f32) + other_ref[rows, :].astype(f32)) * gain_ref[1:2, :]
+            place = pl.ds(rows.start + first, rows.size)
+            total = cot_ref[place, :].astype(f32) + inverse * (
+                scaled - normed * jnp.mean(scaled * normed, axis=-1, keepdims=True)
+            )
+            grad_resid[place, :] = total
+            grad_attention[place, :] = total.astype(bf16)
+
+        row_chunks(part, ROWS, resid_rows)
+    grad_resid_ref[...] = grad_resid[own_rows, :]
     wait_bytes(w_out, load_sems.at[1])
     for begin, size in spans(QUERY_WIDTH, COLS):
         grad_mixed[:, pl.ds(begin, size)] = dot_nt(grad_attention[...], w_out[pl.ds(begin, size), :]).astype(bf16)
@@ -538,9 +586,9 @@
     )
     wait_bytes(w_qkv, load_sems.at[0])
     for begin, size in spans(D, COLS):
-        products = dot_nt(grad_qkv[...], w_qkv[pl.ds(begin, size), :])
-        grad_sum[:, pl.ds(begin, size)] = products
-        grad_ref[:, pl.ds(begin, size)] = products.astype(bf16)
+        grad_sum[:, pl.ds(begin, size)] = dot_nt(grad_qkv[...], w_qkv[pl.ds(begin, size), :])
+    grad_own_ref[...] = grad_sum[own_rows, :].astype(bf16)
+    grad_other_ref[...] = grad_sum[other_rows, :].astype(bf16)
     gain_part[...] = jnp.zeros_like(gain_part)
     bias_part[...] = jnp.zeros_like(bias_part)
 
@@ -554,8 +602,11 @@
         gain_row, bias_row = small_places(owner, wide_count)[::2]
         small_rows = []
         for row in (gain_row, gain_row + 1):
-            source = gain_part if row < D // BLK else gain_two_ref
-            small_rows.append(source[:, pl.ds(row % (D // BLK) * BLK, BLK)])
+            columns = pl.ds(row % (D // BLK) * BLK, BLK)
+            if row < D // BLK:
+                small_rows.append(gain_part[:, columns])
+            else:
+                small_rows.append(gain_two_low_ref[:, columns] + gain_two_high_ref[:, columns])
         small_rows.append(bias_part[:, pl.ds(bias_row * BLK, BLK)])
         small_rows.append(jnp.zeros((SMALL_ROWS - len(small_rows), BLK), f32))
         small_stage[owner, pl.ds(0, SMALL_ROWS), :] = jnp.concatenate(small_rows, axis=0).astype(bf16)
@@ -583,13 +634,13 @@
 ):
     blocks = range(masters_ref.shape[0])
     rights = [right_ref[index].astype(bf16) for index in blocks]
-    products = [dot_nn(grad_in[index].astype(bf16), rights[index]).astype(bf16) for index in blocks]
+    products = [dot_nn(grad_in[index], rights[index]).astype(bf16) for index in blocks]
     lefts = [left_ref[index].astype(bf16) for index in blocks]
     rotated_blocks = [dot_nn(lefts[index].T, products[index]) for index in blocks]
     normalized = []
     for index in blocks:
         rotated = rotated_blocks[index]
-        grad_ref[index] = grad_in[index]
+        grad_ref[index] = grad_in[index].astype(f32)
         new_first = beta_first * first_ref[index] + (1.0 - beta_first) * rotated
         new_second = beta_second * second_ref[index] + (1.0 - beta_second) * rotated * rotated
         new_first_ref[index] = new_first
@@ -612,14 +663,15 @@
     return pl.pallas_call(
         attention_forward,
         out_shape=[
-            shape((length, D), bf16),
+            shape((length // NARROW, D), bf16),
+            shape((length // NARROW, D), bf16),
             shape((D, length), bf16),
             shape((length, QKV_WIDTH), bf16),
             shape((QUERY_WIDTH, length), bf16),
             shape((8, length), f32),
         ],
         in_specs=[SMEM_SPEC] + [VMEM_SPEC] * 6 + [ANY_SPEC],
-        out_specs=[VMEM_SPEC] * 5,
+        out_specs=[VMEM_SPEC] * 6,
         scratch_shapes=[
             pltpu.VMEM((D, QKV_WIDTH), bf16),
             pltpu.VMEM((QUERY_WIDTH, D), bf16),
@@ -657,11 +709,11 @@
     )(rows, cotangent, weights)
 
 
-def run_hidden_grads(rows, x, own, other, gain, active_grad, weights):
-    length = x.shape[0]
+def run_hidden_grads(first_row, rows, x, own, other, gain, active_grad, weights):
+    length = own.shape[0]
     shape = jax.ShapeDtypeStruct
     return pl.pallas_call(
-        hidden_grads,
+        functools.partial(hidden_grads, first_row),
         out_shape=[
             shape((length, D), bf16),
             shape((length, D), f32),
@@ -690,17 +742,16 @@
     )(rows, x, own, other, gain, active_grad, weights)
 
 
-def run_hidden_weight_grads(
-    rows, normed_turned, cotangent, pair_grads, active, active_turned, weights, slots
-):
+def run_hidden_weight_grads(weight_rows, rows, half, cotangent, parts, weights, slots):
     length = cotangent.shape[0]
     shape = jax.ShapeDtypeStruct
     return pl.pallas_call(
         hidden_weight_grads,
-        out_shape=[shape((length, D), bf16), shape((slots, BLK, BLK), bf16)],
-        in_specs=[SMEM_SPEC] + [VMEM_SPEC] * 2 + [ANY_SPEC] * 4,
-        out_specs=[VMEM_SPEC, ANY_SPEC],
+        out_shape=[shape((length // NARROW, D), bf16)] * 2 + [shape((slots, BLK, BLK), bf16)],
+        in_specs=[SMEM_SPEC] * 3 + [VMEM_SPEC] + [ANY_SPEC] * (4 * NARROW + 1),
+        out_specs=[VMEM_SPEC, VMEM_SPEC, ANY_SPEC],
         scratch_shapes=[
+            pltpu.VMEM((D, length), bf16),
             pltpu.VMEM((2, length, 2 * TILE), bf16),
             pltpu.VMEM((2, length, TILE), bf16),
             pltpu.VMEM((2, TILE, length), bf16),
@@ -708,35 +759,42 @@
             pltpu.VMEM((length, D), f32),
             pltpu.VMEM((2, D, 2 * TILE), bf16),
             pltpu.VMEM((2, TILE, D), bf16),
-            pltpu.SemaphoreType.DMA((2, 4)),
+            pltpu.SemaphoreType.DMA((2, 3 * NARROW + 1)),
             pltpu.SemaphoreType.DMA((2, 2)),
+            pltpu.SemaphoreType.DMA((NARROW,)),
         ],
         compiler_params=params(),
         cost_estimate=hidden_cost(length, 4, 2 * TILES * TILE * (4 * D + 4 * length)),
         name="hidden_weight_grads",
-    )(rows, normed_turned, cotangent, pair_grads, active, active_turned, weights)
+    )(weight_rows, rows, half, cotangent, *[array for part in parts for array in part], weights)
 
 
 def run_attention_backward(
-    rows, x, resid, own, other, cotangent, gains, cosine, sine, allowed, normed_turned, qkv, mixed_turned, log_total,
-    gain_two_part, weights, grads, wide_count,
+    weight_rows, rows, half, x, low, high, cotangent, gains, cosine, sine, allowed, normed_turned, qkv, mixed_turned,
+    log_total, gain_two_parts, weights, grads, wide_count,
 ):
     length = x.shape[0]
     shape = jax.ShapeDtypeStruct
     empty_count = max(rows.shape[0] - BLOCK_TOTAL, 1)
+    operands = (
+        weight_rows, rows, half, x, *low, *high, cotangent, gains, cosine, sine, allowed, normed_turned, qkv, mixed_turned,
+        log_total, *gain_two_parts, weights, grads,
+    )
     return pl.pallas_call(
         attention_backward,
         out_shape=[
-            shape((length, D), f32),
-            shape((length, D), bf16),
+            shape((length // NARROW, D), f32),
+            shape((length // NARROW, D), bf16),
+            shape((length // NARROW, D), bf16),
             shape(grads.shape, bf16),
         ],
-        in_specs=[SMEM_SPEC] + [VMEM_SPEC] * 14 + [ANY_SPEC] * 2,
-        out_specs=[VMEM_SPEC] * 2 + [ANY_SPEC],
-        input_output_aliases={16: 2},
+        in_specs=[SMEM_SPEC] * 3 + [VMEM_SPEC] * (len(operands) - 5) + [ANY_SPEC] * 2,
+        out_specs=[VMEM_SPEC] * 3 + [ANY_SPEC],
+        input_output_aliases={len(operands) - 1: 3},
         scratch_shapes=[
             pltpu.VMEM((D, QKV_WIDTH), bf16),
             pltpu.VMEM((QUERY_WIDTH, D), bf16),
+            pltpu.VMEM((length, D), f32),
             pltpu.VMEM((length, D), bf16),
             pltpu.VMEM((length, QUERY_WIDTH), bf16),
             pltpu.VMEM((length, QKV_WIDTH), bf16),
@@ -752,10 +810,7 @@
         ],
         compiler_params=params(),
         name="attention_backward",
-    )(
-        rows, x, resid, own, other, cotangent, gains, cosine, sine, allowed, normed_turned, qkv, mixed_turned, log_total,
-        gain_two_part, weights, grads,
-    )
+    )(*operands)
 
 
 def run_soap(reduced, masters, first_moment, second_moment, left_basis, right_basis):
@@ -776,7 +831,7 @@
 
 def sum_for_owners(
     line, steps, late_steps, grads, out,
-    a_in, a_own, a_sum, a_send, a_cross, a_up, a_down,
+    a_in, a_own, a_sum, a_keep, a_send, a_cross, a_up, a_down,
     b_in, b_own, b_sum, b_keep, b_send, b_cross, b_up, b_down,
     result,
     core_send, core_recv, own_sems, cross_send, cross_recv, up_send, up_recv, down_send, down_recv,
@@ -1039,7 +1094,8 @@
         @pl.when(active(last, steps))
         def _():
             total = result.at[pl.ds(last * EARLY, EARLY)]
-            gather_hops(last, steps, a_sum, sum_depth, a_up, a_down, up_copy, down_copy, 4, total)
+            gather_hops(last, steps, a_sum, sum_depth, a_up, a_down, up_copy, down_copy, 4, a_keep)
+            total[...] = a_keep[...].astype(bf16)
             pltpu.make_async_copy(total, out.at[pl.ds(last * EARLY, EARLY)], out_sem).start()
 
         arrived = step - HOP_LAG * far
@@ -1066,7 +1122,7 @@
             slot = lax.rem(paired, DEPTH)
             b_cross_copy(paired).wait_recv()
             place = steps * EARLY + paired
-            result[place] = b_keep[slot, x] + b_cross[slot].astype(f32)
+            result[place] = (b_keep[slot, x] + b_cross[slot].astype(f32)).astype(bf16)
 
             @pl.when(paired < late_steps - DEPTH)
             def _():
@@ -1103,13 +1159,14 @@
 
     return pl.pallas_call(
         functools.partial(sum_for_owners, line, steps, late_steps),
-        out_shape=jax.ShapeDtypeStruct((slots,) + block, f32),
+        out_shape=jax.ShapeDtypeStruct((slots,) + block, bf16),
         in_specs=[ANY_SPEC],
         out_specs=ANY_SPEC,
         scratch_shapes=[
             vmem(DEPTH, line, 2, EARLY),
             vmem(DEPTH, line, 2, EARLY),
             vmem(sum_depth, line, EARLY),
+            wide_vmem(EARLY),
             vmem(DEPTH, line, EARLY),
             vmem(DEPTH, line, EARLY),
             vmem(hop_depth, line, EARLY),
@@ -1122,7 +1179,7 @@
             vmem(DEPTH),
             vmem(hop_depth, line, 2),
             vmem(hop_depth, line, 2),
-            wide_vmem(slots),
+            vmem(slots),
         ]
         + ([dma((DEPTH,))] * 5 + [dma((hop_depth, line))] * 4) * 2
         + [dma, pltpu.SemaphoreType.REGULAR((8,))],
@@ -1189,7 +1246,6 @@
     tokens_here = tokens.shape[0]
     slots_here = masters.shape[0]
     slots_half = owner_list.shape[0]
-    own_start = half * tokens_here
     gains_here = gains.shape[0]
     biases_here = biases.shape[1]
 
@@ -1198,19 +1254,19 @@
             half == 0, jnp.concatenate([own, other], axis=axis), jnp.concatenate([other, own], axis=axis)
         )
 
-    gain_pair = join_halves(gains, swap_halves(gains))
-    gain_high = lax.reduce_precision(gain_pair, 8, 7)
-    small_values = jnp.concatenate([gain_high, gain_pair - gain_high, biases.reshape(-1)]).astype(bf16)
+    masters_low, gains, biases = lax.optimization_barrier((masters.astype(bf16), gains, biases))
+    weights = lax.all_gather(masters_low, "wide", axis=0, tiled=True)
+    gain_full = lax.all_gather(gains, ("wide", "narrow"), axis=0, tiled=True).reshape(2, D)
+    bias_full = lax.all_gather(biases.reshape(-1).astype(bf16), "wide", axis=0, tiled=True)
+    bias_full = bias_full.astype(f32).reshape(1, QKV_WIDTH)
     pair_gains = 2 * gains_here
-    small_block = jnp.pad(small_values, (0, BLK * BLK - small_values.shape[0])).reshape(1, BLK, BLK)
-    weights = lax.all_gather(
-        jnp.concatenate([masters.astype(bf16), small_block], axis=0), "wide", axis=0, tiled=True
-    )
+
     position = jnp.arange(slots_half, dtype=jnp.int32)
     empty = owner_list == BLOCK_TOTAL
     number = jnp.where(empty, BLOCK_TOTAL - 1 + jnp.cumsum(empty.astype(jnp.int32)), owner_list)
-    slot_rows = position + position // slots_here
-    rows = jnp.zeros((slots_half,), jnp.int32).at[number].set(slot_rows, unique_indices=True)
+    weight_rows = jnp.zeros((slots_half,), jnp.int32).at[number].set(position, unique_indices=True)
+    rows = weight_rows + weight_rows // slots_here
+    half_index = half.astype(jnp.int32).reshape(1)
 
     segment_row = lax.dynamic_index_in_dim(segments, wide_index, 0, keepdims=False)
     cosine, sine = rope_tables(segment_row)
@@ -1220,41 +1276,39 @@
     ).astype(f32)
     tokens_row = join_halves(tokens, swap_halves(tokens))
     cotangent_row = join_halves(cotangent, swap_halves(cotangent))
-    weights, tokens_row, cotangent_row = lax.optimization_barrier((weights, tokens_row, cotangent_row))
-    small_all = weights[slots_here :: slots_here + 1].reshape(wide_count, BLK * BLK)[:, : small_values.shape[0]]
-    small_all = small_all.astype(f32)
-    gain_full = (small_all[:, :pair_gains] + small_all[:, pair_gains : 2 * pair_gains]).reshape(2, D)
-    bias_full = small_all[:, 2 * pair_gains :].reshape(1, QKV_WIDTH)
-
-    attention_part, normed_one_turned, qkv, mixed_turned, log_total = run_attention_forward(
-        rows, tokens_row, gain_full[0:1], bias_full, cosine, sine, allowed_turned, weights
+    weights, tokens_row, cotangent_row, gain_full, bias_full = lax.optimization_barrier(
+        (weights, tokens_row, cotangent_row, gain_full, bias_full)
     )
-    attention_other = swap_halves(attention_part)
-    active_grad = run_active_grads(rows, cotangent_row, weights)
-    grad_two_part, resid, normed_two_turned, gain_two_part, pair_grads, active, active_turned = run_hidden_grads(
-        rows, tokens_row, attention_part, attention_other, gain_full[1:2], active_grad, weights
+
+    low_part, high_part, normed_one_turned, qkv, mixed_turned, log_total = run_attention_forward(
+        weight_rows, tokens_row, gain_full[0:1], bias_full, cosine, sine, allowed_turned, weights
     )
-    grad_two_other = swap_halves(grad_two_part)
-    branch_part, grads = run_hidden_weight_grads(
-        rows, normed_two_turned, cotangent_row, pair_grads, active, active_turned, weights,
+    low_other = swap_halves(low_part)
+    active_grad = run_active_grads(weight_rows, cotangent_row, weights)
+    high_sent, low_other = lax.optimization_barrier((high_part, low_other))
+    high_other = swap_halves(high_sent)
+    gain_two = gain_full[1:2]
+    grad_low, resid_low, turned_low, gain_low, *hidden_low = run_hidden_grads(
+        0, weight_rows, tokens_row, low_part, low_other, gain_two, active_grad, weights
+    )
+    grad_low_other = swap_halves(grad_low)
+    grad_high, resid_high, turned_high, gain_high, *hidden_high = run_hidden_grads(
+        tokens_here, weight_rows, tokens_row, high_part, high_other, gain_two, active_grad, weights
+    )
+    grad_high_other = swap_halves(grad_high)
+    branch_own, branch_sent, grads = run_hidden_weight_grads(
+        weight_rows, rows, half_index, cotangent_row, [(turned_low, *hidden_low), (turned_high, *hidden_high)], weights,
         wide_count * (slots_here + 1),
     )
-    grad_resid, grad_one_part, grads = run_attention_backward(
-        rows, tokens_row, resid, grad_two_part, grad_two_other, cotangent_row, gain_full, cosine, sine, allowed_turned,
-        normed_one_turned, qkv, mixed_turned, log_total, gain_two_part, weights, grads, wide_count,
+    branch_other = swap_halves(branch_sent)
+    grad_resid, grad_one_own, grad_one_sent, grads = run_attention_backward(
+        weight_rows, rows, half_index, tokens_row, (resid_low, grad_low, grad_low_other),
+        (resid_high, grad_high, grad_high_other), cotangent_row, gain_full, cosine, sine, allowed_turned,
+        normed_one_turned, qkv, mixed_turned, log_total, (gain_low, gain_high), weights, grads, wide_count,
     )
-
-    def own_rows(values):
-        return lax.dynamic_slice_in_dim(values, own_start, tokens_here, 0)
-
-    def other_rows(values):
-        return lax.dynamic_slice_in_dim(values, tokens_here - own_start, tokens_here, 0)
-
-    branch_other = swap_halves(other_rows(branch_part))
-    output = (
-        own_rows(resid) + own_rows(branch_part).astype(f32) + branch_other.astype(f32)
-    ).astype(bf16)
-    grad_one_other = swap_halves(other_rows(grad_one_part))
+    grad_one_other = swap_halves(grad_one_sent)
+    resid_own = jnp.where(half == 0, resid_low, resid_high)
+    output = (resid_own + branch_own.astype(f32) + branch_other.astype(f32)).astype(bf16)
 
     if wide_count == 16:
         reduced = run_sum_for_owners(grads, wide_count)
@@ -1262,7 +1316,7 @@
         reduced = lax.psum_scatter(grads, "wide", scatter_dimension=0, tiled=True)
 
     block_grad, new_masters, new_first, new_second = run_soap(
-        reduced.astype(f32), masters, first_moment, second_moment, left_basis, right_basis
+        reduced, masters, first_moment, second_moment, left_basis, right_basis
     )
     places = [small_places(owner, wide_count) for owner in range(wide_count)]
     gain_offset = jnp.asarray([place[1] for place in places], jnp.int32)[wide_index]
@@ -1277,8 +1331,8 @@
     new_biases, new_bias_first, new_bias_second = adam_small(biases, bias_grad, bias_first, bias_second, rate_small)
 
     inverse_one, normed_one = rms_parts(tokens.astype(f32))
-    grad_one = own_rows(grad_one_part).astype(f32) + grad_one_other.astype(f32)
-    input_grad = own_rows(grad_resid) + norm_back(grad_one * gain_full[0:1], normed_one, inverse_one)
+    grad_one = grad_one_own.astype(f32) + grad_one_other.astype(f32)
+    input_grad = grad_resid + norm_back(grad_one * gain_full[0:1], normed_one, inverse_one)
     return (
         output,
         input_grad,

time: 720 us -> 702 us (0.975)
  waiting for transfers between devices: 233 us -> 113 us
  blocking collectives: 0 us -> 97.9 us
  Pallas kernels: 407 us -> 415 us
    unnamed x0 -> x2, blocking collectives: none -> 97.9 us
    all_gather x1, waiting for transfers between devices: 196 us -> 113 us  [body(): weights = lax.all_gather(masters_low, 'wide', axis=0, tiled=True)]
    ppermute x8 -> x9, waiting for transfers between devices: 36.1 us -> 0.02 us  [swap_halves(): return lax.ppermute(values, 'narrow', [(0, 1), (1, 0)])]
    pallas_call x4 -> x5, Pallas kernels: 115 us -> 124 us  [the longest x2 48.8 us: run_hidden_grads(): pl.pallas_call(functools.partial(hidden_grads, first_row), out_shape=[sha...]
  transfers between devices with their start and end apart: 9 -> 10, of which waited for: 4 -> 1; matrix products, arithmetic and copies ran while one was open for 5% -> 4% of each run, Pallas kernels for 49% -> 58%
where the time goes in v3:
time: 702 us; the launch traced here: 694 us
  Pallas kernels  415 us (59%)
  waiting for transfers between devices  113 us (16%)
  blocking collectives  97.9 us (14%)
  other arithmetic  22.8 us (3%)
  between operations  18.7 us (3%)
  local copies, waits for them, and re-layouts  15.4 us (2%)
  starting transfers between devices  10.9 us (2%)
    pallas_call x1, Pallas kernels, run_sum_for_owners(): pl.pallas_call(functools.partial(sum_for_owners, line, steps, late_steps)...  253 us
    all_gather x1, waiting for transfers between devices, body(): weights = lax.all_gather(masters_low, 'wide', axis=0, tiled=True)  113 us
    unnamed x2, blocking collectives  97.9 us
    pallas_call x2, Pallas kernels, run_hidden_grads(): pl.pallas_call(functools.partial(hidden_grads, first_row), out_shape=[sha...  48.8 us
    pallas_call x1, Pallas kernels, run_hidden_weight_grads(): pl.pallas_call(hidden_weight_grads, out_shape=[shape((length // NARROW, D...  38.5 us
    pallas_call x1, Pallas kernels, run_attention_backward(): pl.pallas_call(attention_backward, out_shape=[shape((length // NARROW, D)...  23.6 us
    pallas_call x1, Pallas kernels, run_soap(): pl.pallas_call(soap_update, grid=(slots // group,), out_shape=[shape] * 4...  23.4 us
    pallas_call x1, Pallas kernels, run_active_grads(): pl.pallas_call(active_grads, out_shape=jax.ShapeDtypeStruct((TILES, lengt...  15.1 us
  transfers between devices with their start and end apart: 10, of which 1 were waited for; matrix products, arithmetic and copies ran while one was open for 4% of the time, Pallas kernels for 58%

profile of v3, /device:TPU:0, one launch (start us, length us, event | category | flops | bytes accessed | tf_op | source)
XLA Modules:
  0.0 694.1 jit_solution(1240399061246891177)
XLA Ops:
  7.2 0.0 all-gather.3.cloned.1.call-start
  7.2 4.9 convert_element_type.43
  12.1 0.0 copy-start.16
  12.2 0.0 copy-start.21
  12.2 0.0 all-gather.3.cloned.1.call-update
  12.2 1.1 copy-done
  13.3 3.0 collective-permute-start
  16.2 0.2 collective-permute-start.1
  16.5 0.3 reduce-window.16
  16.8 0.1 slice.55
  16.9 0.9 compare_reduce_fusion
  17.8 0.1 add_select_fusion.1
  17.8 0.3 reduce-window.24
  18.2 0.1 slice.49
  18.3 0.1 slice_reduce_fusion.1
  18.4 0.1 slice_reduce_fusion
  18.5 0.1 fusion.15
  18.6 0.1 add_bitcast_fusion
  18.7 1.0 fusion.9
  19.7 0.3 dynamic-update-slice
  20.0 66.7 %all-reduce.1 = f32[3072]{0:T(1024)S(1)} all-reduce(f32[3072]{0:T(1024)S(1)} %dynamic-update-slice), channel_id=1, replica_groups=mesh['wide'=16,'narrow'=2] {'wide','narrow'}, use_global_device_ids=true, to_apply=%add.1 | all-reduce | flops 3072 | bytes 24576
  86.7 0.6 dynamic-slice.2
  88.0 0.2 dynamic-update-slice.1
  88.2 31.2 %all-reduce.2 = bf16[1024]{0:T(1024)(128)(2,1)S(1)} all-reduce(bf16[1024]{0:T(1024)(128)(2,1)S(1)} %dynamic-update-slice.1), channel_id=2, replica_groups=mesh['wide'=16,'narrow'=2] {'wide'}, use_global_device_ids=true, to_apply=%add.2 | all-reduce | flops 1024 | bytes 4096
  119.4 0.6 reshape.158
  120.0 8.2 %scatter_custom_fusion.rows_ref.weight_rows_ref = s32[1440]{0:T(1024)} fusion(s32[1440]{0:T(1024)S(1)} %compare_select_fusion, s32[1440]{0:T(1024)S(1)} %iota.33, s32[]{:T(128)} %constant.30.clone.1), kind=kCustom, calls=%fused_computation.35 | custom fusion | bytes 5764 | tf_op jit(solution)/shard_map/scatter | solution.py:1267
  128.1 0.7 constant_dynamic-slice_fusion.2
  128.9 1.0 pad_maximum_fusion
  129.9 1.2 fusion.8.allowed_ref
  131.1 3.0 maximum_select_fusion.x_ref
  134.0 1.8 maximum_select_fusion.1.cot_ref
  135.8 113.1 %all-gather.3.cloned.1.call-done.weights.refs_8_ = bf16[1440,128,128]{2,1,0:T(8,128)(2,1)} async-done(((bf16[90,128,128]{2,1,0:T(8,128)(2,1)}), bf16[1440,128,128]{2,1,0:T(8,128)(2,1)}) %all-gather.3.cloned.1.call-update) | async-done | bytes 47185936 | tf_op jit(solution)/shard_map/all_gather | solution.py:1258
  248.9 0.6 slice_reduce_fusion.2
  249.5 13.1 %attention_forward.1 = (bf16[256,1536]{1,0:T(8,128)(2,1)}, bf16[256,1536]{1,0:T(8,128)(2,1)}, bf16[1536,512]{1,0:T(8,128)(2,1)}, bf16[512,1024]{1,0:T(8,128)(2,1...) custom-call(s32[1440]{0:T(1024)} %scatter_custom_fusion.rows_ref.weight_rows_ref, ...), custom_call_target="tpu_custom_call" | custom-call | tf_op jit(solution)/shard_map/attention_forward/pallas_call | solution.py:663
  262.7 1.5 collective-permute-start.2
  264.2 0.6 fusion.10.rows_ref
  264.8 0.6 dynamic_slice.23
  268.6 15.1 %active_grads.1.active_grad = f32[6,512,768]{2,1,0:T(8,128)} custom-call(s32[1440]{0:T(1024)} %scatter_custom_fusion.rows_ref.weight_rows_ref, bf16[512,1536]{1,0:T(8,128)(2,1)} %maximum_select_fusion.1.cot_ref, bf16[1440,128,128]{2,1,0:T(8,128)(2,1)} %all-gather.3.cloned.1.call-done.weights.refs_8_), custom_call_target="tpu_custom_call" | custom-call | flops 7247757312 | bytes 23592960 | tf_op jit(solution)/shard_map/active_grads/pallas_call | solution.py:695
  283.8 0.6 collective-permute-start.3
  284.4 0.2 copy-done.7
  284.7 24.5 %hidden_grads.2 = (bf16[256,1536]{1,0:T(8,128)(2,1)}, f32[256,1536]{1,0:T(8,128)}, bf16[1536,256]{1,0:T(8,128)(2,1)}, f32[1,1536]{1,0:T(1,128)}, bf16[6,256,1536...) custom-call(s32[1440]{0:T(1024)} %scatter_custom_fusion.rows_ref.weight_rows_ref, ...), custom_call_target="tpu_custom_call" | custom-call | flops 14495514624 | bytes 42467328 | tf_op jit(solution)/shard_map/hidden_grads/pallas_call | solution.py:715
  309.2 1.3 collective-permute-start.5
  310.5 0.9 copy-done.8
  311.3 24.3 %hidden_grads.3 = (bf16[256,1536]{1,0:T(8,128)(2,1)}, f32[256,1536]{1,0:T(8,128)}, bf16[1536,256]{1,0:T(8,128)(2,1)}, f32[1,1536]{1,0:T(1,128)}, bf16[6,256,1536...) custom-call(s32[1440]{0:T(1024)} %scatter_custom_fusion.rows_ref.weight_rows_ref, ...), custom_call_target="tpu_custom_call" | custom-call | flops 14495514624 | bytes 42467328 | tf_op jit(solution)/shard_map/hidden_grads/pallas_call | solution.py:715
  335.6 0.9 collective-permute-start.6
  336.5 38.5 %hidden_weight_grads.1 = (bf16[256,1536]{1,0:T(8,128)(2,1)}, bf16[256,1536]{1,0:T(8,128)(2,1)}, bf16[1456,128,128]{2,1,0:T(8,128)(2,1)}) custom-call(s32[1440]{0:T(1024)} %scatter_custom_fusion.rows_ref.weight_rows_ref, s32[1440]{0:T(1024)} %fusion.10.rows_ref, s32[1]{0:T(128)} %bitcast.8.half_ref, bf16[512,1536]{1,0:T(8,128)(2,1)} %maximum_select_fusion.1.cot_ref, ...), custom_call_target="tpu_custom_call" | custom-call | flops 28991029248 | bytes 75497472 | tf_op jit(solution)/shard_map/hidden_weight_grads/pallas_call | solution.py:748
  374.9 1.3 collective-permute-start.4
  376.2 0.2 fusion.6
  376.5 0.8 copy-done.4
  377.4 0.3 copy-done.6
  377.6 23.6 %attention_backward.1 = (f32[256,1536]{1,0:T(8,128)}, bf16[256,1536]{1,0:T(8,128)(2,1)}, bf16[256,1536]{1,0:T(8,128)(2,1)}, bf16[1456,128,128]{2,1,0:T(8,128)(2,1)}) custom-call(s32[1440]{0:T(1024)} %scatter_custom_fusion.rows_ref.weight_rows_ref, s32[1440]{0:T(1024)} %fusion.10.rows_ref, s32[1]{0:T(128)} %bitcast.8.half_ref, ...), custom_call_target="tpu_custom_call", output_to_operand_aliasing={{3}: (22, {})} | custom-call | tf_op jit(solution)/shard_map/attention_backward/pallas_call | solution.py:783
  401.2 0.9 collective-permute-start.7
  402.1 252.8 %sum_for_owners.1.grad_in = bf16[91,128,128]{2,1,0:T(8,128)(2,1)} custom-call(bf16[4,2,2,91,128,128]{5,4,3,2,1,0:T(8,128)(2,1)} %bitcast.28), custom_call_target="tpu_custom_call" | custom-call | bytes 381681664 | tf_op jit(solution)/shard_map/sum_for_owners/pallas_call | solution.py:1160
  654.9 0.7 slice_convert_fusion
  655.6 0.1 dynamic_slice.24
  655.7 0.1 reshape.136
  655.8 1.2 collective-permute-start.8
  657.0 2.7 add_convert_fusion
  659.7 0.6 divide_subtract_fusion
  660.3 23.4 %soap_update.1 = (f32[90,128,128]{2,1,0:T(8,128)}, f32[90,128,128]{2,1,0:T(8,128)}, f32[90,128,128]{2,1,0:T(8,128)}, f32[90,128,128]{2,1,0:T(8,128)}) custom-call(bf16[91,128,128]{2,1,0:T(8,128)(2,1)} %sum_for_owners.1.grad_in, f32[90,128,128]{2,1,0:T(8,128)} %masters_ref.1, f32[90,128,128]{2,1,0:T(8,128)} %first_ref.1, f32[90,128,128]{2,1,0:T(8,128)} %second_ref.1, ...), custom_call_target="tpu_custom_call" | custom-call | tf_op jit(solution)/shard_map/soap_update/pallas_call | solution.py:821
  683.8 0.5 divide_subtract_fusion.1
  684.3 0.5 fusion.2
  684.8 0.3 copy-done.3
  685.1 1.7 fusion.5
  (61 shorter events, 0.3 us)
Async XLA Ops:
  7.2 241.7 %all-gather.3.cloned.1.call-start = ((), (), s32[]{:S(2)}) async-start(), calls=%async_computation | async-start | bytes 50135040 | tf_op jit(solution)/shard_map/all_gather | solution.py:1258
  12.1 1.1 copy-start
  12.1 4.1 copy-start.9
  12.1 4.3 copy-start.12
  12.1 7.5 %copy-start.13 = (f32[1,64]{1,0:T(1,128)S(1)}, f32[1,64]{1,0:T(1,128)}, u32[]{:S(2)}) copy-start(f32[1,64]{1,0:T(1,128)} %param.29) | copy-start | bytes 772
  12.1 7.6 %copy-start.16 = (f32[96]{0:T(128)S(1)}, f32[96]{0:T(128)}, u32[]{:S(2)}) copy-start(f32[96]{0:T(128)} %param.26) | copy-start | bytes 1156
  12.2 74.5 %copy-start.21 = (u32[32]{0:T(128)S(1)}, u32[32]{0:T(128)}, u32[]{:S(2)}) copy-start(u32[32]{0:T(128)} %constant.112) | copy-start | bytes 388
  13.3 117.8 %collective-permute-start = (bf16[256,1536]{1,0:T(8,128)(2,1)S(1)}, bf16[256,1536]{1,0:T(8,128)(2,1)}, u32[]{:S(2)}, u32[]{:S(2)}) collective-permute-start(bf16[256,1536]{1,0:T(8,128)(2,1)S(1)} %copy-done), channel_id=1, source_target_pairs={{0,1},{1,0},{2,3},{3,2},{4,5},{5,4},{6,7},{7,6},{8,9},{9,8},{10,11... | collective-permute-start | bytes 2359304 | tf_op jit(solution)/shard_map/ppermute | solution.py:1223
  16.2 117.8 %collective-permute-start.1 = (bf16[256,1536]{1,0:T(8,128)(2,1)S(1)}, bf16[256,1536]{1,0:T(8,128)(2,1)S(1)}, u32[]{:S(2)}, u32[]{:S(2)}) collective-permute-start(bf16[256,1536]{1,0:T(8,128)(2,1)S(1)} %copy-done.9), channel_id=1, source_target_pairs={{0,1},{1,0},{2,3},{3,2},{4,5},{5,4},{6,7},{7,6},{8,9},{9,8},{10,11... | collective-permute-start | bytes 2359304 | tf_op jit(solution)/shard_map/ppermute | solution.py:1223
  86.7 162.2 %copy-start.11 = (f32[2,1536]{1,0:T(2,128)}, f32[2,1536]{1,0:T(2,128)S(1)}, u32[]{:S(2)}) copy-start(f32[2,1536]{1,0:T(2,128)S(1)} %reshape.129.gain_ref) | copy-start | bytes 36868
  249.5 14.7 %copy-start.10 = (s32[1440]{0:T(1024)S(1)}, s32[1440]{0:T(1024)}, u32[]{:S(2)}) copy-start(s32[1440]{0:T(1024)} %scatter_custom_fusion.rows_ref.weight_rows_ref) | copy-start | bytes 17284
  249.5 15.3 %copy-start.20 = (s32[16]{0:T(128)S(1)}, s32[16]{0:T(128)}, u32[]{:S(2)}) copy-start(s32[16]{0:T(128)} %constant.95.clone) | copy-start | bytes 196
  262.7 21.1 %collective-permute-start.2 = (bf16[256,1536]{1,0:T(8,128)(2,1)}, bf16[256,1536]{1,0:T(8,128)(2,1)S(1)}, u32[]{:S(2)}, u32[]{:S(2)}) collective-permute-start(bf16[256,1536]{1,0:T(8,128)(2,1)} %get-tuple-element.62.own_ref), channel_id=1, source_target_pairs={{0,1},{1,0},{2,3},{3,2},{4,5},{5,4},{6,7},{7,6},{8,9},{9,8},{10,11... | collective-permute-start | bytes 2359304 | tf_op jit(solution)/shard_map/ppermute | solution.py:1223
  268.6 15.2 %copy-start.5 = (bf16[256,1536]{1,0:T(8,128)(2,1)S(1)}, bf16[256,1536]{1,0:T(8,128)(2,1)}, u32[]{:S(2)}) copy-start(bf16[256,1536]{1,0:T(8,128)(2,1)} %get-tuple-element.67.own_ref) | copy-start | bytes 2359300
  283.8 0.9 copy-start.7
  283.8 26.7 %collective-permute-start.3 = (bf16[256,1536]{1,0:T(8,128)(2,1)S(1)}, bf16[256,1536]{1,0:T(8,128)(2,1)S(1)}, u32[]{:S(2)}, u32[]{:S(2)}) collective-permute-start(bf16[256,1536]{1,0:T(8,128)(2,1)S(1)} %copy-done.5), channel_id=1, source_target_pairs={{0,1},{1,0},{2,3},{3,2},{4,5},{5,4},{6,7},{7,6},{8,9},{9,8},{10,11... | collective-permute-start | bytes 2359304 | tf_op jit(solution)/shard_map/ppermute | solution.py:1223
  309.2 67.3 %collective-permute-start.5 = (bf16[256,1536]{1,0:T(8,128)(2,1)}, bf16[256,1536]{1,0:T(8,128)(2,1)S(1)}, u32[]{:S(2)}, u32[]{:S(2)}) collective-permute-start(bf16[256,1536]{1,0:T(8,128)(2,1)} %get-tuple-element.79.own_low_ref), channel_id=1, source_target_pairs={{0,1},{1,0},{2,3},{3,2},{4,5},{5,4},{6,7},{7,6},{8,9},{9,8},{10,11... | collective-permute-start | bytes 2359304 | tf_op jit(solution)/shard_map/ppermute | solution.py:1223
  310.4 0.9 copy-start.8
  335.6 40.9 %collective-permute-start.6 = (bf16[256,1536]{1,0:T(8,128)(2,1)}, bf16[256,1536]{1,0:T(8,128)(2,1)S(1)}, u32[]{:S(2)}, u32[]{:S(2)}) collective-permute-start(bf16[256,1536]{1,0:T(8,128)(2,1)} %get-tuple-element.80.own_high_ref), channel_id=1, source_target_pairs={{0,1},{1,0},{2,3},{3,2},{4,5},{5,4},{6,7},{7,6},{8,9},{9,8},{10,11... | collective-permute-start | bytes 2359304 | tf_op jit(solution)/shard_map/ppermute | solution.py:1223
  374.9 282.1 %collective-permute-start.4 = (bf16[256,1536]{1,0:T(8,128)(2,1)}, bf16[256,1536]{1,0:T(8,128)(2,1)}, u32[]{:S(2)}, u32[]{:S(2)}) collective-permute-start(bf16[256,1536]{1,0:T(8,128)(2,1)} %get-tuple-element.78), channel_id=1, source_target_pairs={{0,1},{1,0},{2,3},{3,2},{4,5},{5,4},{6,7},{7,6},{8,9},{9,8},{10,11... | collective-permute-start | bytes 2359304 | tf_op jit(solution)/shard_map/ppermute | solution.py:1223
  376.5 0.9 copy-start.4
  376.5 1.1 copy-start.6
  401.2 283.1 %collective-permute-start.7 = (bf16[256,1536]{1,0:T(8,128)(2,1)}, bf16[256,1536]{1,0:T(8,128)(2,1)S(1)}, u32[]{:S(2)}, u32[]{:S(2)}) collective-permute-start(bf16[256,1536]{1,0:T(8,128)(2,1)} %get-tuple-element.90), channel_id=1, source_target_pairs={{0,1},{1,0},{2,3},{3,2},{4,5},{5,4},{6,7},{7,6},{8,9},{9,8},{10,11... | collective-permute-start | bytes 2359304 | tf_op jit(solution)/shard_map/ppermute | solution.py:1223
  402.1 254.9 %copy-start.1 = (f32[256,1536]{1,0:T(8,128)S(1)}, f32[256,1536]{1,0:T(8,128)}, u32[]{:S(2)}) copy-start(f32[256,1536]{1,0:T(8,128)} %get-tuple-element.66.resid_low_ref) | copy-start | bytes 4718596
  655.8 27.9 %collective-permute-start.8 = (f32[2,96]{1,0:T(2,128)S(1)}, f32[2,96]{1,0:T(2,128)S(1)}, u32[]{:S(2)}, u32[]{:S(2)}) collective-permute-start(f32[2,96]{1,0:T(2,128)S(1)} %reshape.136), channel_id=1, source_target_pairs={{0,1},{1,0},{2,3},{3,2},{4,5},{5,4},{6,7},{7,6},{8,9},{9,8},{10,11... | collective-permute-start | bytes 2312 | tf_op jit(solution)/shard_map/ppermute | solution.py:1223
  657.0 2.7 copy-start.14
  657.0 2.7 copy-start.15
  660.3 23.4 %copy-start.17 = (f32[96]{0:T(128)S(1)}, f32[96]{0:T(128)}, u32[]{:S(2)}) copy-start(f32[96]{0:T(128)} %param.26) | copy-start | bytes 1156
  660.3 23.4 %copy-start.18 = (f32[96]{0:T(128)S(1)}, f32[96]{0:T(128)}, u32[]{:S(2)}) copy-start(f32[96]{0:T(128)} %param.27) | copy-start | bytes 1156
  660.3 23.4 %copy-start.19 = (f32[96]{0:T(128)S(1)}, f32[96]{0:T(128)}, u32[]{:S(2)}) copy-start(f32[96]{0:T(128)} %param.28) | copy-start | bytes 1156
  660.3 24.0 %copy-start.2 = (bf16[256,1536]{1,0:T(8,128)(2,1)S(1)}, bf16[256,1536]{1,0:T(8,128)(2,1)}, u32[]{:S(2)}) copy-start(bf16[256,1536]{1,0:T(8,128)(2,1)} %get-tuple-element.89) | copy-start | bytes 2359300
  683.7 1.4 copy-start.3
Sparse Core Ops, SparseCore 0:
  12.3 236.5 all-gather.2

commit v4 on v3

--- a/solution.py
+++ b/solution.py
@@ -56,11 +56,14 @@
 ROWS = 64
 SMALL_ROWS = 16
 VMEM_LIMIT = 60 * 2**20
+SUM_VMEM = 27 * 2**20
+UPDATE_VMEM = 27 * 2**20
 
 EARLY = 4
 DEPTH = 3
 CROSS_LAG = 2
 HOP_LAG = 1
+SUM_SCRATCH = 36
 
 VMEM_SPEC = pl.BlockSpec(memory_space=pltpu.VMEM)
 SMEM_SPEC = pl.BlockSpec(memory_space=pltpu.SMEM)
@@ -627,34 +630,78 @@
     second_ref,
     left_ref,
     right_ref,
-    grad_ref,
-    new_masters_ref,
-    new_first_ref,
-    new_second_ref,
+    grad_out,
+    masters_out,
+    first_out,
+    second_out,
+    small_ref,
+    grad_stage,
+    masters_stage,
+    first_stage,
+    second_stage,
+    sems,
 ):
-    blocks = range(masters_ref.shape[0])
-    rights = [right_ref[index].astype(bf16) for index in blocks]
-    products = [dot_nn(grad_in[index], rights[index]).astype(bf16) for index in blocks]
-    lefts = [left_ref[index].astype(bf16) for index in blocks]
-    rotated_blocks = [dot_nn(lefts[index].T, products[index]) for index in blocks]
+    group = grad_stage.shape[1]
+    outputs = (
+        (grad_stage, grad_out), (masters_stage, masters_out), (first_stage, first_out), (second_stage, second_out)
+    )
+    steps = masters_ref.shape[0] // group
+    small_ref[...] = grad_in[masters_ref.shape[0], :SMALL_ROWS].astype(f32)
+
+    def stores(step):
+        slot = lax.rem(step, 2)
+        places = pl.ds(step * group, group)
+        return [
+            pltpu.make_async_copy(stage.at[slot], out.at[places], sems.at[slot, index])
+            for index, (stage, out) in enumerate(outputs)
+        ]
+
+    @pl.loop(0, steps)
+    def _(step):
+        @pl.when(step >= 2)
+        def _():
+            for copy in stores(step - 2):
+                copy.wait()
+
+        soap_group(
+            step * group, lax.rem(step, 2), grad_in, masters_ref, first_ref, second_ref, left_ref, right_ref,
+            *[stage for stage, _ in outputs],
+        )
+        start_all(stores(step))
+
+    for step in range(max(steps - 2, 0), steps):
+        for copy in stores(step):
+            copy.wait()
+
+
+def soap_group(
+    first_block, slot, grad_in, masters_ref, first_ref, second_ref, left_ref, right_ref,
+    grad_stage, masters_stage, first_stage, second_stage,
+):
+    places = range(grad_stage.shape[1])
+    blocks = [first_block + place for place in places]
+    rights = [right_ref[block].astype(bf16) for block in blocks]
+    products = [dot_nn(grad_in[blocks[place]], rights[place]).astype(bf16) for place in places]
+    lefts = [left_ref[block].astype(bf16) for block in blocks]
+    rotated_blocks = [dot_nn(lefts[place].T, products[place]) for place in places]
     normalized = []
-    for index in blocks:
-        rotated = rotated_blocks[index]
-        grad_ref[index] = grad_in[index].astype(f32)
-        new_first = beta_first * first_ref[index] + (1.0 - beta_first) * rotated
-        new_second = beta_second * second_ref[index] + (1.0 - beta_second) * rotated * rotated
-        new_first_ref[index] = new_first
-        new_second_ref[index] = new_second
+    for place, block in enumerate(blocks):
+        rotated = rotated_blocks[place]
+        grad_stage[slot, place] = grad_in[block].astype(f32)
+        new_first = beta_first * first_ref[block] + (1.0 - beta_first) * rotated
+        new_second = beta_second * second_ref[block] + (1.0 - beta_second) * rotated * rotated
+        first_stage[slot, place] = new_first
+        second_stage[slot, place] = new_second
         normalized.append(
             (new_first / first_fix / (jnp.sqrt(new_second / second_fix) + adam_eps)).astype(bf16)
         )
-    products = [dot_nt(normalized[index], rights[index]).astype(bf16) for index in blocks]
-    for index in blocks:
-        new_masters_ref[index] = masters_ref[index] - rate_blocks * dot_nn(lefts[index], products[index])
-
-
-def params(**options):
-    return pltpu.CompilerParams(vmem_limit_bytes=VMEM_LIMIT, **options)
+    products = [dot_nt(normalized[place], rights[place]).astype(bf16) for place in places]
+    for place, block in enumerate(blocks):
+        masters_stage[slot, place] = masters_ref[block] - rate_blocks * dot_nn(lefts[place], products[place])
+
+
+def params(limit=VMEM_LIMIT, **options):
+    return pltpu.CompilerParams(vmem_limit_bytes=limit, **options)
 
 
 def run_attention_forward(rows, x, gain, bias, cosine, sine, allowed, weights):
@@ -816,28 +863,29 @@
 def run_soap(reduced, masters, first_moment, second_moment, left_basis, right_basis):
     slots = masters.shape[0]
     group = max(size for size in range(1, 11) if slots % size == 0)
-    spec = pl.BlockSpec((group, BLK, BLK), lambda step: (step, 0, 0))
     shape = jax.ShapeDtypeStruct(masters.shape, f32)
     return pl.pallas_call(
         soap_update,
-        grid=(slots // group,),
-        out_shape=[shape] * 4,
-        in_specs=[spec] * 6,
-        out_specs=[spec] * 4,
-        compiler_params=params(),
+        out_shape=[shape] * 4 + [jax.ShapeDtypeStruct((SMALL_ROWS, BLK), f32)],
+        in_specs=[VMEM_SPEC] * 6,
+        out_specs=[ANY_SPEC] * 4 + [VMEM_SPEC],
+        scratch_shapes=[pltpu.VMEM((2, group, BLK, BLK), f32)] * 4 + [pltpu.SemaphoreType.DMA((2, 4))],
+        compiler_params=params(UPDATE_VMEM),
         name="soap_update",
     )(reduced, masters, first_moment, second_moment, left_basis, right_basis)
 
 
 def sum_for_owners(
-    line, steps, late_steps, grads, out,
-    a_in, a_own, a_sum, a_keep, a_send, a_cross, a_up, a_down,
-    b_in, b_own, b_sum, b_keep, b_send, b_cross, b_up, b_down,
-    result,
-    core_send, core_recv, own_sems, cross_send, cross_recv, up_send, up_recv, down_send, down_recv,
-    b_core_send, b_core_recv, b_own_sems, b_cross_send, b_cross_recv, b_up_send, b_up_recv, b_down_send, b_down_recv,
-    out_sem, credits,
+    line, steps, late_steps, grads, *refs
 ):
+    held = len(refs[: -SUM_SCRATCH]) // 2
+    sources, (out, *targets), scratch = refs[:held], refs[held:-SUM_SCRATCH], refs[-SUM_SCRATCH:]
+    (
+        a_in, a_own, a_sum, a_keep, a_send, a_cross, a_up, a_down, b_in, b_own, b_sum, b_keep, b_send,
+        b_cross, b_up, b_down, core_send, core_recv, own_sems, cross_send, cross_recv, up_send, up_recv,
+        down_send, down_recv, b_core_send, b_core_recv, b_own_sems, b_cross_send, b_cross_recv, b_up_send,
+        b_up_recv, b_down_send, b_down_recv, held_sems, credits,
+    ) = scratch
     wide = lax.axis_index("wide")
     narrow = lax.axis_index("narrow")
     z = wide // 4
@@ -946,6 +994,11 @@
             remote_copy(step).start()
             local_copy(step).start()
 
+    held_copies = [
+        pltpu.make_async_copy(source, target, held_sems.at[index])
+        for index, (source, target) in enumerate(zip(sources, targets))
+    ]
+    start_all(held_copies)
     for early in range(DEPTH - 1):
         feed(early, steps, 0, core_copy, own_copy)
         feed(early, late_steps, 1, b_core_copy, b_own_copy)
@@ -1093,10 +1146,8 @@
 
         @pl.when(active(last, steps))
         def _():
-            total = result.at[pl.ds(last * EARLY, EARLY)]
             gather_hops(last, steps, a_sum, sum_depth, a_up, a_down, up_copy, down_copy, 4, a_keep)
-            total[...] = a_keep[...].astype(bf16)
-            pltpu.make_async_copy(total, out.at[pl.ds(last * EARLY, EARLY)], out_sem).start()
+            out[pl.ds(last * EARLY, EARLY)] = a_keep[...].astype(bf16)
 
         arrived = step - HOP_LAG * far
 
@@ -1122,13 +1173,11 @@
             slot = lax.rem(paired, DEPTH)
             b_cross_copy(paired).wait_recv()
             place = steps * EARLY + paired
-            result[place] = (b_keep[slot, x] + b_cross[slot].astype(f32)).astype(bf16)
+            out[place] = (b_keep[slot, x] + b_cross[slot].astype(f32)).astype(bf16)
 
             @pl.when(paired < late_steps - DEPTH)
             def _():
                 give(3, cross_peer)
-
-            pltpu.make_async_copy(result.at[place], out.at[place], out_sem).start()
 
         return 0
 
@@ -1138,10 +1187,11 @@
         cross_copy(step).wait_send()
     for step in range(max(late_steps - DEPTH, 0), late_steps):
         b_cross_copy(step).wait_send()
-    pltpu.make_async_copy(result, out, out_sem).wait()
-
-
-def run_sum_for_owners(grads, wide_count):
+    for copy in held_copies:
+        copy.wait()
+
+
+def run_sum_for_owners(grads, wide_count, held):
     line = wide_count // 4
     slots, block = grads.shape[0] // wide_count, grads.shape[1:]
     steps = (slots - 1) // (EARLY + 1)
@@ -1159,9 +1209,9 @@
 
     return pl.pallas_call(
         functools.partial(sum_for_owners, line, steps, late_steps),
-        out_shape=jax.ShapeDtypeStruct((slots,) + block, bf16),
-        in_specs=[ANY_SPEC],
-        out_specs=ANY_SPEC,
+        out_shape=[pltpu.VMEM((slots,) + block, bf16)] + [pltpu.VMEM(array.shape, array.dtype) for array in held],
+        in_specs=[ANY_SPEC] * (1 + len(held)),
+        out_specs=[VMEM_SPEC] * (1 + len(held)),
         scratch_shapes=[
             vmem(DEPTH, line, 2, EARLY),
             vmem(DEPTH, line, 2, EARLY),
@@ -1179,14 +1229,13 @@
             vmem(DEPTH),
             vmem(hop_depth, line, 2),
             vmem(hop_depth, line, 2),
-            vmem(slots),
         ]
         + ([dma((DEPTH,))] * 5 + [dma((hop_depth, line))] * 4) * 2
-        + [dma, pltpu.SemaphoreType.REGULAR((8,))],
-        compiler_params=params(collective_id=0, has_side_effects=True),
+        + [dma((len(held),)), pltpu.SemaphoreType.REGULAR((8,))],
+        compiler_params=params(SUM_VMEM, collective_id=0, has_side_effects=True),
         cost_estimate=pl.CostEstimate(flops=0, bytes_accessed=2 * grads.size * 8, transcendentals=0),
         name="sum_for_owners",
-    )(grads.reshape((line, 2, 2, slots) + block))
+    )(grads.reshape((line, 2, 2, slots) + block), *held)
 
 
 def rope_tables(segment_row):
@@ -1310,29 +1359,32 @@
     resid_own = jnp.where(half == 0, resid_low, resid_high)
     output = (resid_own + branch_own.astype(f32) + branch_other.astype(f32)).astype(bf16)
 
+    held = [masters, first_moment, second_moment, left_basis, right_basis]
     if wide_count == 16:
-        reduced = run_sum_for_owners(grads, wide_count)
+        grads, output = lax.optimization_barrier((grads, output))
+        reduced, *held = [
+            pltpu.with_memory_space_constraint(array, pltpu.VMEM)
+            for array in run_sum_for_owners(grads, wide_count, held)
+        ]
     else:
         reduced = lax.psum_scatter(grads, "wide", scatter_dimension=0, tiled=True)
 
-    block_grad, new_masters, new_first, new_second = run_soap(
-        reduced, masters, first_moment, second_moment, left_basis, right_basis
-    )
+    block_grad, new_masters, new_first, new_second, small_sums = run_soap(reduced, *held)
+    inverse_one, normed_one = rms_parts(tokens.astype(f32))
+    grad_one = grad_one_own.astype(f32) + grad_one_other.astype(f32)
+    input_grad = grad_resid + norm_back(grad_one * gain_full[0:1], normed_one, inverse_one)
     places = [small_places(owner, wide_count) for owner in range(wide_count)]
     gain_offset = jnp.asarray([place[1] for place in places], jnp.int32)[wide_index]
     bias_offset = jnp.asarray([place[3] for place in places], jnp.int32)[wide_index]
-    small_sums = reduced[slots_here, :8].astype(f32)
     gain_sums = lax.dynamic_slice_in_dim(small_sums[:2].reshape(-1), gain_offset, pair_gains, 0)
     gain_sums = gain_sums.reshape(2, gains_here)
-    gain_sums = gain_sums + swap_halves(gain_sums)
+    gain_other, input_grad = lax.optimization_barrier((swap_halves(gain_sums), input_grad))
+    gain_sums = gain_sums + gain_other
     gain_grad = lax.dynamic_index_in_dim(gain_sums, half, 0, keepdims=False)
     bias_grad = lax.dynamic_slice_in_dim(small_sums[2], bias_offset, biases_here, 0).reshape(biases.shape)
     new_gains, new_gain_first, new_gain_second = adam_small(gains, gain_grad, gain_first, gain_second, rate_gains)
     new_biases, new_bias_first, new_bias_second = adam_small(biases, bias_grad, bias_first, bias_second, rate_small)
 
-    inverse_one, normed_one = rms_parts(tokens.astype(f32))
-    grad_one = grad_one_own.astype(f32) + grad_one_other.astype(f32)
-    input_grad = grad_resid + norm_back(grad_one * gain_full[0:1], normed_one, inverse_one)
     return (
         output,
         input_grad,

time: 702 us -> 702 us (level)
    pallas_call x1, Pallas kernels: 23.4 us -> 13.4 us  [run_soap(): pl.pallas_call(soap_update, out_shape=[shape] * 4 + [jax.ShapeDtypeStruct...]
  transfers between devices with their start and end apart: 10 -> 10, of which waited for: 1 -> 2; matrix products, arithmetic and copies ran while one was open for 4% -> 5% of each run, Pallas kernels for 58% -> 57%
where the time goes in v4:
time: 702 us; the launch traced here: 694 us
  Pallas kernels  409 us (58%)
  waiting for transfers between devices  116 us (17%)
  blocking collectives  97.8 us (14%)
  other arithmetic  24.4 us (3%)
  between operations  18.7 us (3%)
  local copies, waits for them, and re-layouts  17 us (2%)
  starting transfers between devices  11.4 us (2%)
    pallas_call x1, Pallas kernels, run_sum_for_owners(): pl.pallas_call(functools.partial(sum_for_owners, line, steps, late_steps)...  257 us
    all_gather x1, waiting for transfers between devices, body(): weights = lax.all_gather(masters_low, 'wide', axis=0, tiled=True)  113 us
    unnamed x2, blocking collectives  97.8 us
    pallas_call x2, Pallas kernels, run_hidden_grads(): pl.pallas_call(functools.partial(hidden_grads, first_row), out_shape=[sha...  48.7 us
    pallas_call x1, Pallas kernels, run_hidden_weight_grads(): pl.pallas_call(hidden_weight_grads, out_shape=[shape((length // NARROW, D...  38.5 us
    pallas_call x1, Pallas kernels, run_attention_backward(): pl.pallas_call(attention_backward, out_shape=[shape((length // NARROW, D)...  23.7 us
    pallas_call x1, Pallas kernels, run_active_grads(): pl.pallas_call(active_grads, out_shape=jax.ShapeDtypeStruct((TILES, lengt...  14.6 us
  transfers between devices with their start and end apart: 10, of which 2 were waited for; matrix products, arithmetic and copies ran while one was open for 5% of the time, Pallas kernels for 57%

profile of v4, /device:TPU:0, one launch (start us, length us, event | category | flops | bytes accessed | tf_op | source)
XLA Modules:
  0.0 694.3 jit_solution(3828483167834146412)
XLA Ops:
  7.2 0.0 all-gather.3.cloned.1.call-start
  7.2 4.9 convert_element_type.39
  12.2 0.0 copy-start.24
  12.2 0.0 all-gather.3.cloned.1.call-update
  12.2 1.1 copy-done
  13.3 3.0 collective-permute-start
  16.2 0.2 collective-permute-start.1
  16.5 0.9 compare_reduce_fusion
  17.4 0.1 add_select_fusion.1
  17.4 0.3 reduce-window.24
  17.7 0.1 slice.44
  17.9 0.3 reduce-window.16
  18.2 0.1 slice.49
  18.3 0.1 slice_reduce_fusion.1
  18.4 0.1 slice_reduce_fusion
  18.5 0.1 fusion.15
  18.6 0.1 add_bitcast_fusion
  18.7 1.0 fusion.9
  19.7 0.3 dynamic-update-slice
  20.0 66.7 %all-reduce.1 = f32[3072]{0:T(1024)S(1)} all-reduce(f32[3072]{0:T(1024)S(1)} %dynamic-update-slice), channel_id=1, replica_groups=mesh['wide'=16,'narrow'=2] {'wide','narrow'}, use_global_device_ids=true, to_apply=%add.1 | all-reduce | flops 3072 | bytes 24576
  86.7 0.6 dynamic-slice.1
  87.9 0.2 dynamic-update-slice.1
  88.2 31.2 %all-reduce.2 = bf16[1024]{0:T(1024)(128)(2,1)S(1)} all-reduce(bf16[1024]{0:T(1024)(128)(2,1)S(1)} %dynamic-update-slice.1), channel_id=2, replica_groups=mesh['wide'=16,'narrow'=2] {'wide'}, use_global_device_ids=true, to_apply=%add.2 | all-reduce | flops 1024 | bytes 4096
  119.4 0.6 reshape.153
  120.0 8.2 %scatter_custom_fusion.rows_ref.weight_rows_ref = s32[1440]{0:T(1024)} fusion(s32[1440]{0:T(1024)S(1)} %compare_select_fusion, s32[1440]{0:T(1024)S(1)} %iota.33, s32[]{:T(128)} %constant.29.clone.1), kind=kCustom, calls=%fused_computation.35 | custom fusion | bytes 5764 | tf_op jit(solution)/shard_map/scatter | solution.py:1316
  128.1 0.7 constant_dynamic-slice_fusion.2
  128.8 1.0 pad_maximum_fusion
  129.8 1.2 fusion.8.allowed_ref
  131.0 3.0 maximum_select_fusion.x_ref
  134.0 1.8 maximum_select_fusion.1.cot_ref
  135.8 113.1 %all-gather.3.cloned.1.call-done.weights.refs_8_ = bf16[1440,128,128]{2,1,0:T(8,128)(2,1)} async-done(((bf16[90,128,128]{2,1,0:T(8,128)(2,1)}), bf16[1440,128,128]{2,1,0:T(8,128)(2,1)}) %all-gather.3.cloned.1.call-update) | async-done | bytes 47185936 | tf_op jit(solution)/shard_map/all_gather | solution.py:1307
  248.9 1.2 slice_reduce_fusion.2
  250.1 13.1 %attention_forward.1 = (bf16[256,1536]{1,0:T(8,128)(2,1)}, bf16[256,1536]{1,0:T(8,128)(2,1)}, bf16[1536,512]{1,0:T(8,128)(2,1)}, bf16[512,1024]{1,0:T(8,128)(2,1...) custom-call(s32[1440]{0:T(1024)} %scatter_custom_fusion.rows_ref.weight_rows_ref, ...), custom_call_target="tpu_custom_call" | custom-call | tf_op jit(solution)/shard_map/attention_forward/pallas_call | solution.py:710
  263.2 1.5 collective-permute-start.2
  264.8 0.6 fusion.10.rows_ref
  265.4 14.6 %active_grads.1.active_grad = f32[6,512,768]{2,1,0:T(8,128)} custom-call(s32[1440]{0:T(1024)} %scatter_custom_fusion.rows_ref.weight_rows_ref, bf16[512,1536]{1,0:T(8,128)(2,1)} %maximum_select_fusion.1.cot_ref, bf16[1440,128,128]{2,1,0:T(8,128)(2,1)} %all-gather.3.cloned.1.call-done.weights.refs_8_), custom_call_target="tpu_custom_call" | custom-call | flops 7247757312 | bytes 23592960 | tf_op jit(solution)/shard_map/active_grads/pallas_call | solution.py:742
  280.0 3.2 collective-permute-done.2.other_ref
  283.2 1.5 collective-permute-start.4
  284.7 24.4 %hidden_grads.2 = (bf16[256,1536]{1,0:T(8,128)(2,1)}, f32[256,1536]{1,0:T(8,128)}, bf16[1536,256]{1,0:T(8,128)(2,1)}, f32[1,1536]{1,0:T(1,128)}, bf16[6,256,1536...) custom-call(s32[1440]{0:T(1024)} %scatter_custom_fusion.rows_ref.weight_rows_ref, ...), custom_call_target="tpu_custom_call" | custom-call | flops 14495514624 | bytes 42467328 | tf_op jit(solution)/shard_map/hidden_grads/pallas_call | solution.py:762
  309.1 0.9 collective-permute-start.3
  310.0 0.9 copy-done.8
  310.9 24.3 %hidden_grads.3 = (bf16[256,1536]{1,0:T(8,128)(2,1)}, f32[256,1536]{1,0:T(8,128)}, bf16[1536,256]{1,0:T(8,128)(2,1)}, f32[1,1536]{1,0:T(1,128)}, bf16[6,256,1536...) custom-call(s32[1440]{0:T(1024)} %scatter_custom_fusion.rows_ref.weight_rows_ref, ...), custom_call_target="tpu_custom_call" | custom-call | flops 14495514624 | bytes 42467328 | tf_op jit(solution)/shard_map/hidden_grads/pallas_call | solution.py:762
  335.2 1.2 collective-permute-start.5
  336.4 38.5 %hidden_weight_grads.1 = (bf16[256,1536]{1,0:T(8,128)(2,1)}, bf16[256,1536]{1,0:T(8,128)(2,1)}, bf16[1456,128,128]{2,1,0:T(8,128)(2,1)}) custom-call(s32[1440]{0:T(1024)} %scatter_custom_fusion.rows_ref.weight_rows_ref, s32[1440]{0:T(1024)} %fusion.10.rows_ref, s32[1]{0:T(128)} %bitcast.2.half_ref, bf16[512,1536]{1,0:T(8,128)(2,1)} %maximum_select_fusion.1.cot_ref, ...), custom_call_target="tpu_custom_call" | custom-call | flops 28991029248 | bytes 75497472 | tf_op jit(solution)/shard_map/hidden_weight_grads/pallas_call | solution.py:795
  374.9 0.9 collective-permute-start.6
  375.9 0.6 dynamic_slice.21
  379.7 0.2 fusion.6
  380.0 0.0 copy-start.6
  380.0 0.8 copy-done.5
  380.8 0.3 copy-done.6
  381.1 23.7 %attention_backward.1 = (f32[256,1536]{1,0:T(8,128)}, bf16[256,1536]{1,0:T(8,128)(2,1)}, bf16[256,1536]{1,0:T(8,128)(2,1)}, bf16[1456,128,128]{2,1,0:T(8,128)(2,1)}) custom-call(s32[1440]{0:T(1024)} %scatter_custom_fusion.rows_ref.weight_rows_ref, s32[1440]{0:T(1024)} %fusion.10.rows_ref, s32[1]{0:T(128)} %bitcast.2.half_ref, ...), custom_call_target="tpu_custom_call", output_to_operand_aliasing={{3}: (22, {})} | custom-call | tf_op jit(solution)/shard_map/attention_backward/pallas_call | solution.py:830
  404.8 1.2 collective-permute-start.8
  406.1 2.7 add_convert_fusion
  408.8 256.6 %sum_for_owners.1 = (bf16[91,128,128]{2,1,0:T(8,128)(2,1)S(1)}, f32[90,128,128]{2,1,0:T(8,128)S(1)}, f32[90,128,128]{2,1,0:T(8,128)S(1)}, f32[90,128,128]{2,1,0:...) custom-call(bf16[4,2,2,91,128,128]{5,4,3,2,1,0:T(8,128)(2,1)} %bitcast.25, ...), custom_call_target="tpu_custom_call" | custom-call | bytes 381681664 | tf_op jit(solution)/shard_map/sum_for_owners/pallas_call | solution.py:1210
  665.4 13.4 %soap_update.1 = (f32[90,128,128]{2,1,0:T(8,128)}, f32[90,128,128]{2,1,0:T(8,128)}, f32[90,128,128]{2,1,0:T(8,128)}, f32[90,128,128]{2,1,0:T(8,128)}, f32[16,128]{1,0:T(8,128)}) custom-call(bf16[91,128,128]{2,1,0:T(8,128)(2,1)S(1)} %get-tuple-element.102.grad_in, f32[90,128,128]{2,1,0:T(8,128)S(1)} %get-tuple-element.103.masters_ref, ...), custom_call_target="tpu_custom_call" | custom-call | tf_op jit(solution)/shard_map/soap_update/pallas_call | solution.py:867
  678.8 0.8 slice.48
  679.6 0.7 slice_bitcast_fusion
  680.3 0.1 dynamic_slice.22
  680.3 0.1 reshape.131
  680.4 0.9 collective-permute-start.7
  681.3 0.6 divide_subtract_fusion
  681.9 1.6 fusion.2
  683.6 2.8 fusion.5
  686.5 0.5 divide_subtract_fusion.1
  (66 shorter events, 0.3 us)
Async XLA Ops:
  7.2 241.7 %all-gather.3.cloned.1.call-start = ((), (), s32[]{:S(2)}) async-start(), calls=%async_computation | async-start | bytes 50135040 | tf_op jit(solution)/shard_map/all_gather | solution.py:1307
  12.1 1.1 copy-start
  12.1 4.1 copy-start.10
  12.1 5.7 copy-start.14
  12.1 7.5 %copy-start.15 = (f32[1,64]{1,0:T(1,128)S(1)}, f32[1,64]{1,0:T(1,128)}, u32[]{:S(2)}) copy-start(f32[1,64]{1,0:T(1,128)} %param.29) | copy-start | bytes 772
  12.1 7.6 %copy-start.19 = (f32[96]{0:T(128)S(1)}, f32[96]{0:T(128)}, u32[]{:S(2)}) copy-start(f32[96]{0:T(128)} %param.26) | copy-start | bytes 1156
  12.2 74.5 %copy-start.24 = (u32[32]{0:T(128)S(1)}, u32[32]{0:T(128)}, u32[]{:S(2)}) copy-start(u32[32]{0:T(128)} %constant.111) | copy-start | bytes 388
  13.3 117.8 %collective-permute-start = (bf16[256,1536]{1,0:T(8,128)(2,1)S(1)}, bf16[256,1536]{1,0:T(8,128)(2,1)}, u32[]{:S(2)}, u32[]{:S(2)}) collective-permute-start(bf16[256,1536]{1,0:T(8,128)(2,1)S(1)} %copy-done), channel_id=1, source_target_pairs={{0,1},{1,0},{2,3},{3,2},{4,5},{5,4},{6,7},{7,6},{8,9},{9,8},{10,11... | collective-permute-start | bytes 2359304 | tf_op jit(solution)/shard_map/ppermute | solution.py:1272
  16.2 117.8 %collective-permute-start.1 = (bf16[256,1536]{1,0:T(8,128)(2,1)S(1)}, bf16[256,1536]{1,0:T(8,128)(2,1)S(1)}, u32[]{:S(2)}, u32[]{:S(2)}) collective-permute-start(bf16[256,1536]{1,0:T(8,128)(2,1)S(1)} %copy-done.10), channel_id=1, source_target_pairs={{0,1},{1,0},{2,3},{3,2},{4,5},{5,4},{6,7},{7,6},{8,9},{9,8},{10,11... | collective-permute-start | bytes 2359304 | tf_op jit(solution)/shard_map/ppermute | solution.py:1272
  86.7 162.2 %copy-start.12 = (f32[2,1536]{1,0:T(2,128)}, f32[2,1536]{1,0:T(2,128)S(1)}, u32[]{:S(2)}) copy-start(f32[2,1536]{1,0:T(2,128)S(1)} %reshape.125.gain_ref) | copy-start | bytes 36868
  250.1 14.7 %copy-start.11 = (s32[1440]{0:T(1024)S(1)}, s32[1440]{0:T(1024)}, u32[]{:S(2)}) copy-start(s32[1440]{0:T(1024)} %scatter_custom_fusion.rows_ref.weight_rows_ref) | copy-start | bytes 17284
  263.2 20.0 %collective-permute-start.2 = (bf16[256,1536]{1,0:T(8,128)(2,1)}, bf16[256,1536]{1,0:T(8,128)(2,1)S(1)}, u32[]{:S(2)}, u32[]{:S(2)}) collective-permute-start(bf16[256,1536]{1,0:T(8,128)(2,1)} %get-tuple-element.73.own_ref), channel_id=1, source_target_pairs={{0,1},{1,0},{2,3},{3,2},{4,5},{5,4},{6,7},{7,6},{8,9},{9,8},{10,11... | collective-permute-start | bytes 2359304 | tf_op jit(solution)/shard_map/ppermute | solution.py:1272
  265.4 17.8 %copy-start.7 = (bf16[256,1536]{1,0:T(8,128)(2,1)S(1)}, bf16[256,1536]{1,0:T(8,128)(2,1)}, u32[]{:S(2)}) copy-start(bf16[256,1536]{1,0:T(8,128)(2,1)} %get-tuple-element.79.own_ref) | copy-start | bytes 2359300
  283.2 1.5 copy-start.9
  283.2 26.8 %collective-permute-start.4 = (bf16[256,1536]{1,0:T(8,128)(2,1)S(1)}, bf16[256,1536]{1,0:T(8,128)(2,1)S(1)}, u32[]{:S(2)}, u32[]{:S(2)}) collective-permute-start(bf16[256,1536]{1,0:T(8,128)(2,1)S(1)} %copy-done.7), channel_id=1, source_target_pairs={{0,1},{1,0},{2,3},{3,2},{4,5},{5,4},{6,7},{7,6},{8,9},{9,8},{10,11... | collective-permute-start | bytes 2359304 | tf_op jit(solution)/shard_map/ppermute | solution.py:1272
  309.1 70.8 %collective-permute-start.3 = (bf16[256,1536]{1,0:T(8,128)(2,1)}, bf16[256,1536]{1,0:T(8,128)(2,1)S(1)}, u32[]{:S(2)}, u32[]{:S(2)}) collective-permute-start(bf16[256,1536]{1,0:T(8,128)(2,1)} %get-tuple-element.78.own_low_ref), channel_id=1, source_target_pairs={{0,1},{1,0},{2,3},{3,2},{4,5},{5,4},{6,7},{7,6},{8,9},{9,8},{10,11... | collective-permute-start | bytes 2359304 | tf_op jit(solution)/shard_map/ppermute | solution.py:1272
  310.0 0.9 copy-start.8
  335.2 44.7 %collective-permute-start.5 = (bf16[256,1536]{1,0:T(8,128)(2,1)}, bf16[256,1536]{1,0:T(8,128)(2,1)S(1)}, u32[]{:S(2)}, u32[]{:S(2)}) collective-permute-start(bf16[256,1536]{1,0:T(8,128)(2,1)} %get-tuple-element.81.own_high_ref), channel_id=1, source_target_pairs={{0,1},{1,0},{2,3},{3,2},{4,5},{5,4},{6,7},{7,6},{8,9},{9,8},{10,11... | collective-permute-start | bytes 2359304 | tf_op jit(solution)/shard_map/ppermute | solution.py:1272
  336.4 39.4 %copy-start.23 = (s32[16]{0:T(128)S(1)}, s32[16]{0:T(128)}, u32[]{:S(2)}) copy-start(s32[16]{0:T(128)} %constant.94.clone) | copy-start | bytes 196
  374.9 31.1 %collective-permute-start.6 = (bf16[256,1536]{1,0:T(8,128)(2,1)}, bf16[256,1536]{1,0:T(8,128)(2,1)}, u32[]{:S(2)}, u32[]{:S(2)}) collective-permute-start(bf16[256,1536]{1,0:T(8,128)(2,1)} %get-tuple-element.99), channel_id=1, source_target_pairs={{0,1},{1,0},{2,3},{3,2},{4,5},{5,4},{6,7},{7,6},{8,9},{9,8},{10,11... | collective-permute-start | bytes 2359304 | tf_op jit(solution)/shard_map/ppermute | solution.py:1272
  379.9 0.9 copy-start.5
  380.0 1.1 copy-start.6
  381.1 25.0 %copy-start.1 = (f32[256,1536]{1,0:T(8,128)S(1)}, f32[256,1536]{1,0:T(8,128)}, u32[]{:S(2)}) copy-start(f32[256,1536]{1,0:T(8,128)} %get-tuple-element.77.resid_low_ref) | copy-start | bytes 4718596
  381.1 25.0 %copy-start.2 = (f32[256,1536]{1,0:T(8,128)S(1)}, f32[256,1536]{1,0:T(8,128)}, u32[]{:S(2)}) copy-start(f32[256,1536]{1,0:T(8,128)} %get-tuple-element.80.resid_high_ref) | copy-start | bytes 4718596
  404.8 277.1 %collective-permute-start.8 = (bf16[256,1536]{1,0:T(8,128)(2,1)}, bf16[256,1536]{1,0:T(8,128)(2,1)}, u32[]{:S(2)}, u32[]{:S(2)}) collective-permute-start(bf16[256,1536]{1,0:T(8,128)(2,1)} %get-tuple-element.111), channel_id=1, source_target_pairs={{0,1},{1,0},{2,3},{3,2},{4,5},{5,4},{6,7},{7,6},{8,9},{9,8},{10,11... | collective-permute-start | bytes 2359304 | tf_op jit(solution)/shard_map/ppermute | solution.py:1272
  665.3 16.0 %copy-start.16 = (f32[1,64]{1,0:T(1,128)S(1)}, f32[1,64]{1,0:T(1,128)}, u32[]{:S(2)}) copy-start(f32[1,64]{1,0:T(1,128)} %param.29) | copy-start | bytes 772
  665.3 16.0 %copy-start.17 = (f32[1,64]{1,0:T(1,128)S(1)}, f32[1,64]{1,0:T(1,128)}, u32[]{:S(2)}) copy-start(f32[1,64]{1,0:T(1,128)} %param.30) | copy-start | bytes 772
  665.4 15.9 %copy-start.18 = (f32[1,64]{1,0:T(1,128)S(1)}, f32[1,64]{1,0:T(1,128)}, u32[]{:S(2)}) copy-start(f32[1,64]{1,0:T(1,128)} %param.31) | copy-start | bytes 772
  665.4 16.5 %copy-start.3 = (bf16[256,1536]{1,0:T(8,128)(2,1)S(1)}, bf16[256,1536]{1,0:T(8,128)(2,1)}, u32[]{:S(2)}) copy-start(bf16[256,1536]{1,0:T(8,128)(2,1)} %get-tuple-element.110) | copy-start | bytes 2359300
  665.4 16.5 %copy-start.13 = (f32[1536]{0:T(1024)S(1)}, f32[1536]{0:T(1024)}, u32[]{:S(2)}) copy-start(f32[1536]{0:T(1024)} %get-tuple-element.126) | copy-start | bytes 18436
  678.8 4.8 copy-start.4
  680.4 6.0 collective-permute-start.7
  683.6 2.9 copy-start.20
  683.6 2.9 copy-start.21
  683.6 2.9 copy-start.22
Sparse Core Ops, SparseCore 0:
  12.3 236.5 all-gather.2

commit v5 on v4

--- a/solution.py
+++ b/solution.py
@@ -56,14 +56,13 @@
 ROWS = 64
 SMALL_ROWS = 16
 VMEM_LIMIT = 60 * 2**20
-SUM_VMEM = 27 * 2**20
-UPDATE_VMEM = 27 * 2**20
+SUM_VMEM = 36 * 2**20
+WRITE_VMEM = 6 * 2**20
 
 EARLY = 4
 DEPTH = 3
 CROSS_LAG = 2
 HOP_LAG = 1
-SUM_SCRATCH = 36
 
 VMEM_SPEC = pl.BlockSpec(memory_space=pltpu.VMEM)
 SMEM_SPEC = pl.BlockSpec(memory_space=pltpu.SMEM)
@@ -132,10 +131,8 @@
 
 
 def small_places(owner, wide_count):
-    gain_first = owner * (2 * D // wide_count)
-    bias_first = owner * (QKV_WIDTH // wide_count)
-    gain_row = min(gain_first // BLK, 2 * D // BLK - 2)
-    return (gain_row, gain_first - gain_row * BLK, bias_first // BLK, bias_first % BLK)
+    gain_row = min(owner * (2 * D // wide_count) // BLK, 2 * D // BLK - 2)
+    return (gain_row, owner * (QKV_WIDTH // wide_count) // BLK)
 
 
 def scores_turned(keys, queries, allowed):
@@ -602,7 +599,7 @@
 
     row_chunks(length, ROWS, gain_rows)
     for owner in range(wide_count):
-        gain_row, bias_row = small_places(owner, wide_count)[::2]
+        gain_row, bias_row = small_places(owner, wide_count)
         small_rows = []
         for row in (gain_row, gain_row + 1):
             columns = pl.ds(row % (D // BLK) * BLK, BLK)
@@ -680,24 +677,34 @@
 ):
     places = range(grad_stage.shape[1])
     blocks = [first_block + place for place in places]
-    rights = [right_ref[block].astype(bf16) for block in blocks]
-    products = [dot_nn(grad_in[blocks[place]], rights[place]).astype(bf16) for place in places]
-    lefts = [left_ref[block].astype(bf16) for block in blocks]
-    rotated_blocks = [dot_nn(lefts[place].T, products[place]) for place in places]
+    for place, block in enumerate(blocks):
+        grad_stage[slot, place] = grad_in[block].astype(f32)
+    soap_blocks(
+        [grad_in[block] for block in blocks],
+        *[[ref.at[block] for block in blocks] for ref in (masters_ref, first_ref, second_ref, left_ref, right_ref)],
+        *[[stage.at[slot, place] for place in places] for stage in (masters_stage, first_stage, second_stage)],
+    )
+
+
+def soap_blocks(grads, masters, firsts, seconds, lefts, rights, masters_out, firsts_out, seconds_out):
+    count = range(len(grads))
+    rights = [right[...].astype(bf16) for right in rights]
+    products = [dot_nn(grads[index].astype(bf16), rights[index]).astype(bf16) for index in count]
+    lefts = [left[...].astype(bf16) for left in lefts]
+    rotated_blocks = [dot_nn(lefts[index].T, products[index]) for index in count]
     normalized = []
-    for place, block in enumerate(blocks):
-        rotated = rotated_blocks[place]
-        grad_stage[slot, place] = grad_in[block].astype(f32)
-        new_first = beta_first * first_ref[block] + (1.0 - beta_first) * rotated
-        new_second = beta_second * second_ref[block] + (1.0 - beta_second) * rotated * rotated
-        first_stage[slot, place] = new_first
-        second_stage[slot, place] = new_second
+    for index in count:
+        rotated = rotated_blocks[index]
+        new_first = beta_first * firsts[index][...] + (1.0 - beta_first) * rotated
+        new_second = beta_second * seconds[index][...] + (1.0 - beta_second) * rotated * rotated
+        firsts_out[index][...] = new_first
+        seconds_out[index][...] = new_second
         normalized.append(
             (new_first / first_fix / (jnp.sqrt(new_second / second_fix) + adam_eps)).astype(bf16)
         )
-    products = [dot_nt(normalized[place], rights[place]).astype(bf16) for place in places]
-    for place, block in enumerate(blocks):
-        masters_stage[slot, place] = masters_ref[block] - rate_blocks * dot_nn(lefts[place], products[place])
+    products = [dot_nt(normalized[index], rights[index]).astype(bf16) for index in count]
+    for index in count:
+        masters_out[index][...] = masters[index][...] - rate_blocks * dot_nn(lefts[index], products[index])
 
 
 def params(limit=VMEM_LIMIT, **options):
@@ -860,9 +867,13 @@
     )(*operands)
 
 
+def largest_group(count):
+    return max(size for size in range(1, 11) if count % size == 0)
+
+
 def run_soap(reduced, masters, first_moment, second_moment, left_basis, right_basis):
     slots = masters.shape[0]
-    group = max(size for size in range(1, 11) if slots % size == 0)
+    group = largest_group(slots)
     shape = jax.ShapeDtypeStruct(masters.shape, f32)
     return pl.pallas_call(
         soap_update,
@@ -870,22 +881,24 @@
         in_specs=[VMEM_SPEC] * 6,
         out_specs=[ANY_SPEC] * 4 + [VMEM_SPEC],
         scratch_shapes=[pltpu.VMEM((2, group, BLK, BLK), f32)] * 4 + [pltpu.SemaphoreType.DMA((2, 4))],
-        compiler_params=params(UPDATE_VMEM),
+        compiler_params=params(),
         name="soap_update",
     )(reduced, masters, first_moment, second_moment, left_basis, right_basis)
 
 
 def sum_for_owners(
-    line, steps, late_steps, grads, *refs
+    line, steps, late_steps,
+    grads, masters, first_moment, second_moment, left_basis, right_basis,
+    grad_resid, grad_own, grad_sent, tokens, gain, resid, branch_own, branch_other,
+    out, new_masters, new_first, new_second, input_grad, output, small_own, small_other,
+    a_in, a_own, a_sum, a_keep, a_send, a_cross, a_up, a_down,
+    b_in, b_own, b_sum, b_keep, b_send, b_cross, b_up, b_down,
+    a_params, b_params, grad_resid_here, grad_own_here, grad_other_here, tokens_here, gain_here, resid_here,
+    branch_own_here, branch_other_here,
+    core_send, core_recv, own_sems, cross_send, cross_recv, up_send, up_recv, down_send, down_recv,
+    b_core_send, b_core_recv, b_own_sems, b_cross_send, b_cross_recv, b_up_send, b_up_recv, b_down_send, b_down_recv,
+    a_param_sems, b_param_sems, token_sems, swap_send, swap_recv, credits,
 ):
-    held = len(refs[: -SUM_SCRATCH]) // 2
-    sources, (out, *targets), scratch = refs[:held], refs[held:-SUM_SCRATCH], refs[-SUM_SCRATCH:]
-    (
-        a_in, a_own, a_sum, a_keep, a_send, a_cross, a_up, a_down, b_in, b_own, b_sum, b_keep, b_send,
-        b_cross, b_up, b_down, core_send, core_recv, own_sems, cross_send, cross_recv, up_send, up_recv,
-        down_send, down_recv, b_core_send, b_core_recv, b_own_sems, b_cross_send, b_cross_recv, b_up_send,
-        b_up_recv, b_down_send, b_down_recv, held_sems, credits,
-    ) = scratch
     wide = lax.axis_index("wide")
     narrow = lax.axis_index("narrow")
     z = wide // 4
@@ -896,6 +909,8 @@
     cross_peer = (wide + 2 - 4 * x, narrow)
     upper = (lax.rem(wide + 4, 4 * line), narrow)
     lower = (lax.rem(wide + 4 * line - 4, 4 * line), narrow)
+    swap_peer = (wide, 1 - narrow)
+    slots = out.shape[0]
     has_upper = z < line - 1
     has_lower = z > 0
     sum_depth = a_sum.shape[0]
@@ -905,6 +920,7 @@
     barrier = pltpu.get_barrier_semaphore()
     pl.semaphore_signal(barrier, inc=1, device_id=core_peer, device_id_type=mesh_id)
     pl.semaphore_signal(barrier, inc=1, device_id=cross_peer, device_id_type=mesh_id)
+    pl.semaphore_signal(barrier, inc=1, device_id=swap_peer, device_id_type=mesh_id)
 
     @pl.when(has_upper)
     def _():
@@ -914,7 +930,7 @@
     def _():
         pl.semaphore_signal(barrier, inc=1, device_id=lower, device_id_type=mesh_id)
 
-    pl.semaphore_wait(barrier, 2 + has_upper.astype(jnp.int32) + has_lower.astype(jnp.int32))
+    pl.semaphore_wait(barrier, 3 + has_upper.astype(jnp.int32) + has_lower.astype(jnp.int32))
 
     def remote(source, target, send_sem, recv_sem, peer):
         return pltpu.make_async_remote_copy(
@@ -934,13 +950,13 @@
 
     def b_core_copy(step):
         slot = lax.rem(step, DEPTH)
-        source = grads.at[:, :, 1 - core, steps * EARLY + step]
+        source = grads.at[:, :, 1 - core, slots - 1 - step]
         return remote(source, b_in.at[slot], b_core_send.at[slot], b_core_recv.at[slot], core_peer)
 
     def b_own_copy(step):
         slot = lax.rem(step, DEPTH)
         return pltpu.make_async_copy(
-            grads.at[:, :, core, steps * EARLY + step], b_own.at[slot], b_own_sems.at[slot]
+            grads.at[:, :, core, slots - 1 - step], b_own.at[slot], b_own_sems.at[slot]
         )
 
     def cross_copy(step):
@@ -994,14 +1010,66 @@
             remote_copy(step).start()
             local_copy(step).start()
 
-    held_copies = [
-        pltpu.make_async_copy(source, target, held_sems.at[index])
-        for index, (source, target) in enumerate(zip(sources, targets))
+    sources = (masters, first_moment, second_moment, left_basis, right_basis)
+
+    def param_loads(step):
+        slot = lax.rem(step, 2)
+        places = pl.ds(step * EARLY, EARLY)
+        return [
+            pltpu.make_async_copy(source.at[places], a_params.at[slot, index], a_param_sems.at[slot, index])
+            for index, source in enumerate(sources)
+        ]
+
+    def b_param_loads(step):
+        slot = lax.rem(step, 2)
+        return [
+            pltpu.make_async_copy(
+                source.at[slots - 1 - step], b_params.at[slot, index], b_param_sems.at[slot, index]
+            )
+            for index, source in enumerate(sources)
+        ]
+
+    token_loads = [
+        pltpu.make_async_copy(source, target, token_sems.at[index])
+        for index, (source, target) in enumerate((
+            (resid, resid_here), (branch_own, branch_own_here), (branch_other, branch_other_here),
+            (grad_resid, grad_resid_here), (grad_own, grad_own_here), (tokens, tokens_here), (gain, gain_here),
+        ))
     ]
-    start_all(held_copies)
+    grad_swap = remote(grad_sent, grad_other_here, swap_send.at[0], swap_recv.at[0], swap_peer)
+    small_swap = remote(small_own, small_other, swap_send.at[1], swap_recv.at[1], swap_peer)
+
+    def finish_output():
+        for copy in token_loads[:3]:
+            copy.wait()
+
+        def rows_of_output(rows):
+            total = resid_here[rows, :] + branch_own_here[rows, :].astype(f32) + branch_other_here[rows, :].astype(f32)
+            output[rows, :] = total.astype(bf16)
+
+        row_chunks(output.shape[0], ROWS, rows_of_output)
+
+    def finish_input_grad():
+        for copy in token_loads[3:]:
+            copy.wait()
+        grad_swap.wait()
+
+        def rows_of_grad(rows):
+            values = tokens_here[rows, :].astype(f32)
+            inverse = rms_inverse(values)
+            scaled = grad_own_here[rows, :].astype(f32) + grad_other_here[rows, :].astype(f32)
+            input_grad[rows, :] = grad_resid_here[rows, :] + norm_back(
+                scaled * gain_here[...], values * inverse, inverse
+            )
+
+        row_chunks(input_grad.shape[0], ROWS, rows_of_grad)
+
+    grad_swap.start()
     for early in range(DEPTH - 1):
         feed(early, steps, 0, core_copy, own_copy)
         feed(early, late_steps, 1, b_core_copy, b_own_copy)
+
+    start_all(param_loads(0) + param_loads(1) + b_param_loads(1) + b_param_loads(2) + token_loads)
 
     def active(step, count):
         return (step >= 0) & (step < count)
@@ -1148,6 +1216,21 @@
         def _():
             gather_hops(last, steps, a_sum, sum_depth, a_up, a_down, up_copy, down_copy, 4, a_keep)
             out[pl.ds(last * EARLY, EARLY)] = a_keep[...].astype(bf16)
+            slot = lax.rem(last, 2)
+            for copy in param_loads(last):
+                copy.wait()
+            soap_blocks(
+                [a_keep[index] for index in range(EARLY)],
+                *[[a_params.at[slot, kind, index] for index in range(EARLY)] for kind in range(5)],
+                *[
+                    [target.at[last * EARLY + index] for index in range(EARLY)]
+                    for target in (new_masters, new_first, new_second)
+                ],
+            )
+
+            @pl.when(last + 2 < steps)
+            def _():
+                start_all(param_loads(last + 2))
 
         arrived = step - HOP_LAG * far
 
@@ -1172,13 +1255,35 @@
         def _():
             slot = lax.rem(paired, DEPTH)
             b_cross_copy(paired).wait_recv()
-            place = steps * EARLY + paired
-            out[place] = (b_keep[slot, x] + b_cross[slot].astype(f32)).astype(bf16)
+            place = slots - 1 - paired
+            total = b_keep[slot, x] + b_cross[slot].astype(f32)
+            out[place] = total.astype(bf16)
 
             @pl.when(paired < late_steps - DEPTH)
             def _():
                 give(3, cross_peer)
 
+            @pl.when(paired == 0)
+            def _():
+                small_own[...] = total[: small_own.shape[0]]
+                small_swap.start()
+
+            @pl.when(paired > 0)
+            def _():
+                slot = lax.rem(paired, 2)
+                for copy in b_param_loads(paired):
+                    copy.wait()
+                soap_blocks(
+                    [total], *[[b_params.at[slot, kind]] for kind in range(5)],
+                    [new_masters.at[place]], [new_first.at[place]], [new_second.at[place]],
+                )
+
+                @pl.when(paired + 2 < late_steps)
+                def _():
+                    start_all(b_param_loads(paired + 2))
+
+        pl.when(step == 4)(finish_output)
+        pl.when(step == 8)(finish_input_grad)
         return 0
 
     lag = HOP_LAG * (line - 1) + CROSS_LAG
@@ -1187,11 +1292,10 @@
         cross_copy(step).wait_send()
     for step in range(max(late_steps - DEPTH, 0), late_steps):
         b_cross_copy(step).wait_send()
-    for copy in held_copies:
-        copy.wait()
-
-
-def run_sum_for_owners(grads, wide_count, held):
+    small_swap.wait()
+
+
+def run_sum_for_owners(grads, wide_count, blocks, token_arrays):
     line = wide_count // 4
     slots, block = grads.shape[0] // wide_count, grads.shape[1:]
     steps = (slots - 1) // (EARLY + 1)
@@ -1209,9 +1313,12 @@
 
     return pl.pallas_call(
         functools.partial(sum_for_owners, line, steps, late_steps),
-        out_shape=[pltpu.VMEM((slots,) + block, bf16)] + [pltpu.VMEM(array.shape, array.dtype) for array in held],
-        in_specs=[ANY_SPEC] * (1 + len(held)),
-        out_specs=[VMEM_SPEC] * (1 + len(held)),
+        out_shape=[pltpu.VMEM((slots,) + block, bf16)]
+        + [pltpu.VMEM(blocks[0].shape, f32)] * 3
+        + [pltpu.VMEM(token_arrays[0].shape, f32), pltpu.VMEM(token_arrays[0].shape, bf16)]
+        + [pltpu.VMEM((SMALL_ROWS, block[-1]), f32)] * 2,
+        in_specs=[ANY_SPEC] * (1 + len(blocks) + len(token_arrays)),
+        out_specs=[VMEM_SPEC] * 8,
         scratch_shapes=[
             vmem(DEPTH, line, 2, EARLY),
             vmem(DEPTH, line, 2, EARLY),
@@ -1229,13 +1336,76 @@
             vmem(DEPTH),
             vmem(hop_depth, line, 2),
             vmem(hop_depth, line, 2),
+            wide_vmem(2, len(blocks), EARLY),
+            wide_vmem(2, len(blocks)),
         ]
+        + [pltpu.VMEM(array.shape, array.dtype) for array in token_arrays]
         + ([dma((DEPTH,))] * 5 + [dma((hop_depth, line))] * 4) * 2
-        + [dma((len(held),)), pltpu.SemaphoreType.REGULAR((8,))],
+        + [dma((2, len(blocks)))] * 2
+        + [dma((len(token_arrays) - 1,)), dma((2,)), dma((2,)), pltpu.SemaphoreType.REGULAR((8,))],
         compiler_params=params(SUM_VMEM, collective_id=0, has_side_effects=True),
         cost_estimate=pl.CostEstimate(flops=0, bytes_accessed=2 * grads.size * 8, transcendentals=0),
         name="sum_for_owners",
-    )(grads.reshape((line, 2, 2, slots) + block), *held)
+    )(grads.reshape((line, 2, 2, slots) + block), *blocks, *token_arrays)
+
+
+def write_results(
+    reduced, masters, first_moment, second_moment, input_grad, output, small_own, small_other,
+    block_grad_out, masters_out, first_out, second_out, input_grad_out, output_out, small_out,
+    stage, stage_sems, sems,
+):
+    copies = [
+        pltpu.make_async_copy(source, target, sems.at[index])
+        for index, (source, target) in enumerate((
+            (masters, masters_out), (first_moment, first_out), (second_moment, second_out),
+            (input_grad, input_grad_out), (output, output_out),
+        ))
+    ]
+    start_all(copies)
+    small_out[0] = small_own[...]
+    small_out[1] = small_other[...]
+    group = stage.shape[1]
+    steps = masters.shape[0] // group
+
+    def store(step):
+        slot = lax.rem(step, 2)
+        return pltpu.make_async_copy(
+            stage.at[slot], block_grad_out.at[pl.ds(step * group, group)], stage_sems.at[slot]
+        )
+
+    @pl.loop(0, steps)
+    def _(step):
+        @pl.when(step >= 2)
+        def _():
+            store(step - 2).wait()
+
+        stage[lax.rem(step, 2)] = reduced[pl.ds(step * group, group)].astype(f32)
+        store(step).start()
+
+    for step in range(max(steps - 2, 0), steps):
+        store(step).wait()
+    for copy in copies:
+        copy.wait()
+
+
+def run_write_results(*arrays):
+    arrays = [pltpu.with_memory_space_constraint(array, pltpu.VMEM) for array in arrays]
+    blocks, rows, small = arrays[1].shape, arrays[4].shape, arrays[-1].shape
+    group = largest_group(blocks[0])
+    shape = jax.ShapeDtypeStruct
+    return pl.pallas_call(
+        write_results,
+        out_shape=[shape(blocks, f32)] * 4 + [shape(rows, f32), shape(rows, bf16), shape((2,) + small, f32)],
+        in_specs=[VMEM_SPEC] * len(arrays),
+        out_specs=[ANY_SPEC] * 6 + [VMEM_SPEC],
+        scratch_shapes=[
+            pltpu.VMEM((2, group) + blocks[1:], f32),
+            pltpu.SemaphoreType.DMA((2,)),
+            pltpu.SemaphoreType.DMA((5,)),
+        ],
+        compiler_params=params(WRITE_VMEM),
+        name="write_results",
+    )(*arrays)
 
 
 def rope_tables(segment_row):
@@ -1355,33 +1525,32 @@
         (resid_high, grad_high, grad_high_other), cotangent_row, gain_full, cosine, sine, allowed_turned,
         normed_one_turned, qkv, mixed_turned, log_total, (gain_low, gain_high), weights, grads, wide_count,
     )
-    grad_one_other = swap_halves(grad_one_sent)
     resid_own = jnp.where(half == 0, resid_low, resid_high)
-    output = (resid_own + branch_own.astype(f32) + branch_other.astype(f32)).astype(bf16)
-
-    held = [masters, first_moment, second_moment, left_basis, right_basis]
+    blocks = [masters, first_moment, second_moment, left_basis, right_basis]
     if wide_count == 16:
-        grads, output = lax.optimization_barrier((grads, output))
-        reduced, *held = [
-            pltpu.with_memory_space_constraint(array, pltpu.VMEM)
-            for array in run_sum_for_owners(grads, wide_count, held)
+        token_arrays = [
+            grad_resid, grad_one_own, grad_one_sent, tokens, gain_full[0:1], resid_own, branch_own, branch_other
         ]
+        block_grad, new_masters, new_first, new_second, input_grad, output, small_sums = run_write_results(
+            *run_sum_for_owners(grads, wide_count, blocks, token_arrays)
+        )
+        gain_parts = small_sums[0, :2] + small_sums[1, :2]
+        bias_row = small_sums[0, 2]
     else:
         reduced = lax.psum_scatter(grads, "wide", scatter_dimension=0, tiled=True)
-
-    block_grad, new_masters, new_first, new_second, small_sums = run_soap(reduced, *held)
-    inverse_one, normed_one = rms_parts(tokens.astype(f32))
-    grad_one = grad_one_own.astype(f32) + grad_one_other.astype(f32)
-    input_grad = grad_resid + norm_back(grad_one * gain_full[0:1], normed_one, inverse_one)
-    places = [small_places(owner, wide_count) for owner in range(wide_count)]
-    gain_offset = jnp.asarray([place[1] for place in places], jnp.int32)[wide_index]
-    bias_offset = jnp.asarray([place[3] for place in places], jnp.int32)[wide_index]
-    gain_sums = lax.dynamic_slice_in_dim(small_sums[:2].reshape(-1), gain_offset, pair_gains, 0)
-    gain_sums = gain_sums.reshape(2, gains_here)
-    gain_other, input_grad = lax.optimization_barrier((swap_halves(gain_sums), input_grad))
-    gain_sums = gain_sums + gain_other
-    gain_grad = lax.dynamic_index_in_dim(gain_sums, half, 0, keepdims=False)
-    bias_grad = lax.dynamic_slice_in_dim(small_sums[2], bias_offset, biases_here, 0).reshape(biases.shape)
+        block_grad, new_masters, new_first, new_second, small_sums = run_soap(reduced, *blocks)
+        gain_parts = small_sums[:2] + swap_halves(small_sums[:2])
+        bias_row = small_sums[2]
+        output = (resid_own + branch_own.astype(f32) + branch_other.astype(f32)).astype(bf16)
+        inverse_one, normed_one = rms_parts(tokens.astype(f32))
+        grad_one = grad_one_own.astype(f32) + swap_halves(grad_one_sent).astype(f32)
+        input_grad = grad_resid + norm_back(grad_one * gain_full[0:1], normed_one, inverse_one)
+
+    gain_first_index = wide_index * pair_gains
+    gain_offset = gain_first_index - jnp.minimum(gain_first_index // BLK, 2 * D // BLK - 2) * BLK
+    bias_offset = lax.rem(wide_index * biases_here, BLK)
+    gain_grad = lax.dynamic_slice_in_dim(gain_parts.reshape(-1), gain_offset + half * gains_here, gains_here, 0)
+    bias_grad = lax.dynamic_slice_in_dim(bias_row, bias_offset, biases_here, 0).reshape(biases.shape)
     new_gains, new_gain_first, new_gain_second = adam_small(gains, gain_grad, gain_first, gain_second, rate_gains)
     new_biases, new_bias_first, new_bias_second = adam_small(biases, bias_grad, bias_first, bias_second, rate_small)
 

time: 702 us -> 683 us (0.973)
  transfers between devices with their start and end apart: 10 -> 8, of which waited for: 2 -> 2; matrix products, arithmetic and copies ran while one was open for 5% -> 3% of each run, Pallas kernels for 57% -> 19%
where the time goes in v5:
time: 683 us; the launch traced here: 674 us
  Pallas kernels  404 us (59%)
  waiting for transfers between devices  117 us (17%)
  blocking collectives  98 us (14%)
  other arithmetic  18.6 us (3%)
  between operations  15.2 us (2%)
  local copies, waits for them, and re-layouts  12 us (2%)
  starting transfers between devices  9.26 us (1%)
    pallas_call x1, Pallas kernels, run_sum_for_owners(): pl.pallas_call(functools.partial(sum_for_owners, line, steps, late_steps)...  255 us
    all_gather x1, waiting for transfers between devices, body(): weights = lax.all_gather(masters_low, 'wide', axis=0, tiled=True)  114 us
    unnamed x2, blocking collectives  98 us
    pallas_call x2, Pallas kernels, run_hidden_grads(): pl.pallas_call(functools.partial(hidden_grads, first_row), out_shape=[sha...  49 us
    pallas_call x1, Pallas kernels, run_hidden_weight_grads(): pl.pallas_call(hidden_weight_grads, out_shape=[shape((length // NARROW, D...  38.8 us
    pallas_call x1, Pallas kernels, run_attention_backward(): pl.pallas_call(attention_backward, out_shape=[shape((length // NARROW, D)...  23.5 us
    pallas_call x1, Pallas kernels, run_active_grads(): pl.pallas_call(active_grads, out_shape=jax.ShapeDtypeStruct((TILES, lengt...  15.1 us
  transfers between devices with their start and end apart: 8, of which 2 were waited for; matrix products, arithmetic and copies ran while one was open for 3% of the time, Pallas kernels for 19%

profile of v5, /device:TPU:0, one launch (start us, length us, event | category | flops | bytes accessed | tf_op | source)
XLA Modules:
  0.0 674.2 jit_solution(11878406139355437525)
XLA Ops:
  7.2 0.0 copy-start.2
  7.2 0.0 all-gather.3.cloned.1.call-start
  7.2 5.0 convert_element_type.21
  12.3 0.0 all-gather.3.cloned.1.call-update
  12.3 0.0 copy-done.2
  12.3 3.0 collective-permute-start
  15.3 0.1 collective-permute-start.1
  15.4 0.9 compare_reduce_fusion
  16.3 0.1 add_select_fusion.1
  16.4 0.3 reduce-window.24
  16.7 0.1 slice.47
  16.8 0.0 copy-done.9
  16.8 0.3 reduce-window.16
  17.1 0.1 slice.53
  17.2 0.1 slice_reduce_fusion.1
  17.4 0.1 slice_reduce_fusion
  17.5 0.1 fusion.8
  17.6 0.1 add_bitcast_fusion
  17.6 1.0 fusion.2
  18.7 0.3 dynamic-update-slice
  19.0 66.8 %all-reduce.1 = f32[3072]{0:T(1024)S(1)} all-reduce(f32[3072]{0:T(1024)S(1)} %dynamic-update-slice), channel_id=1, replica_groups=mesh['wide'=16,'narrow'=2] {'wide','narrow'}, use_global_device_ids=true, to_apply=%add.1 | all-reduce | flops 3072 | bytes 24576
  85.8 0.6 dynamic-slice.1
  87.0 0.2 dynamic-update-slice.1
  87.3 31.2 %all-reduce.2 = bf16[1024]{0:T(1024)(128)(2,1)S(1)} all-reduce(bf16[1024]{0:T(1024)(128)(2,1)S(1)} %dynamic-update-slice.1), channel_id=2, replica_groups=mesh['wide'=16,'narrow'=2] {'wide'}, use_global_device_ids=true, to_apply=%add.2 | all-reduce | flops 1024 | bytes 4096
  118.5 0.6 reshape.168
  119.1 8.2 %scatter_custom_fusion.rows_ref.weight_rows_ref = s32[1440]{0:T(1024)} fusion(s32[1440]{0:T(1024)S(1)} %compare_select_fusion, s32[1440]{0:T(1024)S(1)} %iota.33, s32[]{:T(128)} %constant.33.clone.1), kind=kCustom, calls=%fused_computation.25 | custom fusion | bytes 5764 | tf_op jit(solution)/shard_map/scatter | solution.py:1486
  127.2 0.7 constant_dynamic-slice_fusion.1
  128.0 1.0 pad_maximum_fusion
  129.0 1.2 fusion.1.allowed_ref
  130.2 0.0 collective-permute-done
  130.2 3.0 maximum_select_fusion.x_ref
  133.2 0.0 collective-permute-done.1
  133.2 1.8 maximum_select_fusion.1.cot_ref
  135.0 114.0 %all-gather.3.cloned.1.call-done.weights.refs_8_ = bf16[1440,128,128]{2,1,0:T(8,128)(2,1)} async-done(((bf16[90,128,128]{2,1,0:T(8,128)(2,1)}), bf16[1440,128,128]{2,1,0:T(8,128)(2,1)}) %all-gather.3.cloned.1.call-update) | async-done | bytes 47185936 | tf_op jit(solution)/shard_map/all_gather | solution.py:1477
  249.0 0.6 fusion.15
  249.6 12.8 %attention_forward.1 = (bf16[256,1536]{1,0:T(8,128)(2,1)}, bf16[256,1536]{1,0:T(8,128)(2,1)}, bf16[1536,512]{1,0:T(8,128)(2,1)}, bf16[512,1024]{1,0:T(8,128)(2,1...) custom-call(s32[1440]{0:T(1024)} %scatter_custom_fusion.rows_ref.weight_rows_ref, ...), custom_call_target="tpu_custom_call" | custom-call | tf_op jit(solution)/shard_map/attention_forward/pallas_call | solution.py:717
  262.5 1.5 collective-permute-start.2
  264.0 0.6 fusion.3.rows_ref
  264.6 15.1 %active_grads.1.active_grad = f32[6,512,768]{2,1,0:T(8,128)} custom-call(s32[1440]{0:T(1024)} %scatter_custom_fusion.rows_ref.weight_rows_ref, bf16[512,1536]{1,0:T(8,128)(2,1)} %maximum_select_fusion.1.cot_ref, bf16[1440,128,128]{2,1,0:T(8,128)(2,1)} %all-gather.3.cloned.1.call-done.weights.refs_8_), custom_call_target="tpu_custom_call" | custom-call | flops 7247757312 | bytes 23592960 | tf_op jit(solution)/shard_map/active_grads/pallas_call | solution.py:749
  279.7 2.7 collective-permute-done.2.other_ref
  282.4 1.5 collective-permute-start.4
  283.9 24.4 %hidden_grads.2 = (bf16[256,1536]{1,0:T(8,128)(2,1)}, f32[256,1536]{1,0:T(8,128)}, bf16[1536,256]{1,0:T(8,128)(2,1)}, f32[1,1536]{1,0:T(1,128)}, bf16[6,256,1536...) custom-call(s32[1440]{0:T(1024)} %scatter_custom_fusion.rows_ref.weight_rows_ref, ...), custom_call_target="tpu_custom_call" | custom-call | flops 14495514624 | bytes 42467328 | tf_op jit(solution)/shard_map/hidden_grads/pallas_call | solution.py:769
  308.4 0.9 collective-permute-start.3
  309.3 0.0 collective-permute-done.4.other_ref
  309.3 0.9 copy-done.4
  310.2 24.6 %hidden_grads.3 = (bf16[256,1536]{1,0:T(8,128)(2,1)}, f32[256,1536]{1,0:T(8,128)}, bf16[1536,256]{1,0:T(8,128)(2,1)}, f32[1,1536]{1,0:T(1,128)}, bf16[6,256,1536...) custom-call(s32[1440]{0:T(1024)} %scatter_custom_fusion.rows_ref.weight_rows_ref, ...), custom_call_target="tpu_custom_call" | custom-call | flops 14495514624 | bytes 42467328 | tf_op jit(solution)/shard_map/hidden_grads/pallas_call | solution.py:769
  334.8 1.2 collective-permute-start.5
  336.0 38.8 %hidden_weight_grads.1 = (bf16[256,1536]{1,0:T(8,128)(2,1)}, bf16[256,1536]{1,0:T(8,128)(2,1)}, bf16[1456,128,128]{2,1,0:T(8,128)(2,1)}) custom-call(s32[1440]{0:T(1024)} %scatter_custom_fusion.rows_ref.weight_rows_ref, s32[1440]{0:T(1024)} %fusion.3.rows_ref, s32[1]{0:T(128)} %bitcast.2.half_ref, bf16[512,1536]{1,0:T(8,128)(2,1)} %maximum_select_fusion.1.cot_ref, ...), custom_call_target="tpu_custom_call" | custom-call | flops 28991029248 | bytes 75497472 | tf_op jit(solution)/shard_map/hidden_weight_grads/pallas_call | solution.py:802
  374.9 0.9 collective-permute-start.6
  375.8 1.3 broadcast_select_fusion.resid
  377.1 0.0 collective-permute-done.3.other_low_ref
  377.1 0.0 collective-permute-done.5.other_high_ref
  377.1 23.5 %attention_backward.1 = (f32[256,1536]{1,0:T(8,128)}, bf16[256,1536]{1,0:T(8,128)(2,1)}, bf16[256,1536]{1,0:T(8,128)(2,1)}, bf16[1456,128,128]{2,1,0:T(8,128)(2,1)}) custom-call(s32[1440]{0:T(1024)} %scatter_custom_fusion.rows_ref.weight_rows_ref, s32[1440]{0:T(1024)} %fusion.3.rows_ref, s32[1]{0:T(128)} %bitcast.2.half_ref, ...), custom_call_target="tpu_custom_call", output_to_operand_aliasing={{3}: (22, {})} | custom-call | tf_op jit(solution)/shard_map/attention_backward/pallas_call | solution.py:837
  400.6 0.0 collective-permute-done.6.branch_other
  400.6 254.5 %sum_for_owners.1 = (bf16[91,128,128]{2,1,0:T(8,128)(2,1)S(1)}, f32[90,128,128]{2,1,0:T(8,128)S(1)}, f32[90,128,128]{2,1,0:T(8,128)S(1)}, f32[90,128,128]{2,1,0:...) custom-call(bf16[4,2,2,91,128,128]{5,4,3,2,1,0:T(8,128)(2,1)} %bitca, ...), custom_call_target="tpu_custom_call" | custom-call | bytes 381681664 | tf_op jit(solution)/shard_map/sum_for_owners/pallas_call | solution.py:1314
  655.2 0.0 copy-start.11
  655.2 0.0 copy-start.12
  655.2 0.0 copy-start.13
  655.2 0.0 copy-start.15
  655.2 0.0 copy-start.16
  655.2 0.0 copy-start.17
  655.3 10.6 %write_results.1 = (f32[90,128,128]{2,1,0:T(8,128)}, f32[90,128,128]{2,1,0:T(8,128)}, f32[90,128,128]{2,1,0:T(8,128)}, f32[90,128,128]{2,1,0:T(8,128)}, f32[256,...) custom-call(bf16[91,128,128]{2,1,0:T(8,128)(2,1)S(1)} %get-tuple-element.103.reduced, ...), custom_call_target="tpu_custom_call" | custom-call | tf_op jit(solution)/shard_map/write_results/pallas_call | solution.py:1396
  665.9 0.6 divide_subtract_fusion
  666.6 0.6 divide_subtract_fusion.1
  (41 shorter events, 0.2 us)
Async XLA Ops:
  7.2 5.1 copy-start.2
  7.2 8.2 %copy-start.6 = (bf16[256,1536]{1,0:T(8,128)(2,1)S(1)}, bf16[256,1536]{1,0:T(8,128)(2,1)}, u32[]{:S(2)}) copy-start(bf16[256,1536]{1,0:T(8,128)(2,1)} %param.16) | copy-start | bytes 2359300
  7.2 241.8 %all-gather.3.cloned.1.call-start = ((), (), s32[]{:S(2)}) async-start(), calls=%async_computation | async-start | bytes 50135040 | tf_op jit(solution)/shard_map/all_gather | solution.py:1477
  12.3 4.6 copy-start.9
  12.3 6.4 copy-start.10
  12.3 6.4 copy-start.14
  12.3 73.5 %copy-start.18 = (u32[32]{0:T(128)S(1)}, u32[32]{0:T(128)}, u32[]{:S(2)}) copy-start(u32[32]{0:T(128)} %constant.116) | copy-start | bytes 388
  12.3 117.9 %collective-permute-start = (bf16[256,1536]{1,0:T(8,128)(2,1)S(1)}, bf16[256,1536]{1,0:T(8,128)(2,1)}, u32[]{:S(2)}, u32[]{:S(2)}) collective-permute-start(bf16[256,1536]{1,0:T(8,128)(2,1)S(1)} %copy-done.2), channel_id=1, source_target_pairs={{0,1},{1,0},{2,3},{3,2},{4,5},{5,4},{6,7},{7,6},{8,9},{9,8},{10,11... | collective-permute-start | bytes 2359304 | tf_op jit(solution)/shard_map/ppermute | solution.py:1442
  15.3 117.8 %collective-permute-start.1 = (bf16[256,1536]{1,0:T(8,128)(2,1)S(1)}, bf16[256,1536]{1,0:T(8,128)(2,1)S(1)}, u32[]{:S(2)}, u32[]{:S(2)}) collective-permute-start(bf16[256,1536]{1,0:T(8,128)(2,1)S(1)} %copy-done.6), channel_id=1, source_target_pairs={{0,1},{1,0},{2,3},{3,2},{4,5},{5,4},{6,7},{7,6},{8,9},{9,8},{10,11... | collective-permute-start | bytes 2359304 | tf_op jit(solution)/shard_map/ppermute | solution.py:1442
  85.8 163.2 %copy-start.8 = (f32[2,1536]{1,0:T(2,128)}, f32[2,1536]{1,0:T(2,128)S(1)}, u32[]{:S(2)}) copy-start(f32[2,1536]{1,0:T(2,128)S(1)} %reshape.141.gain_ref) | copy-start | bytes 36868
  249.6 14.4 %copy-start.7 = (s32[1440]{0:T(1024)S(1)}, s32[1440]{0:T(1024)}, u32[]{:S(2)}) copy-start(s32[1440]{0:T(1024)} %scatter_custom_fusion.rows_ref.weight_rows_ref) | copy-start | bytes 17284
  262.5 20.0 %collective-permute-start.2 = (bf16[256,1536]{1,0:T(8,128)(2,1)}, bf16[256,1536]{1,0:T(8,128)(2,1)S(1)}, u32[]{:S(2)}, u32[]{:S(2)}) collective-permute-start(bf16[256,1536]{1,0:T(8,128)(2,1)} %get-tuple-element.73.own_ref), channel_id=1, source_target_pairs={{0,1},{1,0},{2,3},{3,2},{4,5},{5,4},{6,7},{7,6},{8,9},{9,8},{10,11... | collective-permute-start | bytes 2359304 | tf_op jit(solution)/shard_map/ppermute | solution.py:1442
  264.6 17.8 %copy-start.3 = (bf16[256,1536]{1,0:T(8,128)(2,1)S(1)}, bf16[256,1536]{1,0:T(8,128)(2,1)}, u32[]{:S(2)}) copy-start(bf16[256,1536]{1,0:T(8,128)(2,1)} %get-tuple-element.79.own_ref) | copy-start | bytes 2359300
  282.4 1.5 copy-start.5
  282.4 26.9 %collective-permute-start.4 = (bf16[256,1536]{1,0:T(8,128)(2,1)S(1)}, bf16[256,1536]{1,0:T(8,128)(2,1)S(1)}, u32[]{:S(2)}, u32[]{:S(2)}) collective-permute-start(bf16[256,1536]{1,0:T(8,128)(2,1)S(1)} %copy-done.3), channel_id=1, source_target_pairs={{0,1},{1,0},{2,3},{3,2},{4,5},{5,4},{6,7},{7,6},{8,9},{9,8},{10,11... | collective-permute-start | bytes 2359304 | tf_op jit(solution)/shard_map/ppermute | solution.py:1442
  308.4 68.8 %collective-permute-start.3 = (bf16[256,1536]{1,0:T(8,128)(2,1)}, bf16[256,1536]{1,0:T(8,128)(2,1)}, u32[]{:S(2)}, u32[]{:S(2)}) collective-permute-start(bf16[256,1536]{1,0:T(8,128)(2,1)} %get-tuple-element.78.own_low_ref), channel_id=1, source_target_pairs={{0,1},{1,0},{2,3},{3,2},{4,5},{5,4},{6,7},{7,6},{8,9},{9,8},{10,11... | collective-permute-start | bytes 2359304 | tf_op jit(solution)/shard_map/ppermute | solution.py:1442
  309.3 0.9 copy-start.4
  334.8 42.3 %collective-permute-start.5 = (bf16[256,1536]{1,0:T(8,128)(2,1)}, bf16[256,1536]{1,0:T(8,128)(2,1)}, u32[]{:S(2)}, u32[]{:S(2)}) collective-permute-start(bf16[256,1536]{1,0:T(8,128)(2,1)} %get-tuple-element.81.own_high_ref), channel_id=1, source_target_pairs={{0,1},{1,0},{2,3},{3,2},{4,5},{5,4},{6,7},{7,6},{8,9},{9,8},{10,11... | collective-permute-start | bytes 2359304 | tf_op jit(solution)/shard_map/ppermute | solution.py:1442
  336.0 39.8 %copy-start = (f32[256,1536]{1,0:T(8,128)S(1)}, f32[256,1536]{1,0:T(8,128)}, u32[]{:S(2)}) copy-start(f32[256,1536]{1,0:T(8,128)} %get-tuple-element.77.resid_low_ref) | copy-start | bytes 4718596
  336.0 39.8 %copy-start.1 = (f32[256,1536]{1,0:T(8,128)S(1)}, f32[256,1536]{1,0:T(8,128)}, u32[]{:S(2)}) copy-start(f32[256,1536]{1,0:T(8,128)} %get-tuple-element.80.resid_high_ref) | copy-start | bytes 4718596
  374.9 25.8 %collective-permute-start.6 = (bf16[256,1536]{1,0:T(8,128)(2,1)}, bf16[256,1536]{1,0:T(8,128)(2,1)}, u32[]{:S(2)}, u32[]{:S(2)}) collective-permute-start(bf16[256,1536]{1,0:T(8,128)(2,1)} %get-tuple-element.102), channel_id=1, source_target_pairs={{0,1},{1,0},{2,3},{3,2},{4,5},{5,4},{6,7},{7,6},{8,9},{9,8},{10,11... | collective-permute-start | bytes 2359304 | tf_op jit(solution)/shard_map/ppermute | solution.py:1442
  655.2 10.7 %copy-start.11 = (f32[1,64]{1,0:T(1,128)S(1)}, f32[1,64]{1,0:T(1,128)}, u32[]{:S(2)}) copy-start(f32[1,64]{1,0:T(1,128)} %param.27) | copy-start | bytes 772
  655.2 10.7 %copy-start.12 = (f32[1,64]{1,0:T(1,128)S(1)}, f32[1,64]{1,0:T(1,128)}, u32[]{:S(2)}) copy-start(f32[1,64]{1,0:T(1,128)} %param.28) | copy-start | bytes 772
  655.2 10.7 %copy-start.13 = (f32[1,64]{1,0:T(1,128)S(1)}, f32[1,64]{1,0:T(1,128)}, u32[]{:S(2)}) copy-start(f32[1,64]{1,0:T(1,128)} %param.29) | copy-start | bytes 772
  655.2 11.3 %copy-start.15 = (f32[96]{0:T(128)S(1)}, f32[96]{0:T(128)}, u32[]{:S(2)}) copy-start(f32[96]{0:T(128)} %param.24) | copy-start | bytes 1156
  655.2 11.3 %copy-start.16 = (f32[96]{0:T(128)S(1)}, f32[96]{0:T(128)}, u32[]{:S(2)}) copy-start(f32[96]{0:T(128)} %param.25) | copy-start | bytes 1156
  655.2 11.3 %copy-start.17 = (f32[96]{0:T(128)S(1)}, f32[96]{0:T(128)}, u32[]{:S(2)}) copy-start(f32[96]{0:T(128)} %param.26) | copy-start | bytes 1156
Sparse Core Ops, SparseCore 0:
  12.4 236.5 all-gather.2

commit v6 on v5

--- a/solution.py
+++ b/solution.py
@@ -56,7 +56,7 @@
 ROWS = 64
 SMALL_ROWS = 16
 VMEM_LIMIT = 60 * 2**20
-SUM_VMEM = 36 * 2**20
+SUM_VMEM = 39 * 2**20
 WRITE_VMEM = 6 * 2**20
 
 EARLY = 4
@@ -111,6 +111,18 @@
     pltpu.make_async_copy(ref, ref, sem).wait()
 
 
+def copies_between(sources, targets, sems):
+    return [
+        pltpu.make_async_copy(source, target, sems.at[index])
+        for index, (source, target) in enumerate(zip(sources, targets, strict=True))
+    ]
+
+
+def wait_all(copies):
+    for copy in copies:
+        copy.wait()
+
+
 def fetch_attention(rows_ref, weights, w_qkv, w_out, sems):
     fetch_piece(rows_ref, weights, w_qkv, 0, QUERY_COLS, ROW_BLOCKS, QUERY_COLS, 0, sems.at[0])
     fetch_piece(rows_ref, weights, w_qkv, KEY_BASE, PAIR_COLS, ROW_BLOCKS, PAIR_COLS, QUERY_COLS, sems.at[0])
@@ -141,35 +153,52 @@
 
 def attention_forward(
     rows_ref,
-    x_ref,
     gain_ref,
     bias_ref,
+    x_hbm,
+    cos_hbm,
+    sin_hbm,
+    allowed_hbm,
+    weights,
+    part_low_ref,
+    part_high_ref,
+    log_ref,
+    normed_turned_out,
+    qkv_out,
+    mixed_turned_out,
+    x_ref,
     cos_ref,
     sin_ref,
     allowed_ref,
-    weights,
-    part_low_ref,
-    part_high_ref,
-    normed_turned_ref,
-    qkv_ref,
-    mixed_turned_ref,
-    log_ref,
+    normed_turned,
+    qkv,
+    mixed_turned,
     w_qkv,
     w_out,
     normed,
     mixed,
     sems,
+    load_sems,
+    store_sems,
 ):
+    loads = copies_between(
+        (x_hbm, cos_hbm, sin_hbm, allowed_hbm), (x_ref, cos_ref, sin_ref, allowed_ref), load_sems
+    )
+    stores = copies_between(
+        (normed_turned, qkv, mixed_turned), (normed_turned_out, qkv_out, mixed_turned_out), store_sems
+    )
+    start_all(loads)
     fetch_attention(rows_ref, weights, w_qkv, w_out, sems)
     length = x_ref.shape[0]
+    part = length // NARROW
 
     def norm_rows(rows):
         values = x_ref[rows, :].astype(f32)
         normed[rows, :] = (values * rms_inverse(values) * gain_ref[...]).astype(bf16)
 
+    loads[0].wait()
     row_chunks(length, ROWS, norm_rows)
-    for begin, size in spans(D, COLS):
-        normed_turned_ref[pl.ds(begin, size), :] = normed[:, pl.ds(begin, size)].T
+    wait_all(loads[1:])
     wait_bytes(w_qkv, sems.at[0])
     for begin, size in spans(QKV_WIDTH, COLS):
         products = dot_nn(normed[...], w_qkv[:, pl.ds(begin, size)]) + bias_ref[:, pl.ds(begin, size)]
@@ -177,26 +206,34 @@
             head = products[:, offset : offset + width]
             if begin + offset < QUERY_WIDTH + PAIR_COLS * BLK:
                 head = head * cos_ref[...] + pltpu.roll(head, HEAD_DIM // 2, 1) * sin_ref[...]
-            qkv_ref[:, pl.ds(begin + offset, width)] = head.astype(bf16)
-    keys = qkv_ref[:, pl.ds(QUERY_WIDTH, HEAD_DIM)]
-    values_turned = qkv_ref[:, pl.ds(QUERY_WIDTH + HEAD_DIM, HEAD_DIM)].T
+            qkv[:, pl.ds(begin + offset, width)] = head.astype(bf16)
+    for begin, size in spans(D, COLS):
+        normed_turned[pl.ds(begin, size), :] = normed[:, pl.ds(begin, size)].T
+    start_all(stores[:2])
+    values_turned = qkv[:, pl.ds(QUERY_WIDTH + HEAD_DIM, HEAD_DIM)].T
     for head in range(QUERY_COLS):
         columns = pl.ds(head * HEAD_DIM, HEAD_DIM)
-        scores = scores_turned(keys, qkv_ref[:, columns], allowed_ref[...] > 0)
-        peak = jnp.max(scores, axis=0, keepdims=True)
-        expo = jnp.exp(scores - peak)
-        total = jnp.sum(expo, axis=0, keepdims=True)
-        log_ref[pl.ds(head, 1), :] = peak + jnp.log(total)
-        probs = (expo / total).astype(bf16)
-        mixed_head = dot_nn(values_turned, probs).astype(bf16)
-        mixed_turned_ref[columns, :] = mixed_head
-        mixed[:, columns] = mixed_head.T
+        for first in range(0, length, part):
+            tokens, seen = pl.ds(first, part), first + part
+            scores = scores_turned(
+                qkv[:seen, pl.ds(QUERY_WIDTH, HEAD_DIM)], qkv[tokens, columns], allowed_ref[:seen, tokens] > 0
+            )
+            peak = jnp.max(scores, axis=0, keepdims=True)
+            expo = jnp.exp(scores - peak)
+            total = jnp.sum(expo, axis=0, keepdims=True)
+            log_ref[pl.ds(head, 1), tokens] = peak + jnp.log(total)
+            probs = (expo / total).astype(bf16)
+            mixed_head = dot_nn(values_turned[:, :seen], probs).astype(bf16)
+            mixed_turned[columns, tokens] = mixed_head
+            mixed[tokens, columns] = mixed_head.T
+    stores[2].start()
     wait_bytes(w_out, sems.at[1])
-    for part_ref, first in ((part_low_ref, 0), (part_high_ref, length // NARROW)):
+    for part_ref, first in ((part_low_ref, 0), (part_high_ref, part)):
         for begin, size in spans(D, COLS):
             part_ref[:, pl.ds(begin, size)] = dot_nn(
-                mixed[pl.ds(first, length // NARROW), :], w_out[:, pl.ds(begin, size)]
+                mixed[pl.ds(first, part), :], w_out[:, pl.ds(begin, size)]
             ).astype(bf16)
+    wait_all(stores)
 
 
 def pair_copies(rows_ref, blocks_hbm, pair, sem, column, place, outward=False):
@@ -240,50 +277,77 @@
     run(TILES - 1, (TILES - 1) % 2, LAST_BLOCKS, False)
 
 
-def active_grads(rows_ref, cot_ref, weights, out, w_down, stage, load_sems, store_sems):
-    def fetch(tile, slot, place):
-        start_all(
-            down_copies(rows_ref, weights, w_down.at[slot], load_sems.at[slot], hidden_column(tile, place), place)
-        )
-
-    for place in range(TILE_BLOCKS):
-        fetch(0, 0, place)
+def active_grads(rows_ref, cot_ref, weights, out, down_out, w_down, stage, load_sems, store_sems, down_sems):
+    ring = w_down.shape[0]
+
+    def fetch(tile):
+        slot = lax.rem(tile, ring)
+        for place in range(TILE_BLOCKS):
+            start_all(
+                down_copies(rows_ref, weights, w_down.at[slot], load_sems.at[slot], hidden_column(tile, place), place)
+            )
+
+    def store(tile):
+        return pltpu.make_async_copy(stage.at[lax.rem(tile, 2)], out.at[tile], store_sems.at[lax.rem(tile, 2)])
+
+    def store_down(tile):
+        slot = lax.rem(tile, ring)
+        return pltpu.make_async_copy(w_down.at[slot], down_out.at[tile], down_sems.at[slot])
+
+    fetch(0)
 
     def run(tile, slot, blocks, more):
-        wait_bytes(w_down.at[slot], load_sems.at[slot])
+        here = lax.rem(tile, ring)
+
+        @pl.when(tile >= ring - 1)
+        def _():
+            store_down(tile - ring + 1).wait()
+
+        if more:
+            fetch(tile + 1)
+        wait_bytes(w_down.at[here], load_sems.at[here])
+        if blocks < TILE_BLOCKS:
+            w_down[here, pl.ds(blocks * BLK, (TILE_BLOCKS - blocks) * BLK), :] = jnp.zeros(
+                ((TILE_BLOCKS - blocks) * BLK, D), bf16
+            )
+        store_down(tile).start()
 
         @pl.when(tile >= 2)
         def _():
-            wait_bytes(stage.at[slot], store_sems.at[slot])
-
-        if more:
-            for place in range(TILE_BLOCKS):
-                fetch(tile + 1, 1 - slot, place)
+            store(tile - 2).wait()
+
         for begin, size in spans(blocks * BLK, COLS):
-            stage[slot, :, pl.ds(begin, size)] = dot_nt(cot_ref[...], w_down[slot, pl.ds(begin, size), :])
-        pltpu.make_async_copy(stage.at[slot], out.at[tile], store_sems.at[slot]).start()
+            stage[slot, :, pl.ds(begin, size)] = dot_nt(cot_ref[...], w_down[here, pl.ds(begin, size), :])
+        store(tile).start()
 
     hidden_tiles(run)
     for tile in range(max(TILES - 2, 0), TILES):
-        wait_bytes(stage.at[tile % 2], store_sems.at[tile % 2])
+        store(tile).wait()
+    for tile in range(max(TILES - ring + 1, 0), TILES):
+        store_down(tile).wait()
 
 
 def hidden_grads(
     first_row,
     rows_ref,
+    gain_ref,
+    x_hbm,
+    own_hbm,
+    other_hbm,
+    active_grad,
+    weights,
+    grad_ref,
+    gain_part_ref,
+    resid_out,
+    normed_turned_out,
+    pair_grads,
+    active,
+    active_turned,
     x_ref,
     own_ref,
     other_ref,
-    gain_ref,
-    active_grad,
-    weights,
-    grad_ref,
     resid_ref,
     normed_turned_ref,
-    gain_part_ref,
-    pair_grads,
-    active,
-    active_turned,
     w_pair,
     grad_active,
     straight,
@@ -293,8 +357,15 @@
     grad_sum,
     load_sems,
     store_sems,
+    token_sems,
 ):
     length = own_ref.shape[0]
+    token_loads = copies_between(
+        (x_hbm.at[pl.ds(first_row, length)], own_hbm, other_hbm), (x_ref, own_ref, other_ref), token_sems
+    )
+    store_resid = pltpu.make_async_copy(resid_ref, resid_out, token_sems.at[3])
+    store_turned = pltpu.make_async_copy(normed_turned_ref, normed_turned_out, token_sems.at[4])
+    start_all(token_loads)
 
     def fetch(tile, slot, place):
         start_all(
@@ -316,12 +387,13 @@
     load_grad(0, 0).start()
 
     def norm_rows(rows):
-        tokens = x_ref[pl.ds(rows.start + first_row, rows.size), :]
-        values = tokens.astype(f32) + own_ref[rows, :].astype(f32) + other_ref[rows, :].astype(f32)
+        values = x_ref[rows, :].astype(f32) + own_ref[rows, :].astype(f32) + other_ref[rows, :].astype(f32)
         resid_ref[rows, :] = values
         normed[rows, :] = (values * rms_inverse(values) * gain_ref[...]).astype(bf16)
 
+    wait_all(token_loads)
     row_chunks(length, ROWS, norm_rows)
+    store_resid.start()
     grad_sum[...] = jnp.zeros_like(grad_sum)
 
     def run(tile, slot, blocks, more):
@@ -364,6 +436,7 @@
         start_all(stores(tile, slot))
 
     hidden_tiles(run)
+    store_turned.start()
     grad_ref[...] = grad_sum[...].astype(bf16)
     gain_part_ref[...] = jnp.zeros_like(gain_part_ref)
 
@@ -373,57 +446,42 @@
 
     row_chunks(length, ROWS, gain_rows)
     for tile in range(max(TILES - 2, 0), TILES):
-        for copy in stores(tile, tile % 2):
-            copy.wait()
-
-
-def hidden_weight_grads(
-    weight_rows_ref, rows_ref, half_ref, cot_ref, *refs
-):
-    parts, (weights, branch_own_ref, branch_other_ref, grads), scratch = refs[: 4 * NARROW], refs[8:12], refs[12:]
-    normed_turned, pair, straight, turned, w_down, branch_sum, pair_stage, down_stage, load_sems, store_sems, sems = scratch
+        wait_all(stores(tile, tile % 2))
+    store_resid.wait()
+    store_turned.wait()
+
+
+def hidden_weight_grads(rows_ref, cot_ref, *refs):
+    parts, grads, scratch = refs[: 3 * NARROW], refs[3 * NARROW], refs[3 * NARROW + 1 :]
+    normed_turned, pair, turned, pair_stage, down_stage, load_sems, store_sems, sems = scratch
     length = cot_ref.shape[0] // NARROW
 
     def loads(tile, slot):
         copies = []
         for part in range(NARROW):
-            pair_grads, active, active_turned = parts[part * 4 + 1 : part * 4 + 4]
+            pair_grads, active_turned = parts[part * 3 + 1 : part * 3 + 3]
             tokens = pl.ds(part * length, length)
             copies += [
-                pltpu.make_async_copy(pair_grads.at[tile], pair.at[slot, tokens], load_sems.at[slot, part * 3]),
-                pltpu.make_async_copy(active.at[tile], straight.at[slot, tokens], load_sems.at[slot, part * 3 + 1]),
+                pltpu.make_async_copy(pair_grads.at[tile], pair.at[slot, tokens], load_sems.at[slot, part * 2]),
                 pltpu.make_async_copy(
-                    active_turned.at[tile], turned.at[slot, :, tokens], load_sems.at[slot, part * 3 + 2]
+                    active_turned.at[tile], turned.at[slot, :, tokens], load_sems.at[slot, part * 2 + 1]
                 ),
             ]
         return copies
 
-    def fetch(tile, slot, place):
-        start_all(
-            down_copies(
-                weight_rows_ref, weights, w_down.at[slot], load_sems.at[slot, 3 * NARROW], hidden_column(tile, place), place
-            )
-        )
-
     def drain(slot, blocks):
         wait_bytes(pair_stage.at[slot, :, pl.ds(0, 2 * blocks * BLK)], store_sems.at[slot, 0])
         wait_bytes(down_stage.at[slot, pl.ds(0, blocks * BLK)], store_sems.at[slot, 1])
 
     turned_loads = [
-        pltpu.make_async_copy(parts[part * 4], normed_turned.at[:, pl.ds(part * length, length)], sems.at[part])
+        pltpu.make_async_copy(parts[part * 3], normed_turned.at[:, pl.ds(part * length, length)], sems.at[part])
         for part in range(NARROW)
     ]
     start_all(loads(0, 0) + turned_loads)
-    for place in range(TILE_BLOCKS):
-        fetch(0, 0, place)
-    branch_sum[...] = jnp.zeros_like(branch_sum)
-    for copy in turned_loads:
-        copy.wait()
+    wait_all(turned_loads)
 
     def run(tile, slot, blocks, more):
-        for copy in loads(tile, slot):
-            copy.wait()
-        wait_bytes(w_down.at[slot], load_sems.at[slot, 3 * NARROW])
+        wait_all(loads(tile, slot))
         if more:
             start_all(loads(tile + 1, 1 - slot))
 
@@ -449,19 +507,8 @@
             start_all(
                 pair_copies(rows_ref, grads, pair_stage.at[slot], store_sems.at[slot, 0], column, place, outward=True)
             )
-            if more:
-                fetch(tile + 1, 1 - slot, place)
-        if more:
-            for place in range(blocks, TILE_BLOCKS):
-                fetch(tile + 1, 1 - slot, place)
-        for begin, size in spans(D, COLS):
-            columns = pl.ds(begin, size)
-            branch_sum[:, columns] += dot_nn(straight[slot, :, :width], w_down[slot, :width, columns])
 
     hidden_tiles(run)
-    own, other = half_rows(half_ref, length)
-    branch_own_ref[...] = branch_sum[own, :].astype(bf16)
-    branch_other_ref[...] = branch_sum[other, :].astype(bf16)
     if TILES > 1:
         drain((TILES - 2) % 2, TILE_BLOCKS)
     drain((TILES - 1) % 2, LAST_BLOCKS)
@@ -471,7 +518,30 @@
     weight_rows_ref,
     rows_ref,
     half_ref,
-    x_ref,
+    gain_ref,
+    log_ref,
+    gain_two_low_ref,
+    gain_two_high_ref,
+    resid_low_hbm,
+    own_low_hbm,
+    other_low_hbm,
+    resid_high_hbm,
+    own_high_hbm,
+    other_high_hbm,
+    cot_hbm,
+    qkv_hbm,
+    cos_hbm,
+    sin_hbm,
+    allowed_hbm,
+    mixed_turned_hbm,
+    normed_turned_hbm,
+    x_hbm,
+    weights,
+    grads_in,
+    grad_resid_ref,
+    grad_own_ref,
+    grad_other_ref,
+    grads,
     resid_low_ref,
     own_low_ref,
     other_low_ref,
@@ -479,22 +549,13 @@
     own_high_ref,
     other_high_ref,
     cot_ref,
-    gain_ref,
+    qkv_ref,
     cos_ref,
     sin_ref,
     allowed_ref,
+    mixed_turned_ref,
     normed_turned_ref,
-    qkv_ref,
-    mixed_turned_ref,
-    log_ref,
-    gain_two_low_ref,
-    gain_two_high_ref,
-    weights,
-    grads_in,
-    grad_resid_ref,
-    grad_own_ref,
-    grad_other_ref,
-    grads,
+    x_ref,
     w_qkv,
     w_out,
     grad_resid,
@@ -502,6 +563,8 @@
     grad_mixed,
     grad_qkv,
     grad_sum,
+    grad_keys,
+    grad_values,
     gain_part,
     bias_part,
     qkv_stage,
@@ -510,12 +573,26 @@
     blank,
     load_sems,
     store_sems,
+    token_sems,
 ):
     del grads_in
+    loads = copies_between(
+        (
+            cot_hbm, resid_low_hbm, own_low_hbm, other_low_hbm, resid_high_hbm, own_high_hbm, other_high_hbm, qkv_hbm,
+            cos_hbm, sin_hbm, allowed_hbm, mixed_turned_hbm, normed_turned_hbm, x_hbm,
+        ),
+        (
+            cot_ref, resid_low_ref, own_low_ref, other_low_ref, resid_high_ref, own_high_ref, other_high_ref, qkv_ref,
+            cos_ref, sin_ref, allowed_ref, mixed_turned_ref, normed_turned_ref, x_ref,
+        ),
+        token_sems,
+    )
+    start_all(loads[:7])
     wide_count = small_stage.shape[0]
     owner_rows = grads.shape[0] // wide_count
     small_stage[...] = jnp.zeros_like(small_stage)
     fetch_attention(weight_rows_ref, weights, w_qkv, w_out, load_sems)
+    start_all(loads[7:])
     length = x_ref.shape[0]
     empty_count = rows_ref.shape[0] - BLOCK_TOTAL
     blank[...] = jnp.zeros_like(blank)
@@ -524,10 +601,11 @@
 
     part = length // NARROW
     own_rows, other_rows = half_rows(half_ref, part)
-    for first, resid_ref, own_ref, other_ref in (
-        (0, resid_low_ref, own_low_ref, other_low_ref),
-        (part, resid_high_ref, own_high_ref, other_high_ref),
+    for first, resid_ref, own_ref, other_ref, needed in (
+        (0, resid_low_ref, own_low_ref, other_low_ref, loads[:4]),
+        (part, resid_high_ref, own_high_ref, other_high_ref, loads[4:7]),
     ):
+        wait_all(needed)
 
         def resid_rows(rows, first=first, resid_ref=resid_ref, own_ref=own_ref, other_ref=other_ref):
             values = resid_ref[rows, :]
@@ -546,29 +624,35 @@
     wait_bytes(w_out, load_sems.at[1])
     for begin, size in spans(QUERY_WIDTH, COLS):
         grad_mixed[:, pl.ds(begin, size)] = dot_nt(grad_attention[...], w_out[pl.ds(begin, size), :]).astype(bf16)
-    keys = qkv_ref[:, pl.ds(QUERY_WIDTH, HEAD_DIM)]
-    keys_turned = keys.T
-    values = qkv_ref[:, pl.ds(QUERY_WIDTH + HEAD_DIM, HEAD_DIM)]
+    wait_all(loads[7:11])
+    keys_turned = qkv_ref[:, pl.ds(QUERY_WIDTH, HEAD_DIM)].T
 
     def rope_back(vector):
         return vector * cos_ref[...] - pltpu.roll(vector, HEAD_DIM // 2, 1) * sin_ref[...]
 
-    grad_keys = jnp.zeros((length, HEAD_DIM), f32)
-    grad_values = jnp.zeros((length, HEAD_DIM), f32)
+    grad_keys[...] = jnp.zeros_like(grad_keys)
+    grad_values[...] = jnp.zeros_like(grad_values)
     for head in range(QUERY_COLS):
         columns = pl.ds(head * HEAD_DIM, HEAD_DIM)
-        queries = qkv_ref[:, columns]
-        scores = scores_turned(keys, queries, allowed_ref[...] > 0)
-        probs = jnp.exp(scores - log_ref[pl.ds(head, 1), :])
-        grad_values += dot_nn(probs.astype(bf16), grad_mixed[:, columns])
-        grad_probs = dot_nt(values, grad_mixed[:, columns])
-        row_dot = jnp.sum(probs * grad_probs, axis=0, keepdims=True)
-        grad_scores = (probs * (grad_probs - row_dot)).astype(bf16)
-        grad_keys += dot_nn(grad_scores, queries)
-        grad_queries = dot_nn(keys_turned, grad_scores).T * scaling
-        grad_qkv[:, columns] = rope_back(grad_queries).astype(bf16)
-    grad_qkv[:, pl.ds(QUERY_WIDTH, HEAD_DIM)] = rope_back(grad_keys * scaling).astype(bf16)
-    grad_qkv[:, pl.ds(QUERY_WIDTH + HEAD_DIM, HEAD_DIM)] = grad_values.astype(bf16)
+        grad_queries = []
+        for first in range(0, length, part):
+            tokens, seen = pl.ds(first, part), first + part
+            queries = qkv_ref[tokens, columns]
+            grad_mixed_here = grad_mixed[tokens, columns]
+            scores = scores_turned(
+                qkv_ref[:seen, pl.ds(QUERY_WIDTH, HEAD_DIM)], queries, allowed_ref[:seen, tokens] > 0
+            )
+            probs = jnp.exp(scores - log_ref[pl.ds(head, 1), tokens])
+            grad_values[:seen, :] += dot_nn(probs.astype(bf16), grad_mixed_here)
+            grad_probs = dot_nt(qkv_ref[:seen, pl.ds(QUERY_WIDTH + HEAD_DIM, HEAD_DIM)], grad_mixed_here)
+            row_dot = jnp.sum(probs * grad_probs, axis=0, keepdims=True)
+            grad_scores = (probs * (grad_probs - row_dot)).astype(bf16)
+            grad_keys[:seen, :] += dot_nn(grad_scores, queries)
+            grad_queries.append(dot_nn(keys_turned[:, :seen], grad_scores).T * scaling)
+        grad_qkv[:, columns] = rope_back(jnp.concatenate(grad_queries, axis=0)).astype(bf16)
+    grad_qkv[:, pl.ds(QUERY_WIDTH, HEAD_DIM)] = rope_back(grad_keys[...] * scaling).astype(bf16)
+    grad_qkv[:, pl.ds(QUERY_WIDTH + HEAD_DIM, HEAD_DIM)] = grad_values[...].astype(bf16)
+    wait_all(loads[11:])
 
     for begin, size in spans(D, COLS):
         out_stage[:, pl.ds(begin, size)] = dot_nn(
@@ -714,28 +798,32 @@
 def run_attention_forward(rows, x, gain, bias, cosine, sine, allowed, weights):
     length = x.shape[0]
     shape = jax.ShapeDtypeStruct
-    return pl.pallas_call(
+    kept = [((D, length), bf16), ((length, QKV_WIDTH), bf16), ((QUERY_WIDTH, length), bf16)]
+    low, high, log_total, *kept_arrays = pl.pallas_call(
         attention_forward,
         out_shape=[
             shape((length // NARROW, D), bf16),
             shape((length // NARROW, D), bf16),
-            shape((D, length), bf16),
-            shape((length, QKV_WIDTH), bf16),
-            shape((QUERY_WIDTH, length), bf16),
             shape((8, length), f32),
-        ],
-        in_specs=[SMEM_SPEC] + [VMEM_SPEC] * 6 + [ANY_SPEC],
-        out_specs=[VMEM_SPEC] * 6,
-        scratch_shapes=[
+        ]
+        + [shape(*one) for one in kept],
+        in_specs=[SMEM_SPEC] + [VMEM_SPEC] * 2 + [ANY_SPEC] * 5,
+        out_specs=[VMEM_SPEC] * 3 + [ANY_SPEC] * 3,
+        scratch_shapes=[pltpu.VMEM(array.shape, array.dtype) for array in (x, cosine, sine, allowed)]
+        + [pltpu.VMEM(*one) for one in kept]
+        + [
             pltpu.VMEM((D, QKV_WIDTH), bf16),
             pltpu.VMEM((QUERY_WIDTH, D), bf16),
             pltpu.VMEM((length, D), bf16),
             pltpu.VMEM((length, QUERY_WIDTH), bf16),
             pltpu.SemaphoreType.DMA((2,)),
+            pltpu.SemaphoreType.DMA((4,)),
+            pltpu.SemaphoreType.DMA((3,)),
         ],
         compiler_params=params(),
         name="attention_forward",
-    )(rows, x, gain, bias, cosine, sine, allowed, weights)
+    )(rows, gain, bias, x, cosine, sine, allowed, weights)
+    return (low, high, *kept_arrays, log_total)
 
 
 def hidden_cost(length, products, bytes_moved):
@@ -748,14 +836,18 @@
     length = cotangent.shape[0]
     return pl.pallas_call(
         active_grads,
-        out_shape=jax.ShapeDtypeStruct((TILES, length, TILE), f32),
+        out_shape=[
+            jax.ShapeDtypeStruct((TILES, length, TILE), f32),
+            jax.ShapeDtypeStruct((TILES, TILE, D), bf16),
+        ],
         in_specs=[SMEM_SPEC, VMEM_SPEC, ANY_SPEC],
-        out_specs=ANY_SPEC,
+        out_specs=[ANY_SPEC] * 2,
         scratch_shapes=[
-            pltpu.VMEM((2, TILE, D), bf16),
+            pltpu.VMEM((4, TILE, D), bf16),
             pltpu.VMEM((2, length, TILE), f32),
+            pltpu.SemaphoreType.DMA((4,)),
             pltpu.SemaphoreType.DMA((2,)),
-            pltpu.SemaphoreType.DMA((2,)),
+            pltpu.SemaphoreType.DMA((4,)),
         ],
         compiler_params=params(),
         cost_estimate=hidden_cost(length, 1, TILES * TILE * (2 * D + 4 * length)),
@@ -766,20 +858,25 @@
 def run_hidden_grads(first_row, rows, x, own, other, gain, active_grad, weights):
     length = own.shape[0]
     shape = jax.ShapeDtypeStruct
-    return pl.pallas_call(
+    grad, gain_part, *kept = pl.pallas_call(
         functools.partial(hidden_grads, first_row),
         out_shape=[
             shape((length, D), bf16),
+            shape((1, D), f32),
             shape((length, D), f32),
             shape((D, length), bf16),
-            shape((1, D), f32),
             shape((TILES, length, 2 * TILE), bf16),
             shape((TILES, length, TILE), bf16),
             shape((TILES, TILE, length), bf16),
         ],
-        in_specs=[SMEM_SPEC] + [VMEM_SPEC] * 4 + [ANY_SPEC] * 2,
-        out_specs=[VMEM_SPEC] * 4 + [ANY_SPEC] * 3,
+        in_specs=[SMEM_SPEC, VMEM_SPEC] + [ANY_SPEC] * 5,
+        out_specs=[VMEM_SPEC] * 2 + [ANY_SPEC] * 5,
         scratch_shapes=[
+            pltpu.VMEM((length, D), bf16),
+            pltpu.VMEM((length, D), bf16),
+            pltpu.VMEM((length, D), bf16),
+            pltpu.VMEM((length, D), f32),
+            pltpu.VMEM((D, length), bf16),
             pltpu.VMEM((2, D, 2 * TILE), bf16),
             pltpu.VMEM((2, length, TILE), f32),
             pltpu.VMEM((2, length, TILE), bf16),
@@ -789,38 +886,37 @@
             pltpu.VMEM((length, D), f32),
             pltpu.SemaphoreType.DMA((2, 2)),
             pltpu.SemaphoreType.DMA((2, 3)),
+            pltpu.SemaphoreType.DMA((5,)),
         ],
         compiler_params=params(),
         cost_estimate=hidden_cost(length, 4, 2 * TILES * TILE * (2 * D + 6 * length)),
         name="hidden_grads",
-    )(rows, x, own, other, gain, active_grad, weights)
-
-
-def run_hidden_weight_grads(weight_rows, rows, half, cotangent, parts, weights, slots):
+    )(rows, gain, x, own, other, active_grad, weights)
+    resid, normed_turned, *hidden = kept
+    return (grad, resid, normed_turned, gain_part, *hidden)
+
+
+def run_hidden_weight_grads(rows, cotangent, parts, slots):
     length = cotangent.shape[0]
-    shape = jax.ShapeDtypeStruct
     return pl.pallas_call(
         hidden_weight_grads,
-        out_shape=[shape((length // NARROW, D), bf16)] * 2 + [shape((slots, BLK, BLK), bf16)],
-        in_specs=[SMEM_SPEC] * 3 + [VMEM_SPEC] + [ANY_SPEC] * (4 * NARROW + 1),
-        out_specs=[VMEM_SPEC, VMEM_SPEC, ANY_SPEC],
+        out_shape=jax.ShapeDtypeStruct((slots, BLK, BLK), bf16),
+        in_specs=[SMEM_SPEC, VMEM_SPEC] + [ANY_SPEC] * (3 * NARROW),
+        out_specs=ANY_SPEC,
         scratch_shapes=[
             pltpu.VMEM((D, length), bf16),
             pltpu.VMEM((2, length, 2 * TILE), bf16),
-            pltpu.VMEM((2, length, TILE), bf16),
             pltpu.VMEM((2, TILE, length), bf16),
-            pltpu.VMEM((2, TILE, D), bf16),
-            pltpu.VMEM((length, D), f32),
             pltpu.VMEM((2, D, 2 * TILE), bf16),
             pltpu.VMEM((2, TILE, D), bf16),
-            pltpu.SemaphoreType.DMA((2, 3 * NARROW + 1)),
+            pltpu.SemaphoreType.DMA((2, 2 * NARROW)),
             pltpu.SemaphoreType.DMA((2, 2)),
             pltpu.SemaphoreType.DMA((NARROW,)),
         ],
         compiler_params=params(),
-        cost_estimate=hidden_cost(length, 4, 2 * TILES * TILE * (4 * D + 4 * length)),
+        cost_estimate=hidden_cost(length, 3, 2 * TILES * TILE * 3 * (D + length)),
         name="hidden_weight_grads",
-    )(weight_rows, rows, half, cotangent, *[array for part in parts for array in part], weights)
+    )(rows, cotangent, *[array for part in parts for array in part])
 
 
 def run_attention_backward(
@@ -830,10 +926,8 @@
     length = x.shape[0]
     shape = jax.ShapeDtypeStruct
     empty_count = max(rows.shape[0] - BLOCK_TOTAL, 1)
-    operands = (
-        weight_rows, rows, half, x, *low, *high, cotangent, gains, cosine, sine, allowed, normed_turned, qkv, mixed_turned,
-        log_total, *gain_two_parts, weights, grads,
-    )
+    loaded = (*low, *high, cotangent, qkv, cosine, sine, allowed, mixed_turned, normed_turned, x)
+    operands = (weight_rows, rows, half, gains, log_total, *gain_two_parts, *loaded, weights, grads)
     return pl.pallas_call(
         attention_backward,
         out_shape=[
@@ -842,10 +936,11 @@
             shape((length // NARROW, D), bf16),
             shape(grads.shape, bf16),
         ],
-        in_specs=[SMEM_SPEC] * 3 + [VMEM_SPEC] * (len(operands) - 5) + [ANY_SPEC] * 2,
+        in_specs=[SMEM_SPEC] * 3 + [VMEM_SPEC] * 4 + [ANY_SPEC] * (len(loaded) + 2),
         out_specs=[VMEM_SPEC] * 3 + [ANY_SPEC],
         input_output_aliases={len(operands) - 1: 3},
-        scratch_shapes=[
+        scratch_shapes=[pltpu.VMEM(array.shape, array.dtype) for array in loaded]
+        + [
             pltpu.VMEM((D, QKV_WIDTH), bf16),
             pltpu.VMEM((QUERY_WIDTH, D), bf16),
             pltpu.VMEM((length, D), f32),
@@ -853,6 +948,8 @@
             pltpu.VMEM((length, QUERY_WIDTH), bf16),
             pltpu.VMEM((length, QKV_WIDTH), bf16),
             pltpu.VMEM((length, D), f32),
+            pltpu.VMEM((length, HEAD_DIM), f32),
+            pltpu.VMEM((length, HEAD_DIM), f32),
             pltpu.VMEM((1, D), f32),
             pltpu.VMEM((1, QKV_WIDTH), f32),
             pltpu.VMEM((D, QKV_WIDTH), bf16),
@@ -861,6 +958,7 @@
             pltpu.VMEM((empty_count, BLK, BLK), bf16),
             pltpu.SemaphoreType.DMA((2,)),
             pltpu.SemaphoreType.DMA((4,)),
+            pltpu.SemaphoreType.DMA((len(loaded),)),
         ],
         compiler_params=params(),
         name="attention_backward",
@@ -889,15 +987,15 @@
 def sum_for_owners(
     line, steps, late_steps,
     grads, masters, first_moment, second_moment, left_basis, right_basis,
-    grad_resid, grad_own, grad_sent, tokens, gain, resid, branch_own, branch_other,
+    grad_resid, grad_own, grad_sent, tokens, gain, resid, active_low, active_high, down,
     out, new_masters, new_first, new_second, input_grad, output, small_own, small_other,
     a_in, a_own, a_sum, a_keep, a_send, a_cross, a_up, a_down,
     b_in, b_own, b_sum, b_keep, b_send, b_cross, b_up, b_down,
     a_params, b_params, grad_resid_here, grad_own_here, grad_other_here, tokens_here, gain_here, resid_here,
-    branch_own_here, branch_other_here,
+    active_here, down_here, branch_sum, branch_sent, branch_other,
     core_send, core_recv, own_sems, cross_send, cross_recv, up_send, up_recv, down_send, down_recv,
     b_core_send, b_core_recv, b_own_sems, b_cross_send, b_cross_recv, b_up_send, b_up_recv, b_down_send, b_down_recv,
-    a_param_sems, b_param_sems, token_sems, swap_send, swap_recv, credits,
+    a_param_sems, b_param_sems, token_sems, branch_sems, swap_send, swap_recv, credits,
 ):
     wide = lax.axis_index("wide")
     narrow = lax.axis_index("narrow")
@@ -1032,26 +1130,61 @@
     token_loads = [
         pltpu.make_async_copy(source, target, token_sems.at[index])
         for index, (source, target) in enumerate((
-            (resid, resid_here), (branch_own, branch_own_here), (branch_other, branch_other_here),
-            (grad_resid, grad_resid_here), (grad_own, grad_own_here), (tokens, tokens_here), (gain, gain_here),
+            (resid, resid_here), (grad_resid, grad_resid_here), (grad_own, grad_own_here), (tokens, tokens_here), (gain, gain_here),
         ))
     ]
     grad_swap = remote(grad_sent, grad_other_here, swap_send.at[0], swap_recv.at[0], swap_peer)
     small_swap = remote(small_own, small_other, swap_send.at[1], swap_recv.at[1], swap_peer)
 
+    branch_swap = remote(branch_sent, branch_other, swap_send.at[2], swap_recv.at[2], swap_peer)
+
+    def branch_load(index):
+        tile = lax.rem(index, TILES)
+        takes_low = narrow == jnp.where(index < TILES, 1, 0)
+
+        @pl.when(takes_low)
+        def _():
+            pltpu.make_async_copy(active_low.at[tile], active_here, branch_sems.at[0]).start()
+
+        @pl.when(jnp.logical_not(takes_low))
+        def _():
+            pltpu.make_async_copy(active_high.at[tile], active_here, branch_sems.at[0]).start()
+
+        pltpu.make_async_copy(down.at[tile], down_here, branch_sems.at[1]).start()
+
+    def branch_step(index):
+        pltpu.make_async_copy(active_low.at[0], active_here, branch_sems.at[0]).wait()
+        pltpu.make_async_copy(down.at[0], down_here, branch_sems.at[1]).wait()
+
+        @pl.when(lax.rem(index, TILES) == 0)
+        def _():
+            branch_sum[...] = jnp.zeros_like(branch_sum)
+
+        for begin, size in spans(D, COLS):
+            columns = pl.ds(begin, size)
+            branch_sum[:, columns] += dot_nn(active_here[...], down_here[:, columns])
+
+        @pl.when(index < 2 * TILES - 1)
+        def _():
+            branch_load(index + 1)
+
+        @pl.when(index == TILES - 1)
+        def _():
+            branch_sent[...] = branch_sum[...].astype(bf16)
+            branch_swap.start()
+
     def finish_output():
-        for copy in token_loads[:3]:
-            copy.wait()
+        token_loads[0].wait()
+        branch_swap.wait()
 
         def rows_of_output(rows):
-            total = resid_here[rows, :] + branch_own_here[rows, :].astype(f32) + branch_other_here[rows, :].astype(f32)
+            total = resid_here[rows, :] + branch_sum[rows, :] + branch_other[rows, :].astype(f32)
             output[rows, :] = total.astype(bf16)
 
         row_chunks(output.shape[0], ROWS, rows_of_output)
 
     def finish_input_grad():
-        for copy in token_loads[3:]:
-            copy.wait()
+        wait_all(token_loads[1:])
         grad_swap.wait()
 
         def rows_of_grad(rows):
@@ -1070,6 +1203,7 @@
         feed(early, late_steps, 1, b_core_copy, b_own_copy)
 
     start_all(param_loads(0) + param_loads(1) + b_param_loads(1) + b_param_loads(2) + token_loads)
+    branch_load(0)
 
     def active(step, count):
         return (step >= 0) & (step < count)
@@ -1282,12 +1416,16 @@
                 def _():
                     start_all(b_param_loads(paired + 2))
 
-        pl.when(step == 4)(finish_output)
-        pl.when(step == 8)(finish_input_grad)
+        @pl.when((step >= 1) & (step < 2 * TILES + 1))
+        def _():
+            branch_step(step - 1)
+
+        pl.when(step == 2 * TILES + 1)(finish_output)
+        pl.when(step == 4)(finish_input_grad)
         return 0
 
     lag = HOP_LAG * (line - 1) + CROSS_LAG
-    lax.fori_loop(0, max(steps, late_steps) + lag + 2, iteration, 0)
+    lax.fori_loop(0, max(max(steps, late_steps) + lag, 2 * TILES) + 2, iteration, 0)
     for step in range(max(steps - DEPTH, 0), steps):
         cross_copy(step).wait_send()
     for step in range(max(late_steps - DEPTH, 0), late_steps):
@@ -1339,10 +1477,17 @@
             wide_vmem(2, len(blocks), EARLY),
             wide_vmem(2, len(blocks)),
         ]
-        + [pltpu.VMEM(array.shape, array.dtype) for array in token_arrays]
+        + [pltpu.VMEM(array.shape, array.dtype) for array in token_arrays[:6]]
+        + [
+            pltpu.VMEM(token_arrays[6].shape[1:], bf16),
+            pltpu.VMEM(token_arrays[8].shape[1:], bf16),
+            pltpu.VMEM(token_arrays[0].shape, f32),
+            pltpu.VMEM(token_arrays[0].shape, bf16),
+            pltpu.VMEM(token_arrays[0].shape, bf16),
+        ]
         + ([dma((DEPTH,))] * 5 + [dma((hop_depth, line))] * 4) * 2
         + [dma((2, len(blocks)))] * 2
-        + [dma((len(token_arrays) - 1,)), dma((2,)), dma((2,)), pltpu.SemaphoreType.REGULAR((8,))],
+        + [dma((5,)), dma((2,)), dma((3,)), dma((3,)), pltpu.SemaphoreType.REGULAR((8,))],
         compiler_params=params(SUM_VMEM, collective_id=0, has_side_effects=True),
         cost_estimate=pl.CostEstimate(flops=0, bytes_accessed=2 * grads.size * 8, transcendentals=0),
         name="sum_for_owners",
@@ -1503,7 +1648,7 @@
         weight_rows, tokens_row, gain_full[0:1], bias_full, cosine, sine, allowed_turned, weights
     )
     low_other = swap_halves(low_part)
-    active_grad = run_active_grads(weight_rows, cotangent_row, weights)
+    active_grad, down_tiles = run_active_grads(weight_rows, cotangent_row, weights)
     high_sent, low_other = lax.optimization_barrier((high_part, low_other))
     high_other = swap_halves(high_sent)
     gain_two = gain_full[1:2]
@@ -1515,11 +1660,12 @@
         tokens_here, weight_rows, tokens_row, high_part, high_other, gain_two, active_grad, weights
     )
     grad_high_other = swap_halves(grad_high)
-    branch_own, branch_sent, grads = run_hidden_weight_grads(
-        weight_rows, rows, half_index, cotangent_row, [(turned_low, *hidden_low), (turned_high, *hidden_high)], weights,
+    pair_low, active_low, active_turned_low = hidden_low
+    pair_high, active_high, active_turned_high = hidden_high
+    grads = run_hidden_weight_grads(
+        rows, cotangent_row, [(turned_low, pair_low, active_turned_low), (turned_high, pair_high, active_turned_high)],
         wide_count * (slots_here + 1),
     )
-    branch_other = swap_halves(branch_sent)
     grad_resid, grad_one_own, grad_one_sent, grads = run_attention_backward(
         weight_rows, rows, half_index, tokens_row, (resid_low, grad_low, grad_low_other),
         (resid_high, grad_high, grad_high_other), cotangent_row, gain_full, cosine, sine, allowed_turned,
@@ -1529,7 +1675,7 @@
     blocks = [masters, first_moment, second_moment, left_basis, right_basis]
     if wide_count == 16:
         token_arrays = [
-            grad_resid, grad_one_own, grad_one_sent, tokens, gain_full[0:1], resid_own, branch_own, branch_other
+            grad_resid, grad_one_own, grad_one_sent, tokens, gain_full[0:1], resid_own, active_low, active_high, down_tiles
         ]
         block_grad, new_masters, new_first, new_second, input_grad, output, small_sums = run_write_results(
             *run_sum_for_owners(grads, wide_count, blocks, token_arrays)
@@ -1541,7 +1687,13 @@
         block_grad, new_masters, new_first, new_second, small_sums = run_soap(reduced, *blocks)
         gain_parts = small_sums[:2] + swap_halves(small_sums[:2])
         bias_row = small_sums[2]
-        output = (resid_own + branch_own.astype(f32) + branch_other.astype(f32)).astype(bf16)
+        branch_low, branch_high = [
+            jnp.einsum("tik,tkd->id", active, down_tiles, preferred_element_type=f32)
+            for active in (active_low, active_high)
+        ]
+        branch_own = jnp.where(half == 0, branch_low, branch_high)
+        branch_sent = jnp.where(half == 0, branch_high, branch_low).astype(bf16)
+        output = (resid_own + branch_own + swap_halves(branch_sent).astype(f32)).astype(bf16)
         inverse_one, normed_one = rms_parts(tokens.astype(f32))
         grad_one = grad_one_own.astype(f32) + swap_halves(grad_one_sent).astype(f32)
         input_grad = grad_resid + norm_back(grad_one * gain_full[0:1], normed_one, inverse_one)

time: 683 us -> 669 us (0.980)
  Pallas kernels: 404 us -> 395 us
    pallas_call x2, Pallas kernels: 53.9 us -> 45.6 us  [the longest x1 28.6 us: run_hidden_weight_grads(): pl.pallas_call(hidden_weight_grads, out_shape=jax.ShapeDtypeStruct((slots...]
  transfers between devices with their start and end apart: 8 -> 7, of which waited for: 2 -> 2; matrix products, arithmetic and copies ran while one was open for 3% -> 3% of each run, Pallas kernels for 19% -> 14%
where the time goes in v6:
time: 669 us; the launch traced here: 663 us
  Pallas kernels  395 us (59%)
  waiting for transfers between devices  115 us (17%)
  blocking collectives  98 us (15%)
  other arithmetic  18.6 us (3%)
  between operations  15.2 us (2%)
  local copies, waits for them, and re-layouts  12.8 us (2%)
  starting transfers between devices  8.33 us (1%)
    pallas_call x1, Pallas kernels, run_sum_for_owners(): pl.pallas_call(functools.partial(sum_for_owners, line, steps, late_steps)...  255 us
    all_gather x1, waiting for transfers between devices, body(): weights = lax.all_gather(masters_low, 'wide', axis=0, tiled=True)  114 us
    unnamed x2, blocking collectives  98 us
    pallas_call x2, Pallas kernels, run_hidden_grads(): pl.pallas_call(functools.partial(hidden_grads, first_row), out_shape=[sha...  48.4 us
    pallas_call x1, Pallas kernels, run_hidden_weight_grads(): pl.pallas_call(hidden_weight_grads, out_shape=jax.ShapeDtypeStruct((slots...  28.6 us
    pallas_call x1, Pallas kernels, run_attention_backward(): pl.pallas_call(attention_backward, out_shape=[shape((length // NARROW, D)...  23.6 us
    pallas_call x1, Pallas kernels, run_active_grads(): pl.pallas_call(active_grads, out_shape=[jax.ShapeDtypeStruct((TILES, leng...  17 us
  transfers between devices with their start and end apart: 7, of which 2 were waited for; matrix products, arithmetic and copies ran while one was open for 3% of the time, Pallas kernels for 14%

profile of v6, /device:TPU:0, one launch (start us, length us, event | category | flops | bytes accessed | tf_op | source)
XLA Modules:
  0.0 662.5 jit_solution(7558829791991140423)
XLA Ops:
  7.2 0.0 copy-start.2
  7.2 0.0 copy-start.7
  7.2 0.0 all-gather.3.cloned.1.call-start
  7.2 5.0 convert_element_type.21
  12.3 0.0 all-gather.3.cloned.1.call-update
  12.3 3.0 collective-permute-start
  15.3 0.0 copy-done.7
  15.3 0.1 collective-permute-start.1
  15.4 0.9 compare_reduce_fusion
  16.3 0.1 add_select_fusion.1
  16.4 0.3 reduce-window.24
  16.7 0.1 slice.47
  16.8 0.3 reduce-window.16
  17.1 0.1 slice.53
  17.2 0.1 slice_reduce_fusion.1
  17.4 0.1 slice_reduce_fusion
  17.5 0.1 fusion.8
  17.6 0.1 add_bitcast_fusion
  17.6 1.0 fusion.2
  18.7 0.3 dynamic-update-slice
  19.0 66.8 %all-reduce.1 = f32[3072]{0:T(1024)S(1)} all-reduce(f32[3072]{0:T(1024)S(1)} %dynamic-update-slice), channel_id=1, replica_groups=mesh['wide'=16,'narrow'=2] {'wide','narrow'}, use_global_device_ids=true, to_apply=%add.1 | all-reduce | flops 3072 | bytes 24576
  85.8 0.6 dynamic-slice.1
  87.0 0.2 dynamic-update-slice.1
  87.3 31.2 %all-reduce.2 = bf16[1024]{0:T(1024)(128)(2,1)S(1)} all-reduce(bf16[1024]{0:T(1024)(128)(2,1)S(1)} %dynamic-update-slice.1), channel_id=2, replica_groups=mesh['wide'=16,'narrow'=2] {'wide'}, use_global_device_ids=true, to_apply=%add.2 | all-reduce | flops 1024 | bytes 4096
  118.5 0.6 reshape.168
  119.1 8.2 %scatter_custom_fusion.rows_ref.weight_rows_ref = s32[1440]{0:T(1024)} fusion(s32[1440]{0:T(1024)S(1)} %compare_select_fusion, s32[1440]{0:T(1024)S(1)} %iota.33, s32[]{:T(128)} %constant.33.clone.1), kind=kCustom, calls=%fused_computation.25 | custom fusion | bytes 5764 | tf_op jit(solution)/shard_map/scatter | solution.py:1631
  127.2 0.7 constant_dynamic-slice_fusion.1
  128.0 1.0 pad_maximum_fusion
  129.0 1.1 fusion.1.allowed_hbm
  130.1 0.0 collective-permute-done
  130.1 3.0 maximum_select_fusion.x_hbm
  133.1 0.0 collective-permute-done.1
  133.1 1.8 maximum_select_fusion.1.cot_ref.cot_hbm
  134.9 114.0 %all-gather.3.cloned.1.call-done.weights = bf16[1440,128,128]{2,1,0:T(8,128)(2,1)} async-done(((bf16[90,128,128]{2,1,0:T(8,128)(2,1)}), bf16[1440,128,128]{2,1,0:T(8,128)(2,1)}) %all-gather.3.cloned.1.call-update) | async-done | bytes 47185936 | tf_op jit(solution)/shard_map/all_gather | solution.py:1622
  249.0 0.0 copy-done.9
  249.0 0.6 fusion.15
  249.6 11.9 %attention_forward.1 = (bf16[256,1536]{1,0:T(8,128)(2,1)}, bf16[256,1536]{1,0:T(8,128)(2,1)}, f32[8,512]{1,0:T(8,128)}, bf16[1536,512]{1,0:T(8,128)(2,1)}, bf16[...) custom-call(s32[1440]{0:T(1024)} %scatter_custom_fusion.rows_ref.weight_rows_ref, ...), custom_call_target="tpu_custom_call" | custom-call | tf_op jit(solution)/shard_map/attention_forward/pallas_call | solution.py:802
  261.5 1.5 collective-permute-start.2
  263.1 0.6 fusion.3.rows_ref
  263.7 17.0 %active_grads.1 = (f32[6,512,768]{2,1,0:T(8,128)}, bf16[6,768,1536]{2,1,0:T(8,128)(2,1)}) custom-call(s32[1440]{0:T(1024)} %scatter_custom_fusion.rows_ref.weight_rows_ref, bf16[512,1536]{1,0:T(8,128)(2,1)} %maximum_select_fusion.1.cot_ref.cot_hbm, bf16[1440,128,128]{2,1,0:T(8,128)(2,1)} %all-gather.3.cloned.1.call-done.weights), custom_call_target="tpu_custom_call" | custom-call | flops 7247757312 | bytes 23592960 | tf_op jit(solution)/shard_map/active_grads/pallas_call | solution.py:837
  280.7 0.8 collective-permute-done.2.other_hbm
  281.5 1.5 collective-permute-start.3
  283.0 24.2 %hidden_grads.2 = (bf16[256,1536]{1,0:T(8,128)(2,1)}, f32[1,1536]{1,0:T(1,128)}, f32[256,1536]{1,0:T(8,128)}, bf16[1536,256]{1,0:T(8,128)(2,1)}, bf16[6,256,1536...) custom-call(s32[1440]{0:T(1024)} %scatter_custom_fusion.rows_ref.weight_rows_ref, ...), custom_call_target="tpu_custom_call" | custom-call | flops 14495514624 | bytes 42467328 | tf_op jit(solution)/shard_map/hidden_grads/pallas_call | solution.py:861
  307.2 0.9 collective-permute-start.4
  308.2 0.0 collective-permute-done.3.other_hbm
  308.2 0.9 copy-done.6
  309.1 24.2 %hidden_grads.3 = (bf16[256,1536]{1,0:T(8,128)(2,1)}, f32[1,1536]{1,0:T(1,128)}, f32[256,1536]{1,0:T(8,128)}, bf16[1536,256]{1,0:T(8,128)(2,1)}, bf16[6,256,1536...) custom-call(s32[1440]{0:T(1024)} %scatter_custom_fusion.rows_ref.weight_rows_ref, ...), custom_call_target="tpu_custom_call" | custom-call | flops 14495514624 | bytes 42467328 | tf_op jit(solution)/shard_map/hidden_grads/pallas_call | solution.py:861
  333.3 1.2 collective-permute-start.5
  334.5 28.6 %hidden_weight_grads.1.grads_in = bf16[1456,128,128]{2,1,0:T(8,128)(2,1)} custom-call(s32[1440]{0:T(1024)} %fusion.3.rows_ref, bf16[512,1536]{1,0:T(8,128)(2,1)} %maximum_select_fusion.1.cot_ref.cot_hbm, bf16[1536,256]{1,0:T(8,128)(2,1)} %get-tuple-element.88.refs_0_, bf16[6,256,1536]{2,1,0:T(8,128)(2,1)} %get-tuple-element.89.refs_1_, ...), custom_call_target="tpu_custom_call" | custom-call | flops 21743271936 | bytes 56623104 | tf_op jit(solution)/shard_map/hidden_weight_grads/pallas_call | solution.py:901
  363.1 1.3 broadcast_select_fusion.resid
  364.4 0.0 collective-permute-done.4.other_low_hbm
  364.4 0.0 collective-permute-done.5.other_high_hbm
  364.4 0.9 copy-done.5
  365.3 23.6 %attention_backward.1 = (f32[256,1536]{1,0:T(8,128)}, bf16[256,1536]{1,0:T(8,128)(2,1)}, bf16[256,1536]{1,0:T(8,128)(2,1)}, bf16[1456,128,128]{2,1,0:T(8,128)(2,1)}) custom-call(s32[1440]{0:T(1024)} %scatter_custom_fusion.rows_ref.weight_rows_ref, s32[1440]{0:T(1024)} %fusion.3.rows_ref, s32[1]{0:T(128)} %bitcast.2.half_ref, ...), custom_call_target="tpu_custom_call", output_to_operand_aliasing={{3}: (22, {})} | custom-call | tf_op jit(solution)/shard_map/attention_backward/pallas_call | solution.py:931
  388.9 254.6 %sum_for_owners.1 = (bf16[91,128,128]{2,1,0:T(8,128)(2,1)S(1)}, f32[90,128,128]{2,1,0:T(8,128)S(1)}, f32[90,128,128]{2,1,0:T(8,128)S(1)}, f32[90,128,128]{2,1,0:...) custom-call(bf16[4,2,2,91,128,128]{5,4,3,2,1,0:T(8,128)(2,1)} %bitca, ...), custom_call_target="tpu_custom_call" | custom-call | bytes 381681664 | tf_op jit(solution)/shard_map/sum_for_owners/pallas_call | solution.py:1452
  643.5 0.0 copy-start.12
  643.5 0.0 copy-start.13
  643.5 0.0 copy-start.14
  643.5 0.0 copy-start.16
  643.5 0.0 copy-start.17
  643.5 0.0 copy-start.18
  643.5 10.6 %write_results.1 = (f32[90,128,128]{2,1,0:T(8,128)}, f32[90,128,128]{2,1,0:T(8,128)}, f32[90,128,128]{2,1,0:T(8,128)}, f32[90,128,128]{2,1,0:T(8,128)}, f32[256,...) custom-call(bf16[91,128,128]{2,1,0:T(8,128)(2,1)S(1)} %get-tuple-element.101.reduced, ...), custom_call_target="tpu_custom_call" | custom-call | tf_op jit(solution)/shard_map/write_results/pallas_call | solution.py:1541
  654.2 0.6 divide_subtract_fusion
  654.9 0.6 divide_subtract_fusion.1
  (41 shorter events, 0.2 us)
Async XLA Ops:
  7.2 5.1 copy-start.2
  7.2 8.2 %copy-start.7 = (bf16[256,1536]{1,0:T(8,128)(2,1)S(1)}, bf16[256,1536]{1,0:T(8,128)(2,1)}, u32[]{:S(2)}) copy-start(bf16[256,1536]{1,0:T(8,128)(2,1)} %param.16) | copy-start | bytes 2359300
  7.2 241.8 %all-gather.3.cloned.1.call-start = ((), (), s32[]{:S(2)}) async-start(), calls=%async_computation | async-start | bytes 50135040 | tf_op jit(solution)/shard_map/all_gather | solution.py:1622
  12.3 4.6 copy-start.10
  12.3 6.4 copy-start.11
  12.3 6.4 copy-start.15
  12.3 73.5 %copy-start.19 = (u32[32]{0:T(128)S(1)}, u32[32]{0:T(128)}, u32[]{:S(2)}) copy-start(u32[32]{0:T(128)} %constant.116) | copy-start | bytes 388
  12.3 117.8 %collective-permute-start = (bf16[256,1536]{1,0:T(8,128)(2,1)S(1)}, bf16[256,1536]{1,0:T(8,128)(2,1)}, u32[]{:S(2)}, u32[]{:S(2)}) collective-permute-start(bf16[256,1536]{1,0:T(8,128)(2,1)S(1)} %copy-done.2), channel_id=1, source_target_pairs={{0,1},{1,0},{2,3},{3,2},{4,5},{5,4},{6,7},{7,6},{8,9},{9,8},{10,11... | collective-permute-start | bytes 2359304 | tf_op jit(solution)/shard_map/ppermute | solution.py:1587
  15.3 117.8 %collective-permute-start.1 = (bf16[256,1536]{1,0:T(8,128)(2,1)S(1)}, bf16[256,1536]{1,0:T(8,128)(2,1)S(1)}, u32[]{:S(2)}, u32[]{:S(2)}) collective-permute-start(bf16[256,1536]{1,0:T(8,128)(2,1)S(1)} %copy-done.7), channel_id=1, source_target_pairs={{0,1},{1,0},{2,3},{3,2},{4,5},{5,4},{6,7},{7,6},{8,9},{9,8},{10,11... | collective-permute-start | bytes 2359304 | tf_op jit(solution)/shard_map/ppermute | solution.py:1587
  85.8 163.2 %copy-start.9 = (f32[2,1536]{1,0:T(2,128)}, f32[2,1536]{1,0:T(2,128)S(1)}, u32[]{:S(2)}) copy-start(f32[2,1536]{1,0:T(2,128)S(1)} %reshape.141.gain_ref) | copy-start | bytes 36868
  249.6 13.5 %copy-start.8 = (s32[1440]{0:T(1024)S(1)}, s32[1440]{0:T(1024)}, u32[]{:S(2)}) copy-start(s32[1440]{0:T(1024)} %scatter_custom_fusion.rows_ref.weight_rows_ref) | copy-start | bytes 17284
  261.5 20.0 %collective-permute-start.2 = (bf16[256,1536]{1,0:T(8,128)(2,1)}, bf16[256,1536]{1,0:T(8,128)(2,1)S(1)}, u32[]{:S(2)}, u32[]{:S(2)}) collective-permute-start(bf16[256,1536]{1,0:T(8,128)(2,1)} %get-tuple-element.73.own_hbm), channel_id=1, source_target_pairs={{0,1},{1,0},{2,3},{3,2},{4,5},{5,4},{6,7},{7,6},{8,9},{9,8},{10,11... | collective-permute-start | bytes 2359304 | tf_op jit(solution)/shard_map/ppermute | solution.py:1587
  263.7 17.8 %copy-start.3 = (bf16[256,1536]{1,0:T(8,128)(2,1)S(1)}, bf16[256,1536]{1,0:T(8,128)(2,1)}, u32[]{:S(2)}) copy-start(bf16[256,1536]{1,0:T(8,128)(2,1)} %get-tuple-element.79.own_hbm) | copy-start | bytes 2359300
  281.5 1.5 copy-start.4
  281.5 26.7 %collective-permute-start.3 = (bf16[256,1536]{1,0:T(8,128)(2,1)S(1)}, bf16[256,1536]{1,0:T(8,128)(2,1)S(1)}, u32[]{:S(2)}, u32[]{:S(2)}) collective-permute-start(bf16[256,1536]{1,0:T(8,128)(2,1)S(1)} %copy-done.3), channel_id=1, source_target_pairs={{0,1},{1,0},{2,3},{3,2},{4,5},{5,4},{6,7},{7,6},{8,9},{9,8},{10,11... | collective-permute-start | bytes 2359304 | tf_op jit(solution)/shard_map/ppermute | solution.py:1587
  307.2 57.2 %collective-permute-start.4 = (bf16[256,1536]{1,0:T(8,128)(2,1)}, bf16[256,1536]{1,0:T(8,128)(2,1)S(1)}, u32[]{:S(2)}, u32[]{:S(2)}) collective-permute-start(bf16[256,1536]{1,0:T(8,128)(2,1)} %get-tuple-element.82.own_low_hbm), channel_id=1, source_target_pairs={{0,1},{1,0},{2,3},{3,2},{4,5},{5,4},{6,7},{7,6},{8,9},{9,8},{10,11... | collective-permute-start | bytes 2359304 | tf_op jit(solution)/shard_map/ppermute | solution.py:1587
  308.2 0.9 copy-start.6
  333.3 31.2 %collective-permute-start.5 = (bf16[256,1536]{1,0:T(8,128)(2,1)}, bf16[256,1536]{1,0:T(8,128)(2,1)}, u32[]{:S(2)}, u32[]{:S(2)}) collective-permute-start(bf16[256,1536]{1,0:T(8,128)(2,1)} %get-tuple-element.84.own_high_hbm), channel_id=1, source_target_pairs={{0,1},{1,0},{2,3},{3,2},{4,5},{5,4},{6,7},{7,6},{8,9},{9,8},{10,11... | collective-permute-start | bytes 2359304 | tf_op jit(solution)/shard_map/ppermute | solution.py:1587
  334.5 28.6 %copy-start = (f32[256,1536]{1,0:T(8,128)S(1)}, f32[256,1536]{1,0:T(8,128)}, u32[]{:S(2)}) copy-start(f32[256,1536]{1,0:T(8,128)} %get-tuple-element.81.resid_low_hbm) | copy-start | bytes 4718596
  334.5 28.6 %copy-start.1 = (f32[256,1536]{1,0:T(8,128)S(1)}, f32[256,1536]{1,0:T(8,128)}, u32[]{:S(2)}) copy-start(f32[256,1536]{1,0:T(8,128)} %get-tuple-element.83.resid_high_hbm) | copy-start | bytes 4718596
  364.4 0.9 copy-start.5
  643.5 10.7 %copy-start.12 = (f32[1,64]{1,0:T(1,128)S(1)}, f32[1,64]{1,0:T(1,128)}, u32[]{:S(2)}) copy-start(f32[1,64]{1,0:T(1,128)} %param.27) | copy-start | bytes 772
  643.5 10.7 %copy-start.13 = (f32[1,64]{1,0:T(1,128)S(1)}, f32[1,64]{1,0:T(1,128)}, u32[]{:S(2)}) copy-start(f32[1,64]{1,0:T(1,128)} %param.28) | copy-start | bytes 772
  643.5 10.7 %copy-start.14 = (f32[1,64]{1,0:T(1,128)S(1)}, f32[1,64]{1,0:T(1,128)}, u32[]{:S(2)}) copy-start(f32[1,64]{1,0:T(1,128)} %param.29) | copy-start | bytes 772
  643.5 11.3 %copy-start.16 = (f32[96]{0:T(128)S(1)}, f32[96]{0:T(128)}, u32[]{:S(2)}) copy-start(f32[96]{0:T(128)} %param.24) | copy-start | bytes 1156
  643.5 11.3 %copy-start.17 = (f32[96]{0:T(128)S(1)}, f32[96]{0:T(128)}, u32[]{:S(2)}) copy-start(f32[96]{0:T(128)} %param.25) | copy-start | bytes 1156
  643.5 11.3 %copy-start.18 = (f32[96]{0:T(128)S(1)}, f32[96]{0:T(128)}, u32[]{:S(2)}) copy-start(f32[96]{0:T(128)} %param.26) | copy-start | bytes 1156
Sparse Core Ops, SparseCore 0:
  12.4 236.5 all-gather.2

commit v7 on v6

--- a/solution.py
+++ b/solution.py
@@ -123,13 +123,16 @@
         copy.wait()
 
 
-def fetch_attention(rows_ref, weights, w_qkv, w_out, sems):
-    fetch_piece(rows_ref, weights, w_qkv, 0, QUERY_COLS, ROW_BLOCKS, QUERY_COLS, 0, sems.at[0])
-    fetch_piece(rows_ref, weights, w_qkv, KEY_BASE, PAIR_COLS, ROW_BLOCKS, PAIR_COLS, QUERY_COLS, sems.at[0])
+def fetch_qkv(rows_ref, weights, w_qkv, sem):
+    fetch_piece(rows_ref, weights, w_qkv, 0, QUERY_COLS, ROW_BLOCKS, QUERY_COLS, 0, sem)
+    fetch_piece(rows_ref, weights, w_qkv, KEY_BASE, PAIR_COLS, ROW_BLOCKS, PAIR_COLS, QUERY_COLS, sem)
     fetch_piece(
-        rows_ref, weights, w_qkv, VALUE_BASE, PAIR_COLS, ROW_BLOCKS, PAIR_COLS, QUERY_COLS + PAIR_COLS, sems.at[0]
+        rows_ref, weights, w_qkv, VALUE_BASE, PAIR_COLS, ROW_BLOCKS, PAIR_COLS, QUERY_COLS + PAIR_COLS, sem
     )
-    fetch_piece(rows_ref, weights, w_out, OUT_BASE, ROW_BLOCKS, QUERY_COLS, ROW_BLOCKS, 0, sems.at[1])
+
+
+def fetch_out(rows_ref, weights, w_out, sem):
+    fetch_piece(rows_ref, weights, w_out, OUT_BASE, ROW_BLOCKS, QUERY_COLS, ROW_BLOCKS, 0, sem)
 
 
 def rms_inverse(values):
@@ -188,7 +191,8 @@
         (normed_turned, qkv, mixed_turned), (normed_turned_out, qkv_out, mixed_turned_out), store_sems
     )
     start_all(loads)
-    fetch_attention(rows_ref, weights, w_qkv, w_out, sems)
+    fetch_qkv(rows_ref, weights, w_qkv, sems.at[0])
+    fetch_out(rows_ref, weights, w_out, sems.at[1])
     length = x_ref.shape[0]
     part = length // NARROW
 
@@ -337,7 +341,6 @@
     active_grad,
     weights,
     grad_ref,
-    gain_part_ref,
     resid_out,
     normed_turned_out,
     pair_grads,
@@ -438,13 +441,6 @@
     hidden_tiles(run)
     store_turned.start()
     grad_ref[...] = grad_sum[...].astype(bf16)
-    gain_part_ref[...] = jnp.zeros_like(gain_part_ref)
-
-    def gain_rows(rows):
-        values = resid_ref[rows, :]
-        gain_part_ref[...] += jnp.sum(grad_sum[rows, :] * values * rms_inverse(values), axis=0, keepdims=True)
-
-    row_chunks(length, ROWS, gain_rows)
     for tile in range(max(TILES - 2, 0), TILES):
         wait_all(stores(tile, tile % 2))
     store_resid.wait()
@@ -520,8 +516,6 @@
     half_ref,
     gain_ref,
     log_ref,
-    gain_two_low_ref,
-    gain_two_high_ref,
     resid_low_hbm,
     own_low_hbm,
     other_low_hbm,
@@ -566,6 +560,7 @@
     grad_keys,
     grad_values,
     gain_part,
+    gain_two_part,
     bias_part,
     qkv_stage,
     out_stage,
@@ -591,14 +586,16 @@
     wide_count = small_stage.shape[0]
     owner_rows = grads.shape[0] // wide_count
     small_stage[...] = jnp.zeros_like(small_stage)
-    fetch_attention(weight_rows_ref, weights, w_qkv, w_out, load_sems)
+    fetch_out(weight_rows_ref, weights, w_out, load_sems.at[1])
     start_all(loads[7:])
+    fetch_qkv(weight_rows_ref, weights, w_qkv, load_sems.at[0])
     length = x_ref.shape[0]
     empty_count = rows_ref.shape[0] - BLOCK_TOTAL
     blank[...] = jnp.zeros_like(blank)
     for index in range(empty_count):
         pltpu.make_async_copy(blank.at[index], grads.at[rows_ref[BLOCK_TOTAL + index]], store_sems.at[2]).start()
 
+    gain_two_part[...] = jnp.zeros_like(gain_two_part)
     part = length // NARROW
     own_rows, other_rows = half_rows(half_ref, part)
     for first, resid_ref, own_ref, other_ref, needed in (
@@ -611,7 +608,9 @@
             values = resid_ref[rows, :]
             inverse = rms_inverse(values)
             normed = values * inverse
-            scaled = (own_ref[rows, :].astype(f32) + other_ref[rows, :].astype(f32)) * gain_ref[1:2, :]
+            grad_normed = own_ref[rows, :].astype(f32) + other_ref[rows, :].astype(f32)
+            gain_two_part[...] += jnp.sum(grad_normed * normed, axis=0, keepdims=True) / NARROW
+            scaled = grad_normed * gain_ref[1:2, :]
             place = pl.ds(rows.start + first, rows.size)
             total = cot_ref[place, :].astype(f32) + inverse * (
                 scaled - normed * jnp.mean(scaled * normed, axis=-1, keepdims=True)
@@ -674,12 +673,11 @@
     grad_own_ref[...] = grad_sum[own_rows, :].astype(bf16)
     grad_other_ref[...] = grad_sum[other_rows, :].astype(bf16)
     gain_part[...] = jnp.zeros_like(gain_part)
-    bias_part[...] = jnp.zeros_like(bias_part)
+    bias_part[...] = dot_nn(jnp.ones((SMALL_ROWS, length), bf16), grad_qkv[...])[:1]
 
     def gain_rows(rows):
         tokens = x_ref[rows, :].astype(f32)
         gain_part[...] += jnp.sum(grad_sum[rows, :] * tokens * rms_inverse(tokens), axis=0, keepdims=True)
-        bias_part[...] += jnp.sum(grad_qkv[rows, :].astype(f32), axis=0, keepdims=True)
 
     row_chunks(length, ROWS, gain_rows)
     for owner in range(wide_count):
@@ -690,7 +688,7 @@
             if row < D // BLK:
                 small_rows.append(gain_part[:, columns])
             else:
-                small_rows.append(gain_two_low_ref[:, columns] + gain_two_high_ref[:, columns])
+                small_rows.append(gain_two_part[:, columns])
         small_rows.append(bias_part[:, pl.ds(bias_row * BLK, BLK)])
         small_rows.append(jnp.zeros((SMALL_ROWS - len(small_rows), BLK), f32))
         small_stage[owner, pl.ds(0, SMALL_ROWS), :] = jnp.concatenate(small_rows, axis=0).astype(bf16)
@@ -858,11 +856,10 @@
 def run_hidden_grads(first_row, rows, x, own, other, gain, active_grad, weights):
     length = own.shape[0]
     shape = jax.ShapeDtypeStruct
-    grad, gain_part, *kept = pl.pallas_call(
+    return pl.pallas_call(
         functools.partial(hidden_grads, first_row),
         out_shape=[
             shape((length, D), bf16),
-            shape((1, D), f32),
             shape((length, D), f32),
             shape((D, length), bf16),
             shape((TILES, length, 2 * TILE), bf16),
@@ -870,7 +867,7 @@
             shape((TILES, TILE, length), bf16),
         ],
         in_specs=[SMEM_SPEC, VMEM_SPEC] + [ANY_SPEC] * 5,
-        out_specs=[VMEM_SPEC] * 2 + [ANY_SPEC] * 5,
+        out_specs=[VMEM_SPEC] + [ANY_SPEC] * 5,
         scratch_shapes=[
             pltpu.VMEM((length, D), bf16),
             pltpu.VMEM((length, D), bf16),
@@ -892,8 +889,6 @@
         cost_estimate=hidden_cost(length, 4, 2 * TILES * TILE * (2 * D + 6 * length)),
         name="hidden_grads",
     )(rows, gain, x, own, other, active_grad, weights)
-    resid, normed_turned, *hidden = kept
-    return (grad, resid, normed_turned, gain_part, *hidden)
 
 
 def run_hidden_weight_grads(rows, cotangent, parts, slots):
@@ -921,13 +916,13 @@
 
 def run_attention_backward(
     weight_rows, rows, half, x, low, high, cotangent, gains, cosine, sine, allowed, normed_turned, qkv, mixed_turned,
-    log_total, gain_two_parts, weights, grads, wide_count,
+    log_total, weights, grads, wide_count,
 ):
     length = x.shape[0]
     shape = jax.ShapeDtypeStruct
     empty_count = max(rows.shape[0] - BLOCK_TOTAL, 1)
     loaded = (*low, *high, cotangent, qkv, cosine, sine, allowed, mixed_turned, normed_turned, x)
-    operands = (weight_rows, rows, half, gains, log_total, *gain_two_parts, *loaded, weights, grads)
+    operands = (weight_rows, rows, half, gains, log_total, *loaded, weights, grads)
     return pl.pallas_call(
         attention_backward,
         out_shape=[
@@ -936,7 +931,7 @@
             shape((length // NARROW, D), bf16),
             shape(grads.shape, bf16),
         ],
-        in_specs=[SMEM_SPEC] * 3 + [VMEM_SPEC] * 4 + [ANY_SPEC] * (len(loaded) + 2),
+        in_specs=[SMEM_SPEC] * 3 + [VMEM_SPEC] * 2 + [ANY_SPEC] * (len(loaded) + 2),
         out_specs=[VMEM_SPEC] * 3 + [ANY_SPEC],
         input_output_aliases={len(operands) - 1: 3},
         scratch_shapes=[pltpu.VMEM(array.shape, array.dtype) for array in loaded]
@@ -951,6 +946,7 @@
             pltpu.VMEM((length, HEAD_DIM), f32),
             pltpu.VMEM((length, HEAD_DIM), f32),
             pltpu.VMEM((1, D), f32),
+            pltpu.VMEM((1, D), f32),
             pltpu.VMEM((1, QKV_WIDTH), f32),
             pltpu.VMEM((D, QKV_WIDTH), bf16),
             pltpu.VMEM((QUERY_WIDTH, D), bf16),
@@ -987,7 +983,7 @@
 def sum_for_owners(
     line, steps, late_steps,
     grads, masters, first_moment, second_moment, left_basis, right_basis,
-    grad_resid, grad_own, grad_sent, tokens, gain, resid, active_low, active_high, down,
+    grad_resid, grad_own, grad_sent, tokens, gain, resid_low, resid_high, active_low, active_high, down,
     out, new_masters, new_first, new_second, input_grad, output, small_own, small_other,
     a_in, a_own, a_sum, a_keep, a_send, a_cross, a_up, a_down,
     b_in, b_own, b_sum, b_keep, b_send, b_cross, b_up, b_down,
@@ -1128,9 +1124,9 @@
         ]
 
     token_loads = [
-        pltpu.make_async_copy(source, target, token_sems.at[index])
+        pltpu.make_async_copy(source, target, token_sems.at[1 + index])
         for index, (source, target) in enumerate((
-            (resid, resid_here), (grad_resid, grad_resid_here), (grad_own, grad_own_here), (tokens, tokens_here), (gain, gain_here),
+            (grad_resid, grad_resid_here), (grad_own, grad_own_here), (tokens, tokens_here), (gain, gain_here),
         ))
     ]
     grad_swap = remote(grad_sent, grad_other_here, swap_send.at[0], swap_recv.at[0], swap_peer)
@@ -1173,8 +1169,11 @@
             branch_sent[...] = branch_sum[...].astype(bf16)
             branch_swap.start()
 
+    def resid_load(source):
+        return pltpu.make_async_copy(source, resid_here, token_sems.at[0])
+
     def finish_output():
-        token_loads[0].wait()
+        resid_load(resid_low).wait()
         branch_swap.wait()
 
         def rows_of_output(rows):
@@ -1184,7 +1183,7 @@
         row_chunks(output.shape[0], ROWS, rows_of_output)
 
     def finish_input_grad():
-        wait_all(token_loads[1:])
+        wait_all(token_loads)
         grad_swap.wait()
 
         def rows_of_grad(rows):
@@ -1204,6 +1203,8 @@
 
     start_all(param_loads(0) + param_loads(1) + b_param_loads(1) + b_param_loads(2) + token_loads)
     branch_load(0)
+    pl.when(narrow == 0)(lambda: resid_load(resid_low).start())
+    pl.when(narrow != 0)(lambda: resid_load(resid_high).start())
 
     def active(step, count):
         return (step >= 0) & (step < count)
@@ -1479,8 +1480,8 @@
         ]
         + [pltpu.VMEM(array.shape, array.dtype) for array in token_arrays[:6]]
         + [
-            pltpu.VMEM(token_arrays[6].shape[1:], bf16),
-            pltpu.VMEM(token_arrays[8].shape[1:], bf16),
+            pltpu.VMEM(token_arrays[7].shape[1:], bf16),
+            pltpu.VMEM(token_arrays[9].shape[1:], bf16),
             pltpu.VMEM(token_arrays[0].shape, f32),
             pltpu.VMEM(token_arrays[0].shape, bf16),
             pltpu.VMEM(token_arrays[0].shape, bf16),
@@ -1640,9 +1641,7 @@
     ).astype(f32)
     tokens_row = join_halves(tokens, swap_halves(tokens))
     cotangent_row = join_halves(cotangent, swap_halves(cotangent))
-    weights, tokens_row, cotangent_row, gain_full, bias_full = lax.optimization_barrier(
-        (weights, tokens_row, cotangent_row, gain_full, bias_full)
-    )
+    weights, tokens_row, cotangent_row = lax.optimization_barrier((weights, tokens_row, cotangent_row))
 
     low_part, high_part, normed_one_turned, qkv, mixed_turned, log_total = run_attention_forward(
         weight_rows, tokens_row, gain_full[0:1], bias_full, cosine, sine, allowed_turned, weights
@@ -1652,11 +1651,11 @@
     high_sent, low_other = lax.optimization_barrier((high_part, low_other))
     high_other = swap_halves(high_sent)
     gain_two = gain_full[1:2]
-    grad_low, resid_low, turned_low, gain_low, *hidden_low = run_hidden_grads(
+    grad_low, resid_low, turned_low, *hidden_low = run_hidden_grads(
         0, weight_rows, tokens_row, low_part, low_other, gain_two, active_grad, weights
     )
     grad_low_other = swap_halves(grad_low)
-    grad_high, resid_high, turned_high, gain_high, *hidden_high = run_hidden_grads(
+    grad_high, resid_high, turned_high, *hidden_high = run_hidden_grads(
         tokens_here, weight_rows, tokens_row, high_part, high_other, gain_two, active_grad, weights
     )
     grad_high_other = swap_halves(grad_high)
@@ -1669,13 +1668,13 @@
     grad_resid, grad_one_own, grad_one_sent, grads = run_attention_backward(
         weight_rows, rows, half_index, tokens_row, (resid_low, grad_low, grad_low_other),
         (resid_high, grad_high, grad_high_other), cotangent_row, gain_full, cosine, sine, allowed_turned,
-        normed_one_turned, qkv, mixed_turned, log_total, (gain_low, gain_high), weights, grads, wide_count,
+        normed_one_turned, qkv, mixed_turned, log_total, weights, grads, wide_count,
     )
-    resid_own = jnp.where(half == 0, resid_low, resid_high)
     blocks = [masters, first_moment, second_moment, left_basis, right_basis]
     if wide_count == 16:
         token_arrays = [
-            grad_resid, grad_one_own, grad_one_sent, tokens, gain_full[0:1], resid_own, active_low, active_high, down_tiles
+            grad_resid, grad_one_own, grad_one_sent, tokens, gain_full[0:1], resid_low, resid_high, active_low,
+            active_high, down_tiles,
         ]
         block_grad, new_masters, new_first, new_second, input_grad, output, small_sums = run_write_results(
             *run_sum_for_owners(grads, wide_count, blocks, token_arrays)
@@ -1691,6 +1690,7 @@
             jnp.einsum("tik,tkd->id", active, down_tiles, preferred_element_type=f32)
             for active in (active_low, active_high)
         ]
+        resid_own = jnp.where(half == 0, resid_low, resid_high)
         branch_own = jnp.where(half == 0, branch_low, branch_high)
         branch_sent = jnp.where(half == 0, branch_high, branch_low).astype(bf16)
         output = (resid_own + branch_own + swap_halves(branch_sent).astype(f32)).astype(bf16)

time: 669 us -> 668 us (level)
  transfers between devices with their start and end apart: 7 -> 7, of which waited for: 2 -> 1; matrix products, arithmetic and copies ran while one was open for 3% -> 3% of each run, Pallas kernels for 14% -> 14%
where the time goes in v7:
time: 668 us; the launch traced here: 661 us
  Pallas kernels  395 us (59%)
  waiting for transfers between devices  112 us (17%)
  blocking collectives  99.4 us (15%)
  other arithmetic  17.2 us (3%)
  between operations  15.2 us (2%)
  local copies, waits for them, and re-layouts  14.3 us (2%)
  starting transfers between devices  7.85 us (1%)
    pallas_call x1, Pallas kernels, run_sum_for_owners(): pl.pallas_call(functools.partial(sum_for_owners, line, steps, late_steps)...  255 us
    all_gather x1, waiting for transfers between devices, body(): weights = lax.all_gather(masters_low, 'wide', axis=0, tiled=True)  112 us
    unnamed x2, blocking collectives  99.4 us
    pallas_call x2, Pallas kernels, run_hidden_grads(): pl.pallas_call(functools.partial(hidden_grads, first_row), out_shape=[sha...  48.4 us
    pallas_call x1, Pallas kernels, run_hidden_weight_grads(): pl.pallas_call(hidden_weight_grads, out_shape=jax.ShapeDtypeStruct((slots...  28.4 us
    pallas_call x1, Pallas kernels, run_attention_backward(): pl.pallas_call(attention_backward, out_shape=[shape((length // NARROW, D)...  23.9 us
    pallas_call x1, Pallas kernels, run_active_grads(): pl.pallas_call(active_grads, out_shape=[jax.ShapeDtypeStruct((TILES, leng...  17.1 us
  transfers between devices with their start and end apart: 7, of which 1 were waited for; matrix products, arithmetic and copies ran while one was open for 3% of the time, Pallas kernels for 14%

profile of v7, /device:TPU:0, one launch (start us, length us, event | category | flops | bytes accessed | tf_op | source)
XLA Modules:
  0.0 661.0 jit_solution(13120766004567759211)
XLA Ops:
  7.2 0.0 copy-start.13
  7.2 0.0 copy-start
  7.2 0.0 all-gather.3.cloned.1.call-start
  7.3 5.0 convert_element_type.21
  12.3 0.0 all-gather.3.cloned.1.call-update
  12.3 3.0 collective-permute-start
  15.4 0.1 collective-permute-start.1
  15.4 0.9 compare_reduce_fusion
  16.3 0.1 add_select_fusion.1
  16.4 0.3 reduce-window.24
  16.7 0.1 slice.54
  16.9 0.3 reduce-window.16
  17.1 0.1 slice.61
  17.3 0.3 dynamic-update-slice
  17.5 68.2 %all-reduce.1 = f32[3072]{0:T(1024)S(1)} all-reduce(f32[3072]{0:T(1024)S(1)} %dynamic-update-slice), channel_id=1, replica_groups=mesh['wide'=16,'narrow'=2] {'wide','narrow'}, use_global_device_ids=true, to_apply=%add.1 | all-reduce | flops 3072 | bytes 24576
  85.8 0.1 slice_reduce_fusion.1
  85.9 0.1 slice_reduce_fusion
  86.0 0.1 fusion.8
  86.1 0.1 add_bitcast_fusion
  86.2 1.0 fusion.2
  87.2 0.6 slice.51.gain_ref.gain
  87.8 0.6 dynamic-slice.1
  89.1 0.2 dynamic-update-slice.1
  89.3 31.2 %all-reduce.2 = bf16[1024]{0:T(1024)(128)(2,1)S(1)} all-reduce(bf16[1024]{0:T(1024)(128)(2,1)S(1)} %dynamic-update-slice.1), channel_id=2, replica_groups=mesh['wide'=16,'narrow'=2] {'wide'}, use_global_device_ids=true, to_apply=%add.2 | all-reduce | flops 1024 | bytes 4096
  120.5 0.6 reshape.169
  121.1 8.2 %scatter_custom_fusion.rows_ref.weight_rows_ref = s32[1440]{0:T(1024)} fusion(s32[1440]{0:T(1024)S(1)} %compare_select_fusion, s32[1440]{0:T(1024)S(1)} %iota.33, s32[]{:T(128)} %constant.33.clone.1), kind=kCustom, calls=%fused_computation.24 | custom fusion | bytes 5764 | tf_op jit(solution)/shard_map/scatter | solution.py:1632
  129.2 0.7 constant_dynamic-slice_fusion.1
  130.0 1.0 pad_maximum_fusion
  131.0 1.1 fusion.1.allowed_hbm
  132.1 0.0 collective-permute-done
  132.1 3.0 maximum_select_fusion.x_hbm
  135.1 0.0 collective-permute-done.1
  135.1 1.8 maximum_select_fusion.1.cot_ref.cot_hbm
  136.9 112.1 %all-gather.3.cloned.1.call-done.weights = bf16[1440,128,128]{2,1,0:T(8,128)(2,1)} async-done(((bf16[90,128,128]{2,1,0:T(8,128)(2,1)}), bf16[1440,128,128]{2,1,0:T(8,128)(2,1)}) %all-gather.3.cloned.1.call-update) | async-done | bytes 47185936 | tf_op jit(solution)/shard_map/all_gather | solution.py:1623
  249.0 11.9 %attention_forward.1 = (bf16[256,1536]{1,0:T(8,128)(2,1)}, bf16[256,1536]{1,0:T(8,128)(2,1)}, f32[8,512]{1,0:T(8,128)}, bf16[1536,512]{1,0:T(8,128)(2,1)}, bf16[...) custom-call(s32[1440]{0:T(1024)} %scatter_custom_fusion.rows_ref.weight_rows_ref, f32[1,1536]{1,0:T(1,128)} %slice.51.gain_ref.gain, ...), custom_call_target="tpu_custom_call" | custom-call | tf_op jit(solution)/shard_map/attention_forward/pallas_call | solution.py:800
  260.9 1.5 collective-permute-start.2
  262.5 0.6 fusion.3.rows_ref
  263.1 0.6 reshape.142.gain_ref
  263.7 0.6 slice.57.gain_ref
  264.3 17.1 %active_grads.1 = (f32[6,512,768]{2,1,0:T(8,128)}, bf16[6,768,1536]{2,1,0:T(8,128)(2,1)}) custom-call(s32[1440]{0:T(1024)} %scatter_custom_fusion.rows_ref.weight_rows_ref, bf16[512,1536]{1,0:T(8,128)(2,1)} %maximum_select_fusion.1.cot_ref.cot_hbm, bf16[1440,128,128]{2,1,0:T(8,128)(2,1)} %all-gather.3.cloned.1.call-done.weights), custom_call_target="tpu_custom_call" | custom-call | flops 7247757312 | bytes 23592960 | tf_op jit(solution)/shard_map/active_grads/pallas_call | solution.py:835
  281.4 0.0 copy-start.2
  281.4 1.0 collective-permute-start.4
  282.4 24.2 %hidden_grads.2 = (bf16[256,1536]{1,0:T(8,128)(2,1)}, f32[256,1536]{1,0:T(8,128)}, bf16[1536,256]{1,0:T(8,128)(2,1)}, bf16[6,256,1536]{2,1,0:T(8,128)(2,1)}, bf1...) custom-call(s32[1440]{0:T(1024)} %scatter_custom_fusion.rows_ref.weight_rows_ref, f32[1,1536]{1,0:T(1,128)} %slice.57.gain_ref, ...), custom_call_target="tpu_custom_call" | custom-call | flops 14495514624 | bytes 42467328 | tf_op jit(solution)/shard_map/hidden_grads/pallas_call | solution.py:859
  306.6 1.2 collective-permute-start.3
  307.8 0.9 copy-done.5
  308.7 24.2 %hidden_grads.3 = (bf16[256,1536]{1,0:T(8,128)(2,1)}, f32[256,1536]{1,0:T(8,128)}, bf16[1536,256]{1,0:T(8,128)(2,1)}, bf16[6,256,1536]{2,1,0:T(8,128)(2,1)}, bf1...) custom-call(s32[1440]{0:T(1024)} %scatter_custom_fusion.rows_ref.weight_rows_ref, f32[1,1536]{1,0:T(1,128)} %slice.57.gain_ref, ...), custom_call_target="tpu_custom_call" | custom-call | flops 14495514624 | bytes 42467328 | tf_op jit(solution)/shard_map/hidden_grads/pallas_call | solution.py:859
  332.9 1.0 collective-permute-start.5
  333.9 28.4 %hidden_weight_grads.1.grads_in = bf16[1456,128,128]{2,1,0:T(8,128)(2,1)} custom-call(s32[1440]{0:T(1024)} %fusion.3.rows_ref, bf16[512,1536]{1,0:T(8,128)(2,1)} %maximum_select_fusion.1.cot_ref.cot_hbm, bf16[1536,256]{1,0:T(8,128)(2,1)} %get-tuple-element.80.refs_0_, bf16[6,256,1536]{2,1,0:T(8,128)(2,1)} %get-tuple-element.81.refs_1_, ...), custom_call_target="tpu_custom_call" | custom-call | flops 21743271936 | bytes 56623104 | tf_op jit(solution)/shard_map/hidden_weight_grads/pallas_call | solution.py:896
  362.3 0.0 copy-start.3
  362.3 0.0 collective-permute-done.5.other_high_hbm
  362.3 0.0 copy-start.4
  362.4 0.8 copy-done.3
  363.2 0.3 copy-done.4
  363.5 23.9 %attention_backward.1 = (f32[256,1536]{1,0:T(8,128)}, bf16[256,1536]{1,0:T(8,128)(2,1)}, bf16[256,1536]{1,0:T(8,128)(2,1)}, bf16[1456,128,128]{2,1,0:T(8,128)(2,1)}) custom-call(s32[1440]{0:T(1024)} %scatter_custom_fusion.rows_ref.weight_rows_ref, s32[1440]{0:T(1024)} %fusion.3.rows_ref, s32[1]{0:T(128)} %bitcast.2.half_ref, ...), custom_call_target="tpu_custom_call", output_to_operand_aliasing={{3}: (20, {})} | custom-call | tf_op jit(solution)/shard_map/attention_backward/pallas_call | solution.py:926
  387.4 254.6 %sum_for_owners.1 = (bf16[91,128,128]{2,1,0:T(8,128)(2,1)S(1)}, f32[90,128,128]{2,1,0:T(8,128)S(1)}, f32[90,128,128]{2,1,0:T(8,128)S(1)}, f32[90,128,128]{2,1,0:...) custom-call(bf16[4,2,2,91,128,128]{5,4,3,2,1,0:T(8,128)(2,1)} %bitca, ...), custom_call_target="tpu_custom_call" | custom-call | bytes 381681664 | tf_op jit(solution)/shard_map/sum_for_owners/pallas_call | solution.py:1453
  642.0 0.0 copy-start.10
  642.0 0.0 copy-start.11
  642.0 0.0 copy-start.12
  642.0 0.0 copy-start.14
  642.0 0.0 copy-start.15
  642.0 0.0 copy-start.16
  642.0 10.6 %write_results.1 = (f32[90,128,128]{2,1,0:T(8,128)}, f32[90,128,128]{2,1,0:T(8,128)}, f32[90,128,128]{2,1,0:T(8,128)}, f32[90,128,128]{2,1,0:T(8,128)}, f32[256,...) custom-call(bf16[91,128,128]{2,1,0:T(8,128)(2,1)S(1)} %get-tuple-element.93.reduced, ...), custom_call_target="tpu_custom_call" | custom-call | tf_op jit(solution)/shard_map/write_results/pallas_call | solution.py:1542
  652.7 0.6 divide_subtract_fusion
  653.3 0.6 divide_subtract_fusion.1
  (38 shorter events, 0.2 us)
Async XLA Ops:
  7.2 10.1 %copy-start.13 = (f32[96]{0:T(128)S(1)}, f32[96]{0:T(128)}, u32[]{:S(2)}) copy-start(f32[96]{0:T(128)} %param.24) | copy-start | bytes 1156
  7.2 5.1 copy-start
  7.2 8.2 %copy-start.6 = (bf16[256,1536]{1,0:T(8,128)(2,1)S(1)}, bf16[256,1536]{1,0:T(8,128)(2,1)}, u32[]{:S(2)}) copy-start(bf16[256,1536]{1,0:T(8,128)(2,1)} %param.16) | copy-start | bytes 2359300
  7.2 9.6 %copy-start.8 = (s32[1440]{0:T(1024)S(1)}, s32[1440]{0:T(1024)}, u32[]{:S(2)}) copy-start(s32[1440]{0:T(1024)} %param.18) | copy-start | bytes 17284
  7.2 241.8 %all-gather.3.cloned.1.call-start = ((), (), s32[]{:S(2)}) async-start(), calls=%async_computation | async-start | bytes 50135040 | tf_op jit(solution)/shard_map/all_gather | solution.py:1623
  12.3 74.9 %copy-start.9 = (f32[1,64]{1,0:T(1,128)S(1)}, f32[1,64]{1,0:T(1,128)}, u32[]{:S(2)}) copy-start(f32[1,64]{1,0:T(1,128)} %param.27) | copy-start | bytes 772
  12.3 75.5 %copy-start.17 = (u32[32]{0:T(128)S(1)}, u32[32]{0:T(128)}, u32[]{:S(2)}) copy-start(u32[32]{0:T(128)} %constant.116) | copy-start | bytes 388
  12.3 119.8 %collective-permute-start = (bf16[256,1536]{1,0:T(8,128)(2,1)S(1)}, bf16[256,1536]{1,0:T(8,128)(2,1)}, u32[]{:S(2)}, u32[]{:S(2)}) collective-permute-start(bf16[256,1536]{1,0:T(8,128)(2,1)S(1)} %copy-done), channel_id=1, source_target_pairs={{0,1},{1,0},{2,3},{3,2},{4,5},{5,4},{6,7},{7,6},{8,9},{9,8},{10,11... | collective-permute-start | bytes 2359304 | tf_op jit(solution)/shard_map/ppermute | solution.py:1588
  15.4 119.7 %collective-permute-start.1 = (bf16[256,1536]{1,0:T(8,128)(2,1)S(1)}, bf16[256,1536]{1,0:T(8,128)(2,1)S(1)}, u32[]{:S(2)}, u32[]{:S(2)}) collective-permute-start(bf16[256,1536]{1,0:T(8,128)(2,1)S(1)} %copy-done.6), channel_id=1, source_target_pairs={{0,1},{1,0},{2,3},{3,2},{4,5},{5,4},{6,7},{7,6},{8,9},{9,8},{10,11... | collective-permute-start | bytes 2359304 | tf_op jit(solution)/shard_map/ppermute | solution.py:1588
  249.0 13.5 %copy-start.7 = (s32[1440]{0:T(1024)S(1)}, s32[1440]{0:T(1024)}, u32[]{:S(2)}) copy-start(s32[1440]{0:T(1024)} %scatter_custom_fusion.rows_ref.weight_rows_ref) | copy-start | bytes 17284
  260.9 20.4 %collective-permute-start.2 = (bf16[256,1536]{1,0:T(8,128)(2,1)}, bf16[256,1536]{1,0:T(8,128)(2,1)S(1)}, u32[]{:S(2)}, u32[]{:S(2)}) collective-permute-start(bf16[256,1536]{1,0:T(8,128)(2,1)} %get-tuple-element.67.own_hbm), channel_id=1, source_target_pairs={{0,1},{1,0},{2,3},{3,2},{4,5},{5,4},{6,7},{7,6},{8,9},{9,8},{10,11... | collective-permute-start | bytes 2359304 | tf_op jit(solution)/shard_map/ppermute | solution.py:1588
  264.3 17.1 %copy-start.1 = (bf16[256,1536]{1,0:T(8,128)(2,1)S(1)}, bf16[256,1536]{1,0:T(8,128)(2,1)}, u32[]{:S(2)}) copy-start(bf16[256,1536]{1,0:T(8,128)(2,1)} %get-tuple-element.74.own_hbm) | copy-start | bytes 2359300
  281.4 1.0 copy-start.2
  281.4 26.4 %collective-permute-start.4 = (bf16[256,1536]{1,0:T(8,128)(2,1)S(1)}, bf16[256,1536]{1,0:T(8,128)(2,1)S(1)}, u32[]{:S(2)}, u32[]{:S(2)}) collective-permute-start(bf16[256,1536]{1,0:T(8,128)(2,1)S(1)} %copy-done.1), channel_id=1, source_target_pairs={{0,1},{1,0},{2,3},{3,2},{4,5},{5,4},{6,7},{7,6},{8,9},{9,8},{10,11... | collective-permute-start | bytes 2359304 | tf_op jit(solution)/shard_map/ppermute | solution.py:1588
  306.6 55.7 %collective-permute-start.3 = (bf16[256,1536]{1,0:T(8,128)(2,1)}, bf16[256,1536]{1,0:T(8,128)(2,1)S(1)}, u32[]{:S(2)}, u32[]{:S(2)}) collective-permute-start(bf16[256,1536]{1,0:T(8,128)(2,1)} %get-tuple-element.73.own_low_hbm), channel_id=1, source_target_pairs={{0,1},{1,0},{2,3},{3,2},{4,5},{5,4},{6,7},{7,6},{8,9},{9,8},{10,11... | collective-permute-start | bytes 2359304 | tf_op jit(solution)/shard_map/ppermute | solution.py:1588
  307.8 0.9 copy-start.5
  332.9 29.5 %collective-permute-start.5 = (bf16[256,1536]{1,0:T(8,128)(2,1)}, bf16[256,1536]{1,0:T(8,128)(2,1)S(1)}, u32[]{:S(2)}, u32[]{:S(2)}) collective-permute-start(bf16[256,1536]{1,0:T(8,128)(2,1)} %get-tuple-element.76.own_high_hbm), channel_id=1, source_target_pairs={{0,1},{1,0},{2,3},{3,2},{4,5},{5,4},{6,7},{7,6},{8,9},{9,8},{10,11... | collective-permute-start | bytes 2359304 | tf_op jit(solution)/shard_map/ppermute | solution.py:1588
  362.3 0.9 copy-start.3
  362.3 1.1 copy-start.4
  642.0 10.7 %copy-start.10 = (f32[1,64]{1,0:T(1,128)S(1)}, f32[1,64]{1,0:T(1,128)}, u32[]{:S(2)}) copy-start(f32[1,64]{1,0:T(1,128)} %param.27) | copy-start | bytes 772
  642.0 10.7 %copy-start.11 = (f32[1,64]{1,0:T(1,128)S(1)}, f32[1,64]{1,0:T(1,128)}, u32[]{:S(2)}) copy-start(f32[1,64]{1,0:T(1,128)} %param.28) | copy-start | bytes 772
  642.0 10.7 %copy-start.12 = (f32[1,64]{1,0:T(1,128)S(1)}, f32[1,64]{1,0:T(1,128)}, u32[]{:S(2)}) copy-start(f32[1,64]{1,0:T(1,128)} %param.29) | copy-start | bytes 772
  642.0 11.3 %copy-start.14 = (f32[96]{0:T(128)S(1)}, f32[96]{0:T(128)}, u32[]{:S(2)}) copy-start(f32[96]{0:T(128)} %param.24) | copy-start | bytes 1156
  642.0 11.3 %copy-start.15 = (f32[96]{0:T(128)S(1)}, f32[96]{0:T(128)}, u32[]{:S(2)}) copy-start(f32[96]{0:T(128)} %param.25) | copy-start | bytes 1156
  642.0 11.3 %copy-start.16 = (f32[96]{0:T(128)S(1)}, f32[96]{0:T(128)}, u32[]{:S(2)}) copy-start(f32[96]{0:T(128)} %param.26) | copy-start | bytes 1156
Sparse Core Ops, SparseCore 0:
  12.4 236.5 all-gather.2

commit v8 on v7

--- a/solution.py
+++ b/solution.py
@@ -335,9 +335,9 @@
     first_row,
     rows_ref,
     gain_ref,
+    other_ref,
     x_hbm,
     own_hbm,
-    other_hbm,
     active_grad,
     weights,
     grad_ref,
@@ -348,7 +348,6 @@
     active_turned,
     x_ref,
     own_ref,
-    other_ref,
     resid_ref,
     normed_turned_ref,
     w_pair,
@@ -364,7 +363,7 @@
 ):
     length = own_ref.shape[0]
     token_loads = copies_between(
-        (x_hbm.at[pl.ds(first_row, length)], own_hbm, other_hbm), (x_ref, own_ref, other_ref), token_sems
+        (x_hbm.at[pl.ds(first_row, length)], own_hbm), (x_ref, own_ref), token_sems
     )
     store_resid = pltpu.make_async_copy(resid_ref, resid_out, token_sems.at[3])
     store_turned = pltpu.make_async_copy(normed_turned_ref, normed_turned_out, token_sems.at[4])
@@ -516,12 +515,12 @@
     half_ref,
     gain_ref,
     log_ref,
+    other_low_ref,
+    other_high_ref,
     resid_low_hbm,
     own_low_hbm,
-    other_low_hbm,
     resid_high_hbm,
     own_high_hbm,
-    other_high_hbm,
     cot_hbm,
     qkv_hbm,
     cos_hbm,
@@ -538,10 +537,8 @@
     grads,
     resid_low_ref,
     own_low_ref,
-    other_low_ref,
     resid_high_ref,
     own_high_ref,
-    other_high_ref,
     cot_ref,
     qkv_ref,
     cos_ref,
@@ -573,21 +570,19 @@
     del grads_in
     loads = copies_between(
         (
-            cot_hbm, resid_low_hbm, own_low_hbm, other_low_hbm, resid_high_hbm, own_high_hbm, other_high_hbm, qkv_hbm,
-            cos_hbm, sin_hbm, allowed_hbm, mixed_turned_hbm, normed_turned_hbm, x_hbm,
+            cot_hbm, resid_low_hbm, own_low_hbm, resid_high_hbm, own_high_hbm, qkv_hbm, cos_hbm, sin_hbm, allowed_hbm, mixed_turned_hbm, normed_turned_hbm, x_hbm,
         ),
         (
-            cot_ref, resid_low_ref, own_low_ref, other_low_ref, resid_high_ref, own_high_ref, other_high_ref, qkv_ref,
-            cos_ref, sin_ref, allowed_ref, mixed_turned_ref, normed_turned_ref, x_ref,
+            cot_ref, resid_low_ref, own_low_ref, resid_high_ref, own_high_ref, qkv_ref, cos_ref, sin_ref, allowed_ref, mixed_turned_ref, normed_turned_ref, x_ref,
         ),
         token_sems,
     )
-    start_all(loads[:7])
+    start_all(loads[:5])
     wide_count = small_stage.shape[0]
     owner_rows = grads.shape[0] // wide_count
     small_stage[...] = jnp.zeros_like(small_stage)
     fetch_out(weight_rows_ref, weights, w_out, load_sems.at[1])
-    start_all(loads[7:])
+    start_all(loads[5:])
     fetch_qkv(weight_rows_ref, weights, w_qkv, load_sems.at[0])
     length = x_ref.shape[0]
     empty_count = rows_ref.shape[0] - BLOCK_TOTAL
@@ -599,8 +594,8 @@
     part = length // NARROW
     own_rows, other_rows = half_rows(half_ref, part)
     for first, resid_ref, own_ref, other_ref, needed in (
-        (0, resid_low_ref, own_low_ref, other_low_ref, loads[:4]),
-        (part, resid_high_ref, own_high_ref, other_high_ref, loads[4:7]),
+        (0, resid_low_ref, own_low_ref, other_low_ref, loads[:3]),
+        (part, resid_high_ref, own_high_ref, other_high_ref, loads[3:5]),
     ):
         wait_all(needed)
 
@@ -623,7 +618,7 @@
     wait_bytes(w_out, load_sems.at[1])
     for begin, size in spans(QUERY_WIDTH, COLS):
         grad_mixed[:, pl.ds(begin, size)] = dot_nt(grad_attention[...], w_out[pl.ds(begin, size), :]).astype(bf16)
-    wait_all(loads[7:11])
+    wait_all(loads[5:9])
     keys_turned = qkv_ref[:, pl.ds(QUERY_WIDTH, HEAD_DIM)].T
 
     def rope_back(vector):
@@ -651,7 +646,7 @@
         grad_qkv[:, columns] = rope_back(jnp.concatenate(grad_queries, axis=0)).astype(bf16)
     grad_qkv[:, pl.ds(QUERY_WIDTH, HEAD_DIM)] = rope_back(grad_keys[...] * scaling).astype(bf16)
     grad_qkv[:, pl.ds(QUERY_WIDTH + HEAD_DIM, HEAD_DIM)] = grad_values[...].astype(bf16)
-    wait_all(loads[11:])
+    wait_all(loads[9:])
 
     for begin, size in spans(D, COLS):
         out_stage[:, pl.ds(begin, size)] = dot_nn(
@@ -866,10 +861,9 @@
             shape((TILES, length, TILE), bf16),
             shape((TILES, TILE, length), bf16),
         ],
-        in_specs=[SMEM_SPEC, VMEM_SPEC] + [ANY_SPEC] * 5,
+        in_specs=[SMEM_SPEC, VMEM_SPEC, VMEM_SPEC] + [ANY_SPEC] * 4,
         out_specs=[VMEM_SPEC] + [ANY_SPEC] * 5,
         scratch_shapes=[
-            pltpu.VMEM((length, D), bf16),
             pltpu.VMEM((length, D), bf16),
             pltpu.VMEM((length, D), bf16),
             pltpu.VMEM((length, D), f32),
@@ -888,7 +882,7 @@
         compiler_params=params(),
         cost_estimate=hidden_cost(length, 4, 2 * TILES * TILE * (2 * D + 6 * length)),
         name="hidden_grads",
-    )(rows, gain, x, own, other, active_grad, weights)
+    )(rows, gain, in_vmem(other), x, own, active_grad, weights)
 
 
 def run_hidden_weight_grads(rows, cotangent, parts, slots):
@@ -921,8 +915,9 @@
     length = x.shape[0]
     shape = jax.ShapeDtypeStruct
     empty_count = max(rows.shape[0] - BLOCK_TOTAL, 1)
-    loaded = (*low, *high, cotangent, qkv, cosine, sine, allowed, mixed_turned, normed_turned, x)
-    operands = (weight_rows, rows, half, gains, log_total, *loaded, weights, grads)
+    (resid_low, own_low, other_low), (resid_high, own_high, other_high) = low, high
+    loaded = (resid_low, own_low, resid_high, own_high, cotangent, qkv, cosine, sine, allowed, mixed_turned, normed_turned, x)
+    operands = (weight_rows, rows, half, gains, log_total, in_vmem(other_low), in_vmem(other_high), *loaded, weights, grads)
     return pl.pallas_call(
         attention_backward,
         out_shape=[
@@ -931,7 +926,7 @@
             shape((length // NARROW, D), bf16),
             shape(grads.shape, bf16),
         ],
-        in_specs=[SMEM_SPEC] * 3 + [VMEM_SPEC] * 2 + [ANY_SPEC] * (len(loaded) + 2),
+        in_specs=[SMEM_SPEC] * 3 + [VMEM_SPEC] * 4 + [ANY_SPEC] * (len(loaded) + 2),
         out_specs=[VMEM_SPEC] * 3 + [ANY_SPEC],
         input_output_aliases={len(operands) - 1: 3},
         scratch_shapes=[pltpu.VMEM(array.shape, array.dtype) for array in loaded]
@@ -1588,6 +1583,10 @@
     return lax.ppermute(values, "narrow", [(0, 1), (1, 0)])
 
 
+def in_vmem(array):
+    return pltpu.with_memory_space_constraint(array, pltpu.VMEM)
+
+
 def body(
     tokens,
     cotangent,
@@ -1641,16 +1640,17 @@
     ).astype(f32)
     tokens_row = join_halves(tokens, swap_halves(tokens))
     cotangent_row = join_halves(cotangent, swap_halves(cotangent))
-    weights, tokens_row, cotangent_row = lax.optimization_barrier((weights, tokens_row, cotangent_row))
+    weights, tokens_row, cotangent_row, rows, gain_full, gain_one, gain_two = lax.optimization_barrier(
+        (weights, tokens_row, cotangent_row, rows, gain_full, gain_full[0:1], gain_full[1:2])
+    )
 
     low_part, high_part, normed_one_turned, qkv, mixed_turned, log_total = run_attention_forward(
-        weight_rows, tokens_row, gain_full[0:1], bias_full, cosine, sine, allowed_turned, weights
+        weight_rows, tokens_row, gain_one, bias_full, cosine, sine, allowed_turned, weights
     )
     low_other = swap_halves(low_part)
     active_grad, down_tiles = run_active_grads(weight_rows, cotangent_row, weights)
     high_sent, low_other = lax.optimization_barrier((high_part, low_other))
     high_other = swap_halves(high_sent)
-    gain_two = gain_full[1:2]
     grad_low, resid_low, turned_low, *hidden_low = run_hidden_grads(
         0, weight_rows, tokens_row, low_part, low_other, gain_two, active_grad, weights
     )
@@ -1673,7 +1673,7 @@
     blocks = [masters, first_moment, second_moment, left_basis, right_basis]
     if wide_count == 16:
         token_arrays = [
-            grad_resid, grad_one_own, grad_one_sent, tokens, gain_full[0:1], resid_low, resid_high, active_low,
+            grad_resid, grad_one_own, grad_one_sent, tokens, gain_one, resid_low, resid_high, active_low,
             active_high, down_tiles,
         ]
         block_grad, new_masters, new_first, new_second, input_grad, output, small_sums = run_write_results(

time: 668 us -> 665 us (level)
  transfers between devices with their start and end apart: 7 -> 7, of which waited for: 1 -> 2; matrix products, arithmetic and copies ran while one was open for 3% -> 3% of each run, Pallas kernels for 14% -> 14%
where the time goes in v8:
time: 665 us; the launch traced here: 658 us
  Pallas kernels  394 us (59%)
  waiting for transfers between devices  113 us (17%)
  blocking collectives  99.4 us (15%)
  other arithmetic  16 us (2%)
  between operations  15.2 us (2%)
  local copies, waits for them, and re-layouts  11.7 us (2%)
  starting transfers between devices  8.32 us (1%)
    pallas_call x1, Pallas kernels, run_sum_for_owners(): pl.pallas_call(functools.partial(sum_for_owners, line, steps, late_steps)...  255 us
    all_gather x1, waiting for transfers between devices, body(): weights = lax.all_gather(masters_low, 'wide', axis=0, tiled=True)  112 us
    unnamed x2, blocking collectives  99.4 us
    pallas_call x2, Pallas kernels, run_hidden_grads(): pl.pallas_call(functools.partial(hidden_grads, first_row), out_shape=[sha...  47.9 us
    pallas_call x1, Pallas kernels, run_hidden_weight_grads(): pl.pallas_call(hidden_weight_grads, out_shape=jax.ShapeDtypeStruct((slots...  28.4 us
    pallas_call x1, Pallas kernels, run_attention_backward(): pl.pallas_call(attention_backward, out_shape=[shape((length // NARROW, D)...  23.6 us
    pallas_call x1, Pallas kernels, run_active_grads(): pl.pallas_call(active_grads, out_shape=[jax.ShapeDtypeStruct((TILES, leng...  17 us
  transfers between devices with their start and end apart: 7, of which 2 were waited for; matrix products, arithmetic and copies ran while one was open for 3% of the time, Pallas kernels for 14%

profile of v8, /device:TPU:0, one launch (start us, length us, event | category | flops | bytes accessed | tf_op | source)
XLA Modules:
  0.0 658.1 jit_solution(16289114040507056705)
XLA Ops:
  7.2 0.0 copy-start.9
  7.2 0.0 copy-start
  7.2 0.0 copy-start.2
  7.2 0.0 all-gather.3.cloned.1.call-start
  7.3 5.0 convert_element_type.21
  12.3 0.0 all-gather.3.cloned.1.call-update
  12.3 0.0 copy-done
  12.3 3.0 collective-permute-start
  15.4 0.1 collective-permute-start.1
  15.4 0.9 compare_reduce_fusion
  16.3 0.1 add_select_fusion.1
  16.4 0.3 reduce-window.24
  16.7 0.1 slice.55
  16.9 0.3 reduce-window.16
  17.1 0.1 slice.60
  17.3 0.3 dynamic-update-slice
  17.5 68.2 %all-reduce.1 = f32[3072]{0:T(1024)S(1)} all-reduce(f32[3072]{0:T(1024)S(1)} %dynamic-update-slice), channel_id=1, replica_groups=mesh['wide'=16,'narrow'=2] {'wide','narrow'}, use_global_device_ids=true, to_apply=%add.1 | all-reduce | flops 3072 | bytes 24576
  85.8 0.1 slice_reduce_fusion.1
  85.9 0.1 slice_reduce_fusion
  86.0 0.1 fusion.8
  86.1 1.0 fusion.2
  87.1 1.0 pad_maximum_fusion
  88.1 0.1 add_bitcast_fusion
  88.2 0.7 constant_dynamic-slice_fusion.1
  89.0 0.6 reshape.141.gain_ref
  89.6 0.6 slice.50.gain_ref.gain
  90.2 0.6 slice.52.gain_ref
  90.8 0.6 dynamic-slice.1
  92.0 0.2 dynamic-update-slice.1
  92.2 31.2 %all-reduce.2 = bf16[1024]{0:T(1024)(128)(2,1)S(1)} all-reduce(bf16[1024]{0:T(1024)(128)(2,1)S(1)} %dynamic-update-slice.1), channel_id=2, replica_groups=mesh['wide'=16,'narrow'=2] {'wide'}, use_global_device_ids=true, to_apply=%add.2 | all-reduce | flops 1024 | bytes 4096
  123.4 0.6 reshape.169
  124.0 7.6 %scatter_custom_fusion.rows_ref.weight_rows_ref = s32[1440]{0:T(1024)S(1)} fusion(s32[1440]{0:T(1024)S(1)} %compare_select_fusion, s32[1440]{0:T(1024)S(1)} %iota.33, s32[]{:T(128)} %constant.33.clone.1), kind=kCustom, calls=%fused_computation.24 | custom fusion | bytes 5764 | tf_op jit(solution)/shard_map/scatter | solution.py:1631
  131.6 0.6 fusion.3.rows_ref
  132.2 1.1 fusion.1.allowed_hbm
  133.4 0.0 collective-permute-done
  133.4 1.8 maximum_select_fusion.x_hbm
  135.2 0.0 collective-permute-done.1
  135.2 1.8 maximum_select_fusion.1.cot_ref.cot_hbm
  137.0 112.0 %all-gather.3.cloned.1.call-done.weights = bf16[1440,128,128]{2,1,0:T(8,128)(2,1)} async-done(((bf16[90,128,128]{2,1,0:T(8,128)(2,1)}), bf16[1440,128,128]{2,1,0:T(8,128)(2,1)}) %all-gather.3.cloned.1.call-update) | async-done | bytes 47185936 | tf_op jit(solution)/shard_map/all_gather | solution.py:1622
  249.0 11.8 %attention_forward.1 = (bf16[256,1536]{1,0:T(8,128)(2,1)}, bf16[256,1536]{1,0:T(8,128)(2,1)}, f32[8,512]{1,0:T(8,128)}, bf16[1536,512]{1,0:T(8,128)(2,1)}, bf16[...) custom-call(s32[1440]{0:T(1024)} %copy-done.3, f32[1,1536]{1,0:T(1,128)} %slice.50.gain_ref.gain, f32[1,1024]{1,0:T(1,128)} %bitcast.26, ...), custom_call_target="tpu_custom_call" | custom-call | tf_op jit(solution)/shard_map/attention_forward/pallas_call | solution.py:795
  260.8 1.5 collective-permute-start.2
  262.4 17.0 %active_grads.1 = (f32[6,512,768]{2,1,0:T(8,128)}, bf16[6,768,1536]{2,1,0:T(8,128)(2,1)}) custom-call(s32[1440]{0:T(1024)} %copy-done.3, bf16[512,1536]{1,0:T(8,128)(2,1)} %maximum_select_fusion.1.cot_ref.cot_hbm, bf16[1440,128,128]{2,1,0:T(8,128)(2,1)} %all-gather.3.cloned.1.call-done.weights), custom_call_target="tpu_custom_call" | custom-call | flops 7247757312 | bytes 23592960 | tf_op jit(solution)/shard_map/active_grads/pallas_call | solution.py:830
  279.4 1.4 collective-permute-done.2.other_ref
  280.8 1.5 collective-permute-start.4
  282.3 24.0 %hidden_grads.2 = (bf16[256,1536]{1,0:T(8,128)(2,1)}, f32[256,1536]{1,0:T(8,128)}, bf16[1536,256]{1,0:T(8,128)(2,1)}, bf16[6,256,1536]{2,1,0:T(8,128)(2,1)}, bf1...) custom-call(s32[1440]{0:T(1024)} %copy-done.3, f32[1,1536]{1,0:T(1,128)} %slice.52.gain_ref, ...), custom_call_target="tpu_custom_call" | custom-call | flops 14495514624 | bytes 42467328 | tf_op jit(solution)/shard_map/hidden_grads/pallas_call | solution.py:854
  306.3 0.6 collective-permute-start.3
  306.9 0.0 collective-permute-done.4.other_ref
  306.9 23.9 %hidden_grads.3 = (bf16[256,1536]{1,0:T(8,128)(2,1)}, f32[256,1536]{1,0:T(8,128)}, bf16[1536,256]{1,0:T(8,128)(2,1)}, bf16[6,256,1536]{2,1,0:T(8,128)(2,1)}, bf1...) custom-call(s32[1440]{0:T(1024)} %copy-done.3, f32[1,1536]{1,0:T(1,128)} %slice.52.gain_ref, ...), custom_call_target="tpu_custom_call" | custom-call | flops 14495514624 | bytes 42467328 | tf_op jit(solution)/shard_map/hidden_grads/pallas_call | solution.py:854
  330.8 1.5 collective-permute-start.5
  332.4 28.4 %hidden_weight_grads.1.grads_in = bf16[1456,128,128]{2,1,0:T(8,128)(2,1)} custom-call(s32[1440]{0:T(1024)} %fusion.3.rows_ref, bf16[512,1536]{1,0:T(8,128)(2,1)} %maximum_select_fusion.1.cot_ref.cot_hbm, bf16[1536,256]{1,0:T(8,128)(2,1)} %get-tuple-element.88.refs_0_, bf16[6,256,1536]{2,1,0:T(8,128)(2,1)} %get-tuple-element.89.refs_1_, ...), custom_call_target="tpu_custom_call" | custom-call | flops 21743271936 | bytes 56623104 | tf_op jit(solution)/shard_map/hidden_weight_grads/pallas_call | solution.py:890
  360.8 0.0 collective-permute-done.3.other_low_ref
  360.8 0.0 collective-permute-done.5.other_high_ref
  360.8 23.6 %attention_backward.1 = (f32[256,1536]{1,0:T(8,128)}, bf16[256,1536]{1,0:T(8,128)(2,1)}, bf16[256,1536]{1,0:T(8,128)(2,1)}, bf16[1456,128,128]{2,1,0:T(8,128)(2,1)}) custom-call(s32[1440]{0:T(1024)} %copy-done.3, s32[1440]{0:T(1024)} %fusion.3.rows_ref, s32[1]{0:T(128)} %bitcast.2.half_ref, ...), custom_call_target="tpu_custom_call", output_to_operand_aliasing={{3}: (20, {})} | custom-call | tf_op jit(solution)/shard_map/attention_backward/pallas_call | solution.py:921
  384.4 254.6 %sum_for_owners.1 = (bf16[91,128,128]{2,1,0:T(8,128)(2,1)S(1)}, f32[90,128,128]{2,1,0:T(8,128)S(1)}, f32[90,128,128]{2,1,0:T(8,128)S(1)}, f32[90,128,128]{2,1,0:...) custom-call(bf16[4,2,2,91,128,128]{5,4,3,2,1,0:T(8,128)(2,1)} %bitca, ...), custom_call_target="tpu_custom_call" | custom-call | bytes 381681664 | tf_op jit(solution)/shard_map/sum_for_owners/pallas_call | solution.py:1448
  639.0 0.0 copy-start.6
  639.0 0.0 copy-start.7
  639.0 0.0 copy-start.8
  639.1 0.0 copy-start.10
  639.1 0.0 copy-start.11
  639.1 0.0 copy-start.12
  639.1 10.6 %write_results.1 = (f32[90,128,128]{2,1,0:T(8,128)}, f32[90,128,128]{2,1,0:T(8,128)}, f32[90,128,128]{2,1,0:T(8,128)}, f32[90,128,128]{2,1,0:T(8,128)}, f32[256,...) custom-call(bf16[91,128,128]{2,1,0:T(8,128)(2,1)S(1)} %get-tuple-element.101.reduced, ...), custom_call_target="tpu_custom_call" | custom-call | tf_op jit(solution)/shard_map/write_results/pallas_call | solution.py:1537
  649.8 0.6 divide_subtract_fusion
  650.4 0.0 copy-done.12
  650.4 0.6 divide_subtract_fusion.1
  (30 shorter events, 0.2 us)
Async XLA Ops:
  7.2 10.1 %copy-start.9 = (f32[96]{0:T(128)S(1)}, f32[96]{0:T(128)}, u32[]{:S(2)}) copy-start(f32[96]{0:T(128)} %param.24) | copy-start | bytes 1156
  7.2 5.1 copy-start
  7.2 8.2 %copy-start.2 = (bf16[256,1536]{1,0:T(8,128)(2,1)S(1)}, bf16[256,1536]{1,0:T(8,128)(2,1)}, u32[]{:S(2)}) copy-start(bf16[256,1536]{1,0:T(8,128)(2,1)} %param.16) | copy-start | bytes 2359300
  7.2 9.6 %copy-start.4 = (s32[1440]{0:T(1024)S(1)}, s32[1440]{0:T(1024)}, u32[]{:S(2)}) copy-start(s32[1440]{0:T(1024)} %param.18) | copy-start | bytes 17284
  7.2 241.8 %all-gather.3.cloned.1.call-start = ((), (), s32[]{:S(2)}) async-start(), calls=%async_computation | async-start | bytes 50135040 | tf_op jit(solution)/shard_map/all_gather | solution.py:1622
  12.3 75.9 %copy-start.5 = (f32[1,64]{1,0:T(1,128)S(1)}, f32[1,64]{1,0:T(1,128)}, u32[]{:S(2)}) copy-start(f32[1,64]{1,0:T(1,128)} %param.27) | copy-start | bytes 772
  12.3 78.5 %copy-start.13 = (u32[32]{0:T(128)S(1)}, u32[32]{0:T(128)}, u32[]{:S(2)}) copy-start(u32[32]{0:T(128)} %constant.116) | copy-start | bytes 388
  12.3 121.1 %collective-permute-start = (bf16[256,1536]{1,0:T(8,128)(2,1)S(1)}, bf16[256,1536]{1,0:T(8,128)(2,1)S(1)}, u32[]{:S(2)}, u32[]{:S(2)}) collective-permute-start(bf16[256,1536]{1,0:T(8,128)(2,1)S(1)} %copy-done), channel_id=1, source_target_pairs={{0,1},{1,0},{2,3},{3,2},{4,5},{5,4},{6,7},{7,6},{8,9},{9,8},{10,11... | collective-permute-start | bytes 2359304 | tf_op jit(solution)/shard_map/ppermute | solution.py:1583
  15.4 119.8 %collective-permute-start.1 = (bf16[256,1536]{1,0:T(8,128)(2,1)S(1)}, bf16[256,1536]{1,0:T(8,128)(2,1)S(1)}, u32[]{:S(2)}, u32[]{:S(2)}) collective-permute-start(bf16[256,1536]{1,0:T(8,128)(2,1)S(1)} %copy-done.2), channel_id=1, source_target_pairs={{0,1},{1,0},{2,3},{3,2},{4,5},{5,4},{6,7},{7,6},{8,9},{9,8},{10,11... | collective-permute-start | bytes 2359304 | tf_op jit(solution)/shard_map/ppermute | solution.py:1583
  131.6 5.4 copy-start.3
  260.8 20.0 %collective-permute-start.2 = (bf16[256,1536]{1,0:T(8,128)(2,1)}, bf16[256,1536]{1,0:T(8,128)(2,1)S(1)}, u32[]{:S(2)}, u32[]{:S(2)}) collective-permute-start(bf16[256,1536]{1,0:T(8,128)(2,1)} %get-tuple-element.76.own_hbm), channel_id=1, source_target_pairs={{0,1},{1,0},{2,3},{3,2},{4,5},{5,4},{6,7},{7,6},{8,9},{9,8},{10,11... | collective-permute-start | bytes 2359304 | tf_op jit(solution)/shard_map/ppermute | solution.py:1583
  262.4 18.4 %copy-start.1 = (bf16[256,1536]{1,0:T(8,128)(2,1)S(1)}, bf16[256,1536]{1,0:T(8,128)(2,1)}, u32[]{:S(2)}) copy-start(bf16[256,1536]{1,0:T(8,128)(2,1)} %get-tuple-element.81.own_hbm) | copy-start | bytes 2359300
  280.8 26.1 %collective-permute-start.4 = (bf16[256,1536]{1,0:T(8,128)(2,1)S(1)}, bf16[256,1536]{1,0:T(8,128)(2,1)S(1)}, u32[]{:S(2)}, u32[]{:S(2)}) collective-permute-start(bf16[256,1536]{1,0:T(8,128)(2,1)S(1)} %copy-done.1), channel_id=1, source_target_pairs={{0,1},{1,0},{2,3},{3,2},{4,5},{5,4},{6,7},{7,6},{8,9},{9,8},{10,11... | collective-permute-start | bytes 2359304 | tf_op jit(solution)/shard_map/ppermute | solution.py:1583
  306.3 54.5 %collective-permute-start.3 = (bf16[256,1536]{1,0:T(8,128)(2,1)}, bf16[256,1536]{1,0:T(8,128)(2,1)S(1)}, u32[]{:S(2)}, u32[]{:S(2)}) collective-permute-start(bf16[256,1536]{1,0:T(8,128)(2,1)} %get-tuple-element.80.own_low_hbm), channel_id=1, source_target_pairs={{0,1},{1,0},{2,3},{3,2},{4,5},{5,4},{6,7},{7,6},{8,9},{9,8},{10,11... | collective-permute-start | bytes 2359304 | tf_op jit(solution)/shard_map/ppermute | solution.py:1583
  330.8 30.0 %collective-permute-start.5 = (bf16[256,1536]{1,0:T(8,128)(2,1)}, bf16[256,1536]{1,0:T(8,128)(2,1)S(1)}, u32[]{:S(2)}, u32[]{:S(2)}) collective-permute-start(bf16[256,1536]{1,0:T(8,128)(2,1)} %get-tuple-element.82.own_high_hbm), channel_id=1, source_target_pairs={{0,1},{1,0},{2,3},{3,2},{4,5},{5,4},{6,7},{7,6},{8,9},{9,8},{10,11... | collective-permute-start | bytes 2359304 | tf_op jit(solution)/shard_map/ppermute | solution.py:1583
  639.0 10.7 %copy-start.6 = (f32[1,64]{1,0:T(1,128)S(1)}, f32[1,64]{1,0:T(1,128)}, u32[]{:S(2)}) copy-start(f32[1,64]{1,0:T(1,128)} %param.27) | copy-start | bytes 772
  639.0 10.7 %copy-start.7 = (f32[1,64]{1,0:T(1,128)S(1)}, f32[1,64]{1,0:T(1,128)}, u32[]{:S(2)}) copy-start(f32[1,64]{1,0:T(1,128)} %param.28) | copy-start | bytes 772
  639.0 10.7 %copy-start.8 = (f32[1,64]{1,0:T(1,128)S(1)}, f32[1,64]{1,0:T(1,128)}, u32[]{:S(2)}) copy-start(f32[1,64]{1,0:T(1,128)} %param.29) | copy-start | bytes 772
  639.1 11.3 %copy-start.10 = (f32[96]{0:T(128)S(1)}, f32[96]{0:T(128)}, u32[]{:S(2)}) copy-start(f32[96]{0:T(128)} %param.24) | copy-start | bytes 1156
  639.1 11.3 %copy-start.11 = (f32[96]{0:T(128)S(1)}, f32[96]{0:T(128)}, u32[]{:S(2)}) copy-start(f32[96]{0:T(128)} %param.25) | copy-start | bytes 1156
  639.1 11.3 %copy-start.12 = (f32[96]{0:T(128)S(1)}, f32[96]{0:T(128)}, u32[]{:S(2)}) copy-start(f32[96]{0:T(128)} %param.26) | copy-start | bytes 1156
Sparse Core Ops, SparseCore 0:
  12.4 236.5 all-gather.2

commit v9 on v8

--- a/solution.py
+++ b/solution.py
@@ -788,6 +788,38 @@
     return pltpu.CompilerParams(vmem_limit_bytes=limit, **options)
 
 
+def cast_blocks(source, out, wide, low, load_sems, store_sems):
+    parts = load_sems.shape[0]
+    group = source.shape[0] // parts
+    places = [pl.ds(part * group, group) for part in range(parts)]
+    loads = copies_between([source.at[place] for place in places], [wide.at[place] for place in places], load_sems)
+    stores = copies_between([low.at[place] for place in places], [out.at[place] for place in places], store_sems)
+    start_all(loads)
+    for place, load, store in zip(places, loads, stores):
+        load.wait()
+        low[place] = wide[place].astype(bf16)
+        store.start()
+    wait_all(stores)
+
+
+def run_cast(blocks):
+    parts = blocks.shape[0] // largest_group(blocks.shape[0])
+    return pl.pallas_call(
+        cast_blocks,
+        out_shape=jax.ShapeDtypeStruct(blocks.shape, bf16),
+        in_specs=[ANY_SPEC],
+        out_specs=ANY_SPEC,
+        scratch_shapes=[
+            pltpu.VMEM(blocks.shape, f32),
+            pltpu.VMEM(blocks.shape, bf16),
+            pltpu.SemaphoreType.DMA((parts,)),
+            pltpu.SemaphoreType.DMA((parts,)),
+        ],
+        compiler_params=params(),
+        name="cast_blocks",
+    )(blocks)
+
+
 def run_attention_forward(rows, x, gain, bias, cosine, sine, allowed, weights):
     length = x.shape[0]
     shape = jax.ShapeDtypeStruct
@@ -1618,7 +1650,7 @@
             half == 0, jnp.concatenate([own, other], axis=axis), jnp.concatenate([other, own], axis=axis)
         )
 
-    masters_low, gains, biases = lax.optimization_barrier((masters.astype(bf16), gains, biases))
+    masters_low, gains, biases = lax.optimization_barrier((run_cast(masters), gains, biases))
     weights = lax.all_gather(masters_low, "wide", axis=0, tiled=True)
     gain_full = lax.all_gather(gains, ("wide", "narrow"), axis=0, tiled=True).reshape(2, D)
     bias_full = lax.all_gather(biases.reshape(-1).astype(bf16), "wide", axis=0, tiled=True)

time: 665 us -> 664 us (level)
  no operation moved by 1% of the time
where the time goes in v9:
time: 664 us; the launch traced here: 657 us
  Pallas kernels  398 us (60%)
  waiting for transfers between devices  113 us (17%)
  blocking collectives  99.4 us (15%)
  between operations  15.2 us (2%)
  local copies, waits for them, and re-layouts  11.7 us (2%)
  other arithmetic  11 us (2%)
  starting transfers between devices  8.31 us (1%)
    pallas_call x1, Pallas kernels, run_sum_for_owners(): pl.pallas_call(functools.partial(sum_for_owners, line, steps, late_steps)...  255 us
    all_gather x1, waiting for transfers between devices, body(): weights = lax.all_gather(masters_low, 'wide', axis=0, tiled=True)  112 us
    unnamed x2, blocking collectives  99.4 us
    pallas_call x2, Pallas kernels, run_hidden_grads(): pl.pallas_call(functools.partial(hidden_grads, first_row), out_shape=[sha...  47.9 us
    pallas_call x1, Pallas kernels, run_hidden_weight_grads(): pl.pallas_call(hidden_weight_grads, out_shape=jax.ShapeDtypeStruct((slots...  28.4 us
    pallas_call x1, Pallas kernels, run_attention_backward(): pl.pallas_call(attention_backward, out_shape=[shape((length // NARROW, D)...  23.6 us
    pallas_call x1, Pallas kernels, run_active_grads(): pl.pallas_call(active_grads, out_shape=[jax.ShapeDtypeStruct((TILES, leng...  17 us
  transfers between devices with their start and end apart: 7, of which 2 were waited for; matrix products, arithmetic and copies ran while one was open for 3% of the time, Pallas kernels for 14%

profile of v9, /device:TPU:0, one launch (start us, length us, event | category | flops | bytes accessed | tf_op | source)
XLA Modules:
  0.0 657.4 jit_solution(11256058322966370568)
XLA Ops:
  7.2 0.0 copy-start.9
  7.2 0.0 copy-start
  7.2 0.0 all-gather.3.cloned.1.call-start
  7.3 4.4 cast_blocks.1
  11.7 0.0 copy-start.5
  11.7 0.0 copy-start.13
  11.7 0.0 all-gather.3.cloned.1.call-update
  11.7 3.0 collective-permute-start
  14.8 0.0 copy-done.2
  14.8 0.1 collective-permute-start.1
  14.9 0.9 compare_reduce_fusion
  15.7 0.1 add_select_fusion.1
  15.8 0.3 reduce-window.24
  16.1 0.1 slice.55
  16.3 0.3 reduce-window.16
  16.5 0.1 slice.60
  16.7 0.3 dynamic-update-slice
  17.0 68.2 %all-reduce.1 = f32[3072]{0:T(1024)S(1)} all-reduce(f32[3072]{0:T(1024)S(1)} %dynamic-update-slice), channel_id=1, replica_groups=mesh['wide'=16,'narrow'=2] {'wide','narrow'}, use_global_device_ids=true, to_apply=%add.1 | all-reduce | flops 3072 | bytes 24576
  85.2 0.1 slice_reduce_fusion.1
  85.3 0.1 slice_reduce_fusion
  85.4 0.1 fusion.8
  85.5 1.0 fusion.2
  86.5 1.0 pad_maximum_fusion
  87.5 0.1 add_bitcast_fusion
  87.6 0.7 constant_dynamic-slice_fusion.1
  88.4 0.6 reshape.141.gain_ref
  89.0 0.6 slice.50.gain_ref.gain
  89.6 0.6 slice.52.gain_ref
  90.2 0.6 dynamic-slice.1
  91.4 0.2 dynamic-update-slice.1
  91.7 31.2 %all-reduce.2 = bf16[1024]{0:T(1024)(128)(2,1)S(1)} all-reduce(bf16[1024]{0:T(1024)(128)(2,1)S(1)} %dynamic-update-slice.1), channel_id=2, replica_groups=mesh['wide'=16,'narrow'=2] {'wide'}, use_global_device_ids=true, to_apply=%add.2 | all-reduce | flops 1024 | bytes 4096
  122.8 0.6 reshape.169
  123.4 7.6 %scatter_custom_fusion.rows_ref.weight_rows_ref = s32[1440]{0:T(1024)S(1)} fusion(s32[1440]{0:T(1024)S(1)} %compare_select_fusion, s32[1440]{0:T(1024)S(1)} %iota.33, s32[]{:T(128)} %constant.33.clone.1), kind=kCustom, calls=%fused_computation.24 | custom fusion | bytes 5764 | tf_op jit(solution)/shard_map/scatter | solution.py:1663
  131.0 0.6 fusion.3.rows_ref
  131.7 1.1 fusion.1.allowed_hbm
  132.8 0.0 collective-permute-done
  132.8 1.8 maximum_select_fusion.x_hbm
  134.6 0.0 collective-permute-done.1
  134.6 1.8 maximum_select_fusion.1.cot_ref.cot_hbm
  136.4 112.0 %all-gather.3.cloned.1.call-done.weights = bf16[1440,128,128]{2,1,0:T(8,128)(2,1)} async-done(((bf16[90,128,128]{2,1,0:T(8,128)(2,1)}), bf16[1440,128,128]{2,1,0:T(8,128)(2,1)}) %all-gather.3.cloned.1.call-update) | async-done | bytes 47185936 | tf_op jit(solution)/shard_map/all_gather | solution.py:1654
  248.4 11.8 %attention_forward.1 = (bf16[256,1536]{1,0:T(8,128)(2,1)}, bf16[256,1536]{1,0:T(8,128)(2,1)}, f32[8,512]{1,0:T(8,128)}, bf16[1536,512]{1,0:T(8,128)(2,1)}, bf16[...) custom-call(s32[1440]{0:T(1024)} %copy-done.3, f32[1,1536]{1,0:T(1,128)} %slice.50.gain_ref.gain, f32[1,1024]{1,0:T(1,128)} %bitcast.26, ...), custom_call_target="tpu_custom_call" | custom-call | tf_op jit(solution)/shard_map/attention_forward/pallas_call | solution.py:827
  260.2 1.5 collective-permute-start.2
  261.7 17.0 %active_grads.1 = (f32[6,512,768]{2,1,0:T(8,128)}, bf16[6,768,1536]{2,1,0:T(8,128)(2,1)}) custom-call(s32[1440]{0:T(1024)} %copy-done.3, bf16[512,1536]{1,0:T(8,128)(2,1)} %maximum_select_fusion.1.cot_ref.cot_hbm, bf16[1440,128,128]{2,1,0:T(8,128)(2,1)} %all-gather.3.cloned.1.call-done.weights), custom_call_target="tpu_custom_call" | custom-call | flops 7247757312 | bytes 23592960 | tf_op jit(solution)/shard_map/active_grads/pallas_call | solution.py:862
  278.8 1.4 collective-permute-done.2.other_ref
  280.2 1.5 collective-permute-start.4
  281.7 24.0 %hidden_grads.2 = (bf16[256,1536]{1,0:T(8,128)(2,1)}, f32[256,1536]{1,0:T(8,128)}, bf16[1536,256]{1,0:T(8,128)(2,1)}, bf16[6,256,1536]{2,1,0:T(8,128)(2,1)}, bf1...) custom-call(s32[1440]{0:T(1024)} %copy-done.3, f32[1,1536]{1,0:T(1,128)} %slice.52.gain_ref, ...), custom_call_target="tpu_custom_call" | custom-call | flops 14495514624 | bytes 42467328 | tf_op jit(solution)/shard_map/hidden_grads/pallas_call | solution.py:886
  305.7 0.6 collective-permute-start.3
  306.3 0.0 collective-permute-done.4.other_ref
  306.3 23.9 %hidden_grads.3 = (bf16[256,1536]{1,0:T(8,128)(2,1)}, f32[256,1536]{1,0:T(8,128)}, bf16[1536,256]{1,0:T(8,128)(2,1)}, bf16[6,256,1536]{2,1,0:T(8,128)(2,1)}, bf1...) custom-call(s32[1440]{0:T(1024)} %copy-done.3, f32[1,1536]{1,0:T(1,128)} %slice.52.gain_ref, ...), custom_call_target="tpu_custom_call" | custom-call | flops 14495514624 | bytes 42467328 | tf_op jit(solution)/shard_map/hidden_grads/pallas_call | solution.py:886
  330.2 1.5 collective-permute-start.5
  331.7 28.4 %hidden_weight_grads.1.grads_in = bf16[1456,128,128]{2,1,0:T(8,128)(2,1)} custom-call(s32[1440]{0:T(1024)} %fusion.3.rows_ref, bf16[512,1536]{1,0:T(8,128)(2,1)} %maximum_select_fusion.1.cot_ref.cot_hbm, bf16[1536,256]{1,0:T(8,128)(2,1)} %get-tuple-element.88.refs_0_, bf16[6,256,1536]{2,1,0:T(8,128)(2,1)} %get-tuple-element.89.refs_1_, ...), custom_call_target="tpu_custom_call" | custom-call | flops 21743271936 | bytes 56623104 | tf_op jit(solution)/shard_map/hidden_weight_grads/pallas_call | solution.py:922
  360.2 0.0 collective-permute-done.3.other_low_ref
  360.2 0.0 collective-permute-done.5.other_high_ref
  360.2 23.6 %attention_backward.1 = (f32[256,1536]{1,0:T(8,128)}, bf16[256,1536]{1,0:T(8,128)(2,1)}, bf16[256,1536]{1,0:T(8,128)(2,1)}, bf16[1456,128,128]{2,1,0:T(8,128)(2,1)}) custom-call(s32[1440]{0:T(1024)} %copy-done.3, s32[1440]{0:T(1024)} %fusion.3.rows_ref, s32[1]{0:T(128)} %bitcast.2.half_ref, ...), custom_call_target="tpu_custom_call", output_to_operand_aliasing={{3}: (20, {})} | custom-call | tf_op jit(solution)/shard_map/attention_backward/pallas_call | solution.py:953
  383.8 254.6 %sum_for_owners.1 = (bf16[91,128,128]{2,1,0:T(8,128)(2,1)S(1)}, f32[90,128,128]{2,1,0:T(8,128)S(1)}, f32[90,128,128]{2,1,0:T(8,128)S(1)}, f32[90,128,128]{2,1,0:...) custom-call(bf16[4,2,2,91,128,128]{5,4,3,2,1,0:T(8,128)(2,1)} %bitca, ...), custom_call_target="tpu_custom_call" | custom-call | bytes 381681664 | tf_op jit(solution)/shard_map/sum_for_owners/pallas_call | solution.py:1480
  638.4 0.0 copy-start.6
  638.4 0.0 copy-start.7
  638.4 0.0 copy-start.8
  638.4 0.0 copy-start.10
  638.4 0.0 copy-start.11
  638.4 0.0 copy-start.12
  638.4 10.6 %write_results.1 = (f32[90,128,128]{2,1,0:T(8,128)}, f32[90,128,128]{2,1,0:T(8,128)}, f32[90,128,128]{2,1,0:T(8,128)}, f32[90,128,128]{2,1,0:T(8,128)}, f32[256,...) custom-call(bf16[91,128,128]{2,1,0:T(8,128)(2,1)S(1)} %get-tuple-element.101.reduced, ...), custom_call_target="tpu_custom_call" | custom-call | tf_op jit(solution)/shard_map/write_results/pallas_call | solution.py:1569
  649.1 0.6 divide_subtract_fusion
  649.8 0.6 divide_subtract_fusion.1
  (30 shorter events, 0.2 us)
Async XLA Ops:
  7.2 9.5 %copy-start.9 = (f32[96]{0:T(128)S(1)}, f32[96]{0:T(128)}, u32[]{:S(2)}) copy-start(f32[96]{0:T(128)} %param.24) | copy-start | bytes 1156
  7.2 4.5 copy-start
  7.2 7.6 %copy-start.2 = (bf16[256,1536]{1,0:T(8,128)(2,1)S(1)}, bf16[256,1536]{1,0:T(8,128)(2,1)}, u32[]{:S(2)}) copy-start(bf16[256,1536]{1,0:T(8,128)(2,1)} %param.16) | copy-start | bytes 2359300
  7.2 9.0 %copy-start.4 = (s32[1440]{0:T(1024)S(1)}, s32[1440]{0:T(1024)}, u32[]{:S(2)}) copy-start(s32[1440]{0:T(1024)} %param.18) | copy-start | bytes 17284
  7.2 241.2 %all-gather.3.cloned.1.call-start = ((), (), s32[]{:S(2)}) async-start(), calls=%async_computation | async-start | bytes 50135040 | tf_op jit(solution)/shard_map/all_gather | solution.py:1654
  11.7 76.0 %copy-start.5 = (f32[1,64]{1,0:T(1,128)S(1)}, f32[1,64]{1,0:T(1,128)}, u32[]{:S(2)}) copy-start(f32[1,64]{1,0:T(1,128)} %param.27) | copy-start | bytes 772
  11.7 78.5 %copy-start.13 = (u32[32]{0:T(128)S(1)}, u32[32]{0:T(128)}, u32[]{:S(2)}) copy-start(u32[32]{0:T(128)} %constant.116) | copy-start | bytes 388
  11.7 121.1 %collective-permute-start = (bf16[256,1536]{1,0:T(8,128)(2,1)S(1)}, bf16[256,1536]{1,0:T(8,128)(2,1)S(1)}, u32[]{:S(2)}, u32[]{:S(2)}) collective-permute-start(bf16[256,1536]{1,0:T(8,128)(2,1)S(1)} %copy-done), channel_id=1, source_target_pairs={{0,1},{1,0},{2,3},{3,2},{4,5},{5,4},{6,7},{7,6},{8,9},{9,8},{10,11... | collective-permute-start | bytes 2359304 | tf_op jit(solution)/shard_map/ppermute | solution.py:1615
  14.8 119.8 %collective-permute-start.1 = (bf16[256,1536]{1,0:T(8,128)(2,1)S(1)}, bf16[256,1536]{1,0:T(8,128)(2,1)S(1)}, u32[]{:S(2)}, u32[]{:S(2)}) collective-permute-start(bf16[256,1536]{1,0:T(8,128)(2,1)S(1)} %copy-done.2), channel_id=1, source_target_pairs={{0,1},{1,0},{2,3},{3,2},{4,5},{5,4},{6,7},{7,6},{8,9},{9,8},{10,11... | collective-permute-start | bytes 2359304 | tf_op jit(solution)/shard_map/ppermute | solution.py:1615
  131.0 5.4 copy-start.3
  260.2 20.0 %collective-permute-start.2 = (bf16[256,1536]{1,0:T(8,128)(2,1)}, bf16[256,1536]{1,0:T(8,128)(2,1)S(1)}, u32[]{:S(2)}, u32[]{:S(2)}) collective-permute-start(bf16[256,1536]{1,0:T(8,128)(2,1)} %get-tuple-element.76.own_hbm), channel_id=1, source_target_pairs={{0,1},{1,0},{2,3},{3,2},{4,5},{5,4},{6,7},{7,6},{8,9},{9,8},{10,11... | collective-permute-start | bytes 2359304 | tf_op jit(solution)/shard_map/ppermute | solution.py:1615
  261.7 18.4 %copy-start.1 = (bf16[256,1536]{1,0:T(8,128)(2,1)S(1)}, bf16[256,1536]{1,0:T(8,128)(2,1)}, u32[]{:S(2)}) copy-start(bf16[256,1536]{1,0:T(8,128)(2,1)} %get-tuple-element.81.own_hbm) | copy-start | bytes 2359300
  280.2 26.1 %collective-permute-start.4 = (bf16[256,1536]{1,0:T(8,128)(2,1)S(1)}, bf16[256,1536]{1,0:T(8,128)(2,1)S(1)}, u32[]{:S(2)}, u32[]{:S(2)}) collective-permute-start(bf16[256,1536]{1,0:T(8,128)(2,1)S(1)} %copy-done.1), channel_id=1, source_target_pairs={{0,1},{1,0},{2,3},{3,2},{4,5},{5,4},{6,7},{7,6},{8,9},{9,8},{10,11... | collective-permute-start | bytes 2359304 | tf_op jit(solution)/shard_map/ppermute | solution.py:1615
  305.7 54.5 %collective-permute-start.3 = (bf16[256,1536]{1,0:T(8,128)(2,1)}, bf16[256,1536]{1,0:T(8,128)(2,1)S(1)}, u32[]{:S(2)}, u32[]{:S(2)}) collective-permute-start(bf16[256,1536]{1,0:T(8,128)(2,1)} %get-tuple-element.80.own_low_hbm), channel_id=1, source_target_pairs={{0,1},{1,0},{2,3},{3,2},{4,5},{5,4},{6,7},{7,6},{8,9},{9,8},{10,11... | collective-permute-start | bytes 2359304 | tf_op jit(solution)/shard_map/ppermute | solution.py:1615
  330.2 30.0 %collective-permute-start.5 = (bf16[256,1536]{1,0:T(8,128)(2,1)}, bf16[256,1536]{1,0:T(8,128)(2,1)S(1)}, u32[]{:S(2)}, u32[]{:S(2)}) collective-permute-start(bf16[256,1536]{1,0:T(8,128)(2,1)} %get-tuple-element.82.own_high_hbm), channel_id=1, source_target_pairs={{0,1},{1,0},{2,3},{3,2},{4,5},{5,4},{6,7},{7,6},{8,9},{9,8},{10,11... | collective-permute-start | bytes 2359304 | tf_op jit(solution)/shard_map/ppermute | solution.py:1615
  638.4 10.7 %copy-start.6 = (f32[1,64]{1,0:T(1,128)S(1)}, f32[1,64]{1,0:T(1,128)}, u32[]{:S(2)}) copy-start(f32[1,64]{1,0:T(1,128)} %param.27) | copy-start | bytes 772
  638.4 10.7 %copy-start.7 = (f32[1,64]{1,0:T(1,128)S(1)}, f32[1,64]{1,0:T(1,128)}, u32[]{:S(2)}) copy-start(f32[1,64]{1,0:T(1,128)} %param.28) | copy-start | bytes 772
  638.4 10.7 %copy-start.8 = (f32[1,64]{1,0:T(1,128)S(1)}, f32[1,64]{1,0:T(1,128)}, u32[]{:S(2)}) copy-start(f32[1,64]{1,0:T(1,128)} %param.29) | copy-start | bytes 772
  638.4 11.3 %copy-start.10 = (f32[96]{0:T(128)S(1)}, f32[96]{0:T(128)}, u32[]{:S(2)}) copy-start(f32[96]{0:T(128)} %param.24) | copy-start | bytes 1156
  638.4 11.3 %copy-start.11 = (f32[96]{0:T(128)S(1)}, f32[96]{0:T(128)}, u32[]{:S(2)}) copy-start(f32[96]{0:T(128)} %param.25) | copy-start | bytes 1156
  638.4 11.3 %copy-start.12 = (f32[96]{0:T(128)S(1)}, f32[96]{0:T(128)}, u32[]{:S(2)}) copy-start(f32[96]{0:T(128)} %param.26) | copy-start | bytes 1156
Sparse Core Ops, SparseCore 0:
  11.8 236.5 all-gather.2

commit v10 on v9

--- a/solution.py
+++ b/solution.py
@@ -53,7 +53,7 @@
 LAST_BLOCKS = HIDDEN_COLS - (TILES - 1) * TILE_BLOCKS
 TILE = TILE_BLOCKS * BLK
 COLS = 256
-ROWS = 64
+ROWS = 128
 SMALL_ROWS = 16
 VMEM_LIMIT = 60 * 2**20
 SUM_VMEM = 39 * 2**20

time: 664 us -> 664 us (level)
  no operation moved by 1% of the time
where the time goes in v10:
time: 664 us; the launch traced here: 657 us
  Pallas kernels  398 us (60%)
  waiting for transfers between devices  113 us (17%)
  blocking collectives  99.4 us (15%)
  between operations  15.3 us (2%)
  local copies, waits for them, and re-layouts  11.7 us (2%)
  other arithmetic  11 us (2%)
  starting transfers between devices  8.33 us (1%)
    pallas_call x1, Pallas kernels, run_sum_for_owners(): pl.pallas_call(functools.partial(sum_for_owners, line, steps, late_steps)...  255 us
    all_gather x1, waiting for transfers between devices, body(): weights = lax.all_gather(masters_low, 'wide', axis=0, tiled=True)  112 us
    unnamed x2, blocking collectives  99.4 us
    pallas_call x2, Pallas kernels, run_hidden_grads(): pl.pallas_call(functools.partial(hidden_grads, first_row), out_shape=[sha...  48 us
    pallas_call x1, Pallas kernels, run_hidden_weight_grads(): pl.pallas_call(hidden_weight_grads, out_shape=jax.ShapeDtypeStruct((slots...  28.2 us
    pallas_call x1, Pallas kernels, run_attention_backward(): pl.pallas_call(attention_backward, out_shape=[shape((length // NARROW, D)...  23.4 us
    pallas_call x1, Pallas kernels, run_active_grads(): pl.pallas_call(active_grads, out_shape=[jax.ShapeDtypeStruct((TILES, leng...  17.1 us
  transfers between devices with their start and end apart: 7, of which 2 were waited for; matrix products, arithmetic and copies ran while one was open for 3% of the time, Pallas kernels for 14%

profile of v10, /device:TPU:0, one launch (start us, length us, event | category | flops | bytes accessed | tf_op | source)
XLA Modules:
  0.0 657.2 jit_solution(5810151700840213655)
XLA Ops:
  7.2 0.0 copy-start.9
  7.2 0.0 copy-start
  7.2 0.0 all-gather.3.cloned.1.call-start
  7.3 4.4 cast_blocks.1
  11.7 0.0 copy-start.5
  11.7 0.0 copy-start.13
  11.7 0.0 all-gather.3.cloned.1.call-update
  11.7 3.0 collective-permute-start
  14.8 0.0 copy-done.2
  14.8 0.1 collective-permute-start.1
  14.9 0.9 compare_reduce_fusion
  15.7 0.1 add_select_fusion.1
  15.8 0.3 reduce-window.24
  16.1 0.1 slice.55
  16.3 0.3 reduce-window.16
  16.5 0.1 slice.60
  16.7 0.3 dynamic-update-slice
  17.0 68.2 %all-reduce.1 = f32[3072]{0:T(1024)S(1)} all-reduce(f32[3072]{0:T(1024)S(1)} %dynamic-update-slice), channel_id=1, replica_groups=mesh['wide'=16,'narrow'=2] {'wide','narrow'}, use_global_device_ids=true, to_apply=%add.1 | all-reduce | flops 3072 | bytes 24576
  85.2 0.1 slice_reduce_fusion.1
  85.3 0.1 slice_reduce_fusion
  85.4 0.1 fusion.8
  85.5 1.0 fusion.2
  86.5 1.0 pad_maximum_fusion
  87.5 0.1 add_bitcast_fusion
  87.6 0.7 constant_dynamic-slice_fusion.1
  88.4 0.6 reshape.141.gain_ref
  89.0 0.6 slice.50.gain_ref.gain
  89.6 0.6 slice.52.gain_ref
  90.2 0.6 dynamic-slice.1
  91.4 0.2 dynamic-update-slice.1
  91.7 31.2 %all-reduce.2 = bf16[1024]{0:T(1024)(128)(2,1)S(1)} all-reduce(bf16[1024]{0:T(1024)(128)(2,1)S(1)} %dynamic-update-slice.1), channel_id=2, replica_groups=mesh['wide'=16,'narrow'=2] {'wide'}, use_global_device_ids=true, to_apply=%add.2 | all-reduce | flops 1024 | bytes 4096
  122.8 0.6 reshape.169
  123.4 7.6 %scatter_custom_fusion.rows_ref.weight_rows_ref = s32[1440]{0:T(1024)S(1)} fusion(s32[1440]{0:T(1024)S(1)} %compare_select_fusion, s32[1440]{0:T(1024)S(1)} %iota.33, s32[]{:T(128)} %constant.33.clone.1), kind=kCustom, calls=%fused_computation.24 | custom fusion | bytes 5764 | tf_op jit(solution)/shard_map/scatter | solution.py:1663
  131.0 0.6 fusion.3.rows_ref
  131.7 1.1 fusion.1.allowed_hbm
  132.8 0.0 collective-permute-done
  132.8 1.8 maximum_select_fusion.x_hbm
  134.6 0.0 collective-permute-done.1
  134.6 1.8 maximum_select_fusion.1.cot_ref.cot_hbm
  136.4 112.0 %all-gather.3.cloned.1.call-done.weights = bf16[1440,128,128]{2,1,0:T(8,128)(2,1)} async-done(((bf16[90,128,128]{2,1,0:T(8,128)(2,1)}), bf16[1440,128,128]{2,1,0:T(8,128)(2,1)}) %all-gather.3.cloned.1.call-update) | async-done | bytes 47185936 | tf_op jit(solution)/shard_map/all_gather | solution.py:1654
  248.4 11.8 %attention_forward.1 = (bf16[256,1536]{1,0:T(8,128)(2,1)}, bf16[256,1536]{1,0:T(8,128)(2,1)}, f32[8,512]{1,0:T(8,128)}, bf16[1536,512]{1,0:T(8,128)(2,1)}, bf16[...) custom-call(s32[1440]{0:T(1024)} %copy-done.3, f32[1,1536]{1,0:T(1,128)} %slice.50.gain_ref.gain, f32[1,1024]{1,0:T(1,128)} %bitcast.26, ...), custom_call_target="tpu_custom_call" | custom-call | tf_op jit(solution)/shard_map/attention_forward/pallas_call | solution.py:827
  260.2 1.5 collective-permute-start.2
  261.8 17.1 %active_grads.1 = (f32[6,512,768]{2,1,0:T(8,128)}, bf16[6,768,1536]{2,1,0:T(8,128)(2,1)}) custom-call(s32[1440]{0:T(1024)} %copy-done.3, bf16[512,1536]{1,0:T(8,128)(2,1)} %maximum_select_fusion.1.cot_ref.cot_hbm, bf16[1440,128,128]{2,1,0:T(8,128)(2,1)} %all-gather.3.cloned.1.call-done.weights), custom_call_target="tpu_custom_call" | custom-call | flops 7247757312 | bytes 23592960 | tf_op jit(solution)/shard_map/active_grads/pallas_call | solution.py:862
  278.8 1.4 collective-permute-done.2.other_ref
  280.2 1.5 collective-permute-start.4
  281.7 24.2 %hidden_grads.2 = (bf16[256,1536]{1,0:T(8,128)(2,1)}, f32[256,1536]{1,0:T(8,128)}, bf16[1536,256]{1,0:T(8,128)(2,1)}, bf16[6,256,1536]{2,1,0:T(8,128)(2,1)}, bf1...) custom-call(s32[1440]{0:T(1024)} %copy-done.3, f32[1,1536]{1,0:T(1,128)} %slice.52.gain_ref, ...), custom_call_target="tpu_custom_call" | custom-call | flops 14495514624 | bytes 42467328 | tf_op jit(solution)/shard_map/hidden_grads/pallas_call | solution.py:886
  305.9 0.6 collective-permute-start.3
  306.5 0.0 collective-permute-done.4.other_ref
  306.5 23.8 %hidden_grads.3 = (bf16[256,1536]{1,0:T(8,128)(2,1)}, f32[256,1536]{1,0:T(8,128)}, bf16[1536,256]{1,0:T(8,128)(2,1)}, bf16[6,256,1536]{2,1,0:T(8,128)(2,1)}, bf1...) custom-call(s32[1440]{0:T(1024)} %copy-done.3, f32[1,1536]{1,0:T(1,128)} %slice.52.gain_ref, ...), custom_call_target="tpu_custom_call" | custom-call | flops 14495514624 | bytes 42467328 | tf_op jit(solution)/shard_map/hidden_grads/pallas_call | solution.py:886
  330.4 1.5 collective-permute-start.5
  331.9 28.2 %hidden_weight_grads.1.grads_in = bf16[1456,128,128]{2,1,0:T(8,128)(2,1)} custom-call(s32[1440]{0:T(1024)} %fusion.3.rows_ref, bf16[512,1536]{1,0:T(8,128)(2,1)} %maximum_select_fusion.1.cot_ref.cot_hbm, bf16[1536,256]{1,0:T(8,128)(2,1)} %get-tuple-element.88.refs_0_, bf16[6,256,1536]{2,1,0:T(8,128)(2,1)} %get-tuple-element.89.refs_1_, ...), custom_call_target="tpu_custom_call" | custom-call | flops 21743271936 | bytes 56623104 | tf_op jit(solution)/shard_map/hidden_weight_grads/pallas_call | solution.py:922
  360.1 0.0 collective-permute-done.3.other_low_ref
  360.1 0.0 collective-permute-done.5.other_high_ref
  360.1 23.4 %attention_backward.1 = (f32[256,1536]{1,0:T(8,128)}, bf16[256,1536]{1,0:T(8,128)(2,1)}, bf16[256,1536]{1,0:T(8,128)(2,1)}, bf16[1456,128,128]{2,1,0:T(8,128)(2,1)}) custom-call(s32[1440]{0:T(1024)} %copy-done.3, s32[1440]{0:T(1024)} %fusion.3.rows_ref, s32[1]{0:T(128)} %bitcast.2.half_ref, ...), custom_call_target="tpu_custom_call", output_to_operand_aliasing={{3}: (20, {})} | custom-call | tf_op jit(solution)/shard_map/attention_backward/pallas_call | solution.py:953
  383.5 254.6 %sum_for_owners.1 = (bf16[91,128,128]{2,1,0:T(8,128)(2,1)S(1)}, f32[90,128,128]{2,1,0:T(8,128)S(1)}, f32[90,128,128]{2,1,0:T(8,128)S(1)}, f32[90,128,128]{2,1,0:...) custom-call(bf16[4,2,2,91,128,128]{5,4,3,2,1,0:T(8,128)(2,1)} %bitca, ...), custom_call_target="tpu_custom_call" | custom-call | bytes 381681664 | tf_op jit(solution)/shard_map/sum_for_owners/pallas_call | solution.py:1480
  638.1 0.0 copy-start.6
  638.1 0.0 copy-start.7
  638.1 0.0 copy-start.8
  638.1 0.0 copy-start.10
  638.2 0.0 copy-start.11
  638.2 0.0 copy-start.12
  638.2 10.6 %write_results.1 = (f32[90,128,128]{2,1,0:T(8,128)}, f32[90,128,128]{2,1,0:T(8,128)}, f32[90,128,128]{2,1,0:T(8,128)}, f32[90,128,128]{2,1,0:T(8,128)}, f32[256,...) custom-call(bf16[91,128,128]{2,1,0:T(8,128)(2,1)S(1)} %get-tuple-element.101.reduced, ...), custom_call_target="tpu_custom_call" | custom-call | tf_op jit(solution)/shard_map/write_results/pallas_call | solution.py:1569
  648.9 0.6 divide_subtract_fusion
  649.5 0.6 divide_subtract_fusion.1
  (30 shorter events, 0.2 us)
Async XLA Ops:
  7.2 9.5 %copy-start.9 = (f32[96]{0:T(128)S(1)}, f32[96]{0:T(128)}, u32[]{:S(2)}) copy-start(f32[96]{0:T(128)} %param.24) | copy-start | bytes 1156
  7.2 4.5 copy-start
  7.2 7.6 %copy-start.2 = (bf16[256,1536]{1,0:T(8,128)(2,1)S(1)}, bf16[256,1536]{1,0:T(8,128)(2,1)}, u32[]{:S(2)}) copy-start(bf16[256,1536]{1,0:T(8,128)(2,1)} %param.16) | copy-start | bytes 2359300
  7.2 9.0 %copy-start.4 = (s32[1440]{0:T(1024)S(1)}, s32[1440]{0:T(1024)}, u32[]{:S(2)}) copy-start(s32[1440]{0:T(1024)} %param.18) | copy-start | bytes 17284
  7.2 241.2 %all-gather.3.cloned.1.call-start = ((), (), s32[]{:S(2)}) async-start(), calls=%async_computation | async-start | bytes 50135040 | tf_op jit(solution)/shard_map/all_gather | solution.py:1654
  11.7 76.0 %copy-start.5 = (f32[1,64]{1,0:T(1,128)S(1)}, f32[1,64]{1,0:T(1,128)}, u32[]{:S(2)}) copy-start(f32[1,64]{1,0:T(1,128)} %param.27) | copy-start | bytes 772
  11.7 78.5 %copy-start.13 = (u32[32]{0:T(128)S(1)}, u32[32]{0:T(128)}, u32[]{:S(2)}) copy-start(u32[32]{0:T(128)} %constant.116) | copy-start | bytes 388
  11.7 121.1 %collective-permute-start = (bf16[256,1536]{1,0:T(8,128)(2,1)S(1)}, bf16[256,1536]{1,0:T(8,128)(2,1)S(1)}, u32[]{:S(2)}, u32[]{:S(2)}) collective-permute-start(bf16[256,1536]{1,0:T(8,128)(2,1)S(1)} %copy-done), channel_id=1, source_target_pairs={{0,1},{1,0},{2,3},{3,2},{4,5},{5,4},{6,7},{7,6},{8,9},{9,8},{10,11... | collective-permute-start | bytes 2359304 | tf_op jit(solution)/shard_map/ppermute | solution.py:1615
  14.8 119.8 %collective-permute-start.1 = (bf16[256,1536]{1,0:T(8,128)(2,1)S(1)}, bf16[256,1536]{1,0:T(8,128)(2,1)S(1)}, u32[]{:S(2)}, u32[]{:S(2)}) collective-permute-start(bf16[256,1536]{1,0:T(8,128)(2,1)S(1)} %copy-done.2), channel_id=1, source_target_pairs={{0,1},{1,0},{2,3},{3,2},{4,5},{5,4},{6,7},{7,6},{8,9},{9,8},{10,11... | collective-permute-start | bytes 2359304 | tf_op jit(solution)/shard_map/ppermute | solution.py:1615
  131.0 5.4 copy-start.3
  260.2 20.0 %collective-permute-start.2 = (bf16[256,1536]{1,0:T(8,128)(2,1)}, bf16[256,1536]{1,0:T(8,128)(2,1)S(1)}, u32[]{:S(2)}, u32[]{:S(2)}) collective-permute-start(bf16[256,1536]{1,0:T(8,128)(2,1)} %get-tuple-element.76.own_hbm), channel_id=1, source_target_pairs={{0,1},{1,0},{2,3},{3,2},{4,5},{5,4},{6,7},{7,6},{8,9},{9,8},{10,11... | collective-permute-start | bytes 2359304 | tf_op jit(solution)/shard_map/ppermute | solution.py:1615
  261.8 18.4 %copy-start.1 = (bf16[256,1536]{1,0:T(8,128)(2,1)S(1)}, bf16[256,1536]{1,0:T(8,128)(2,1)}, u32[]{:S(2)}) copy-start(bf16[256,1536]{1,0:T(8,128)(2,1)} %get-tuple-element.81.own_hbm) | copy-start | bytes 2359300
  280.2 26.3 %collective-permute-start.4 = (bf16[256,1536]{1,0:T(8,128)(2,1)S(1)}, bf16[256,1536]{1,0:T(8,128)(2,1)S(1)}, u32[]{:S(2)}, u32[]{:S(2)}) collective-permute-start(bf16[256,1536]{1,0:T(8,128)(2,1)S(1)} %copy-done.1), channel_id=1, source_target_pairs={{0,1},{1,0},{2,3},{3,2},{4,5},{5,4},{6,7},{7,6},{8,9},{9,8},{10,11... | collective-permute-start | bytes 2359304 | tf_op jit(solution)/shard_map/ppermute | solution.py:1615
  305.9 54.2 %collective-permute-start.3 = (bf16[256,1536]{1,0:T(8,128)(2,1)}, bf16[256,1536]{1,0:T(8,128)(2,1)S(1)}, u32[]{:S(2)}, u32[]{:S(2)}) collective-permute-start(bf16[256,1536]{1,0:T(8,128)(2,1)} %get-tuple-element.80.own_low_hbm), channel_id=1, source_target_pairs={{0,1},{1,0},{2,3},{3,2},{4,5},{5,4},{6,7},{7,6},{8,9},{9,8},{10,11... | collective-permute-start | bytes 2359304 | tf_op jit(solution)/shard_map/ppermute | solution.py:1615
  330.4 29.7 %collective-permute-start.5 = (bf16[256,1536]{1,0:T(8,128)(2,1)}, bf16[256,1536]{1,0:T(8,128)(2,1)S(1)}, u32[]{:S(2)}, u32[]{:S(2)}) collective-permute-start(bf16[256,1536]{1,0:T(8,128)(2,1)} %get-tuple-element.82.own_high_hbm), channel_id=1, source_target_pairs={{0,1},{1,0},{2,3},{3,2},{4,5},{5,4},{6,7},{7,6},{8,9},{9,8},{10,11... | collective-permute-start | bytes 2359304 | tf_op jit(solution)/shard_map/ppermute | solution.py:1615
  638.1 10.7 %copy-start.6 = (f32[1,64]{1,0:T(1,128)S(1)}, f32[1,64]{1,0:T(1,128)}, u32[]{:S(2)}) copy-start(f32[1,64]{1,0:T(1,128)} %param.27) | copy-start | bytes 772
  638.1 10.7 %copy-start.7 = (f32[1,64]{1,0:T(1,128)S(1)}, f32[1,64]{1,0:T(1,128)}, u32[]{:S(2)}) copy-start(f32[1,64]{1,0:T(1,128)} %param.28) | copy-start | bytes 772
  638.1 10.7 %copy-start.8 = (f32[1,64]{1,0:T(1,128)S(1)}, f32[1,64]{1,0:T(1,128)}, u32[]{:S(2)}) copy-start(f32[1,64]{1,0:T(1,128)} %param.29) | copy-start | bytes 772
  638.1 11.3 %copy-start.10 = (f32[96]{0:T(128)S(1)}, f32[96]{0:T(128)}, u32[]{:S(2)}) copy-start(f32[96]{0:T(128)} %param.24) | copy-start | bytes 1156
  638.2 11.3 %copy-start.11 = (f32[96]{0:T(128)S(1)}, f32[96]{0:T(128)}, u32[]{:S(2)}) copy-start(f32[96]{0:T(128)} %param.25) | copy-start | bytes 1156
  638.2 11.3 %copy-start.12 = (f32[96]{0:T(128)S(1)}, f32[96]{0:T(128)}, u32[]{:S(2)}) copy-start(f32[96]{0:T(128)} %param.26) | copy-start | bytes 1156
Sparse Core Ops, SparseCore 0:
  11.8 236.5 all-gather.2
